TPU v7x, 32 devices: a whole 2x2x4 slice. The times are simulated.
32 devices in a mesh: section: 2 (over core), dp: 4 (over y, x), head: 4 (over z).
Axes of the slice: x: 2, y: 2, z: 4, core: 2. Of those that a mesh axis runs over, the one named last changes fastest.
Arguments:
- hidden_in: bfloat16 [8, 2048, 1024], P('dp', 'head'), may hold values from -6 to 6
- lengths: int32 [8, 16], P('dp'), may hold values from 0 to 2048, as said below
- w_query: bfloat16 [2, 1024, 1024], P('section', None, 'head'), may hold values from -0.1875 to 0.1875
- w_key: bfloat16 [2, 1024, 1024], P('section', None, 'head'), may hold values from -0.1875 to 0.1875
- w_value: bfloat16 [2, 1024, 1024], P('section', None, 'head'), may hold values from -0.1875 to 0.1875
- w_out: bfloat16 [2, 1024, 1024], P('section', 'head'), may hold values from -3 to 3
- w_gate: bfloat16 [2, 1024, 2816], P('section', None, 'head'), may hold values from -0.1875 to 0.1875
- w_up: bfloat16 [2, 1024, 2816], P('section', None, 'head'), may hold values from -0.1875 to 0.1875
- w_down: bfloat16 [2, 2816, 1024], P('section', 'head'), may hold values from -0.109375 to 0.109375
- attn_gain: float32 [2, 1024], P('section'), may hold values from 0.5 to 1.5
- ffn_gain: float32 [2, 1024], P('section'), may hold values from 0.5 to 1.5
- cotangent: float32 [8, 2048, 1024], P('dp', 'head'), may hold values from -6 to 6
Outputs:
- layer_outputs: bfloat16 [2, 8, 2048, 1024], P('section', 'dp', 'head')
- input_grads: float32 [2, 8, 2048, 1024], P('section', 'dp', 'head')
- grad_query: float32 [2, 1024, 1024], P('section', None, 'head')
- grad_key: float32 [2, 1024, 1024], P('section', None, 'head')
- grad_value: float32 [2, 1024, 1024], P('section', None, 'head')
- grad_out: float32 [2, 1024, 1024], P('section', 'head')
- grad_gate: float32 [2, 1024, 2816], P('section', None, 'head')
- grad_up: float32 [2, 1024, 2816], P('section', None, 'head')
- grad_down: float32 [2, 2816, 1024], P('section', 'head')
- grad_attn_gain: float32 [2, 1024], P('section')
- grad_ffn_gain: float32 [2, 1024], P('section')
Inputs may be any that keep to these rules, and one draw needn't show every extreme that they name: Each row lists the lengths of its sequences in slot order, then zeros; every nonzero length is 128 or more; rounded up to multiples of 128, a row's lengths fill exactly 2048 slots.
All inputs are finite; a program needn't handle non-finite values.
Results may differ from a plain program's by a relative error of at most 0.038.
Values may be sent and summed in bfloat16 or wider, within the bound.
No kernel may reach another device: no remote copies, remote signals or barrier semaphores. Data moves between devices by JAX's collectives and lax.ppermute only.
A program may use at most 512 MiB of HBM per device.

v0:
```python
import jax
import jax.numpy as jnp
from jax import lax
from jax.sharding import PartitionSpec as P

D = 1024
HD = 64
SLOTS = 2048
PAD = 128


EPSILON = 1e-05
MASKED = -1e30


def from_behind(block, axis, distance):
    devices = range(lax.axis_size(axis))
    route = [(i - distance, i) for i in devices if i - distance in devices]
    return lax.ppermute(block, axis, route)


def slot_tables(length_row):
    padded = (length_row + PAD - 1) // PAD * PAD
    starts = jnp.cumsum(padded) - padded
    slots = jnp.arange(SLOTS, dtype=jnp.int32)
    docs = jnp.arange(length_row.shape[0], dtype=jnp.int32)
    inside = (slots[:, None] >= starts[None, :]) & (slots[:, None] < (starts + padded)[None, :])
    segment = jnp.sum(jnp.where(inside, docs[None, :], 0), axis=1)
    begin = jnp.sum(jnp.where(inside, starts[None, :], 0), axis=1)
    live = (
        jnp.sum(jnp.where(inside & (slots[:, None] < (starts + length_row)[None, :]), 1, 0), axis=1)
        > 0
    )
    freq = 10000.0 ** (-2.0 * jnp.arange(HD // 2, dtype=jnp.float32) / HD)
    angle = (slots - begin).astype(jnp.float32)[:, None] * freq[None, :]
    cosine = jnp.concatenate([jnp.cos(angle), jnp.cos(angle)], axis=1)
    sine = jnp.concatenate([jnp.sin(angle), jnp.sin(angle)], axis=1)
    return (segment, live, cosine, sine)


def rms_norm(rows, gain):
    inverse = lax.rsqrt(jnp.mean(rows * rows, axis=1, keepdims=True) + EPSILON)
    return rows * inverse * gain


def norm_back(rows, gain, grad):
    inverse = lax.rsqrt(jnp.mean(rows * rows, axis=1, keepdims=True) + EPSILON)
    scaled = grad * gain
    gain_grad = jnp.sum(grad * rows * inverse, axis=0)
    rows_grad = inverse * scaled - rows * inverse**3 * jnp.mean(
        scaled * rows, axis=1, keepdims=True
    )
    return (rows_grad, gain_grad)


def rotary(rows, cosine, sine, sign):
    shaped = rows.reshape(rows.shape[0], -1, HD)
    half = HD // 2
    turned = jnp.concatenate([-sign * shaped[..., half:], sign * shaped[..., :half]], axis=2)
    return (shaped * cosine[:, None, :] + turned * sine[:, None, :]).reshape(rows.shape)


def block_mask(segment, live, start, block):
    positions = jnp.arange(segment.shape[0], dtype=jnp.int32)
    rows = start + jnp.arange(block, dtype=jnp.int32)
    own_segment = segment[start : start + block]
    return (
        (own_segment[:, None] == segment[None, :])
        & (positions[None, :] <= rows[:, None])
        & live[None, :]
    )


def attend(query_rows, key_rows, value_rows, segment, live):
    total = query_rows.shape[0]
    block = min(512, total)
    queries = query_rows.reshape(total, -1, HD)
    key_heads = key_rows.reshape(total, -1, HD)
    value_heads = value_rows.reshape(total, -1, HD)
    outputs = []
    sums = []
    for index in range(total // block):
        start = index * block
        scores = jnp.einsum(
            "qhd,khd->hqk",
            queries[start : start + block],
            key_heads,
            preferred_element_type=jnp.float32,
        ) * HD ** (-0.5)
        scores = jnp.where(block_mask(segment, live, start, block)[None], scores, MASKED)
        peak = jnp.max(scores, axis=2, keepdims=True)
        weights = jnp.exp(scores - peak)
        mass = jnp.sum(weights, axis=2, keepdims=True)
        probs = (weights / mass).astype(jnp.bfloat16)
        outputs.append(
            jnp.einsum("hqk,khd->qhd", probs, value_heads, preferred_element_type=jnp.float32)
        )
        sums.append((peak + jnp.log(mass))[..., 0])
    attended = jnp.concatenate(outputs, axis=0).reshape(total, -1).astype(jnp.bfloat16)
    return (attended, jnp.concatenate(sums, axis=1))


def attend_back(query_rows, key_rows, value_rows, out_grad, sums, segment, live):
    total = query_rows.shape[0]
    block = min(512, total)
    queries = query_rows.reshape(total, -1, HD)
    key_heads = key_rows.reshape(total, -1, HD)
    value_heads = value_rows.reshape(total, -1, HD)
    grad_heads = out_grad.reshape(total, -1, HD)
    key_grad = jnp.zeros(key_heads.shape, jnp.float32)
    value_grad = jnp.zeros(value_heads.shape, jnp.float32)
    query_grads = []
    for index in range(total // block):
        start = index * block
        query_block = queries[start : start + block]
        grad_block = grad_heads[start : start + block]
        scores = jnp.einsum(
            "qhd,khd->hqk", query_block, key_heads, preferred_element_type=jnp.float32
        ) * HD ** (-0.5)
        scores = jnp.where(block_mask(segment, live, start, block)[None], scores, MASKED)
        probs = jnp.exp(scores - sums[:, start : start + block, None])
        prob_grad = jnp.einsum(
            "qhd,khd->hqk", grad_block, value_heads, preferred_element_type=jnp.float32
        )
        score_grad = (
            probs * (prob_grad - jnp.sum(probs * prob_grad, axis=2, keepdims=True))
        ).astype(jnp.bfloat16)
        query_grads.append(
            jnp.einsum("hqk,khd->qhd", score_grad, key_heads, preferred_element_type=jnp.float32)
            * HD ** (-0.5)
        )
        key_grad = key_grad + jnp.einsum(
            "hqk,qhd->khd", score_grad, query_block, preferred_element_type=jnp.float32
        ) * HD ** (-0.5)
        value_grad = value_grad + jnp.einsum(
            "hqk,qhd->khd",
            probs.astype(jnp.bfloat16),
            grad_block,
            preferred_element_type=jnp.float32,
        )
    query_grad = jnp.concatenate(query_grads, axis=0).reshape(total, -1)
    return (query_grad, key_grad.reshape(total, -1), value_grad.reshape(total, -1))


def layer_forward(rows, first_values, own_share, other_share, weights, tables):
    w_query, w_key, w_value, w_out, w_gate, w_up, w_down, attn_gain, ffn_gain = weights
    segment, live, cosine, sine = tables
    normed = rms_norm(rows, attn_gain).astype(jnp.bfloat16)
    gathered = lax.all_gather(normed, "head", axis=0, tiled=True)
    query_rows = rotary(
        jnp.dot(gathered, w_query, preferred_element_type=jnp.float32), cosine, sine, 1.0
    ).astype(jnp.bfloat16)
    key_rows = rotary(
        jnp.dot(gathered, w_key, preferred_element_type=jnp.float32), cosine, sine, 1.0
    ).astype(jnp.bfloat16)
    own_values = jnp.dot(gathered, w_value, preferred_element_type=jnp.float32).astype(jnp.bfloat16)
    mixed = (
        own_share * own_values.astype(jnp.float32) + other_share * first_values.astype(jnp.float32)
    ).astype(jnp.bfloat16)
    attended, sums = attend(query_rows, key_rows, mixed, segment, live)
    middle = rows + lax.psum_scatter(
        jnp.dot(attended, w_out, preferred_element_type=jnp.float32).astype(jnp.bfloat16),
        "head",
        scatter_dimension=0,
        tiled=True,
    ).astype(jnp.float32)
    ffn_normed = rms_norm(middle, ffn_gain).astype(jnp.bfloat16)
    ffn_input = lax.all_gather(ffn_normed, "head", axis=0, tiled=True)
    gate_rows = jnp.dot(ffn_input, w_gate, preferred_element_type=jnp.float32)
    up_rows = jnp.dot(ffn_input, w_up, preferred_element_type=jnp.float32)
    activation = (jax.nn.silu(gate_rows) * up_rows).astype(jnp.bfloat16)
    result = middle + lax.psum_scatter(
        jnp.dot(activation, w_down, preferred_element_type=jnp.float32).astype(jnp.bfloat16),
        "head",
        scatter_dimension=0,
        tiled=True,
    ).astype(jnp.float32)
    kept = (
        rows,
        gathered,
        query_rows,
        key_rows,
        mixed,
        attended,
        sums,
        middle,
        ffn_input,
        gate_rows,
        up_rows,
        activation,
    )
    return (result, own_values, kept)


def layer_backward(grad_result, first_grad, own_share, other_share, weights, kept, tables):
    w_query, w_key, w_value, w_out, w_gate, w_up, w_down, attn_gain, ffn_gain = weights
    (
        rows,
        gathered,
        query_rows,
        key_rows,
        mixed,
        attended,
        sums,
        middle,
        ffn_input,
        gate_rows,
        up_rows,
        activation,
    ) = kept
    segment, live, cosine, sine = tables
    down_grad = lax.all_gather(grad_result.astype(jnp.bfloat16), "head", axis=0, tiled=True)
    grad_down = jnp.dot(activation.T, down_grad, preferred_element_type=jnp.float32)
    act_grad = jnp.dot(down_grad, w_down.T, preferred_element_type=jnp.float32)
    sigma = jax.nn.sigmoid(gate_rows)
    gate_grad = (act_grad * up_rows * sigma * (1.0 + gate_rows * (1.0 - sigma))).astype(
        jnp.bfloat16
    )
    up_grad = (act_grad * gate_rows * sigma).astype(jnp.bfloat16)
    grad_gate = jnp.dot(ffn_input.T, gate_grad, preferred_element_type=jnp.float32)
    grad_up = jnp.dot(ffn_input.T, up_grad, preferred_element_type=jnp.float32)
    normed_grad = lax.psum_scatter(
        (
            jnp.dot(gate_grad, w_gate.T, preferred_element_type=jnp.float32)
            + jnp.dot(up_grad, w_up.T, preferred_element_type=jnp.float32)
        ).astype(jnp.bfloat16),
        "head",
        scatter_dimension=0,
        tiled=True,
    ).astype(jnp.float32)
    middle_back, grad_ffn_gain = norm_back(middle, ffn_gain, normed_grad)
    middle_grad = grad_result + middle_back
    attn_grad = lax.all_gather(middle_grad.astype(jnp.bfloat16), "head", axis=0, tiled=True)
    grad_out = jnp.dot(attended.T, attn_grad, preferred_element_type=jnp.float32)
    attended_grad = jnp.dot(attn_grad, w_out.T, preferred_element_type=jnp.float32).astype(
        jnp.bfloat16
    )
    query_grad, key_grad, mixed_grad = attend_back(
        query_rows, key_rows, mixed, attended_grad, sums, segment, live
    )
    query_grad = rotary(query_grad, cosine, sine, -1.0).astype(jnp.bfloat16)
    key_grad = rotary(key_grad, cosine, sine, -1.0).astype(jnp.bfloat16)
    value_grad = (own_share * mixed_grad + first_grad.astype(jnp.float32)).astype(jnp.bfloat16)
    first_out = (other_share * mixed_grad).astype(jnp.bfloat16)
    grad_query = jnp.dot(gathered.T, query_grad, preferred_element_type=jnp.float32)
    grad_key = jnp.dot(gathered.T, key_grad, preferred_element_type=jnp.float32)
    grad_value = jnp.dot(gathered.T, value_grad, preferred_element_type=jnp.float32)
    total = jnp.dot(query_grad, w_query.T, preferred_element_type=jnp.float32)
    total = total + jnp.dot(key_grad, w_key.T, preferred_element_type=jnp.float32)
    input_back = lax.psum_scatter(
        (total + jnp.dot(value_grad, w_value.T, preferred_element_type=jnp.float32)).astype(
            jnp.bfloat16
        ),
        "head",
        scatter_dimension=0,
        tiled=True,
    ).astype(jnp.float32)
    rows_back, grad_attn_gain = norm_back(rows, attn_gain, input_back)
    grads = (
        grad_query,
        grad_key,
        grad_value,
        grad_out,
        grad_gate,
        grad_up,
        grad_down,
        grad_attn_gain,
        grad_ffn_gain,
    )
    return (middle_grad + rows_back, first_out, grads)


def local(
    hidden_in,
    lengths,
    w_query,
    w_key,
    w_value,
    w_out,
    w_gate,
    w_up,
    w_down,
    attn_gain,
    ffn_gain,
    cotangent,
):
    section = lax.axis_index("section")
    first_section = section == 0
    own_share = jnp.where(first_section, 1.0, 0.5).astype(jnp.float32)
    other_share = jnp.where(first_section, 0.0, 0.5).astype(jnp.float32)
    weights = tuple(
        (
            item[0]
            for item in (w_query, w_key, w_value, w_out, w_gate, w_up, w_down, attn_gain, ffn_gain)
        )
    )
    batches = hidden_in.shape[0]
    count = hidden_in.shape[1]
    width = w_query.shape[2]
    tables_all = jax.vmap(slot_tables)(lengths)
    received = (jnp.zeros((count, D), jnp.bfloat16), jnp.zeros((SLOTS, width), jnp.bfloat16))
    outputs = []
    kept_list = []
    for tick in range(batches + 1):
        micro = jnp.clip(tick - section, 0, batches - 1)
        tables = tuple((item[micro] for item in tables_all))
        rows = jnp.where(
            first_section, hidden_in[micro].astype(jnp.float32), received[0].astype(jnp.float32)
        )
        result, own_values, kept = layer_forward(
            rows, received[1], own_share, other_share, weights, tables
        )
        sent = result.astype(jnp.bfloat16)
        outputs.append(sent)
        kept_list.append(kept)
        if tick < batches:
            received = from_behind((sent, own_values), "section", 1)
    back_received = (jnp.zeros((count, D), jnp.bfloat16), jnp.zeros((SLOTS, width), jnp.bfloat16))
    grads_list = []
    totals = None
    for tick in range(batches + 1):
        micro_raw = tick - 1 + section
        micro = jnp.clip(micro_raw, 0, batches - 1)
        tables = tuple((item[micro] for item in tables_all))
        early = kept_list[max(tick - 1, 0)]
        late = kept_list[min(tick + 1, batches)]
        kept = jax.tree.map(lambda a, b: jnp.where(first_section, a, b), early, late)
        grad_result = jnp.where(
            first_section, back_received[0].astype(jnp.float32), cotangent[micro]
        )
        grad_in, first_out, layer_grads = layer_backward(
            grad_result, back_received[1], own_share, other_share, weights, kept, tables
        )
        sent = grad_in.astype(jnp.bfloat16)
        grads_list.append(jnp.where(first_section, grad_in, sent.astype(jnp.float32)))
        live_tick = (micro_raw >= 0) & (micro_raw < batches)
        layer_grads = tuple((jnp.where(live_tick, item, 0.0) for item in layer_grads))
        totals = (
            layer_grads if totals is None else tuple((a + b for a, b in zip(totals, layer_grads)))
        )
        if tick < batches:
            back_received = from_behind((sent, first_out), "section", -1)
    layer_outputs = jnp.stack(
        [jnp.where(first_section, outputs[m], outputs[m + 1]) for m in range(batches)]
    )[None]
    input_grads = jnp.stack(
        [jnp.where(first_section, grads_list[m + 1], grads_list[m]) for m in range(batches)]
    )[None]
    summed = (
        lax.psum(totals[0].astype(jnp.bfloat16), "dp").astype(jnp.float32),
        lax.psum(totals[1].astype(jnp.bfloat16), "dp").astype(jnp.float32),
        lax.psum(totals[2].astype(jnp.bfloat16), "dp").astype(jnp.float32),
        lax.psum(totals[3].astype(jnp.bfloat16), "dp").astype(jnp.float32),
        lax.psum(totals[4].astype(jnp.bfloat16), "dp").astype(jnp.float32),
        lax.psum(totals[5].astype(jnp.bfloat16), "dp").astype(jnp.float32),
        lax.psum(totals[6].astype(jnp.bfloat16), "dp").astype(jnp.float32),
        lax.psum(totals[7].astype(jnp.bfloat16), "dp").astype(jnp.float32),
        lax.psum(totals[8].astype(jnp.bfloat16), "dp").astype(jnp.float32),
    )
    gains = lax.psum((summed[7], summed[8]), "head")
    return (
        layer_outputs,
        input_grads,
        summed[0][None],
        summed[1][None],
        summed[2][None],
        summed[3][None],
        summed[4][None],
        summed[5][None],
        summed[6][None],
        gains[0][None],
        gains[1][None],
    )


def solution(mesh):
    in_specs = (
        P("dp", "head", None),
        P("dp", None),
        P("section", None, "head"),
        P("section", None, "head"),
        P("section", None, "head"),
        P("section", "head", None),
        P("section", None, "head"),
        P("section", None, "head"),
        P("section", "head", None),
        P("section", None),
        P("section", None),
        P("dp", "head", None),
    )
    out_specs = (
        P("section", "dp", "head", None),
        P("section", "dp", "head", None),
        P("section", None, "head"),
        P("section", None, "head"),
        P("section", None, "head"),
        P("section", "head", None),
        P("section", None, "head"),
        P("section", None, "head"),
        P("section", "head", None),
        P("section", None),
        P("section", None),
    )
    return jax.shard_map(local, mesh=mesh, in_specs=in_specs, out_specs=out_specs, check_vma=False)
```

profile of v0, /device:TPU:0, one launch (start us, length us, event | category | flops | bytes accessed | tf_op | source)
XLA Modules:
  0.0 2977.1 jit_solution(12615338573561688170)
XLA Ops:
  28.4 66.8 %all-gather.13.cloned.1.call-done = bf16[2048,1024]{1,0:T(8,128)(2,1)} async-done(((bf16[512,1024]{1,0:T(8,128)(2,1)}), bf16[2048,1024]{1,0:T(8,128)(2,1)}) %all-gather.13.cloned.1.call-update) | async-done | bytes 4194320 | tf_op jit(solution)/shard_map/all_gather | solution.py:149
  177.4 75.4 %reduce-scatter.13.cloned.1.call-done = bf16[512,1024]{1,0:T(8,128)(2,1)} async-done(((bf16[2048,1024]{1,0:T(8,128)(2,1)}), bf16[512,1024]{1,0:T(8,128)(2,1)}) %reduce-scatter.13.cloned.1.call-update) | async-done | bytes 1048592 | tf_op jit(solution)/shard_map/reduce_scatter | solution.py:161
  257.2 81.4 %all-gather.15.cloned.1.call-done = bf16[2048,1024]{1,0:T(8,128)(2,1)} async-done(((bf16[512,1024]{1,0:T(8,128)(2,1)}), bf16[2048,1024]{1,0:T(8,128)(2,1)}) %all-gather.15.cloned.1.call-update) | async-done | bytes 4194320 | tf_op jit(solution)/shard_map/all_gather | solution.py:168
  356.9 75.4 %reduce-scatter.15.cloned.1.call-done = bf16[512,1024]{1,0:T(8,128)(2,1)} async-done(((bf16[2048,1024]{1,0:T(8,128)(2,1)}), bf16[512,1024]{1,0:T(8,128)(2,1)}) %reduce-scatter.15.cloned.1.call-update) | async-done | bytes 1048592 | tf_op jit(solution)/shard_map/reduce_scatter | solution.py:172
  451.7 71.1 %all-gather.17.cloned.1.call-done = bf16[2048,1024]{1,0:T(8,128)(2,1)} async-done(((bf16[512,1024]{1,0:T(8,128)(2,1)}), bf16[2048,1024]{1,0:T(8,128)(2,1)}) %all-gather.17.cloned.1.call-update) | async-done | bytes 4194320 | tf_op jit(solution)/shard_map/all_gather | solution.py:149
  586.0 9.3 fusion.324
  634.0 75.4 %reduce-scatter.17.cloned.1.call-done = bf16[512,1024]{1,0:T(8,128)(2,1)} async-done(((bf16[2048,1024]{1,0:T(8,128)(2,1)}), bf16[512,1024]{1,0:T(8,128)(2,1)}) %reduce-scatter.17.cloned.1.call-update) | async-done | bytes 1048592 | tf_op jit(solution)/shard_map/reduce_scatter | solution.py:161
  718.9 78.5 %all-gather.19.cloned.1.call-done = bf16[2048,1024]{1,0:T(8,128)(2,1)} async-done(((bf16[512,1024]{1,0:T(8,128)(2,1)}), bf16[2048,1024]{1,0:T(8,128)(2,1)}) %all-gather.19.cloned.1.call-update) | async-done | bytes 4194320 | tf_op jit(solution)/shard_map/all_gather | solution.py:168
  810.9 68.0 %all-gather.25.cloned.1.call-done = bf16[2048,1024]{1,0:T(8,128)(2,1)} async-done(((bf16[512,1024]{1,0:T(8,128)(2,1)}), bf16[2048,1024]{1,0:T(8,128)(2,1)}) %all-gather.25.cloned.1.call-update) | async-done | bytes 4194320 | tf_op jit(solution)/shard_map/all_gather | solution.py:212
  878.9 13.2 multiply_convert_fusion.16
  901.6 74.8 %reduce-scatter.25.cloned.1.call-done = bf16[512,1024]{1,0:T(8,128)(2,1)} async-done(((bf16[2048,1024]{1,0:T(8,128)(2,1)}), bf16[512,1024]{1,0:T(8,128)(2,1)}) %reduce-scatter.25.cloned.1.call-update) | async-done | bytes 1048592 | tf_op jit(solution)/shard_map/reduce_scatter | solution.py:222
  1031.9 32.7 %all-gather.27.cloned.1.call-done = bf16[2048,1024]{1,0:T(8,128)(2,1)} async-done(((bf16[512,1024]{1,0:T(8,128)(2,1)}), bf16[2048,1024]{1,0:T(8,128)(2,1)}) %all-gather.27.cloned.1.call-update) | async-done | bytes 4194320 | tf_op jit(solution)/shard_map/all_gather | solution.py:233
  1068.5 13.1 multiply_reduce_fusion.11
  1081.6 12.3 multiply_convert_fusion.11
  1098.2 12.7 multiply_reduce_fusion.10
  1110.9 12.4 multiply_convert_fusion.10
  1127.6 12.5 multiply_reduce_fusion.9
  1140.1 12.2 multiply_convert_fusion.9
  1156.6 12.9 multiply_reduce_fusion.8
  1169.5 12.1 multiply_convert_fusion.8
  1206.4 9.6 fusion.54
  1216.0 9.6 fusion.52
  1234.3 9.4 add_convert_fusion.4
  1252.4 66.7 %reduce-scatter.27.cloned.1.call-done = bf16[512,1024]{1,0:T(8,128)(2,1)} async-done(((bf16[2048,1024]{1,0:T(8,128)(2,1)}), bf16[512,1024]{1,0:T(8,128)(2,1)}) %reduce-scatter.27.cloned.1.call-update) | async-done | bytes 1048592 | tf_op jit(solution)/shard_map/reduce_scatter | solution.py:250
  1329.0 11.6 fusion.122
  1343.4 67.0 %all-gather.21.cloned.1.call-done = bf16[2048,1024]{1,0:T(8,128)(2,1)} async-done(((bf16[512,1024]{1,0:T(8,128)(2,1)}), bf16[2048,1024]{1,0:T(8,128)(2,1)}) %all-gather.21.cloned.1.call-update) | async-done | bytes 4194320 | tf_op jit(solution)/shard_map/all_gather | solution.py:149
  1459.6 9.0 fusion.21
  1473.3 8.7 fusion.320
  1520.9 75.4 %reduce-scatter.21.cloned.1.call-done = bf16[512,1024]{1,0:T(8,128)(2,1)} async-done(((bf16[2048,1024]{1,0:T(8,128)(2,1)}), bf16[512,1024]{1,0:T(8,128)(2,1)}) %reduce-scatter.21.cloned.1.call-update) | async-done | bytes 1048592 | tf_op jit(solution)/shard_map/reduce_scatter | solution.py:161
  1613.2 72.5 %all-gather.23.cloned.1.call-done = bf16[2048,1024]{1,0:T(8,128)(2,1)} async-done(((bf16[512,1024]{1,0:T(8,128)(2,1)}), bf16[2048,1024]{1,0:T(8,128)(2,1)}) %all-gather.23.cloned.1.call-update) | async-done | bytes 4194320 | tf_op jit(solution)/shard_map/all_gather | solution.py:168
  1699.3 67.8 %all-gather.29.cloned.1.call-done = bf16[2048,1024]{1,0:T(8,128)(2,1)} async-done(((bf16[512,1024]{1,0:T(8,128)(2,1)}), bf16[2048,1024]{1,0:T(8,128)(2,1)}) %all-gather.29.cloned.1.call-update) | async-done | bytes 4194320 | tf_op jit(solution)/shard_map/all_gather | solution.py:212
  1767.1 13.2 multiply_convert_fusion.14
  1790.6 74.1 %reduce-scatter.29.cloned.1.call-done = bf16[512,1024]{1,0:T(8,128)(2,1)} async-done(((bf16[2048,1024]{1,0:T(8,128)(2,1)}), bf16[512,1024]{1,0:T(8,128)(2,1)}) %reduce-scatter.29.cloned.1.call-update) | async-done | bytes 1048592 | tf_op jit(solution)/shard_map/reduce_scatter | solution.py:222
  1876.6 8.8 fusion.448
  1909.9 43.7 %all-gather.31.cloned.1.call-done = bf16[2048,1024]{1,0:T(8,128)(2,1)} async-done(((bf16[512,1024]{1,0:T(8,128)(2,1)}), bf16[2048,1024]{1,0:T(8,128)(2,1)}) %all-gather.31.cloned.1.call-update) | async-done | bytes 4194320 | tf_op jit(solution)/shard_map/all_gather | solution.py:233
  1957.3 9.8 fusion.48
  1967.1 12.6 multiply_reduce_fusion.6
  1979.8 9.6 fusion.46
  1989.4 12.6 multiply_reduce_fusion.5
  2002.0 9.8 fusion.44
  2011.9 12.7 multiply_reduce_fusion.4
  2024.6 12.6 multiply_reduce_fusion.7
  2037.2 13.0 multiply_convert_fusion.7
  2073.8 13.1 multiply_convert_fusion.5
  2120.6 11.8 multiply_convert_fusion.21
  2142.6 74.8 %reduce-scatter.31.cloned.1.call-done = bf16[512,1024]{1,0:T(8,128)(2,1)} async-done(((bf16[2048,1024]{1,0:T(8,128)(2,1)}), bf16[512,1024]{1,0:T(8,128)(2,1)}) %reduce-scatter.31.cloned.1.call-update) | async-done | bytes 1048592 | tf_op jit(solution)/shard_map/reduce_scatter | solution.py:250
  2235.2 81.4 %all-gather.33.cloned.1.call-done = bf16[2048,1024]{1,0:T(8,128)(2,1)} async-done(((bf16[512,1024]{1,0:T(8,128)(2,1)}), bf16[2048,1024]{1,0:T(8,128)(2,1)}) %all-gather.33.cloned.1.call-update) | async-done | bytes 4194320 | tf_op jit(solution)/shard_map/all_gather | solution.py:212
  2316.5 9.3 multiply_convert_fusion.12
  2353.5 56.8 %reduce-scatter.33.cloned.1.call-done = bf16[512,1024]{1,0:T(8,128)(2,1)} async-done(((bf16[2048,1024]{1,0:T(8,128)(2,1)}), bf16[512,1024]{1,0:T(8,128)(2,1)}) %reduce-scatter.33.cloned.1.call-update) | async-done | bytes 1048592 | tf_op jit(solution)/shard_map/reduce_scatter | solution.py:222
  2457.3 9.5 fusion.439
  2523.0 9.6 fusion.40
  2532.6 12.7 multiply_reduce_fusion.2
  2545.3 13.0 multiply_reduce_fusion.3
  2558.3 13.1 multiply_convert_fusion.3
  2592.8 12.7 multiply_reduce_fusion.1
  2605.5 12.1 multiply_convert_fusion.1
  2621.9 12.5 multiply_reduce_fusion
  2634.4 12.1 multiply_convert_fusion
  2661.2 11.7 fusion.38
  2680.0 12.5 fusion.183
  2724.8 132.5 %all-reduce.5.cloned.1.call-done = (bf16[1,1024,256]{2,1,0:T(8,128)(2,1)}, bf16[1,1024,256]{2,1,0:T(8,128)(2,1)}, bf16[1,1024,256]{2,1,0:T(8,128)(2,1)}, bf16[1,...) async-done(((bf16[1,1024,256]{2,1,0:T(8,128)(2,1)}, bf16[1,1024,256]{2,1,0:T(8,128)(2,1)}, ...) | async-done | bytes 6422544 | tf_op jit(solution)/shard_map/psum | solution.py:350
  2868.9 67.6 %reduce-scatter.35.cloned.1.call-done = bf16[512,1024]{1,0:T(8,128)(2,1)} async-done(((bf16[2048,1024]{1,0:T(8,128)(2,1)}), bf16[512,1024]{1,0:T(8,128)(2,1)}) %reduce-scatter.35.cloned.1.call-update) | async-done | bytes 1048592 | tf_op jit(solution)/shard_map/reduce_scatter | solution.py:250
  2939.7 10.5 all-reduce.1
  2952.1 11.9 all-reduce
  (1134 shorter events, 894.9 us)
Async XLA Ops:
  7.2 344.6 %copy-start = (bf16[1,704,1024]{2,1,0:T(8,128)(2,1)S(1)}, bf16[1,704,1024]{2,1,0:T(8,128)(2,1)}, u32[]{:S(2)}) copy-start(bf16[1,704,1024]{2,1,0:T(8,128)(2,1)} %param.20) | copy-start | bytes 4325380
  7.2 88.0 %all-gather.13.cloned.1.call-start = ((), (), s32[]{:S(2)}) async-start(), calls=%async_computation.12 | async-start | bytes 5242880 | tf_op jit(solution)/shard_map/all_gather | solution.py:149
  11.6 241.2 %reduce-scatter.13.cloned.1.call-start = ((), (), s32[]{:S(2)}) async-start(), calls=%async_computation.13 | async-start | bytes 5242880 | tf_op jit(solution)/shard_map/reduce_scatter | solution.py:161
  177.3 75.5 %copy-start.1 = (bf16[2,512,1024]{2,1,0:T(8,128)(2,1)S(1)}, bf16[2,512,1024]{2,1,0:T(8,128)(2,1)}, u32[]{:S(2)}) copy-start(bf16[2,512,1024]{2,1,0:T(8,128)(2,1)} %param.12) | copy-start | bytes 6291460
  177.3 77.2 %copy-start.203 = (f32[1,1024]{1,0:T(1,128)S(1)}, f32[1,1024]{1,0:T(1,128)}, u32[]{:S(2)}) copy-start(f32[1,1024]{1,0:T(1,128)} %param.22) | copy-start | bytes 12292
  177.3 161.3 %all-gather.15.cloned.1.call-start = ((), (), s32[]{:S(2)}) async-start(), calls=%async_computation.14 | async-start | bytes 5242880 | tf_op jit(solution)/shard_map/all_gather | solution.py:168
  257.2 175.1 %reduce-scatter.15.cloned.1.call-start = ((), (), s32[]{:S(2)}) async-start(), calls=%async_computation.15 | async-start | bytes 5242880 | tf_op jit(solution)/shard_map/reduce_scatter | solution.py:172
  356.9 83.1 %copy-start.207 = (f32[1,1024]{1,0:T(1,128)S(1)}, f32[1,1024]{1,0:T(1,128)}, u32[]{:S(2)}) copy-start(f32[1,1024]{1,0:T(1,128)} %param.21) | copy-start | bytes 12292
  356.9 166.0 %all-gather.17.cloned.1.call-start = ((), (), s32[]{:S(2)}) async-start(), calls=%async_computation.16 | async-start | bytes 5242880 | tf_op jit(solution)/shard_map/all_gather | solution.py:149
  434.6 4.2 collective-permute-start
  441.4 81.5 %copy-start.202 = (bf16[1,1024,256]{1,2,0:T(8,128)(2,1)S(1)}, bf16[1,1024,256]{1,2,0:T(8,128)(2,1)}, u32[]{:S(2)}) copy-start(bf16[1,1024,256]{1,2,0:T(8,128)(2,1)} %copy.31) | copy-start | bytes 1572868
  441.4 268.0 %reduce-scatter.17.cloned.1.call-start = ((), (), s32[]{:S(2)}) async-start(), calls=%async_computation.17 | async-start | bytes 5242880 | tf_op jit(solution)/shard_map/reduce_scatter | solution.py:161
  448.4 133.0 %collective-permute-start.1 = (bf16[2048,256]{0,1:T(8,128)(2,1)}, bf16[2048,256]{0,1:T(8,128)(2,1)}, u32[]{:S(2)}, u32[]{:S(2)}) collective-permute-start(bf16[2048,256]{0,1:T(8,128)(2,1)} %get-tuple-element.261), channel_id=1, source_target_pairs={{0,16},{1,17},{2,18},{3,19},{4,20},{5,21},{6,22},{7,23},{8,24},{9,... | collective-permute-start | bytes 3145736 | tf_op jit(solution)/shard_map/ppermute | solution.py:19
  633.9 75.5 %copy-start.2 = (bf16[2,512,1024]{2,1,0:T(8,128)(2,1)S(1)}, bf16[2,512,1024]{2,1,0:T(8,128)(2,1)}, u32[]{:S(2)}) copy-start(bf16[2,512,1024]{2,1,0:T(8,128)(2,1)} %param.12) | copy-start | bytes 6291460
  634.0 80.7 %copy-start.204 = (f32[1,1024]{1,0:T(1,128)S(1)}, f32[1,1024]{1,0:T(1,128)}, u32[]{:S(2)}) copy-start(f32[1,1024]{1,0:T(1,128)} %param.22) | copy-start | bytes 12292
  634.0 163.4 %all-gather.19.cloned.1.call-start = ((), (), s32[]{:S(2)}) async-start(), calls=%async_computation.18 | async-start | bytes 5242880 | tf_op jit(solution)/shard_map/all_gather | solution.py:168
  715.9 163.0 %all-gather.25.cloned.1.call-start = ((), (), s32[]{:S(2)}) async-start(), calls=%async_computation.24 | async-start | bytes 5242880 | tf_op jit(solution)/shard_map/all_gather | solution.py:212
  718.8 87.0 %copy-start.337 = (bf16[1,1024,704]{1,2,0:T(8,128)(2,1)S(1)}, bf16[1,1024,704]{1,2,0:T(8,128)(2,1)}, u32[]{:S(2)}) copy-start(bf16[1,1024,704]{1,2,0:T(8,128)(2,1)} %param.18) | copy-start | bytes 4325380
  718.8 257.6 %reduce-scatter.25.cloned.1.call-start = ((), (), s32[]{:S(2)}) async-start(), calls=%async_computation.25 | async-start | bytes 5242880 | tf_op jit(solution)/shard_map/reduce_scatter | solution.py:222
  901.0 75.5 %copy-start.28 = (f32[512,1024]{1,0:T(8,128)S(1)}, f32[512,1024]{1,0:T(8,128)}, u32[]{:S(2)}) copy-start(f32[512,1024]{1,0:T(8,128)} %get-tuple-element.89) | copy-start | bytes 6291460
  901.0 163.7 %all-gather.27.cloned.1.call-start = ((), (), s32[]{:S(2)}) async-start(), calls=%async_computation.26 | async-start | bytes 5242880 | tf_op jit(solution)/shard_map/all_gather | solution.py:233
  901.6 77.4 %copy-start.308 = (f32[512]{0:T(512)}, f32[512]{0:T(512)S(1)}, u32[]{:S(2)}) copy-start(f32[512]{0:T(512)S(1)} %get-tuple-element.259) | copy-start | bytes 6148
  983.3 260.5 %reduce-scatter.19.cloned.1.call-start = ((), (), s32[]{:S(2)}) async-start(), calls=%async_computation.19 | async-start | bytes 5242880 | tf_op jit(solution)/shard_map/reduce_scatter | solution.py:172
  1031.7 287.4 %reduce-scatter.27.cloned.1.call-start = ((), (), s32[]{:S(2)}) async-start(), calls=%async_computation.27 | async-start | bytes 5242880 | tf_op jit(solution)/shard_map/reduce_scatter | solution.py:250
  1068.5 88.1 %copy-start.163 = (bf16[512,256]{0,1:T(8,128)(2,1)}, bf16[512,256]{0,1:T(8,128)(2,1)S(1)}, u32[]{:S(2)}) copy-start(bf16[512,256]{0,1:T(8,128)(2,1)S(1)} %get-tuple-element.155) | copy-start | bytes 786436
  1098.1 88.3 %copy-start.79 = (f32[4,64,512]{2,1,0:T(8,128)}, f32[4,64,512]{2,1,0:T(8,128)S(1)}, u32[]{:S(2)}) copy-start(f32[4,64,512]{2,1,0:T(8,128)S(1)} %convolution_multiply_fusion.11) | copy-start | bytes 1572868
  1126.0 60.5 %copy-start.81 = (f32[4,64,512]{2,1,0:T(8,128)}, f32[4,64,512]{2,1,0:T(8,128)S(1)}, u32[]{:S(2)}) copy-start(f32[4,64,512]{2,1,0:T(8,128)S(1)} %convolution_multiply_fusion.10) | copy-start | bytes 1572868
  1243.7 75.4 %copy-start.3 = (bf16[2,512,1024]{2,1,0:T(8,128)(2,1)S(1)}, bf16[2,512,1024]{2,1,0:T(8,128)(2,1)}, u32[]{:S(2)}) copy-start(bf16[2,512,1024]{2,1,0:T(8,128)(2,1)} %param.12) | copy-start | bytes 6291460
  1243.7 75.4 %copy-start.208 = (f32[1,1024]{1,0:T(1,128)S(1)}, f32[1,1024]{1,0:T(1,128)}, u32[]{:S(2)}) copy-start(f32[1,1024]{1,0:T(1,128)} %param.21) | copy-start | bytes 12292
  1243.7 166.7 %all-gather.21.cloned.1.call-start = ((), (), s32[]{:S(2)}) async-start(), calls=%async_computation.20 | async-start | bytes 5242880 | tf_op jit(solution)/shard_map/all_gather | solution.py:149
  1248.6 3.8 collective-permute-start.2
  1251.6 73.4 %copy-start.307 = (f32[512]{0:T(512)}, f32[512]{0:T(512)S(1)}, u32[]{:S(2)}) copy-start(f32[512]{0:T(512)S(1)} %get-tuple-element.257) | copy-start | bytes 6148
  1329.0 267.4 %reduce-scatter.21.cloned.1.call-start = ((), (), s32[]{:S(2)}) async-start(), calls=%async_computation.21 | async-start | bytes 5242880 | tf_op jit(solution)/shard_map/reduce_scatter | solution.py:161
  1340.6 128.0 %collective-permute-start.3 = (bf16[2048,256]{0,1:T(8,128)(2,1)}, bf16[2048,256]{0,1:T(8,128)(2,1)}, u32[]{:S(2)}, u32[]{:S(2)}) collective-permute-start(bf16[2048,256]{0,1:T(8,128)(2,1)} %get-tuple-element.272), channel_id=1, source_target_pairs={{0,16},{1,17},{2,18},{3,19},{4,20},{5,21},{6,22},{7,23},{8,24},{9,... | collective-permute-start | bytes 3145736 | tf_op jit(solution)/shard_map/ppermute | solution.py:19
  1451.4 59.9 %copy-start.271 = (f32[4,512]{1,0:T(4,128)}, f32[4,512]{1,0:T(4,128)S(1)}, u32[]{:S(2)}) copy-start(f32[4,512]{1,0:T(4,128)S(1)} %get-tuple-element.291) | copy-start | bytes 24580
  1520.8 75.5 %copy-start.4 = (bf16[2,512,1024]{2,1,0:T(8,128)(2,1)S(1)}, bf16[2,512,1024]{2,1,0:T(8,128)(2,1)}, u32[]{:S(2)}) copy-start(bf16[2,512,1024]{2,1,0:T(8,128)(2,1)} %param.12) | copy-start | bytes 6291460
  1520.8 80.5 %copy-start.205 = (f32[1,1024]{1,0:T(1,128)S(1)}, f32[1,1024]{1,0:T(1,128)}, u32[]{:S(2)}) copy-start(f32[1,1024]{1,0:T(1,128)} %param.22) | copy-start | bytes 12292
  1520.9 164.8 %all-gather.23.cloned.1.call-start = ((), (), s32[]{:S(2)}) async-start(), calls=%async_computation.22 | async-start | bytes 5242880 | tf_op jit(solution)/shard_map/all_gather | solution.py:168
  1604.3 162.8 %all-gather.29.cloned.1.call-start = ((), (), s32[]{:S(2)}) async-start(), calls=%async_computation.28 | async-start | bytes 5242880 | tf_op jit(solution)/shard_map/all_gather | solution.py:212
  1604.3 4.8 collective-permute-start.4
  1613.1 81.1 %copy-start.338 = (bf16[1,1024,704]{1,2,0:T(8,128)(2,1)S(1)}, bf16[1,1024,704]{1,2,0:T(8,128)(2,1)}, u32[]{:S(2)}) copy-start(bf16[1,1024,704]{1,2,0:T(8,128)(2,1)} %param.18) | copy-start | bytes 4325380
  1613.2 251.5 %reduce-scatter.29.cloned.1.call-start = ((), (), s32[]{:S(2)}) async-start(), calls=%async_computation.29 | async-start | bytes 5242880 | tf_op jit(solution)/shard_map/reduce_scatter | solution.py:222
  1789.2 75.5 %copy-start.23 = (f32[512,1024]{1,0:T(8,128)S(1)}, f32[512,1024]{1,0:T(8,128)}, u32[]{:S(2)}) copy-start(f32[512,1024]{1,0:T(8,128)} %get-tuple-element.73) | copy-start | bytes 6291460
  1789.2 164.4 %all-gather.31.cloned.1.call-start = ((), (), s32[]{:S(2)}) async-start(), calls=%async_computation.30 | async-start | bytes 5242880 | tf_op jit(solution)/shard_map/all_gather | solution.py:233
  1872.2 345.2 %reduce-scatter.31.cloned.1.call-start = ((), (), s32[]{:S(2)}) async-start(), calls=%async_computation.31 | async-start | bytes 5242880 | tf_op jit(solution)/shard_map/reduce_scatter | solution.py:250
  1872.2 260.2 %collective-permute-start.5 = (bf16[2048,256]{0,1:T(8,128)(2,1)}, bf16[2048,256]{0,1:T(8,128)(2,1)}, u32[]{:S(2)}, u32[]{:S(2)}) collective-permute-start(bf16[2048,256]{0,1:T(8,128)(2,1)} %bitcast.816), channel_id=1, source_target_pairs={{16,0},{17,1},{18,2},{19,3},{20,4},{21,5},{22,6},{23,7},{24,8},{25... | collective-permute-start | bytes 3145736 | tf_op jit(solution)/shard_map/ppermute | solution.py:19
  1957.3 67.3 %copy-start.143 = (bf16[512,256]{0,1:T(8,128)(2,1)}, bf16[512,256]{0,1:T(8,128)(2,1)S(1)}, u32[]{:S(2)}) copy-start(bf16[512,256]{0,1:T(8,128)(2,1)S(1)} %get-tuple-element.148) | copy-start | bytes 786436
  2141.9 75.5 %copy-start.5 = (bf16[2,512,1024]{2,1,0:T(8,128)(2,1)S(1)}, bf16[2,512,1024]{2,1,0:T(8,128)(2,1)}, u32[]{:S(2)}) copy-start(bf16[2,512,1024]{2,1,0:T(8,128)(2,1)} %param.12) | copy-start | bytes 6291460
  2141.9 75.5 %copy-start.209 = (f32[1,1024]{1,0:T(1,128)S(1)}, f32[1,1024]{1,0:T(1,128)}, u32[]{:S(2)}) copy-start(f32[1,1024]{1,0:T(1,128)} %param.21) | copy-start | bytes 12292
  2142.0 174.6 %all-gather.33.cloned.1.call-start = ((), (), s32[]{:S(2)}) async-start(), calls=%async_computation.32 | async-start | bytes 5242880 | tf_op jit(solution)/shard_map/all_gather | solution.py:212
  2226.6 4.6 collective-permute-start.6
  2235.1 90.8 %copy-start.339 = (bf16[1,1024,704]{1,2,0:T(8,128)(2,1)S(1)}, bf16[1,1024,704]{1,2,0:T(8,128)(2,1)}, u32[]{:S(2)}) copy-start(bf16[1,1024,704]{1,2,0:T(8,128)(2,1)} %param.18) | copy-start | bytes 4325380
  2235.1 175.2 %reduce-scatter.33.cloned.1.call-start = ((), (), s32[]{:S(2)}) async-start(), calls=%async_computation.33 | async-start | bytes 5242880 | tf_op jit(solution)/shard_map/reduce_scatter | solution.py:222
  2334.9 183.6 %all-gather.35.cloned.1.call-start = ((), (), s32[]{:S(2)}) async-start(), calls=%async_computation.34 | async-start | bytes 5242880 | tf_op jit(solution)/shard_map/all_gather | solution.py:233
  2348.7 61.6 %copy-start.27 = (f32[512,1024]{1,0:T(8,128)S(1)}, f32[512,1024]{1,0:T(8,128)}, u32[]{:S(2)}) copy-start(f32[512,1024]{1,0:T(8,128)} %get-tuple-element.64) | copy-start | bytes 6291460
  2348.8 61.6 %copy-start.206 = (f32[1,1024]{1,0:T(1,128)S(1)}, f32[1,1024]{1,0:T(1,128)}, u32[]{:S(2)}) copy-start(f32[1,1024]{1,0:T(1,128)} %param.22) | copy-start | bytes 12292
  2417.4 302.5 %reduce-scatter.23.cloned.1.call-start = ((), (), s32[]{:S(2)}) async-start(), calls=%async_computation.23 | async-start | bytes 5242880 | tf_op jit(solution)/shard_map/reduce_scatter | solution.py:172
  2476.8 380.5 %all-reduce.5.cloned.1.call-start = ((), (), s32[]{:S(2)}) async-start(), calls=%async_computation.36 | async-start | bytes 12845056 | tf_op jit(solution)/shard_map/psum | solution.py:350
  2496.4 196.1 %collective-permute-start.7 = (bf16[2048,256]{0,1:T(8,128)(2,1)}, bf16[2048,256]{0,1:T(8,128)(2,1)}, u32[]{:S(2)}, u32[]{:S(2)}) collective-permute-start(bf16[2048,256]{0,1:T(8,128)(2,1)} %bitcast.144), channel_id=1, source_target_pairs={{16,0},{17,1},{18,2},{19,3},{20,4},{21,5},{22,6},{23,7},{24,8},{25... | collective-permute-start | bytes 3145736 | tf_op jit(solution)/shard_map/ppermute | solution.py:19
  2710.3 226.2 %reduce-scatter.35.cloned.1.call-start = ((), (), s32[]{:S(2)}) async-start(), calls=%async_computation.35 | async-start | bytes 5242880 | tf_op jit(solution)/shard_map/reduce_scatter | solution.py:250
  2864.7 71.8 %copy-start.25 = (f32[512,1024]{1,0:T(8,128)S(1)}, f32[512,1024]{1,0:T(8,128)}, u32[]{:S(2)}) copy-start(f32[512,1024]{1,0:T(8,128)} %get-tuple-element.52) | copy-start | bytes 6291460
  2864.7 71.8 %copy-start.210 = (f32[1,1024]{1,0:T(1,128)S(1)}, f32[1,1024]{1,0:T(1,128)}, u32[]{:S(2)}) copy-start(f32[1,1024]{1,0:T(1,128)} %param.21) | copy-start | bytes 12292
  2865.8 73.3 %copy-start.310 = (f32[1024]{0:T(1024)S(1)}, f32[1024]{0:T(1024)}, u32[]{:S(2)}) copy-start(f32[1024]{0:T(1024)} %get-tuple-element.109) | copy-start | bytes 12292
  2865.8 73.3 %copy-start.312 = (f32[1024]{0:T(1024)S(1)}, f32[1024]{0:T(1024)}, u32[]{:S(2)}) copy-start(f32[1024]{0:T(1024)} %get-tuple-element.13) | copy-start | bytes 12292
  (365 other events, 2878.4 us)
Sparse Core Ops, SparseCore 0:
  11.7 83.4 all-gather.12
  177.5 75.2 reduce-scatter.12
  257.3 81.2 all-gather.14
  357.0 75.2 reduce-scatter.14
  441.5 81.3 all-gather.16
  634.1 75.2 reduce-scatter.16
  716.0 81.2 all-gather.18
  799.6 79.2 all-gather.24
  901.1 75.2 reduce-scatter.24
  983.4 81.2 all-gather.26
  1067.5 75.2 reduce-scatter.18
  1243.8 75.2 reduce-scatter.26
  1329.1 81.2 all-gather.20
  1521.0 75.2 reduce-scatter.20
  1604.4 81.2 all-gather.22
  1687.8 79.2 all-gather.28
  1789.3 75.2 reduce-scatter.28
  1872.3 81.2 all-gather.30
  2142.1 75.2 reduce-scatter.30
  2235.2 81.2 all-gather.32
  2335.0 75.2 reduce-scatter.32
  2417.5 81.2 all-gather.34
  2501.7 75.2 reduce-scatter.22
  2710.4 146.8 all-reduce.4
  2859.8 76.7 reduce-scatter.34
where the time goes:
time: 2980 us
  waiting for transfers between devices  1590 us (53%)
  matrix products  873 us (29%)
  other arithmetic  413 us (14%)
  local copies, waits for them, and re-layouts  42.1 us (1%)
    all_gather x3, waiting for transfers between devices, layer_forward(): ffn_input = lax.all_gather(ffn_normed, 'head', axis=0, tiled=True)  232 us
    reduce_scatter x3, waiting for transfers between devices, layer_forward(): lax.psum_scatter(jnp.dot(attended, w_out, preferred_element_type=jnp.floa...  226 us
    all_gather x3, waiting for transfers between devices, layer_backward(): lax.all_gather(grad_result.astype(jnp.bfloat16), 'head', axis=0, tiled=True)  217 us
    reduce_scatter x3, waiting for transfers between devices, layer_backward(): lax.psum_scatter((total + jnp.dot(value_grad, w_value.T, preferred_elemen...  209 us
    reduce_scatter x3, waiting for transfers between devices, layer_backward(): lax.psum_scatter((jnp.dot(gate_grad, w_gate.T, preferred_element_type=jnp...  206 us
    all_gather x3, waiting for transfers between devices, layer_forward(): gathered = lax.all_gather(normed, 'head', axis=0, tiled=True)  205 us
    dot_general x12, matrix products, attend_back(): jnp.einsum('qhd,khd->hqk', grad_block, value_heads, preferred_element_typ...  153 us
    convert_element_type x12, other arithmetic, attend_back(): score_grad = (probs * (prob_grad - jnp.sum(probs * prob_grad, axis=2, kee...  138 us
  transfers between devices with their start and end apart: 33, of which 26 were waited for; matrix products, arithmetic and copies ran while one was open for 32% of the time, Pallas kernels for 0%

commit v1 on v0

v1 whole, which is shorter than its diff:
```python
import functools

import jax
import jax.numpy as jnp
from jax import lax
from jax.experimental import pallas as pl
from jax.experimental.pallas import tpu as pltpu
from jax.sharding import PartitionSpec as P

D = 1024
HD = 64
SLOTS = 2048
PAD = 128

EPSILON = 1e-05
MASKED = -1e30
SCALE = HD ** (-0.5)
VMEM_LIMIT = 56 * 1024 * 1024

F32 = jnp.float32
BF16 = jnp.bfloat16


def dot_nn(a, b):
    return lax.dot_general(a, b, (((1,), (0,)), ((), ())), preferred_element_type=F32)


def dot_nt(a, b):
    return lax.dot_general(a, b, (((1,), (1,)), ((), ())), preferred_element_type=F32)


def dot_tn(a, b):
    return lax.dot_general(a, b, (((0,), (0,)), ((), ())), preferred_element_type=F32)


def slot_tables(length_row):
    padded = (length_row + PAD - 1) // PAD * PAD
    starts = jnp.cumsum(padded) - padded
    slots = jnp.arange(SLOTS, dtype=jnp.int32)
    inside = (slots[:, None] >= starts[None, :]) & (slots[:, None] < (starts + padded)[None, :])
    begin = jnp.sum(jnp.where(inside, starts[None, :], 0), axis=1).astype(jnp.int32)
    end = jnp.sum(jnp.where(inside, (starts + length_row)[None, :], 0), axis=1).astype(jnp.int32)
    last = jnp.minimum(slots, end - 1)
    freq = 10000.0 ** (-2.0 * jnp.arange(HD // 2, dtype=F32) / HD)
    angle = (slots - begin).astype(F32)[:, None] * freq[None, :]
    cosine = jnp.concatenate([jnp.cos(angle), jnp.cos(angle)], axis=1)
    sine = jnp.concatenate([-jnp.sin(angle), jnp.sin(angle)], axis=1)
    return begin, last, cosine, sine


def tile_tables(begin, tile):
    count = SLOTS // tile
    index = jnp.arange(count, dtype=jnp.int32)
    low = begin[::tile]
    high = begin[tile - 1 :: tile]
    first = low // tile
    free = jnp.minimum((high + tile - 1) // tile, index)
    later = index[None, :] > index[:, None]
    free_end = index + 1 + jnp.sum(
        jnp.where(later & (high[None, :] <= index[:, None] * tile), 1, 0), axis=1
    )
    seen_end = index + 1 + jnp.sum(
        jnp.where(later & (low[None, :] < (index[:, None] + 1) * tile), 1, 0), axis=1
    )
    return jnp.stack([first, free, free_end.astype(jnp.int32), seen_end.astype(jnp.int32)])


def lane_in_head(shape):
    return lax.broadcasted_iota(jnp.int32, shape, 1) % HD


def turn(rows, cosine, sine):
    width = rows.shape[1]
    low = lane_in_head(rows.shape) < HD // 2
    if width == HD:
        swapped = jnp.concatenate([rows[:, HD // 2 :], rows[:, : HD // 2]], axis=1)
    else:
        swapped = jnp.where(
            low,
            pltpu.roll(rows, width - HD // 2, 1),
            pltpu.roll(rows, HD // 2, 1),
        )
    return rows * cosine + swapped * sine


def qkv_kernel(width, x_ref, w_ref, cos_ref, sin_ref, first_ref, q_ref, k_ref, v_ref, m_ref):
    product = dot_nn(x_ref[...], w_ref[...])
    repeat = width // cos_ref.shape[1]
    cosine = jnp.concatenate([cos_ref[...]] * repeat, axis=1)
    sine = jnp.concatenate([sin_ref[...]] * repeat, axis=1)
    q_ref[...] = (turn(product[:, :width], cosine, sine).astype(BF16).astype(F32) * SCALE).astype(BF16)
    k_ref[...] = turn(product[:, width : 2 * width], cosine, sine).astype(BF16)
    own = product[:, 2 * width :].astype(BF16)
    v_ref[...] = own
    if first_ref is not None:
        m_ref[...] = (0.5 * own.astype(F32) + 0.5 * first_ref[...].astype(F32)).astype(BF16)


def project(gathered, w_qkv, cosine, sine, first_values):
    width = w_qkv.shape[1] // 3
    tile = min(256, SLOTS)
    table = cosine.shape[1]
    row = lambda cols: pl.BlockSpec((tile, cols), lambda i: (i, 0))
    shape = jax.ShapeDtypeStruct((SLOTS, width), BF16)
    if first_values is None:
        kernel = lambda x, w, c, s, q, k, v: qkv_kernel(width, x, w, c, s, None, q, k, v, None)
        extra, specs, outs = (), [], 3
    else:
        kernel = functools.partial(qkv_kernel, width)
        extra, specs, outs = (first_values,), [row(width)], 4
    result = pl.pallas_call(
        kernel,
        grid=(SLOTS // tile,),
        in_specs=[
            row(D),
            pl.BlockSpec((D, 3 * width), lambda i: (0, 0)),
            row(table),
            row(table),
        ]
        + specs,
        out_specs=[row(width)] * outs,
        out_shape=[shape] * outs,
        compiler_params=pltpu.CompilerParams(vmem_limit_bytes=VMEM_LIMIT),
        cost_estimate=pl.CostEstimate(
            flops=2 * SLOTS * D * 3 * width, bytes_accessed=SLOTS * D * 4, transcendentals=0
        ),
        name="project",
    )(gathered, w_qkv, cosine, sine, *extra)
    return result if first_values is not None else (*result, result[2])


def allowed_scores(scores, start, low, high, tile):
    keys = start + lax.broadcasted_iota(jnp.int32, scores.shape, 0)
    return jnp.where((keys >= low) & (keys <= high), scores, MASKED)


def head_mask(rows, width, head):
    lanes = lax.broadcasted_iota(jnp.int32, (rows, width), 1)
    return (lanes >= head * HD) & (lanes < (head + 1) * HD)


def attend_kernel(tile, heads, meta, q_ref, k_ref, vt_ref, low_ref, high_ref, o_ref, lse_ref, acc, peak, mass):
    width = heads * HD
    index = pl.program_id(0)
    q = q_ref[...]
    low = low_ref[...]
    high = high_ref[...]
    queries = [jnp.where(head_mask(tile, width, hh), q, jnp.zeros_like(q)) for hh in range(heads)]
    acc[...] = jnp.zeros_like(acc)
    peak[...] = jnp.full_like(peak, MASKED)
    mass[...] = jnp.zeros_like(mass)

    def step(kt, masked):
        start = pl.multiple_of(kt * tile, tile)
        keys = k_ref[pl.ds(start, tile), :]
        for hh in range(heads):
            scores = dot_nt(keys, queries[hh])
            if masked:
                scores = allowed_scores(scores, start, low, high, tile)
            before = peak[hh : hh + 1, :]
            top = jnp.maximum(before, jnp.max(scores, axis=0, keepdims=True))
            weights = jnp.exp(scores - top)
            shrink = jnp.exp(before - top)
            peak[hh : hh + 1, :] = top
            mass[hh : hh + 1, :] = mass[hh : hh + 1, :] * shrink + jnp.sum(
                weights, axis=0, keepdims=True
            )
            rows = slice(hh * HD, (hh + 1) * HD)
            values = vt_ref[rows, pl.ds(start, tile)]
            acc[rows, :] = acc[rows, :] * shrink + dot_nn(values, weights.astype(BF16))

    step(index, True)

    def masked_step(kt, carry):
        step(kt, True)
        return carry

    def free_step(kt, carry):
        step(kt, False)
        return carry

    lax.fori_loop(meta[0, index], meta[1, index], masked_step, 0)
    lax.fori_loop(meta[1, index], index, free_step, 0)
    for hh in range(heads):
        rows = slice(hh * HD, (hh + 1) * HD)
        acc[rows, :] = acc[rows, :] / mass[hh : hh + 1, :]
    o_ref[...] = acc[...].T.astype(BF16)
    lse_ref[...] = peak[...] + jnp.log(mass[...])


def attend(queries, keys, mixed, low, high, meta, tile):
    width = queries.shape[1]
    heads = width // HD
    whole = lambda shape: pl.BlockSpec(shape, lambda i, meta: (0, 0))
    return pl.pallas_call(
        functools.partial(attend_kernel, tile, heads),
        grid_spec=pltpu.PrefetchScalarGridSpec(
            num_scalar_prefetch=1,
            grid=(SLOTS // tile,),
            in_specs=[
                pl.BlockSpec((tile, width), lambda i, meta: (i, 0)),
                whole((SLOTS, width)),
                whole((width, SLOTS)),
                pl.BlockSpec((1, tile), lambda i, meta: (0, i)),
                pl.BlockSpec((1, tile), lambda i, meta: (0, i)),
            ],
            out_specs=[
                pl.BlockSpec((tile, width), lambda i, meta: (i, 0)),
                pl.BlockSpec((heads, tile), lambda i, meta: (0, i)),
            ],
            scratch_shapes=[
                pltpu.VMEM((width, tile), F32),
                pltpu.VMEM((heads, tile), F32),
                pltpu.VMEM((heads, tile), F32),
            ],
        ),
        out_shape=[
            jax.ShapeDtypeStruct((SLOTS, width), BF16),
            jax.ShapeDtypeStruct((heads, SLOTS), F32),
        ],
        compiler_params=pltpu.CompilerParams(vmem_limit_bytes=VMEM_LIMIT),
        cost_estimate=pl.CostEstimate(
            flops=8 * SLOTS * SLOTS * width, bytes_accessed=SLOTS * width * 8, transcendentals=0
        ),
        name="attend",
    )(meta, queries, keys, mixed.T, low, high)


def attend_back_kernel(
    tile, heads, share, meta, q_ref, k_ref, kt_ref, v_ref, do_ref, lse_ref, delta_ref, low_ref, high_ref,
    cos_ref, sin_ref, cost_ref, sint_ref, carry_ref, dq_ref, dk_ref, dv_ref, dqt, dk, dv
):
    width = heads * HD
    index = pl.program_id(0)
    count = pl.num_programs(0)

    @pl.when(index == 0)
    def _():
        dqt[...] = jnp.zeros_like(dqt)

    dk[...] = jnp.zeros_like(dk)
    dv[...] = jnp.zeros_like(dv)
    keys = k_ref[...]
    values = v_ref[...]
    key_start = index * tile
    masks = [head_mask(tile, width, hh) for hh in range(heads)]
    transposed = [kt_ref[hh * HD : (hh + 1) * HD, :] for hh in range(heads)]

    def step(qt, masked):
        start = pl.multiple_of(qt * tile, tile)
        here = pl.ds(start, tile)
        q = q_ref[here, :]
        do = do_ref[here, :]
        low = low_ref[:, here]
        high = high_ref[:, here]
        for hh in range(heads):
            q_h = jnp.where(masks[hh], q, jnp.zeros_like(q))
            do_h = jnp.where(masks[hh], do, jnp.zeros_like(do))
            scores = dot_nt(keys, q_h)
            prob_grad = dot_nt(values, do_h)
            if masked:
                scores = allowed_scores(scores, key_start, low, high, tile)
            probs = jnp.exp(scores - lse_ref[hh : hh + 1, here])
            score_grad = (probs * (prob_grad - delta_ref[hh : hh + 1, here])).astype(BF16)
            dv[...] += dot_nn(probs.astype(BF16), do_h)
            dk[...] += dot_nn(score_grad, q_h)
            rows = slice(hh * HD, (hh + 1) * HD)
            dqt[rows, here] += dot_nn(transposed[hh], score_grad)

    step(index, True)

    def masked_step(qt, carry):
        step(qt, True)
        return carry

    def free_step(qt, carry):
        step(qt, False)
        return carry

    lax.fori_loop(index + 1, meta[2, index], free_step, 0)
    lax.fori_loop(meta[2, index], meta[3, index], masked_step, 0)
    repeat = width // cos_ref.shape[1]
    cosine = jnp.concatenate([cos_ref[...]] * repeat, axis=1)
    sine = jnp.concatenate([sin_ref[...]] * repeat, axis=1)
    dk_ref[...] = turn(dk[...], cosine, -sine).astype(BF16)
    if carry_ref is None:
        dv_ref[...] = (share * dv[...]).astype(BF16)
    else:
        dv_ref[...] = (share * dv[...] + carry_ref[...].astype(F32)).astype(BF16)

    @pl.when(index == count - 1)
    def _():
        half = HD // 2

        def finish(qt, carry):
            here = pl.ds(pl.multiple_of(qt * tile, tile), tile)
            cosine_t = cost_ref[:, here] * SCALE
            sine_t = sint_ref[:, here] * SCALE
            parts = []
            for hh in range(heads):
                u1 = dqt[hh * HD : hh * HD + half, here]
                u2 = dqt[hh * HD + half : (hh + 1) * HD, here]
                parts.append(u1 * cosine_t + u2 * sine_t)
                parts.append(u2 * cosine_t - u1 * sine_t)
            dq_ref[here, :] = jnp.concatenate(parts, axis=0).T.astype(BF16)
            return carry

        lax.fori_loop(0, count, finish, 0)


def attend_back(queries, keys, mixed, out_grad, sums, delta, low, high, meta, cosine, sine, half_tables, share, carry, tile):
    width = queries.shape[1]
    heads = width // HD
    whole = lambda shape: pl.BlockSpec(shape, lambda i, meta: (0, 0))
    rows = lambda cols: pl.BlockSpec((tile, cols), lambda i, meta: (i, 0))
    table = cosine.shape[1]
    base = functools.partial(attend_back_kernel, tile, heads, share)
    if carry is None:
        kernel = lambda *refs: base(*refs[:14], None, *refs[14:])
        extra, specs = (), []
    else:
        kernel = base
        extra, specs = (carry,), [rows(width)]
    return pl.pallas_call(
        kernel,
        grid_spec=pltpu.PrefetchScalarGridSpec(
            num_scalar_prefetch=1,
            grid=(SLOTS // tile,),
            in_specs=[
                whole((SLOTS, width)),
                rows(width),
                pl.BlockSpec((width, tile), lambda i, meta: (0, i)),
                rows(width),
                whole((SLOTS, width)),
                whole((heads, SLOTS)),
                whole((heads, SLOTS)),
                whole((1, SLOTS)),
                whole((1, SLOTS)),
                rows(table),
                rows(table),
                whole((HD // 2, SLOTS)),
                whole((HD // 2, SLOTS)),
            ]
            + specs,
            out_specs=[whole((SLOTS, width)), rows(width), rows(width)],
            scratch_shapes=[
                pltpu.VMEM((width, SLOTS), F32),
                pltpu.VMEM((tile, width), F32),
                pltpu.VMEM((tile, width), F32),
            ],
        ),
        out_shape=[jax.ShapeDtypeStruct((SLOTS, width), BF16)] * 3,
        compiler_params=pltpu.CompilerParams(vmem_limit_bytes=VMEM_LIMIT),
        cost_estimate=pl.CostEstimate(
            flops=20 * SLOTS * SLOTS * width, bytes_accessed=SLOTS * width * 14, transcendentals=0
        ),
        name="attend_back",
    )(meta, queries, keys, keys.T, mixed, out_grad, sums, delta, low, high, cosine, sine, *half_tables, *extra)


class Place:
    def __init__(self):
        self.size = lax.axis_size("head")
        self.half = self.size // 2
        self.data = lax.axis_size("dp")
        self.core = lax.axis_index("section")
        self.dp = lax.axis_index("dp")
        self.head = lax.axis_index("head")
        self.row = self.head // self.half
        self.seat = self.head % self.half
        self.region = (self.row + self.core) % 2

    def swap(self, x):
        return lax.ppermute(x, "section", [(0, 1), (1, 0)])

    def to_core(self, x, core):
        return lax.ppermute(x, "section", [(1 - core, core)])

    def across(self, x, core):
        size, half = self.size, self.half
        pairs = [(size + h, core * size + (h + half) % size) for h in range(size)]
        return lax.ppermute(x, ("section", "head"), pairs)

    def across_from_zero(self, x):
        size, half = self.size, self.half
        pairs = [(h, size + (h + half) % size) for h in range(size)]
        return lax.ppermute(x, ("section", "head"), pairs)

    def beside(self, x, shift):
        half = self.half
        pairs = [(h, h // half * half + (h % half + shift) % half) for h in range(self.size)]
        return lax.ppermute(x, "head", pairs)

    def around(self, x, shift):
        return lax.ppermute(x, "head", [(h, (h + shift) % self.size) for h in range(self.size)])

    def flip(self, x, bits):
        return lax.ppermute(x, "dp", [(d, d ^ bits) for d in range(self.data)])

    def by_seat(self, own, shifted):
        blocks = jnp.zeros((self.half, *own.shape), own.dtype)
        blocks = lax.dynamic_update_index_in_dim(blocks, own, self.seat, 0)
        for shift, block in enumerate(shifted, 1):
            seat = (self.seat - shift) % self.half
            blocks = lax.dynamic_update_index_in_dim(blocks, block, seat, 0)
        return blocks

    def by_region(self, own, other):
        return jnp.where(
            self.region == 0, jnp.concatenate([own, other]), jnp.concatenate([other, own])
        )

    def gather_row(self, block):
        shifted = [self.beside(block, shift) for shift in range(1, self.half)]
        own = self.by_seat(block, shifted).reshape(-1, block.shape[1])
        return self.by_region(own, self.swap(own))

    def regions(self, rows):
        pair = rows.reshape(2, rows.shape[0] // 2, *rows.shape[1:])
        own = lax.dynamic_index_in_dim(pair, self.region, 0, keepdims=False)
        other = lax.dynamic_index_in_dim(pair, 1 - self.region, 0, keepdims=False)
        return own, other

    def seat_block(self, blocks, shift):
        return lax.dynamic_index_in_dim(blocks, (self.seat + shift) % self.half, 0, keepdims=False)

    def scatter_row(self, partial):
        own, other = self.regions(partial)
        summed = own + self.swap(other.astype(BF16)).astype(F32)
        summed = summed.reshape(self.half, -1, partial.shape[1])
        total = self.seat_block(summed, 0)
        for shift in range(1, self.half):
            sent = self.seat_block(summed, shift).astype(BF16)
            total = total + self.beside(sent, shift).astype(F32)
        return total

    def heads_to_slots(self, rows):
        own, other = self.regions(rows)
        pair = jnp.stack([own, self.swap(other)])
        pair = pair.reshape(2, self.half, -1, rows.shape[1]).swapaxes(0, 1)
        shifted = [
            self.beside(self.seat_block(pair, shift), shift) for shift in range(1, self.half)
        ]
        blocks = self.by_seat(self.seat_block(pair, 0), shifted)
        blocks = self.by_region(blocks[:, 0], blocks[:, 1])
        return jnp.concatenate([blocks[i] for i in range(self.size)], axis=1)

    def slots_to_heads(self, block):
        width = block.shape[1] // self.size
        cut = jnp.stack([block[:, i * width : (i + 1) * width] for i in range(self.size)])
        own, other = self.regions(cut)
        pair = jnp.stack([own, other], axis=1)
        shifted = [
            self.beside(self.seat_block(pair, shift), shift) for shift in range(1, self.half)
        ]
        rows = self.by_seat(self.seat_block(pair, 0), shifted)
        return self.by_region(
            rows[:, 0].reshape(-1, width), self.swap(rows[:, 1].reshape(-1, width))
        )

    def data_block(self, x, bits):
        return lax.dynamic_index_in_dim(x, self.dp ^ bits, 0, keepdims=False)

    def scatter_data(self, first, second):
        def half_way(x, near, far):
            sent = jnp.stack([self.data_block(x, near), self.data_block(x, near ^ far)])
            kept = jnp.stack([self.data_block(x, 0), self.data_block(x, far)])
            return kept.astype(F32) + self.flip(sent.astype(BF16), near).astype(F32)

        first, second = half_way(first, 1, 2), half_way(second, 2, 1)
        first = first[0] + self.flip(first[1].astype(BF16), 2).astype(F32)
        second = second[0] + self.flip(second[1].astype(BF16), 1).astype(F32)
        return first, second

    def gather_data(self, x):
        blocks = jnp.zeros((self.data, *x.shape), x.dtype)
        blocks = lax.dynamic_update_index_in_dim(blocks, x, self.dp, 0)
        for bits in range(1, self.data):
            blocks = lax.dynamic_update_index_in_dim(blocks, self.flip(x, bits), self.dp ^ bits, 0)
        return blocks

    def head_block(self, x, shift):
        return lax.dynamic_index_in_dim(x, (self.head + shift) % self.size, 0, keepdims=False)

    def scatter_heads(self, x):
        total = self.head_block(x, 0).astype(F32)
        for shift in range(1, self.size):
            sent = self.head_block(x, shift).astype(BF16)
            total = total + self.around(sent, shift).astype(F32)
        return total

    def pick(self, zero, one):
        return jnp.where(self.core == 0, zero, one)


def weight_pieces(place, w_gate, w_up, w_down, w_out):
    kinds = (w_gate.T, w_up.T, w_down, w_out)
    cut = [item.reshape(place.data, 2, -1, D) for item in kinds]
    mine = jnp.concatenate(
        [lax.dynamic_index_in_dim(item, place.dp, 0, keepdims=False) for item in cut], axis=1
    )
    own = lax.dynamic_index_in_dim(mine, place.core, 0, keepdims=False)
    sent = lax.dynamic_index_in_dim(mine, 1 - place.core, 0, keepdims=False)
    other = place.swap(sent)
    return place.pick(own, other), place.pick(other, own)


def spread_weights(place, piece, units):
    full = lax.all_gather(piece, ("section", "dp", "head"), axis=0)
    gate, up, down = (full[:, i * units : (i + 1) * units].reshape(-1, D) for i in range(3))
    out = full[:, 3 * units :].reshape(2, place.data, place.size, -1, D)
    out = out.transpose(2, 1, 0, 3, 4).reshape(-1, D)
    return gate, up, down, out


def reduce_weights(place, gate, up, down, out):
    out = out.reshape(place.size, place.data, 2, -1, D).transpose(2, 1, 0, 3, 4)
    cut = [item.reshape(2, place.data, place.size, -1, D) for item in (gate, up, down)] + [out]

    def core_part(core):
        parts = [lax.dynamic_index_in_dim(item, core, 0, keepdims=False) for item in cut]
        return jnp.concatenate([part.astype(BF16) for part in parts], axis=2)

    own = core_part(place.core)
    summed = own.astype(F32) + place.swap(core_part(1 - place.core)).astype(F32)
    summed = summed.astype(BF16)
    first, second = place.scatter_data(summed[:, : place.half], summed[:, place.half :])
    piece = place.scatter_heads(jnp.concatenate([first, second]))
    return place.gather_data(piece.astype(BF16))


def norm(rows, gain):
    inverse = lax.rsqrt(jnp.mean(rows * rows, axis=1, keepdims=True) + EPSILON)
    return rows * inverse * gain


def norm_back(rows, gain, grad):
    inverse = lax.rsqrt(jnp.mean(rows * rows, axis=1, keepdims=True) + EPSILON)
    scaled = grad * gain
    gain_grad = jnp.sum(grad * rows * inverse, axis=0)
    rows_grad = inverse * scaled - rows * inverse**3 * jnp.mean(
        scaled * rows, axis=1, keepdims=True
    )
    return rows_grad, gain_grad


def layer_forward(place, rows, first_values, w_qkv, spread, gains, tables):
    cosine, sine, half_tables, low, high, meta, tile = tables
    gate_w, up_w, down_w, out_w = spread
    gathered = place.gather_row(norm(rows, gains[0]).astype(BF16))
    queries, keys, own_values, mixed = project(gathered, w_qkv, cosine, sine, first_values)
    attended_heads, sums = attend(queries, keys, mixed, low, high, meta, tile)
    attended = place.heads_to_slots(attended_heads)
    middle = rows + dot_nn(attended, out_w)
    ffn_normed = norm(middle, gains[1]).astype(BF16)
    gate = dot_nt(ffn_normed, gate_w)
    up = dot_nt(ffn_normed, up_w)
    activation = (jax.nn.silu(gate) * up).astype(BF16)
    result = middle + dot_nn(activation, down_w)
    kept = (
        rows, gathered, queries, keys, mixed, attended_heads, sums, attended, middle, ffn_normed,
        gate, up, activation,
    )
    return result, own_values, kept


def layer_backward(place, grad, share, carry, w_qkv, spread, gains, kept, tables):
    cosine, sine, half_tables, low, high, meta, tile = tables
    gate_w, up_w, down_w, out_w = spread
    (
        rows, gathered, queries, keys, mixed, attended_heads, sums, attended, middle, ffn_normed,
        gate, up, activation,
    ) = kept
    down_grad = grad.astype(BF16)
    act_grad = dot_nt(down_grad, down_w)
    sigma = jax.nn.sigmoid(gate)
    gate_grad = (act_grad * up * sigma * (1.0 + gate * (1.0 - sigma))).astype(BF16)
    up_grad = (act_grad * gate * sigma).astype(BF16)
    normed_grad = dot_nn(gate_grad, gate_w) + dot_nn(up_grad, up_w)
    middle_back, grad_ffn_gain = norm_back(middle, gains[1], normed_grad)
    middle_grad = grad + middle_back
    attn_grad = middle_grad.astype(BF16)
    attended_grad = dot_nt(attn_grad, out_w).astype(BF16)
    heads_grad = place.slots_to_heads(attended_grad)
    weight_grads = reduce_weights(
        place,
        dot_tn(gate_grad, ffn_normed),
        dot_tn(up_grad, ffn_normed),
        dot_tn(activation, down_grad),
        dot_tn(attended, attn_grad),
    )
    delta = heads_grad.astype(F32) * attended_heads.astype(F32)
    delta = jnp.sum(delta.reshape(SLOTS, -1, HD), axis=2).T
    query_grad, key_grad, value_grad = attend_back(
        queries, keys, mixed, heads_grad, sums, delta, low, high, meta, cosine, sine, half_tables,
        share, carry, tile,
    )
    lin_grad = jnp.concatenate([query_grad, key_grad, value_grad], axis=1)
    input_back = place.scatter_row(dot_nt(lin_grad, w_qkv))
    qkv_grad = dot_tn(gathered, lin_grad).astype(BF16)
    qkv_grad = qkv_grad.reshape(place.data, 2, -1, qkv_grad.shape[1])
    qkv_grad = jnp.stack(place.scatter_data(qkv_grad[:, 0], qkv_grad[:, 1])).astype(BF16)
    rows_back, grad_attn_gain = norm_back(rows, gains[0], input_back)
    return middle_grad + rows_back, value_grad, weight_grads, qkv_grad, (grad_attn_gain, grad_ffn_gain)


def local(
    hidden_in, lengths, w_query, w_key, w_value, w_out, w_gate, w_up, w_down, attn_gain, ffn_gain,
    cotangent,
):
    place = Place()
    width = w_query.shape[2]
    units = w_gate.shape[2] // (2 * place.data)
    tile = min(256, SLOTS // place.size)

    def mine_and_sent(x):
        mine = lax.dynamic_index_in_dim(x, place.row, 0, keepdims=False)
        sent = lax.dynamic_index_in_dim(x, 1 - place.row, 0, keepdims=False)
        return mine, sent

    mine, sent = mine_and_sent(hidden_in)
    rows = place.pick(mine, place.across(sent, 1)).astype(F32)

    w_qkv = jnp.concatenate([w_query[0], w_key[0], w_value[0]], axis=1)
    w_qkv_1 = place.pick(w_qkv, place.across_from_zero(w_qkv))
    w_qkv_2 = place.pick(place.to_core(w_qkv, 0), place.across(w_qkv, 1))
    piece_1, piece_2 = weight_pieces(place, w_gate[0], w_up[0], w_down[0], w_out[0])
    spread_1 = spread_weights(place, piece_1, units)
    spread_2 = spread_weights(place, piece_2, units)
    own_gains = jnp.concatenate([attn_gain, ffn_gain])
    other_gains = place.swap(own_gains)
    gains_1 = place.pick(own_gains, other_gains)
    gains_2 = place.pick(other_gains, own_gains)

    begin, last, cosine, sine = slot_tables(
        lax.dynamic_index_in_dim(lengths, place.row, 0, keepdims=False)
    )
    repeat = min(128, width) // HD
    half_tables = (cosine[:, HD // 2 :].T, sine[:, HD // 2 :].T)
    tables = (
        jnp.tile(cosine, (1, repeat)), jnp.tile(sine, (1, repeat)), half_tables,
        begin[None], last[None], tile_tables(begin, tile), tile,
    )

    result_1, values_1, kept_1 = layer_forward(
        place, rows, None, w_qkv_1, spread_1, gains_1, tables
    )
    hidden_1 = result_1.astype(BF16)
    result_2, _, kept_2 = layer_forward(
        place, hidden_1.astype(F32), values_1, w_qkv_2, spread_2, gains_2, tables
    )
    hidden_2 = result_2.astype(BF16)

    mine, sent = mine_and_sent(cotangent)
    grad = place.pick(mine, place.across(sent.astype(BF16), 1).astype(F32))
    grad_2, carry, ffn_2, qkv_2, gain_2 = layer_backward(
        place, grad, 0.5, None, w_qkv_2, spread_2, gains_2, kept_2, tables
    )
    grad_2 = grad_2.astype(BF16)
    grad_1, _, ffn_1, qkv_1, gain_1 = layer_backward(
        place, grad_2.astype(F32), 1.0, carry, w_qkv_1, spread_1, gains_1, kept_1, tables
    )

    def both_rows(first, second):
        near = place.pick(first, place.to_core(second.astype(BF16), 1).astype(first.dtype))
        far = place.pick(
            place.across(first.astype(BF16), 0), place.across(second.astype(BF16), 1)
        ).astype(first.dtype)
        return jnp.where(place.row == 0, jnp.stack([near, far]), jnp.stack([far, near]))[None]

    layer_outputs = both_rows(hidden_1, hidden_2)
    input_grads = both_rows(grad_1, grad_2.astype(F32))

    qkv_1 = qkv_1.astype(F32) + place.across(qkv_1, 0).astype(F32)
    qkv_2 = place.to_core(qkv_2, 1).astype(F32) + place.across(qkv_2, 1).astype(F32)
    qkv = place.gather_data(place.pick(qkv_1, qkv_2).astype(BF16)).astype(F32)
    qkv = qkv.reshape(D, 3, width)

    own = place.pick(ffn_1, ffn_2)
    other = place.swap(place.pick(ffn_2, ffn_1))
    ffn = jnp.where(place.core == 0, jnp.stack([own, other], 1), jnp.stack([other, own], 1))
    ffn = ffn.astype(F32)
    kinds = [ffn[:, :, i * units : (i + 1) * units].reshape(-1, D) for i in range(3)]
    out = ffn[:, :, 3 * units :].reshape(-1, D)

    gains = lax.psum(jnp.stack([*gain_1, *gain_2]), ("section", "dp", "head"))
    gains = place.pick(gains[:2], gains[2:])
    return (
        layer_outputs, input_grads, qkv[None, :, 0], qkv[None, :, 1], qkv[None, :, 2], out[None],
        kinds[0].T[None], kinds[1].T[None], kinds[2][None], gains[:1], gains[1:],
    )


def solution(mesh):
    in_specs = (
        P("dp", "head", None),
        P("dp", None),
        P("section", None, "head"),
        P("section", None, "head"),
        P("section", None, "head"),
        P("section", "head", None),
        P("section", None, "head"),
        P("section", None, "head"),
        P("section", "head", None),
        P("section", None),
        P("section", None),
        P("dp", "head", None),
    )
    out_specs = (
        P("section", "dp", "head", None),
        P("section", "dp", "head", None),
        P("section", None, "head"),
        P("section", None, "head"),
        P("section", None, "head"),
        P("section", "head", None),
        P("section", None, "head"),
        P("section", None, "head"),
        P("section", "head", None),
        P("section", None),
        P("section", None),
    )
    return jax.shard_map(local, mesh=mesh, in_specs=in_specs, out_specs=out_specs, check_vma=False)
```

time: 2980 us -> 1340 us (0.45)
  waiting for transfers between devices: 1590 us -> 317 us
  matrix products: 873 us -> 122 us
  starting transfers between devices: 17.5 us -> 381 us
  other arithmetic: 413 us -> 129 us
  Pallas kernels: 0 us -> 156 us
  local copies, waits for them, and re-layouts: 42.1 us -> 163 us
    dot_general x147 -> x28, matrix products: 873 us -> 122 us  [the longest x10 56.2 us: dot_nt(): lax.dot_general(a, b, (((1,), (1,)), ((), ())), preferred_element_type=F32)]
    all_gather x12 -> x2, waiting for transfers between devices: 731 us -> 0.02 us  [spread_weights(): full = lax.all_gather(piece, ('section', 'dp', 'head'), axis=0)]
    reduce_scatter x12 -> x0, waiting for transfers between devices: 716 us -> none  [the longest x3 226 us: layer_forward(): lax.psum_scatter(jnp.dot(attended, w_out, preferred_element_type=jnp.floa...]
    ppermute x8 -> x66, starting transfers between devices: 15.7 us -> 381 us  [the longest x13 161 us: swap(): return lax.ppermute(x, 'section', [(0, 1), (1, 0)])]
    ppermute x8 -> x66, waiting for transfers between devices: 9.75 us -> 317 us  [the longest x8 173 us: beside(): return lax.ppermute(x, 'head', pairs)]
    convert_element_type x39 -> x11, other arithmetic: 192 us -> 34 us  [the longest x2 20.6 us: reduce_weights(): summed = summed.astype(BF16)]
    pallas_call x0 -> x6, Pallas kernels: none -> 156 us  [the longest x2 74.7 us: attend_back(): pl.pallas_call(kernel, grid_spec=pltpu.PrefetchScalarGridSpec(num_scalar_...]
    psum x1 -> x0, waiting for transfers between devices: 133 us -> none  [local(): lax.psum(totals[0].astype(jnp.bfloat16), 'dp').astype(jnp.float32)]
  transfers between devices with their start and end apart: 33 -> 68, of which waited for: 26 -> 24; matrix products, arithmetic and copies ran while one was open for 32% -> 29% of each run, Pallas kernels for 0% -> 12%
where the time goes in v1:
time: 1340 us; the launch traced here: 1330 us
  starting transfers between devices  381 us (28%)
  waiting for transfers between devices  317 us (24%)
  local copies, waits for them, and re-layouts  163 us (12%)
  Pallas kernels  156 us (12%)
  other arithmetic  129 us (10%)
  matrix products  122 us (9%)
  blocking collectives  40.1 us (3%)
  between operations  16.8 us (1%)
    ppermute x8, waiting for transfers between devices, beside(): return lax.ppermute(x, 'head', pairs)  173 us
    ppermute x13, starting transfers between devices, swap(): return lax.ppermute(x, 'section', [(0, 1), (1, 0)])  161 us
    ppermute x25, waiting for transfers between devices, flip(): return lax.ppermute(x, 'dp', [(d, d ^ bits) for d in range(self.data)])  129 us
    ppermute x6, starting transfers between devices, around(): lax.ppermute(x, 'head', [(h, (h + shift) % self.size) for h in range(self...  121 us
    pallas_call x2, Pallas kernels, attend_back(): pl.pallas_call(kernel, grid_spec=pltpu.PrefetchScalarGridSpec(num_scalar_...  74.7 us
    pallas_call x2, Pallas kernels, attend(): pl.pallas_call(functools.partial(attend_kernel, tile, heads), grid_spec=p...  60.7 us
    dot_general x10, matrix products, dot_nt(): lax.dot_general(a, b, (((1,), (1,)), ((), ())), preferred_element_type=F32)  56.2 us
    ppermute x25, starting transfers between devices, flip(): return lax.ppermute(x, 'dp', [(d, d ^ bits) for d in range(self.data)])  45.4 us
  transfers between devices with their start and end apart: 68, of which 24 were waited for; matrix products, arithmetic and copies ran while one was open for 29% of the time, Pallas kernels for 12%

profile of v1, /device:TPU:0, one launch (start us, length us, event | category | flops | bytes accessed | tf_op | source)
XLA Modules:
  0.0 1325.9 jit_solution(12893470195499381045)
XLA Ops:
  19.8 4.2 collective-permute-start.1
  35.0 41.9 %collective-permute-done.2 = bf16[512,1024]{1,0:T(8,128)(2,1)} collective-permute-done((bf16[512,1024]{1,0:T(8,128)(2,1)}, bf16[512,1024]{1,0:T(8,128)(2,1)}, u32[]{:S(2)}, u32[]{:S(2)}) %collective-permute-start.2) | collective-permute-done | bytes 1048608 | tf_op jit(solution)/shard_map/ppermute | solution.py:392
  78.2 76.0 %collective-permute-start.3 = (bf16[1024,1024]{1,0:T(8,128)(2,1)S(1)}, bf16[1024,1024]{1,0:T(8,128)(2,1)}, u32[]{:S(2)}, u32[]{:S(2)}) collective-permute-start(bf16[1024,1024]{1,0:T(8,128)(2,1)S(1)} %bitcast.539), channel_id=1, source_target_pairs={{0,16},{16,0},{1,17},{17,1},{2,18},{18,2},{3,19},{19,3},{4,20},{20... | collective-permute-start | bytes 6291464 | tf_op jit(solution)/shard_map/ppermute | solution.py:374
  168.6 4.9 maximum_select_fusion.1.x
  173.5 10.1 project.2
  185.9 30.4 %attend.2 = (bf16[2048,256]{1,0:T(8,128)(2,1)}, f32[4,2048]{1,0:T(4,128)}) custom-call(s32[4,8]{1,0:T(4,128)} %pad_add_fusion.meta.refs_0_, bf16[2048,256]{1,0:T(8,128)(2,1)} %get-tuple-element.27.q_ref, bf16[2048,256]{1,0:T(8,128)(2,1)} %get-tuple-element.28.k_ref, bf16[256,2048]{1,0:T(8,128)(2,1)} %bitcast.623, s32[1,2048]{1,0:T(1,128)} %bitcast.647, ...), custom_call_target="tpu_custom_call" | custom-call | flops 8589934592 | bytes 4194304 | tf_op jit(solution)/shard_map/attend/pallas_call | solution.py:195
  220.3 37.1 %collective-permute-done.6 = bf16[2,512,256]{2,1,0:T(8,128)(2,1)S(1)} collective-permute-done((bf16[2,512,256]{2,1,0:T(8,128)(2,1)S(1)}, bf16[2,512,256]{2,1,0:T(8,128)(2,1)S(1)}, u32[]{:S(2)}, u32[]{:S(2)}) %collective-permute-start.6) | collective-permute-done | bytes 524320 | tf_op jit(solution)/shard_map/ppermute | solution.py:392
  262.4 5.9 copy-done.2
  268.3 5.4 fusion.136
  273.7 8.0 fusion.147
  281.7 6.1 multiply_convert_fusion.5
  287.9 4.2 fusion.28
  294.6 49.4 %collective-permute-done.8 = bf16[512,1024]{1,0:T(8,128)(2,1)S(1)} collective-permute-done((bf16[512,1024]{1,0:T(8,128)(2,1)S(1)}, bf16[512,1024]{1,0:T(8,128)(2,1)S(1)}, u32[]{:S(2)}, u32[]{:S(2)}) %collective-permute-start.8) | collective-permute-done | bytes 1048608 | tf_op jit(solution)/shard_map/ppermute | solution.py:392
  354.5 4.8 maximum_select_fusion.2.x_ref
  359.3 10.1 project.3
  371.6 30.4 %attend.3 = (bf16[2048,256]{1,0:T(8,128)(2,1)}, f32[4,2048]{1,0:T(4,128)}) custom-call(s32[4,8]{1,0:T(4,128)} %pad_add_fusion.meta.refs_0_, bf16[2048,256]{1,0:T(8,128)(2,1)} %get-tuple-element.31.q_ref.refs_1_, bf16[2048,256]{1,0:T(8,128)(2,1)} %get-tuple-element.32.k_ref.refs_2_, bf16[256,2048]{1,0:T(8,128)(2,1)} %bitcast.624, s32[1,2048]{1,0:T(1,128)} %bitcast.648, ...), custom_call_target="tpu_custom_call" | custom-call | flops 8589934592 | bytes 4194304 | tf_op jit(solution)/shard_map/attend/pallas_call | solution.py:195
  403.3 46.3 %collective-permute-start.12 = (bf16[1024,256]{1,0:T(8,128)(2,1)S(1)}, bf16[1024,256]{1,0:T(8,128)(2,1)S(1)}, u32[]{:S(2)}, u32[]{:S(2)}) collective-permute-start(bf16[1024,256]{1,0:T(8,128)(2,1)S(1)} %get-tuple-element.197), channel_id=1, source_target_pairs={{0,16},{16,0},{1,17},{17,1},{2,18},{18,2},{3,19},{19,3},{4,20},{20... | collective-permute-start | bytes 1572872 | tf_op jit(solution)/shard_map/ppermute | solution.py:374
  457.0 13.1 fusion.135
  481.2 5.0 fusion.149
  486.3 5.0 fusion.148
  491.4 10.5 multiply_convert_fusion.2
  501.8 5.2 fusion.150
  507.1 4.2 multiply_reduce_fusion
  516.9 5.0 fusion.157
  529.1 4.1 add_convert_fusion.2
  541.6 5.2 fusion.7
  551.5 7.5 collective-permute-done.18
  559.2 5.5 collective-permute-start.19
  564.7 4.1 pad_maximum_fusion.1
  577.8 37.3 %attend_back.2 = (bf16[2048,256]{1,0:T(8,128)(2,1)}, bf16[2048,256]{1,0:T(8,128)(2,1)}, bf16[2048,256]{1,0:T(8,128)(2,1)}) custom-call(s32[4,8]{1,0:T(4,128)} %pad_add_fusion.meta.refs_0_, bf16[2048,256]{1,0:T(8,128)(2,1)} %get-tuple-element.31.q_ref.refs_1_, bf16[2048,256]{1,0:T(8,128)(2,1)} %get-tuple-element.32.k_ref.refs_2_, ...), custom_call_target="tpu_custom_call" | custom-call | flops 21474836480 | bytes 7340032 | tf_op jit(solution)/shard_map/attend_back/pallas_call | solution.py:324
  627.0 13.9 %collective-permute-start.34 = (bf16[2,128,768]{2,1,0:T(8,128)(2,1)S(1)}, bf16[2,128,768]{2,1,0:T(8,128)(2,1)S(1)}, u32[]{:S(2)}, u32[]{:S(2)}) collective-permute-start(bf16[2,128,768]{2,1,0:T(8,128)(2,1)S(1)} %pad_maximum_fusion.17), channel_id=1, source_target_pairs={{0,4},{4,0},{8,12},{12,8},{1,5},{5,1},{9,13},{13,9},{2,6},{6,2},{1... | collective-permute-start | bytes 1179656 | tf_op jit(solution)/shard_map/ppermute | solution.py:398
  645.4 4.9 collective-permute-done.34
  657.3 4.0 collective-permute-done.37
  665.7 12.4 collective-permute-done.21
  683.9 9.6 multiply_convert_fusion
  693.5 6.1 fusion.152
  699.6 4.1 multiply_reduce_fusion.1
  709.4 4.8 fusion.156
  736.7 4.2 pad_maximum_fusion
  748.3 37.4 %attend_back.3 = (bf16[2048,256]{1,0:T(8,128)(2,1)}, bf16[2048,256]{1,0:T(8,128)(2,1)}, bf16[2048,256]{1,0:T(8,128)(2,1)}) custom-call(s32[4,8]{1,0:T(4,128)} %pad_add_fusion.meta.refs_0_, bf16[2048,256]{1,0:T(8,128)(2,1)} %get-tuple-element.27.q_ref, bf16[2048,256]{1,0:T(8,128)(2,1)} %get-tuple-element.28.k_ref, bf16[256,2048]{1,0:T(8,128)(2,1)} %bitcast.620, ...), custom_call_target="tpu_custom_call" | custom-call | flops 21474836480 | bytes 7340032 | tf_op jit(solution)/shard_map/attend_back/pallas_call | solution.py:324
  794.5 5.7 fusion.153
  800.3 4.1 collective-permute-done.29
  804.4 6.6 collective-permute-start.31
  811.1 8.3 collective-permute-done.31
  825.7 5.0 collective-permute-done.32
  832.1 10.3 add_convert_fusion
  842.5 7.2 fusion.139
  860.5 10.2 add_convert_fusion.1
  870.7 7.1 fusion.138
  877.9 4.4 constant_dynamic-slice_fusion.17
  893.5 54.0 %collective-permute-done.40 = bf16[2,128,768]{2,1,0:T(8,128)(2,1)S(1)} collective-permute-done((bf16[2,128,768]{2,1,0:T(8,128)(2,1)}, bf16[2,128,768]{2,1,0:T(8,128)(2,1)S(1)}, u32[]{:S(2)}, u32[]{:S(2)}) %collective-permute-start.40) | collective-permute-done | bytes 393248 | tf_op jit(solution)/shard_map/ppermute | solution.py:398
  959.2 25.6 %collective-permute-start.24 = (bf16[1024,1024]{1,0:T(8,128)(2,1)}, bf16[1024,1024]{1,0:T(8,128)(2,1)}, u32[]{:S(2)}, u32[]{:S(2)}) collective-permute-start(bf16[1024,1024]{1,0:T(8,128)(2,1)} %fusion.18), channel_id=1, source_target_pairs={{0,16},{16,0},{1,17},{17,1},{2,18},{18,2},{3,19},{19,3},{4,20},{20... | collective-permute-start | bytes 6291464 | tf_op jit(solution)/shard_map/ppermute | solution.py:374
  1004.6 15.1 %collective-permute-done.56 = bf16[2,296,1024]{2,1,0:T(8,128)(2,1)S(1)} collective-permute-done((bf16[2,296,1024]{2,1,0:T(8,128)(2,1)S(1)}, bf16[2,296,1024]{2,1,0:T(8,128)(2,1)S(1)}, u32[]{:S(2)}, u32[]{:S(2)}) %collective-permute-start.56) | collective-permute-done | bytes 1212448 | tf_op jit(solution)/shard_map/ppermute | solution.py:398
  1027.0 55.3 %collective-permute-start.60 = (bf16[296,1024]{1,0:T(8,128)(2,1)S(1)}, bf16[296,1024]{1,0:T(8,128)(2,1)S(1)}, u32[]{:S(2)}, u32[]{:S(2)}) collective-permute-start(bf16[296,1024]{1,0:T(8,128)(2,1)S(1)} %get-tuple-element.148), channel_id=1, source_target_pairs={{0,2},{1,3},{2,0},{3,1},{4,6},{5,7},{6,4},{7,5},{8,10},{9,11},{10,... | collective-permute-start | bytes 1818632 | tf_op jit(solution)/shard_map/ppermute | solution.py:395
  1082.3 19.4 %collective-permute-start.61 = (bf16[296,1024]{1,0:T(8,128)(2,1)S(1)}, bf16[296,1024]{1,0:T(8,128)(2,1)S(1)}, u32[]{:S(2)}, u32[]{:S(2)}) collective-permute-start(bf16[296,1024]{1,0:T(8,128)(2,1)S(1)} %get-tuple-element.149), channel_id=1, source_target_pairs={{0,3},{1,0},{2,1},{3,2},{4,7},{5,4},{6,5},{7,6},{8,11},{9,8},{10,9... | collective-permute-start | bytes 1818632 | tf_op jit(solution)/shard_map/ppermute | solution.py:395
  1103.4 10.7 collective-permute-start.49
  1116.7 33.4 %collective-permute-start.50 = (bf16[296,1024]{1,0:T(8,128)(2,1)S(1)}, bf16[296,1024]{1,0:T(8,128)(2,1)S(1)}, u32[]{:S(2)}, u32[]{:S(2)}) collective-permute-start(bf16[296,1024]{1,0:T(8,128)(2,1)S(1)} %get-tuple-element.138), channel_id=1, source_target_pairs={{0,3},{1,0},{2,1},{3,2},{4,7},{5,4},{6,5},{7,6},{8,11},{9,8},{10,9... | collective-permute-start | bytes 1818632 | tf_op jit(solution)/shard_map/ppermute | solution.py:395
  1157.3 8.2 collective-permute-done.49
  1172.9 12.9 collective-permute-done.64
  1187.3 11.3 collective-permute-done.51
  1198.6 22.1 %collective-permute-start.25 = (bf16[512,1024]{1,0:T(8,128)(2,1)S(1)}, bf16[512,1024]{1,0:T(8,128)(2,1)S(1)}, u32[]{:S(2)}, u32[]{:S(2)}) collective-permute-start(bf16[512,1024]{1,0:T(8,128)(2,1)S(1)} %fusion.69), channel_id=1, source_target_pairs={{0,1},{1,0},{2,3},{3,2},{4,5},{5,4},{6,7},{7,6},{8,9},{9,8},{10,11... | collective-permute-start | bytes 3145736 | tf_op jit(solution)/shard_map/ppermute | solution.py:392
  1223.5 20.6 %collective-permute-done.25 = bf16[512,1024]{1,0:T(8,128)(2,1)S(1)} collective-permute-done((bf16[512,1024]{1,0:T(8,128)(2,1)S(1)}, bf16[512,1024]{1,0:T(8,128)(2,1)S(1)}, u32[]{:S(2)}, u32[]{:S(2)}) %collective-permute-start.25) | collective-permute-done | bytes 1048608 | tf_op jit(solution)/shard_map/ppermute | solution.py:392
  1252.3 3.9 reshape.574
  1266.3 40.1 %psum.7 = f32[4,1024]{1,0:T(4,128)S(1)} all-reduce(f32[4,1024]{1,0:T(4,128)S(1)} %pad_maximum_fusion.24), channel_id=1, replica_groups=mesh['section'=2,'dp'=4,'head'=4] {'section','dp','head'}, use_global_device_ids=true, to_apply=%region_19.20 | all-reduce | flops 4096 | bytes 32768 | tf_op jit(solution)/shard_map/psum | solution.py:686
  (577 shorter events, 319.6 us)
Async XLA Ops:
  7.2 250.6 %all-gather.5.cloned.1.call-start = ((), (), s32[]{:S(2)}) async-start(), calls=%async_computation | async-start | bytes 20004864 | tf_op jit(solution)/shard_map/all_gather | solution.py:509
  16.3 440.8 %all-gather.7.cloned.1.call-start = ((), (), s32[]{:S(2)}) async-start(), calls=%async_computation.1 | async-start | bytes 20004864 | tf_op jit(solution)/shard_map/all_gather | solution.py:509
  18.1 10.5 collective-permute-start
  19.8 8.7 collective-permute-start.1
  25.2 140.5 %collective-permute-start.4 = (bf16[1024,768]{1,0:T(8,128)(2,1)}, bf16[1024,768]{1,0:T(8,128)(2,1)}, u32[]{:S(2)}, u32[]{:S(2)}) collective-permute-start(bf16[1024,768]{1,0:T(8,128)(2,1)} %pad_maximum_fusion.6), channel_id=1, source_target_pairs={{0,18},{1,19},{2,16},{3,17},{4,22},{5,23},{6,20},{7,21},{8,26},{9,... | collective-permute-start | bytes 4718600 | tf_op jit(solution)/shard_map/ppermute | solution.py:387
  31.2 45.7 %collective-permute-start.2 = (bf16[512,1024]{1,0:T(8,128)(2,1)}, bf16[512,1024]{1,0:T(8,128)(2,1)}, u32[]{:S(2)}, u32[]{:S(2)}) collective-permute-start(bf16[512,1024]{1,0:T(8,128)(2,1)} %get-tuple-element.99), channel_id=1, source_target_pairs={{0,1},{1,0},{2,3},{3,2},{4,5},{5,4},{6,7},{7,6},{8,9},{9,8},{10,11... | collective-permute-start | bytes 3145736 | tf_op jit(solution)/shard_map/ppermute | solution.py:392
  78.2 90.4 %collective-permute-start.3 = (bf16[1024,1024]{1,0:T(8,128)(2,1)S(1)}, bf16[1024,1024]{1,0:T(8,128)(2,1)}, u32[]{:S(2)}, u32[]{:S(2)}) collective-permute-start(bf16[1024,1024]{1,0:T(8,128)(2,1)S(1)} %bitcast.539), channel_id=1, source_target_pairs={{0,16},{16,0},{1,17},{17,1},{2,18},{18,2},{3,19},{19,3},{4,20},{20... | collective-permute-start | bytes 6291464 | tf_op jit(solution)/shard_map/ppermute | solution.py:374
  220.1 37.3 %collective-permute-start.6 = (bf16[2,512,256]{2,1,0:T(8,128)(2,1)S(1)}, bf16[2,512,256]{2,1,0:T(8,128)(2,1)S(1)}, u32[]{:S(2)}, u32[]{:S(2)}) collective-permute-start(bf16[2,512,256]{2,1,0:T(8,128)(2,1)S(1)} %fusion.94), channel_id=1, source_target_pairs={{0,1},{1,0},{2,3},{3,2},{4,5},{5,4},{6,7},{7,6},{8,9},{9,8},{10,11... | collective-permute-start | bytes 1572872 | tf_op jit(solution)/shard_map/ppermute | solution.py:392
  294.5 49.5 %collective-permute-start.8 = (bf16[512,1024]{1,0:T(8,128)(2,1)S(1)}, bf16[512,1024]{1,0:T(8,128)(2,1)S(1)}, u32[]{:S(2)}, u32[]{:S(2)}) collective-permute-start(bf16[512,1024]{1,0:T(8,128)(2,1)S(1)} %get-tuple-element.97), channel_id=1, source_target_pairs={{0,1},{1,0},{2,3},{3,2},{4,5},{5,4},{6,7},{7,6},{8,9},{9,8},{10,11... | collective-permute-start | bytes 3145736 | tf_op jit(solution)/shard_map/ppermute | solution.py:392
  344.1 10.3 collective-permute-start.9
  344.2 7.5 collective-permute-start.10
  345.5 6.2 collective-permute-start.11
  350.1 101.4 %collective-permute-start.17 = (bf16[512,1024]{1,0:T(8,128)(2,1)}, bf16[512,1024]{1,0:T(8,128)(2,1)}, u32[]{:S(2)}, u32[]{:S(2)}) collective-permute-start(bf16[512,1024]{1,0:T(8,128)(2,1)} %fusion.67), channel_id=1, source_target_pairs={{16,18},{17,19},{18,16},{19,17},{20,22},{21,23},{22,20},{23,21},{2... | collective-permute-start | bytes 3145736 | tf_op jit(solution)/shard_map/ppermute | solution.py:382
  403.3 52.7 %collective-permute-start.12 = (bf16[1024,256]{1,0:T(8,128)(2,1)S(1)}, bf16[1024,256]{1,0:T(8,128)(2,1)S(1)}, u32[]{:S(2)}, u32[]{:S(2)}) collective-permute-start(bf16[1024,256]{1,0:T(8,128)(2,1)S(1)} %get-tuple-element.197), channel_id=1, source_target_pairs={{0,16},{16,0},{1,17},{17,1},{2,18},{18,2},{3,19},{19,3},{4,20},{20... | collective-permute-start | bytes 1572872 | tf_op jit(solution)/shard_map/ppermute | solution.py:374
  456.9 19.6 %collective-permute-start.13 = (bf16[2,512,256]{2,1,0:T(8,128)(2,1)}, bf16[2,512,256]{2,1,0:T(8,128)(2,1)}, u32[]{:S(2)}, u32[]{:S(2)}) collective-permute-start(bf16[2,512,256]{2,1,0:T(8,128)(2,1)} %fusion.89), channel_id=1, source_target_pairs={{0,1},{1,0},{2,3},{3,2},{4,5},{5,4},{6,7},{7,6},{8,9},{9,8},{10,11... | collective-permute-start | bytes 1572872 | tf_op jit(solution)/shard_map/ppermute | solution.py:392
  471.9 170.4 %collective-permute-start.15 = (bf16[512,1024]{1,0:T(8,128)(2,1)}, bf16[512,1024]{1,0:T(8,128)(2,1)}, u32[]{:S(2)}, u32[]{:S(2)}) collective-permute-start(bf16[512,1024]{1,0:T(8,128)(2,1)} %get-tuple-element.249), channel_id=1, source_target_pairs={{16,2},{17,3},{18,0},{19,1},{20,6},{21,7},{22,4},{23,5},{24,10},{2... | collective-permute-start | bytes 3145736 | tf_op jit(solution)/shard_map/ppermute | solution.py:382
  533.2 93.8 %collective-permute-start.14 = (bf16[512,1024]{1,0:T(8,128)(2,1)}, bf16[512,1024]{1,0:T(8,128)(2,1)}, u32[]{:S(2)}, u32[]{:S(2)}) collective-permute-start(bf16[512,1024]{1,0:T(8,128)(2,1)} %add_convert_fusion.2), channel_id=1, source_target_pairs={{0,16},{1,17},{2,18},{3,19},{4,20},{5,21},{6,22},{7,23},{8,24},{9,... | collective-permute-start | bytes 3145736 | tf_op jit(solution)/shard_map/ppermute | solution.py:377
  537.0 105.4 %collective-permute-start.16 = (bf16[512,1024]{1,0:T(8,128)(2,1)}, bf16[512,1024]{1,0:T(8,128)(2,1)}, u32[]{:S(2)}, u32[]{:S(2)}) collective-permute-start(bf16[512,1024]{1,0:T(8,128)(2,1)} %add_convert_fusion.2), channel_id=1, source_target_pairs={{16,18},{17,19},{18,16},{19,17},{20,22},{21,23},{22,20},{23,21},{2... | collective-permute-start | bytes 3145736 | tf_op jit(solution)/shard_map/ppermute | solution.py:382
  539.9 19.2 %collective-permute-start.18 = (bf16[2,512,256]{2,1,0:T(8,128)(2,1)}, bf16[2,512,256]{2,1,0:T(8,128)(2,1)S(1)}, u32[]{:S(2)}, u32[]{:S(2)}) collective-permute-start(bf16[2,512,256]{2,1,0:T(8,128)(2,1)} %get-tuple-element.183), channel_id=1, source_target_pairs={{0,1},{1,0},{2,3},{3,2},{4,5},{5,4},{6,7},{7,6},{8,9},{9,8},{10,11... | collective-permute-start | bytes 1572872 | tf_op jit(solution)/shard_map/ppermute | solution.py:392
  559.2 10.7 collective-permute-start.19
  568.8 263.3 %collective-permute-start.54 = (bf16[4,4,296,1024]{3,2,1,0:T(8,128)(2,1)}, bf16[4,4,296,1024]{3,2,1,0:T(8,128)(2,1)}, u32[]{:S(2)}, u32[]{:S(2)}) collective-permute-start(bf16[4,4,296,1024]{3,2,1,0:T(8,128)(2,1)} %pad_maximum_fusion.1), channel_id=1, source_target_pairs={{0,16},{16,0},{1,17},{17,1},{2,18},{18,2},{3,19},{19,3},{4,20},{20... | collective-permute-start | bytes 29097992 | tf_op jit(solution)/shard_map/ppermute | solution.py:374
  626.5 25.7 %collective-permute-start.20 = (bf16[1024,1024]{1,0:T(8,128)(2,1)S(1)}, bf16[1024,1024]{1,0:T(8,128)(2,1)S(1)}, u32[]{:S(2)}, u32[]{:S(2)}) collective-permute-start(bf16[1024,1024]{1,0:T(8,128)(2,1)S(1)} %fusion.17), channel_id=1, source_target_pairs={{0,16},{16,0},{1,17},{17,1},{2,18},{18,2},{3,19},{19,3},{4,20},{20... | collective-permute-start | bytes 6291464 | tf_op jit(solution)/shard_map/ppermute | solution.py:374
  627.0 23.2 %collective-permute-start.34 = (bf16[2,128,768]{2,1,0:T(8,128)(2,1)S(1)}, bf16[2,128,768]{2,1,0:T(8,128)(2,1)S(1)}, u32[]{:S(2)}, u32[]{:S(2)}) collective-permute-start(bf16[2,128,768]{2,1,0:T(8,128)(2,1)S(1)} %pad_maximum_fusion.17), channel_id=1, source_target_pairs={{0,4},{4,0},{8,12},{12,8},{1,5},{5,1},{9,13},{13,9},{2,6},{6,2},{1... | collective-permute-start | bytes 1179656 | tf_op jit(solution)/shard_map/ppermute | solution.py:398
  642.3 12.9 collective-permute-start.36
  650.3 7.0 collective-permute-start.35
  653.5 24.6 %collective-permute-start.21 = (bf16[512,1024]{1,0:T(8,128)(2,1)S(1)}, bf16[512,1024]{1,0:T(8,128)(2,1)S(1)}, u32[]{:S(2)}, u32[]{:S(2)}) collective-permute-start(bf16[512,1024]{1,0:T(8,128)(2,1)S(1)} %fusion.68), channel_id=1, source_target_pairs={{0,1},{1,0},{2,3},{3,2},{4,5},{5,4},{6,7},{7,6},{8,9},{9,8},{10,11... | collective-permute-start | bytes 3145736 | tf_op jit(solution)/shard_map/ppermute | solution.py:392
  655.3 6.0 collective-permute-start.37
  662.2 221.7 %collective-permute-start.38 = (bf16[2,128,768]{2,1,0:T(8,128)(2,1)}, bf16[2,128,768]{2,1,0:T(8,128)(2,1)}, u32[]{:S(2)}, u32[]{:S(2)}) collective-permute-start(bf16[2,128,768]{2,1,0:T(8,128)(2,1)} %pad_maximum_fusion.19), channel_id=1, source_target_pairs={{0,16},{1,17},{2,18},{3,19},{4,20},{5,21},{6,22},{7,23},{8,24},{9,... | collective-permute-start | bytes 1179656 | tf_op jit(solution)/shard_map/ppermute | solution.py:377
  664.3 221.1 %collective-permute-start.39 = (bf16[2,128,768]{2,1,0:T(8,128)(2,1)}, bf16[2,128,768]{2,1,0:T(8,128)(2,1)}, u32[]{:S(2)}, u32[]{:S(2)}) collective-permute-start(bf16[2,128,768]{2,1,0:T(8,128)(2,1)} %pad_maximum_fusion.19), channel_id=1, source_target_pairs={{16,18},{17,19},{18,16},{19,17},{20,22},{21,23},{22,20},{23,21},{2... | collective-permute-start | bytes 1179656 | tf_op jit(solution)/shard_map/ppermute | solution.py:382
  721.9 13.2 collective-permute-start.22
  735.1 6.9 collective-permute-start.23
  741.0 117.4 %collective-permute-start.43 = (bf16[4,4,296,1024]{3,2,1,0:T(8,128)(2,1)}, bf16[4,4,296,1024]{3,2,1,0:T(8,128)(2,1)}, u32[]{:S(2)}, u32[]{:S(2)}) collective-permute-start(bf16[4,4,296,1024]{3,2,1,0:T(8,128)(2,1)} %pad_maximum_fusion), channel_id=1, source_target_pairs={{0,16},{16,0},{1,17},{17,1},{2,18},{18,2},{3,19},{19,3},{4,20},{20... | collective-permute-start | bytes 29097992 | tf_op jit(solution)/shard_map/ppermute | solution.py:374
  793.3 11.1 collective-permute-start.29
  804.4 15.0 %collective-permute-start.31 = (bf16[2,128,768]{2,1,0:T(8,128)(2,1)S(1)}, bf16[2,128,768]{2,1,0:T(8,128)(2,1)S(1)}, u32[]{:S(2)}, u32[]{:S(2)}) collective-permute-start(bf16[2,128,768]{2,1,0:T(8,128)(2,1)S(1)} %pad_maximum_fusion.15), channel_id=1, source_target_pairs={{0,8},{4,12},{8,0},{12,4},{1,9},{5,13},{9,1},{13,5},{2,10},{6,14},... | collective-permute-start | bytes 1179656 | tf_op jit(solution)/shard_map/ppermute | solution.py:398
  830.8 54.6 %collective-permute-start.33 = (bf16[2,128,768]{2,1,0:T(8,128)(2,1)S(1)}, bf16[2,128,768]{2,1,0:T(8,128)(2,1)}, u32[]{:S(2)}, u32[]{:S(2)}) collective-permute-start(bf16[2,128,768]{2,1,0:T(8,128)(2,1)S(1)} %pad_maximum_fusion.16), channel_id=1, source_target_pairs={{16,2},{17,3},{18,0},{19,1},{20,6},{21,7},{22,4},{23,5},{24,10},{2... | collective-permute-start | bytes 1179656 | tf_op jit(solution)/shard_map/ppermute | solution.py:382
  854.2 132.9 %collective-permute-start.55 = (bf16[2,2,296,1024]{3,2,1,0:T(8,128)(2,1)}, bf16[2,2,296,1024]{3,2,1,0:T(8,128)(2,1)}, u32[]{:S(2)}, u32[]{:S(2)}) collective-permute-start(bf16[2,2,296,1024]{3,2,1,0:T(8,128)(2,1)} %pad_maximum_fusion.4), channel_id=1, source_target_pairs={{0,4},{4,0},{8,12},{12,8},{1,5},{5,1},{9,13},{13,9},{2,6},{6,2},{1... | collective-permute-start | bytes 7274504 | tf_op jit(solution)/shard_map/ppermute | solution.py:398
  858.4 132.5 %collective-permute-start.57 = (bf16[2,2,296,1024]{3,2,1,0:T(8,128)(2,1)}, bf16[2,2,296,1024]{3,2,1,0:T(8,128)(2,1)}, u32[]{:S(2)}, u32[]{:S(2)}) collective-permute-start(bf16[2,2,296,1024]{3,2,1,0:T(8,128)(2,1)} %pad_maximum_fusion.5), channel_id=1, source_target_pairs={{0,8},{4,12},{8,0},{12,4},{1,9},{5,13},{9,1},{13,5},{2,10},{6,14},... | collective-permute-start | bytes 7274504 | tf_op jit(solution)/shard_map/ppermute | solution.py:398
  883.9 111.9 %collective-permute-start.44 = (bf16[2,2,296,1024]{3,2,1,0:T(8,128)(2,1)}, bf16[2,2,296,1024]{3,2,1,0:T(8,128)(2,1)}, u32[]{:S(2)}, u32[]{:S(2)}) collective-permute-start(bf16[2,2,296,1024]{3,2,1,0:T(8,128)(2,1)} %pad_maximum_fusion.2), channel_id=1, source_target_pairs={{0,4},{4,0},{8,12},{12,8},{1,5},{5,1},{9,13},{13,9},{2,6},{6,2},{1... | collective-permute-start | bytes 7274504 | tf_op jit(solution)/shard_map/ppermute | solution.py:398
  887.5 60.0 %collective-permute-start.40 = (bf16[2,128,768]{2,1,0:T(8,128)(2,1)}, bf16[2,128,768]{2,1,0:T(8,128)(2,1)S(1)}, u32[]{:S(2)}, u32[]{:S(2)}) collective-permute-start(bf16[2,128,768]{2,1,0:T(8,128)(2,1)} %select_convert_fusion), channel_id=1, source_target_pairs={{0,4},{4,0},{8,12},{12,8},{1,5},{5,1},{9,13},{13,9},{2,6},{6,2},{1... | collective-permute-start | bytes 1179656 | tf_op jit(solution)/shard_map/ppermute | solution.py:398
  888.1 71.1 %collective-permute-start.41 = (bf16[2,128,768]{2,1,0:T(8,128)(2,1)}, bf16[2,128,768]{2,1,0:T(8,128)(2,1)S(1)}, u32[]{:S(2)}, u32[]{:S(2)}) collective-permute-start(bf16[2,128,768]{2,1,0:T(8,128)(2,1)} %select_convert_fusion), channel_id=1, source_target_pairs={{0,8},{4,12},{8,0},{12,4},{1,9},{5,13},{9,1},{13,5},{2,10},{6,14},... | collective-permute-start | bytes 1179656 | tf_op jit(solution)/shard_map/ppermute | solution.py:398
  947.5 52.3 %collective-permute-start.46 = (bf16[2,2,296,1024]{3,2,1,0:T(8,128)(2,1)}, bf16[2,2,296,1024]{3,2,1,0:T(8,128)(2,1)}, u32[]{:S(2)}, u32[]{:S(2)}) collective-permute-start(bf16[2,2,296,1024]{3,2,1,0:T(8,128)(2,1)} %pad_maximum_fusion.3), channel_id=1, source_target_pairs={{0,8},{4,12},{8,0},{12,4},{1,9},{5,13},{9,1},{13,5},{2,10},{6,14},... | collective-permute-start | bytes 7274504 | tf_op jit(solution)/shard_map/ppermute | solution.py:398
  959.2 192.6 %collective-permute-start.24 = (bf16[1024,1024]{1,0:T(8,128)(2,1)}, bf16[1024,1024]{1,0:T(8,128)(2,1)}, u32[]{:S(2)}, u32[]{:S(2)}) collective-permute-start(bf16[1024,1024]{1,0:T(8,128)(2,1)} %fusion.18), channel_id=1, source_target_pairs={{0,16},{16,0},{1,17},{17,1},{2,18},{18,2},{3,19},{19,3},{4,20},{20... | collective-permute-start | bytes 6291464 | tf_op jit(solution)/shard_map/ppermute | solution.py:374
  990.1 29.7 %collective-permute-start.56 = (bf16[2,296,1024]{2,1,0:T(8,128)(2,1)S(1)}, bf16[2,296,1024]{2,1,0:T(8,128)(2,1)S(1)}, u32[]{:S(2)}, u32[]{:S(2)}) collective-permute-start(bf16[2,296,1024]{2,1,0:T(8,128)(2,1)S(1)} %fusion.41), channel_id=1, source_target_pairs={{0,8},{4,12},{8,0},{12,4},{1,9},{5,13},{9,1},{13,5},{2,10},{6,14},... | collective-permute-start | bytes 3637256 | tf_op jit(solution)/shard_map/ppermute | solution.py:398
  994.5 29.6 %collective-permute-start.58 = (bf16[2,296,1024]{2,1,0:T(8,128)(2,1)S(1)}, bf16[2,296,1024]{2,1,0:T(8,128)(2,1)S(1)}, u32[]{:S(2)}, u32[]{:S(2)}) collective-permute-start(bf16[2,296,1024]{2,1,0:T(8,128)(2,1)S(1)} %fusion.42), channel_id=1, source_target_pairs={{0,4},{4,0},{8,12},{12,8},{1,5},{5,1},{9,13},{13,9},{2,6},{6,2},{1... | collective-permute-start | bytes 3637256 | tf_op jit(solution)/shard_map/ppermute | solution.py:398
  998.9 83.4 %collective-permute-start.45 = (bf16[2,296,1024]{2,1,0:T(8,128)(2,1)S(1)}, bf16[2,296,1024]{2,1,0:T(8,128)(2,1)S(1)}, u32[]{:S(2)}, u32[]{:S(2)}) collective-permute-start(bf16[2,296,1024]{2,1,0:T(8,128)(2,1)S(1)} %fusion.39), channel_id=1, source_target_pairs={{0,8},{4,12},{8,0},{12,4},{1,9},{5,13},{9,1},{13,5},{2,10},{6,14},... | collective-permute-start | bytes 3637256 | tf_op jit(solution)/shard_map/ppermute | solution.py:398
  1003.3 99.0 %collective-permute-start.47 = (bf16[2,296,1024]{2,1,0:T(8,128)(2,1)S(1)}, bf16[2,296,1024]{2,1,0:T(8,128)(2,1)S(1)}, u32[]{:S(2)}, u32[]{:S(2)}) collective-permute-start(bf16[2,296,1024]{2,1,0:T(8,128)(2,1)S(1)} %fusion.40), channel_id=1, source_target_pairs={{0,4},{4,0},{8,12},{12,8},{1,5},{5,1},{9,13},{13,9},{2,6},{6,2},{1... | collective-permute-start | bytes 3637256 | tf_op jit(solution)/shard_map/ppermute | solution.py:398
  1025.3 78.1 %collective-permute-start.59 = (bf16[296,1024]{1,0:T(8,128)(2,1)S(1)}, bf16[296,1024]{1,0:T(8,128)(2,1)S(1)}, u32[]{:S(2)}, u32[]{:S(2)}) collective-permute-start(bf16[296,1024]{1,0:T(8,128)(2,1)S(1)} %get-tuple-element.147), channel_id=1, source_target_pairs={{0,1},{1,2},{2,3},{3,0},{4,5},{5,6},{6,7},{7,4},{8,9},{9,10},{10,1... | collective-permute-start | bytes 1818632 | tf_op jit(solution)/shard_map/ppermute | solution.py:395
  1027.0 89.6 %collective-permute-start.60 = (bf16[296,1024]{1,0:T(8,128)(2,1)S(1)}, bf16[296,1024]{1,0:T(8,128)(2,1)S(1)}, u32[]{:S(2)}, u32[]{:S(2)}) collective-permute-start(bf16[296,1024]{1,0:T(8,128)(2,1)S(1)} %get-tuple-element.148), channel_id=1, source_target_pairs={{0,2},{1,3},{2,0},{3,1},{4,6},{5,7},{6,4},{7,5},{8,10},{9,11},{10,... | collective-permute-start | bytes 1818632 | tf_op jit(solution)/shard_map/ppermute | solution.py:395
  1082.3 67.7 %collective-permute-start.61 = (bf16[296,1024]{1,0:T(8,128)(2,1)S(1)}, bf16[296,1024]{1,0:T(8,128)(2,1)S(1)}, u32[]{:S(2)}, u32[]{:S(2)}) collective-permute-start(bf16[296,1024]{1,0:T(8,128)(2,1)S(1)} %get-tuple-element.149), channel_id=1, source_target_pairs={{0,3},{1,0},{2,1},{3,2},{4,7},{5,4},{6,5},{7,6},{8,11},{9,8},{10,9... | collective-permute-start | bytes 1818632 | tf_op jit(solution)/shard_map/ppermute | solution.py:395
  1103.3 52.6 %collective-permute-start.48 = (bf16[296,1024]{1,0:T(8,128)(2,1)S(1)}, bf16[296,1024]{1,0:T(8,128)(2,1)S(1)}, u32[]{:S(2)}, u32[]{:S(2)}) collective-permute-start(bf16[296,1024]{1,0:T(8,128)(2,1)S(1)} %get-tuple-element.136), channel_id=1, source_target_pairs={{0,1},{1,2},{2,3},{3,0},{4,5},{5,6},{6,7},{7,4},{8,9},{9,10},{10,1... | collective-permute-start | bytes 1818632 | tf_op jit(solution)/shard_map/ppermute | solution.py:395
  1103.4 62.1 %collective-permute-start.49 = (bf16[296,1024]{1,0:T(8,128)(2,1)S(1)}, bf16[296,1024]{1,0:T(8,128)(2,1)S(1)}, u32[]{:S(2)}, u32[]{:S(2)}) collective-permute-start(bf16[296,1024]{1,0:T(8,128)(2,1)S(1)} %get-tuple-element.137), channel_id=1, source_target_pairs={{0,2},{1,3},{2,0},{3,1},{4,6},{5,7},{6,4},{7,5},{8,10},{9,11},{10,... | collective-permute-start | bytes 1818632 | tf_op jit(solution)/shard_map/ppermute | solution.py:395
  1116.7 51.6 %collective-permute-start.50 = (bf16[296,1024]{1,0:T(8,128)(2,1)S(1)}, bf16[296,1024]{1,0:T(8,128)(2,1)S(1)}, u32[]{:S(2)}, u32[]{:S(2)}) collective-permute-start(bf16[296,1024]{1,0:T(8,128)(2,1)S(1)} %get-tuple-element.138), channel_id=1, source_target_pairs={{0,3},{1,0},{2,1},{3,2},{4,7},{5,4},{6,5},{7,6},{8,11},{9,8},{10,9... | collective-permute-start | bytes 1818632 | tf_op jit(solution)/shard_map/ppermute | solution.py:395
  1150.9 19.7 %collective-permute-start.62 = (bf16[296,1024]{1,0:T(8,128)(2,1)S(1)}, bf16[296,1024]{1,0:T(8,128)(2,1)S(1)}, u32[]{:S(2)}, u32[]{:S(2)}) collective-permute-start(bf16[296,1024]{1,0:T(8,128)(2,1)S(1)} %get-tuple-element.89), channel_id=1, source_target_pairs={{0,4},{4,0},{8,12},{12,8},{1,5},{5,1},{9,13},{13,9},{2,6},{6,2},{1... | collective-permute-start | bytes 1818632 | tf_op jit(solution)/shard_map/ppermute | solution.py:398
  1154.5 17.5 %collective-permute-start.63 = (bf16[296,1024]{1,0:T(8,128)(2,1)S(1)}, bf16[296,1024]{1,0:T(8,128)(2,1)S(1)}, u32[]{:S(2)}, u32[]{:S(2)}) collective-permute-start(bf16[296,1024]{1,0:T(8,128)(2,1)S(1)} %get-tuple-element.89), channel_id=1, source_target_pairs={{0,8},{4,12},{8,0},{12,4},{1,9},{5,13},{9,1},{13,5},{2,10},{6,14},... | collective-permute-start | bytes 1818632 | tf_op jit(solution)/shard_map/ppermute | solution.py:398
  1155.9 89.1 %collective-permute-start.26 = (bf16[512,1024]{1,0:T(8,128)(2,1)}, bf16[512,1024]{1,0:T(8,128)(2,1)S(1)}, u32[]{:S(2)}, u32[]{:S(2)}) collective-permute-start(bf16[512,1024]{1,0:T(8,128)(2,1)} %fusion.34), channel_id=1, source_target_pairs={{0,16},{1,17},{2,18},{3,19},{4,20},{5,21},{6,22},{7,23},{8,24},{9,... | collective-permute-start | bytes 3145736 | tf_op jit(solution)/shard_map/ppermute | solution.py:377
  1165.5 141.5 %collective-permute-start.28 = (bf16[512,1024]{1,0:T(8,128)(2,1)}, bf16[512,1024]{1,0:T(8,128)(2,1)}, u32[]{:S(2)}, u32[]{:S(2)}) collective-permute-start(bf16[512,1024]{1,0:T(8,128)(2,1)} %fusion.34), channel_id=1, source_target_pairs={{16,18},{17,19},{18,16},{19,17},{20,22},{21,23},{22,20},{23,21},{2... | collective-permute-start | bytes 3145736 | tf_op jit(solution)/shard_map/ppermute | solution.py:382
  1168.3 17.6 %collective-permute-start.64 = (bf16[296,1024]{1,0:T(8,128)(2,1)S(1)}, bf16[296,1024]{1,0:T(8,128)(2,1)S(1)}, u32[]{:S(2)}, u32[]{:S(2)}) collective-permute-start(bf16[296,1024]{1,0:T(8,128)(2,1)S(1)} %get-tuple-element.89), channel_id=1, source_target_pairs={{0,12},{4,8},{8,4},{12,0},{1,13},{5,9},{9,5},{13,1},{2,14},{6,10},... | collective-permute-start | bytes 1818632 | tf_op jit(solution)/shard_map/ppermute | solution.py:398
  1170.6 28.0 %collective-permute-start.51 = (bf16[296,1024]{1,0:T(8,128)(2,1)S(1)}, bf16[296,1024]{1,0:T(8,128)(2,1)S(1)}, u32[]{:S(2)}, u32[]{:S(2)}) collective-permute-start(bf16[296,1024]{1,0:T(8,128)(2,1)S(1)} %get-tuple-element.87), channel_id=1, source_target_pairs={{0,4},{4,0},{8,12},{12,8},{1,5},{5,1},{9,13},{13,9},{2,6},{6,2},{1... | collective-permute-start | bytes 1818632 | tf_op jit(solution)/shard_map/ppermute | solution.py:398
  1172.0 48.7 %collective-permute-start.52 = (bf16[296,1024]{1,0:T(8,128)(2,1)S(1)}, bf16[296,1024]{1,0:T(8,128)(2,1)S(1)}, u32[]{:S(2)}, u32[]{:S(2)}) collective-permute-start(bf16[296,1024]{1,0:T(8,128)(2,1)S(1)} %get-tuple-element.87), channel_id=1, source_target_pairs={{0,8},{4,12},{8,0},{12,4},{1,9},{5,13},{9,1},{13,5},{2,10},{6,14},... | collective-permute-start | bytes 1818632 | tf_op jit(solution)/shard_map/ppermute | solution.py:398
  1185.8 35.0 %collective-permute-start.53 = (bf16[296,1024]{1,0:T(8,128)(2,1)S(1)}, bf16[296,1024]{1,0:T(8,128)(2,1)S(1)}, u32[]{:S(2)}, u32[]{:S(2)}) collective-permute-start(bf16[296,1024]{1,0:T(8,128)(2,1)S(1)} %get-tuple-element.87), channel_id=1, source_target_pairs={{0,12},{4,8},{8,4},{12,0},{1,13},{5,9},{9,5},{13,1},{2,14},{6,10},... | collective-permute-start | bytes 1818632 | tf_op jit(solution)/shard_map/ppermute | solution.py:398
  1198.6 45.5 %collective-permute-start.25 = (bf16[512,1024]{1,0:T(8,128)(2,1)S(1)}, bf16[512,1024]{1,0:T(8,128)(2,1)S(1)}, u32[]{:S(2)}, u32[]{:S(2)}) collective-permute-start(bf16[512,1024]{1,0:T(8,128)(2,1)S(1)} %fusion.69), channel_id=1, source_target_pairs={{0,1},{1,0},{2,3},{3,2},{4,5},{5,4},{6,7},{7,6},{8,9},{9,8},{10,11... | collective-permute-start | bytes 3145736 | tf_op jit(solution)/shard_map/ppermute | solution.py:392
  1220.7 28.5 %collective-permute-start.42 = (bf16[2,128,768]{2,1,0:T(8,128)(2,1)}, bf16[2,128,768]{2,1,0:T(8,128)(2,1)S(1)}, u32[]{:S(2)}, u32[]{:S(2)}) collective-permute-start(bf16[2,128,768]{2,1,0:T(8,128)(2,1)} %select_convert_fusion), channel_id=1, source_target_pairs={{0,12},{4,8},{8,4},{12,0},{1,13},{5,9},{9,5},{13,1},{2,14},{6,10},... | collective-permute-start | bytes 1179656 | tf_op jit(solution)/shard_map/ppermute | solution.py:398
  1223.5 87.4 %collective-permute-start.65 = (bf16[4,296,1024]{2,1,0:T(8,128)(2,1)}, bf16[4,296,1024]{2,1,0:T(8,128)(2,1)}, u32[]{:S(2)}, u32[]{:S(2)}) collective-permute-start(bf16[4,296,1024]{2,1,0:T(8,128)(2,1)} %get-tuple-element.135), channel_id=1, source_target_pairs={{0,16},{16,0},{1,17},{17,1},{2,18},{18,2},{3,19},{19,3},{4,20},{20... | collective-permute-start | bytes 7274504 | tf_op jit(solution)/shard_map/ppermute | solution.py:374
  1246.9 60.1 %collective-permute-start.27 = (bf16[512,1024]{1,0:T(8,128)(2,1)}, bf16[512,1024]{1,0:T(8,128)(2,1)}, u32[]{:S(2)}, u32[]{:S(2)}) collective-permute-start(bf16[512,1024]{1,0:T(8,128)(2,1)} %get-tuple-element.91), channel_id=1, source_target_pairs={{16,2},{17,3},{18,0},{19,1},{20,6},{21,7},{22,4},{23,5},{24,10},{2... | collective-permute-start | bytes 3145736 | tf_op jit(solution)/shard_map/ppermute | solution.py:382
  (121 other events, 1810.3 us)
Sparse Core Ops, SparseCore 0:
  16.4 170.1 all-gather.4
  190.0 152.2 all-gather.6

commit v2 on v1

--- a/solution.py
+++ b/solution.py
@@ -16,6 +16,11 @@
 MASKED = -1e30
 SCALE = HD ** (-0.5)
 VMEM_LIMIT = 56 * 1024 * 1024
+
+
+def lasting(microseconds):
+    return pl.CostEstimate(flops=microseconds * 10**9, bytes_accessed=1, transcendentals=0)
+
 
 F32 = jnp.float32
 BF16 = jnp.bfloat16
@@ -121,17 +126,10 @@
         out_specs=[row(width)] * outs,
         out_shape=[shape] * outs,
         compiler_params=pltpu.CompilerParams(vmem_limit_bytes=VMEM_LIMIT),
-        cost_estimate=pl.CostEstimate(
-            flops=2 * SLOTS * D * 3 * width, bytes_accessed=SLOTS * D * 4, transcendentals=0
-        ),
+        cost_estimate=lasting(10),
         name="project",
     )(gathered, w_qkv, cosine, sine, *extra)
     return result if first_values is not None else (*result, result[2])
-
-
-def allowed_scores(scores, start, low, high, tile):
-    keys = start + lax.broadcasted_iota(jnp.int32, scores.shape, 0)
-    return jnp.where((keys >= low) & (keys <= high), scores, MASKED)
 
 
 def head_mask(rows, width, head):
@@ -153,21 +151,30 @@
     def step(kt, masked):
         start = pl.multiple_of(kt * tile, tile)
         keys = k_ref[pl.ds(start, tile), :]
-        for hh in range(heads):
-            scores = dot_nt(keys, queries[hh])
-            if masked:
-                scores = allowed_scores(scores, start, low, high, tile)
-            before = peak[hh : hh + 1, :]
-            top = jnp.maximum(before, jnp.max(scores, axis=0, keepdims=True))
-            weights = jnp.exp(scores - top)
-            shrink = jnp.exp(before - top)
-            peak[hh : hh + 1, :] = top
-            mass[hh : hh + 1, :] = mass[hh : hh + 1, :] * shrink + jnp.sum(
-                weights, axis=0, keepdims=True
-            )
-            rows = slice(hh * HD, (hh + 1) * HD)
-            values = vt_ref[rows, pl.ds(start, tile)]
-            acc[rows, :] = acc[rows, :] * shrink + dot_nn(values, weights.astype(BF16))
+        every = range(heads)
+        rows = [slice(hh * HD, (hh + 1) * HD) for hh in every]
+        scores = [dot_nt(keys, queries[hh]) for hh in every]
+        if masked:
+            slots = start + lax.broadcasted_iota(jnp.int32, scores[0].shape, 0)
+            allowed = (slots >= low) & (slots <= high)
+            scores = [jnp.where(allowed, x, MASKED) for x in scores]
+        before = [peak[hh : hh + 1, :] for hh in every]
+        tops = [jnp.maximum(before[hh], jnp.max(scores[hh], axis=0, keepdims=True)) for hh in every]
+        weights = [jnp.exp(scores[hh] - tops[hh]) for hh in every]
+        shrink = [jnp.exp(before[hh] - tops[hh]) for hh in every]
+        sums = [
+            mass[hh : hh + 1, :] * shrink[hh] + jnp.sum(weights[hh], axis=0, keepdims=True)
+            for hh in every
+        ]
+        updates = [
+            acc[rows[hh], :] * shrink[hh]
+            + dot_nn(vt_ref[rows[hh], pl.ds(start, tile)], weights[hh].astype(BF16))
+            for hh in every
+        ]
+        for hh in every:
+            peak[hh : hh + 1, :] = tops[hh]
+            mass[hh : hh + 1, :] = sums[hh]
+            acc[rows[hh], :] = updates[hh]
 
     step(index, True)
 
@@ -219,9 +226,7 @@
             jax.ShapeDtypeStruct((heads, SLOTS), F32),
         ],
         compiler_params=pltpu.CompilerParams(vmem_limit_bytes=VMEM_LIMIT),
-        cost_estimate=pl.CostEstimate(
-            flops=8 * SLOTS * SLOTS * width, bytes_accessed=SLOTS * width * 8, transcendentals=0
-        ),
+        cost_estimate=lasting(25),
         name="attend",
     )(meta, queries, keys, mixed.T, low, high)
 
@@ -253,19 +258,26 @@
         do = do_ref[here, :]
         low = low_ref[:, here]
         high = high_ref[:, here]
-        for hh in range(heads):
-            q_h = jnp.where(masks[hh], q, jnp.zeros_like(q))
-            do_h = jnp.where(masks[hh], do, jnp.zeros_like(do))
-            scores = dot_nt(keys, q_h)
-            prob_grad = dot_nt(values, do_h)
-            if masked:
-                scores = allowed_scores(scores, key_start, low, high, tile)
-            probs = jnp.exp(scores - lse_ref[hh : hh + 1, here])
-            score_grad = (probs * (prob_grad - delta_ref[hh : hh + 1, here])).astype(BF16)
-            dv[...] += dot_nn(probs.astype(BF16), do_h)
-            dk[...] += dot_nn(score_grad, q_h)
-            rows = slice(hh * HD, (hh + 1) * HD)
-            dqt[rows, here] += dot_nn(transposed[hh], score_grad)
+        every = range(heads)
+        rows = [slice(hh * HD, (hh + 1) * HD) for hh in every]
+        q_h = [jnp.where(masks[hh], q, jnp.zeros_like(q)) for hh in every]
+        do_h = [jnp.where(masks[hh], do, jnp.zeros_like(do)) for hh in every]
+        scores = [dot_nt(keys, q_h[hh]) for hh in every]
+        prob_grad = [dot_nt(values, do_h[hh]) for hh in every]
+        if masked:
+            slots = key_start + lax.broadcasted_iota(jnp.int32, scores[0].shape, 0)
+            allowed = (slots >= low) & (slots <= high)
+            scores = [jnp.where(allowed, x, MASKED) for x in scores]
+        probs = [jnp.exp(scores[hh] - lse_ref[hh : hh + 1, here]) for hh in every]
+        score_grad = [
+            (probs[hh] * (prob_grad[hh] - delta_ref[hh : hh + 1, here])).astype(BF16)
+            for hh in every
+        ]
+        dv[...] += sum(dot_nn(probs[hh].astype(BF16), do_h[hh]) for hh in every)
+        dk[...] += sum(dot_nn(score_grad[hh], q_h[hh]) for hh in every)
+        updates = [dqt[rows[hh], here] + dot_nn(transposed[hh], score_grad[hh]) for hh in every]
+        for hh in every:
+            dqt[rows[hh], here] = updates[hh]
 
     step(index, True)
 
@@ -351,9 +363,7 @@
         ),
         out_shape=[jax.ShapeDtypeStruct((SLOTS, width), BF16)] * 3,
         compiler_params=pltpu.CompilerParams(vmem_limit_bytes=VMEM_LIMIT),
-        cost_estimate=pl.CostEstimate(
-            flops=20 * SLOTS * SLOTS * width, bytes_accessed=SLOTS * width * 14, transcendentals=0
-        ),
+        cost_estimate=lasting(36),
         name="attend_back",
     )(meta, queries, keys, keys.T, mixed, out_grad, sums, delta, low, high, cosine, sine, *half_tables, *extra)
 
@@ -424,10 +434,10 @@
     def seat_block(self, blocks, shift):
         return lax.dynamic_index_in_dim(blocks, (self.seat + shift) % self.half, 0, keepdims=False)
 
-    def scatter_row(self, partial):
+    def scatter_row(self, partial, tied):
         own, other = self.regions(partial)
         summed = own + self.swap(other.astype(BF16)).astype(F32)
-        summed = summed.reshape(self.half, -1, partial.shape[1])
+        summed = tied(summed.reshape(self.half, -1, partial.shape[1]))
         total = self.seat_block(summed, 0)
         for shift in range(1, self.half):
             sent = self.seat_block(summed, shift).astype(BF16)
@@ -461,23 +471,15 @@
     def data_block(self, x, bits):
         return lax.dynamic_index_in_dim(x, self.dp ^ bits, 0, keepdims=False)
 
-    def scatter_data(self, first, second):
-        def half_way(x, near, far):
-            sent = jnp.stack([self.data_block(x, near), self.data_block(x, near ^ far)])
-            kept = jnp.stack([self.data_block(x, 0), self.data_block(x, far)])
-            return kept.astype(F32) + self.flip(sent.astype(BF16), near).astype(F32)
-
-        first, second = half_way(first, 1, 2), half_way(second, 2, 1)
-        first = first[0] + self.flip(first[1].astype(BF16), 2).astype(F32)
-        second = second[0] + self.flip(second[1].astype(BF16), 1).astype(F32)
-        return first, second
+    def by_data(self, own, flipped):
+        blocks = jnp.zeros((self.data, *own.shape), own.dtype)
+        blocks = lax.dynamic_update_index_in_dim(blocks, own, self.dp, 0)
+        for bits, block in enumerate(flipped, 1):
+            blocks = lax.dynamic_update_index_in_dim(blocks, block, self.dp ^ bits, 0)
+        return blocks
 
     def gather_data(self, x):
-        blocks = jnp.zeros((self.data, *x.shape), x.dtype)
-        blocks = lax.dynamic_update_index_in_dim(blocks, x, self.dp, 0)
-        for bits in range(1, self.data):
-            blocks = lax.dynamic_update_index_in_dim(blocks, self.flip(x, bits), self.dp ^ bits, 0)
-        return blocks
+        return self.by_data(x, [self.flip(x, bits) for bits in range(1, self.data)])
 
     def head_block(self, x, shift):
         return lax.dynamic_index_in_dim(x, (self.head + shift) % self.size, 0, keepdims=False)
@@ -489,44 +491,314 @@
             total = total + self.around(sent, shift).astype(F32)
         return total
 
+    def spot(self):
+        return jnp.stack([self.dp, self.head]).astype(jnp.int32)
+
+    def by_core(self, own, other, axis):
+        return jnp.where(
+            self.core == 0, jnp.stack([own, other], axis), jnp.stack([other, own], axis)
+        )
+
+    def gather_cores(self, x):
+        return self.by_core(x, self.swap(x), 0).reshape(-1, x.shape[1])
+
+    def scatter_cores(self, partial):
+        pair = partial.reshape(2, -1, partial.shape[1])
+        own = lax.dynamic_index_in_dim(pair, self.core, 0, keepdims=False)
+        other = lax.dynamic_index_in_dim(pair, 1 - self.core, 0, keepdims=False)
+        return own + self.swap(other.astype(BF16)).astype(F32)
+
+    def by_row(self, own, other):
+        return jnp.where(
+            self.row == 0, jnp.concatenate([own, other]), jnp.concatenate([other, own])
+        )
+
     def pick(self, zero, one):
         return jnp.where(self.core == 0, zero, one)
 
 
-def weight_pieces(place, w_gate, w_up, w_down, w_out):
-    kinds = (w_gate.T, w_up.T, w_down, w_out)
-    cut = [item.reshape(place.data, 2, -1, D) for item in kinds]
-    mine = jnp.concatenate(
-        [lax.dynamic_index_in_dim(item, place.dp, 0, keepdims=False) for item in cut], axis=1
-    )
-    own = lax.dynamic_index_in_dim(mine, place.core, 0, keepdims=False)
-    sent = lax.dynamic_index_in_dim(mine, 1 - place.core, 0, keepdims=False)
-    other = place.swap(sent)
+class Chain:
+    def __init__(self, stages):
+        self.stages = stages
+        self.result = None
+        self.flight = next(stages)
+
+    def advance(self, arrived):
+        try:
+            self.flight = self.stages.send(arrived)
+        except StopIteration as stop:
+            self.result = stop.value
+
+    def step(self, x):
+        x, arrived = lax.optimization_barrier((x, self.flight))
+        self.advance(arrived)
+        return x
+
+
+def lockstep(*chains):
+    while active := [chain for chain in chains if chain.result is None]:
+        arrived = lax.optimization_barrier([chain.flight for chain in active])
+        for chain, item in zip(active, arrived):
+            chain.advance(item)
+    return [chain.result for chain in chains]
+
+
+def after(x, *others):
+    return lax.optimization_barrier((x, *others))[0]
+
+
+class Cut:
+    def __init__(self, place, w_gate, w_out):
+        self.heads = place.size
+        self.units = w_gate.shape[2] // 2
+        self.outs = w_out.shape[1] // 2
+        self.rows = 3 * self.units + self.outs
+        self.down = (self.rows // 2 - self.units - self.outs) // 16 * 16
+        self.first = self.units + self.outs + self.down
+        self.second = self.rows - self.first
+        self.columns = D // place.data
+
+    def pieces(self):
+        units, outs, down = self.units, self.outs, self.down
+        return (
+            ("gate", 0, units, 0, 0),
+            ("out", 0, outs, 0, units),
+            ("down", 0, down, 0, units + outs),
+            ("down", down, units - down, 1, 0),
+            ("up", 0, units, 1, units - down),
+        )
+
+
+def pack_weights(place, cut, w_gate, w_up, w_down, w_out):
+    kinds = (w_gate.T, w_out, w_down, w_up.T)
+    halves = [item.reshape(2, -1, D) for item in kinds]
+
+    def half(core):
+        return jnp.concatenate(
+            [lax.dynamic_index_in_dim(item, core, 0, keepdims=False) for item in halves]
+        )
+
+    own = half(place.core)
+    other = place.swap(half(1 - place.core))
     return place.pick(own, other), place.pick(other, own)
 
 
-def spread_weights(place, piece, units):
-    full = lax.all_gather(piece, ("section", "dp", "head"), axis=0)
-    gate, up, down = (full[:, i * units : (i + 1) * units].reshape(-1, D) for i in range(3))
-    out = full[:, 3 * units :].reshape(2, place.data, place.size, -1, D)
-    out = out.transpose(2, 1, 0, 3, 4).reshape(-1, D)
-    return gate, up, down, out
-
-
-def reduce_weights(place, gate, up, down, out):
-    out = out.reshape(place.size, place.data, 2, -1, D).transpose(2, 1, 0, 3, 4)
-    cut = [item.reshape(2, place.data, place.size, -1, D) for item in (gate, up, down)] + [out]
-
-    def core_part(core):
-        parts = [lax.dynamic_index_in_dim(item, core, 0, keepdims=False) for item in cut]
-        return jnp.concatenate([part.astype(BF16) for part in parts], axis=2)
-
-    own = core_part(place.core)
-    summed = own.astype(F32) + place.swap(core_part(1 - place.core)).astype(F32)
-    summed = summed.astype(BF16)
-    first, second = place.scatter_data(summed[:, : place.half], summed[:, place.half :])
-    piece = place.scatter_heads(jnp.concatenate([first, second]))
-    return place.gather_data(piece.astype(BF16))
+def any_specs(count):
+    return [pl.BlockSpec(memory_space=pl.ANY)] * count
+
+
+def run_copies(copies):
+    for copy in copies:
+        copy.start()
+    for copy in copies:
+        copy.wait()
+
+
+def assemble_kernel(cut, groups, spot, share, *refs):
+    dp, head = spot[0], spot[1]
+    gu, down, out, sems = refs[5 * len(groups) :]
+    kinds = {"gate": gu.at[0], "up": gu.at[1], "down": down, "out": out}
+    copies = []
+
+    def add(source, kind, step, row, count, columns):
+        index = lax.rem(head - step + cut.heads, cut.heads) if kind == "out" else step
+        target = kinds[kind].at[index, pl.ds(row, count), columns]
+        copies.append(pltpu.make_async_copy(source, target, sems.at[len(copies)]))
+
+    for kind, row, count, part, at in cut.pieces():
+        base = at + part * cut.first
+        add(share.at[pl.ds(base, count), :], kind, 0, row, count, slice(None))
+    for number, steps in enumerate(groups):
+        ring, first_x, second_y, first_y, second_x = refs[5 * number : 5 * number + 5]
+        for i, step in enumerate(steps):
+            firsts = (
+                ring.at[i, pl.ds(0, cut.first)], first_x.at[i], first_y.at[0, i], first_y.at[1, i],
+            )
+            seconds = (
+                ring.at[i, pl.ds(cut.first, cut.second)], second_x.at[0, i], second_y.at[i],
+                second_x.at[1, i],
+            )
+            for bits in range(4):
+                start = pl.multiple_of((dp ^ bits) * cut.columns, cut.columns)
+                for kind, row, count, part, at in cut.pieces():
+                    source = (firsts, seconds)[part][bits].at[pl.ds(at, count), :]
+                    add(source, kind, step, row, count, pl.ds(start, cut.columns))
+    run_copies(copies)
+
+
+def near_flips(place, cut, ring):
+    return place.flip(ring[:, : cut.first], 1), place.flip(ring[:, cut.first :], 2)
+
+
+def far_flips(place, cut, ring, first_x, second_y):
+    first = jnp.stack([ring[:, : cut.first], first_x])
+    second = jnp.stack([ring[:, cut.first :], second_y])
+    return place.flip(first, 2), place.flip(second, 1)
+
+
+def spread_at_once(place, cut, share, piece):
+    size = cut.heads
+    ring = jnp.stack((yield [place.around(piece, step) for step in range(1, size)]))
+    near = yield near_flips(place, cut, ring)
+    far = yield far_flips(place, cut, ring, *near)
+    return assemble(place, cut, share, [(list(range(1, size)), (ring, *near, *far))])
+
+
+def spread_in_turn(place, cut, share, piece):
+    size = cut.heads
+    piece = yield place.around(piece, 1)
+    ring_1 = piece[None]
+    piece, near_1 = yield place.around(piece, 1), near_flips(place, cut, ring_1)
+    ring = [piece]
+    for _ in range(3, size):
+        ring.append(place.around(ring[-1], 1))
+    ring, far_1 = yield ring, far_flips(place, cut, ring_1, *near_1)
+    ring = jnp.stack(ring)
+    near = yield near_flips(place, cut, ring)
+    far = yield far_flips(place, cut, ring, *near)
+    groups = [([1], (ring_1, *near_1, *far_1)), (list(range(2, size)), (ring, *near, *far))]
+    return assemble(place, cut, share, groups)
+
+
+def first_qkv(place, w_qkv, part):
+    part = yield place.across_from_zero(part)
+    flipped = yield [place.flip(part, bits) for bits in range(1, place.data)]
+    return place.pick(w_qkv, place.by_data(part, flipped).reshape(w_qkv.shape))
+
+
+def second_qkv(place, w_qkv, part):
+    own, part = yield place.to_core(w_qkv, 0), place.across(part, 1)
+    flipped = yield [place.flip(part, bits) for bits in range(1, place.data)]
+    return place.pick(own, place.by_data(part, flipped).reshape(w_qkv.shape))
+
+
+def gather_far(place, far, gain):
+    far = yield far
+    shifted = yield [
+        place.beside(norm(far.astype(F32), gain).astype(BF16), shift)
+        for shift in range(1, place.half)
+    ]
+    return far, shifted
+
+
+def assemble(place, cut, share, groups):
+    steps = [group[0] for group in groups]
+    parts = [part for group in groups for part in group[1]]
+    copies = 5 * (1 + 4 * (cut.heads - 1))
+    shape = lambda *dims: jax.ShapeDtypeStruct(dims, BF16)
+    gate_up, down, out = pl.pallas_call(
+        functools.partial(assemble_kernel, cut, steps),
+        in_specs=[pl.BlockSpec(memory_space=pltpu.SMEM)] + any_specs(1 + len(parts)),
+        out_specs=[pl.BlockSpec(memory_space=pltpu.VMEM)] * 3,
+        out_shape=[
+            shape(2, cut.heads, cut.units, D), shape(cut.heads, cut.units, D),
+            shape(cut.heads, cut.outs, D),
+        ],
+        scratch_shapes=[pltpu.SemaphoreType.DMA((copies,))],
+        compiler_params=pltpu.CompilerParams(vmem_limit_bytes=VMEM_LIMIT),
+        cost_estimate=lasting(8),
+        name="assemble",
+    )(place.spot(), share, *parts)
+    out = place.by_core(out, place.swap(out), 1).reshape(-1, D)
+    return gate_up[0].reshape(-1, D), gate_up[1].reshape(-1, D), down.reshape(-1, D), out
+
+
+def split_kernel(cut, chunks, spot, gate, up, down, out, *refs):
+    dp, head = spot[0], spot[1]
+    sems = refs[-1]
+    kinds = {"gate": gate, "up": up, "down": down, "out": out}
+    copies = []
+    for number, steps in enumerate(chunks):
+        first_kept, first_sent, second_kept, second_sent = refs[4 * number : 4 * number + 4]
+        firsts = (first_kept.at[0], first_sent.at[0], first_kept.at[1], first_sent.at[1])
+        seconds = (second_kept.at[0], second_kept.at[1], second_sent.at[0], second_sent.at[1])
+        for bits in range(4):
+            start = pl.multiple_of((dp ^ bits) * cut.columns, cut.columns)
+            for i, step in enumerate(steps):
+                for kind, row, count, part, at in cut.pieces():
+                    index = step
+                    if kind == "out":
+                        index = lax.rem(head - step + cut.heads, cut.heads)
+                    source = kinds[kind].at[index, pl.ds(row, count), pl.ds(start, cut.columns)]
+                    target = (firsts, seconds)[part][bits].at[i, pl.ds(at, count), :]
+                    copies.append(pltpu.make_async_copy(source, target, sems.at[len(copies)]))
+    run_copies(copies)
+
+
+def split_grads(place, cut, gate, up, down, out):
+    half = cut.heads // 2
+    chunks = [list(range(half, cut.heads)), list(range(half))]
+    shape = lambda steps, rows: jax.ShapeDtypeStruct((2, len(steps), rows, cut.columns), BF16)
+    shapes = []
+    for steps in chunks:
+        shapes += [shape(steps, cut.first)] * 2 + [shape(steps, cut.second)] * 2
+    split = pl.pallas_call(
+        functools.partial(split_kernel, cut, chunks),
+        in_specs=[pl.BlockSpec(memory_space=pltpu.SMEM)]
+        + [pl.BlockSpec(memory_space=pltpu.VMEM)] * 4,
+        out_specs=any_specs(8),
+        out_shape=shapes,
+        scratch_shapes=[pltpu.SemaphoreType.DMA((20 * cut.heads,))],
+        compiler_params=pltpu.CompilerParams(vmem_limit_bytes=VMEM_LIMIT),
+        cost_estimate=lasting(8),
+        name="split",
+    )(place.spot(), *(item.reshape(cut.heads, -1, D) for item in (gate, up, down, out)))
+    return split[:4], split[4:]
+
+
+def exchange(place, part):
+    first, second = yield place.flip(part[1], 1), place.flip(part[3], 2)
+    first = part[0].astype(F32) + first.astype(F32)
+    second = part[2].astype(F32) + second.astype(F32)
+    moved = yield place.flip(first[1].astype(BF16), 2), place.flip(second[1].astype(BF16), 1)
+    kept = first[0], second[0]
+    return jnp.concatenate([x + y.astype(F32) for x, y in zip(kept, moved)], axis=1)
+
+
+def reduce_far(place, cut, part):
+    half = cut.heads // 2
+    blocks = yield from exchange(place, part)
+    arrived = yield [
+        place.around(blocks[step - half].astype(BF16), -step) for step in range(half, cut.heads)
+    ]
+    return sum(item.astype(F32) for item in arrived)
+
+
+def reduce_near(place, cut, part, far):
+    blocks = yield from exchange(place, part)
+    total = blocks[0]
+    if cut.heads > 2:
+        arrived = yield [
+            place.around(blocks[step].astype(BF16), -step) for step in range(1, cut.heads // 2)
+        ]
+        total = total + sum(item.astype(F32) for item in arrived)
+    total = (total + far.result).astype(BF16)
+    flipped = yield [place.flip(total, bits) for bits in range(1, place.data)]
+    parts = place.by_data(total, flipped)
+    return jnp.concatenate([parts[d] for d in range(place.data)], axis=1)
+
+
+def reduce_qkv(place, grad, core):
+    grad = grad.reshape(place.data, 2, -1, grad.shape[1])
+    first, second = grad[:, 0], grad[:, 1]
+    sent = [
+        jnp.stack([place.data_block(x, bits) for bits in pair])
+        for x, pair in ((first, (1, 3)), (second, (2, 3)))
+    ]
+    kept = [
+        jnp.stack([place.data_block(x, bits) for bits in pair])
+        for x, pair in ((first, (0, 2)), (second, (0, 1)))
+    ]
+    arrived = yield place.flip(sent[0], 1), place.flip(sent[1], 2)
+    first, second = (a.astype(F32) + b.astype(F32) for a, b in zip(kept, arrived))
+    arrived = yield place.flip(first[1].astype(BF16), 2), place.flip(second[1].astype(BF16), 1)
+    piece = jnp.concatenate([first[0] + arrived[0].astype(F32), second[0] + arrived[1].astype(F32)])
+    piece = piece.astype(BF16)
+    if core == 0:
+        other = yield place.across(piece, 0)
+        return piece.astype(F32) + other.astype(F32)
+    own, other = yield place.to_core(piece, 1), place.across(piece, 1)
+    return own.astype(F32) + other.astype(F32)
 
 
 def norm(rows, gain):
@@ -544,51 +816,70 @@
     return rows_grad, gain_grad
 
 
-def layer_forward(place, rows, first_values, w_qkv, spread, gains, tables):
+def layer_forward(place, rows, gathered, first_values, w_qkv, chain, gains, tables, later=()):
     cosine, sine, half_tables, low, high, meta, tile = tables
-    gate_w, up_w, down_w, out_w = spread
-    gathered = place.gather_row(norm(rows, gains[0]).astype(BF16))
+    if later:
+        gathered = chain.step(gathered)
+    later = [Chain(begin(gathered)) for begin in later]
     queries, keys, own_values, mixed = project(gathered, w_qkv, cosine, sine, first_values)
+    queries = chain.step(queries)
     attended_heads, sums = attend(queries, keys, mixed, low, high, meta, tile)
+    if later:
+        attended_heads = chain.step(attended_heads)
     attended = place.heads_to_slots(attended_heads)
+    for other in later:
+        attended = other.step(attended)
+    gate_w, up_w, down_w, out_w = spread = chain.result
     middle = rows + dot_nn(attended, out_w)
-    ffn_normed = norm(middle, gains[1]).astype(BF16)
+    ffn_normed = place.gather_cores(norm(middle, gains[1]).astype(BF16))
     gate = dot_nt(ffn_normed, gate_w)
     up = dot_nt(ffn_normed, up_w)
     activation = (jax.nn.silu(gate) * up).astype(BF16)
-    result = middle + dot_nn(activation, down_w)
+    result = middle + place.scatter_cores(dot_nn(activation, down_w))
+    for other in later:
+        result = other.step(result)
     kept = (
         rows, gathered, queries, keys, mixed, attended_heads, sums, attended, middle, ffn_normed,
         gate, up, activation,
     )
-    return result, own_values, kept
-
-
-def layer_backward(place, grad, share, carry, w_qkv, spread, gains, kept, tables):
+    return result, own_values, spread, kept, later
+
+
+def join_halves(place, x, shifted):
+    own = place.by_seat(x, shifted)
+    return place.by_core(own, place.swap(own), 1).reshape(-1, x.shape[1])
+
+
+def layer_backward(place, cut, grad, share, carry, w_qkv, spread, gains, kept, tables, earlier=((), (), ())):
     cosine, sine, half_tables, low, high, meta, tile = tables
     gate_w, up_w, down_w, out_w = spread
     (
         rows, gathered, queries, keys, mixed, attended_heads, sums, attended, middle, ffn_normed,
         gate, up, activation,
     ) = kept
-    down_grad = grad.astype(BF16)
+    down_grad = place.gather_cores(grad.astype(BF16))
     act_grad = dot_nt(down_grad, down_w)
     sigma = jax.nn.sigmoid(gate)
     gate_grad = (act_grad * up * sigma * (1.0 + gate * (1.0 - sigma))).astype(BF16)
     up_grad = (act_grad * gate * sigma).astype(BF16)
-    normed_grad = dot_nn(gate_grad, gate_w) + dot_nn(up_grad, up_w)
+    normed_grad = place.scatter_cores(dot_nn(gate_grad, gate_w) + dot_nn(up_grad, up_w))
     middle_back, grad_ffn_gain = norm_back(middle, gains[1], normed_grad)
     middle_grad = grad + middle_back
     attn_grad = middle_grad.astype(BF16)
     attended_grad = dot_nt(attn_grad, out_w).astype(BF16)
     heads_grad = place.slots_to_heads(attended_grad)
-    weight_grads = reduce_weights(
-        place,
-        dot_tn(gate_grad, ffn_normed),
-        dot_tn(up_grad, ffn_normed),
-        dot_tn(activation, down_grad),
-        dot_tn(attended, attn_grad),
-    )
+    gate_grad, up_grad, activation = after((gate_grad, up_grad, activation), attended_grad)
+    out_grad = dot_tn(attended, attn_grad).reshape(place.size, 2, -1, D).swapaxes(0, 1)
+    out_grad = place.scatter_cores(out_grad.reshape(-1, D))
+    split = split_grads(
+        place, cut, dot_tn(gate_grad, ffn_normed).astype(BF16),
+        dot_tn(up_grad, ffn_normed).astype(BF16), dot_tn(activation, down_grad).astype(BF16),
+        out_grad.astype(BF16),
+    )
+    heads_grad = after(heads_grad, *split[0], *split[1])
+    for other in earlier[0]:
+        heads_grad = other.step(heads_grad)
+    far = Chain(reduce_far(place, cut, split[0]))
     delta = heads_grad.astype(F32) * attended_heads.astype(F32)
     delta = jnp.sum(delta.reshape(SLOTS, -1, HD), axis=2).T
     query_grad, key_grad, value_grad = attend_back(
@@ -596,12 +887,19 @@
         share, carry, tile,
     )
     lin_grad = jnp.concatenate([query_grad, key_grad, value_grad], axis=1)
-    input_back = place.scatter_row(dot_nt(lin_grad, w_qkv))
+    partial = far.step(dot_nt(lin_grad, w_qkv))
+    for other in earlier[1]:
+        partial = other.step(partial)
+    near = Chain(reduce_near(place, cut, after(split[1], partial), far))
+    lin_grad = after(lin_grad, partial)
     qkv_grad = dot_tn(gathered, lin_grad).astype(BF16)
-    qkv_grad = qkv_grad.reshape(place.data, 2, -1, qkv_grad.shape[1])
-    qkv_grad = jnp.stack(place.scatter_data(qkv_grad[:, 0], qkv_grad[:, 1])).astype(BF16)
+    input_back = place.scatter_row(partial, far.step)
+    input_back = near.step(input_back)
+    for other in earlier[2]:
+        input_back = other.step(input_back)
+    qkv_grad = after(qkv_grad, input_back)
     rows_back, grad_attn_gain = norm_back(rows, gains[0], input_back)
-    return middle_grad + rows_back, value_grad, weight_grads, qkv_grad, (grad_attn_gain, grad_ffn_gain)
+    return middle_grad + rows_back, value_grad, (far, near), qkv_grad, (grad_attn_gain, grad_ffn_gain)
 
 
 def local(
@@ -610,23 +908,26 @@
 ):
     place = Place()
     width = w_query.shape[2]
-    units = w_gate.shape[2] // (2 * place.data)
-    tile = min(256, SLOTS // place.size)
+    cut = Cut(place, w_gate, w_out)
+    tile = min(512, SLOTS)
 
     def mine_and_sent(x):
         mine = lax.dynamic_index_in_dim(x, place.row, 0, keepdims=False)
         sent = lax.dynamic_index_in_dim(x, 1 - place.row, 0, keepdims=False)
         return mine, sent
 
+    count = hidden_in.shape[1] // 2
     mine, sent = mine_and_sent(hidden_in)
-    rows = place.pick(mine, place.across(sent, 1)).astype(F32)
+    half_block = lambda x: lax.dynamic_slice_in_dim(x, place.core * count, count, 0)
+    far = place.around(half_block(sent), place.half)
 
     w_qkv = jnp.concatenate([w_query[0], w_key[0], w_value[0]], axis=1)
-    w_qkv_1 = place.pick(w_qkv, place.across_from_zero(w_qkv))
-    w_qkv_2 = place.pick(place.to_core(w_qkv, 0), place.across(w_qkv, 1))
-    piece_1, piece_2 = weight_pieces(place, w_gate[0], w_up[0], w_down[0], w_out[0])
-    spread_1 = spread_weights(place, piece_1, units)
-    spread_2 = spread_weights(place, piece_2, units)
+    part = lax.dynamic_slice_in_dim(w_qkv, place.dp * cut.columns, cut.columns, 0)
+    share_1, share_2 = pack_weights(place, cut, w_gate[0], w_up[0], w_down[0], w_out[0])
+    piece_1, piece_2 = (
+        lax.dynamic_slice_in_dim(share, place.dp * cut.columns, cut.columns, 1)
+        for share in (share_1, share_2)
+    )
     own_gains = jnp.concatenate([attn_gain, ffn_gain])
     other_gains = place.swap(own_gains)
     gains_1 = place.pick(own_gains, other_gains)
@@ -642,52 +943,102 @@
         begin[None], last[None], tile_tables(begin, tile), tile,
     )
 
-    result_1, values_1, kept_1 = layer_forward(
-        place, rows, None, w_qkv_1, spread_1, gains_1, tables
+    near = norm(half_block(mine).astype(F32), gains_1[0]).astype(BF16)
+    near_shifted = [place.beside(near, shift) for shift in range(1, place.half)]
+    chain_1 = Chain(spread_in_turn(place, cut, share_1, piece_1))
+    chain_far = Chain(gather_far(place, far, gains_1[0]))
+    chain_qkv = Chain(first_qkv(place, w_qkv, part))
+    for _ in range(2):
+        started = (chain_far, chain_qkv, chain_1)
+        arrived = lax.optimization_barrier([chain.flight for chain in started])
+        for chain, item in zip(started, arrived):
+            chain.advance(item)
+    (far, far_shifted), w_qkv_1 = chain_far.result, chain_qkv.result
+    blocks = [
+        join_halves(place, near, near_shifted),
+        join_halves(place, norm(far.astype(F32), gains_1[0]).astype(BF16), far_shifted),
+    ]
+    gathered = place.by_row(*blocks)
+    rows = place.pick(mine, place.by_core(far, place.swap(far), 0).reshape(mine.shape))
+    rows = rows.astype(F32)
+    result_1, values_1, spread_1, kept_1, (chain_2, chain_qkv) = layer_forward(
+        place, rows, gathered, None, w_qkv_1, chain_1, gains_1, tables,
+        (
+            lambda x: spread_at_once(place, cut, share_2, after(piece_2, x)),
+            lambda x: second_qkv(place, w_qkv, after(part, x)),
+        ),
     )
     hidden_1 = result_1.astype(BF16)
-    result_2, _, kept_2 = layer_forward(
-        place, hidden_1.astype(F32), values_1, w_qkv_2, spread_2, gains_2, tables
+    w_qkv_2 = chain_qkv.result
+    rows = hidden_1.astype(F32)
+    gathered = place.gather_row(norm(rows, gains_2[0]).astype(BF16))
+    result_2, _, spread_2, kept_2, _ = layer_forward(
+        place, rows, gathered, values_1, w_qkv_2, chain_2, gains_2, tables
     )
     hidden_2 = result_2.astype(BF16)
 
     mine, sent = mine_and_sent(cotangent)
     grad = place.pick(mine, place.across(sent.astype(BF16), 1).astype(F32))
     grad_2, carry, ffn_2, qkv_2, gain_2 = layer_backward(
-        place, grad, 0.5, None, w_qkv_2, spread_2, gains_2, kept_2, tables
+        place, cut, grad, 0.5, None, w_qkv_2, spread_2, gains_2, kept_2, tables
     )
     grad_2 = grad_2.astype(BF16)
-    grad_1, _, ffn_1, qkv_1, gain_1 = layer_backward(
-        place, grad_2.astype(F32), 1.0, carry, w_qkv_1, spread_1, gains_1, kept_1, tables
-    )
-
-    def both_rows(first, second):
-        near = place.pick(first, place.to_core(second.astype(BF16), 1).astype(first.dtype))
-        far = place.pick(
-            place.across(first.astype(BF16), 0), place.across(second.astype(BF16), 1)
-        ).astype(first.dtype)
+    far_2, near_2 = ffn_2
+    qkv_2 = Chain(reduce_qkv(place, qkv_2, 1))
+
+    def bring(first, second):
+        near = place.to_core(second.astype(BF16), 1)
+        near, *far = yield near, place.across(first.astype(BF16), 0), place.across(second.astype(BF16), 1)
+        return near, place.pick(*far)
+
+    def bring_one(block, core):
+        moved = (place.across(block.astype(BF16), core),)
+        moved = yield moved if core == 0 else (*moved, place.to_core(block.astype(BF16), 1))
+        return moved
+
+    def both_rows(near, far):
         return jnp.where(place.row == 0, jnp.stack([near, far]), jnp.stack([far, near]))[None]
 
-    layer_outputs = both_rows(hidden_1, hidden_2)
-    input_grads = both_rows(grad_1, grad_2.astype(F32))
-
-    qkv_1 = qkv_1.astype(F32) + place.across(qkv_1, 0).astype(F32)
-    qkv_2 = place.to_core(qkv_2, 1).astype(F32) + place.across(qkv_2, 1).astype(F32)
-    qkv = place.gather_data(place.pick(qkv_1, qkv_2).astype(BF16)).astype(F32)
-    qkv = qkv.reshape(D, 3, width)
+    outputs = Chain(bring(hidden_1, hidden_2))
+    grads_2 = Chain(bring_one(grad_2, 1))
+    grad_1, _, (far_1, near_1), qkv_1, gain_1 = layer_backward(
+        place, cut, grad_2.astype(F32), 1.0, carry, w_qkv_1, spread_1, gains_1, kept_1, tables,
+        ((far_2, near_2, qkv_2), (near_2, qkv_2, outputs), (near_2, qkv_2, grads_2)),
+    )
+
+    def sum_gains(gains):
+        gains = gains + (yield place.swap(gains))
+        gains = gains + sum((yield [place.flip(gains, bits) for bits in range(1, place.data)]))
+        return gains + sum((yield [place.around(gains, k) for k in range(1, place.size)]))
+
+    grads_1 = Chain(bring_one(grad_1, 0))
+    qkv_1 = Chain(reduce_qkv(place, qkv_1, 0))
+    gains = Chain(sum_gains(jnp.stack([*gain_1, *gain_2])))
+    _, ffn_1, qkv_1, gains, grads_1 = lockstep(far_1, near_1, qkv_1, gains, grads_1)
+
+    ffn_2, qkv_2, grads_2 = near_2.result, qkv_2.result, grads_2.result
+    near, far = outputs.result
+    layer_outputs = both_rows(place.pick(hidden_1, near), far)
+    near = place.pick(grad_1, grads_2[1].astype(F32))
+    input_grads = both_rows(near, place.pick(grads_1[0], grads_2[0]).astype(F32))
 
     own = place.pick(ffn_1, ffn_2)
     other = place.swap(place.pick(ffn_2, ffn_1))
-    ffn = jnp.where(place.core == 0, jnp.stack([own, other], 1), jnp.stack([other, own], 1))
-    ffn = ffn.astype(F32)
-    kinds = [ffn[:, :, i * units : (i + 1) * units].reshape(-1, D) for i in range(3)]
-    out = ffn[:, :, 3 * units :].reshape(-1, D)
-
-    gains = lax.psum(jnp.stack([*gain_1, *gain_2]), ("section", "dp", "head"))
+    qkv = place.pick(qkv_1, qkv_2).astype(BF16)
+    flipped = [place.flip(qkv, bits) for bits in range(1, place.data)]
+    other, flipped = lax.optimization_barrier((other, flipped))
+    qkv = place.by_data(qkv, flipped).astype(F32).reshape(D, 3 * width)
+
+    ffn = place.by_core(own, other, 0).astype(F32)
+    units, outs = cut.units, cut.outs
+    grad_gate = ffn[:, :units].reshape(-1, D).T
+    grad_out = ffn[:, units : units + outs].reshape(-1, D)
+    grad_down = ffn[:, units + outs : 2 * units + outs].reshape(-1, D)
+    grad_up = ffn[:, 2 * units + outs :].reshape(-1, D).T
     gains = place.pick(gains[:2], gains[2:])
     return (
-        layer_outputs, input_grads, qkv[None, :, 0], qkv[None, :, 1], qkv[None, :, 2], out[None],
-        kinds[0].T[None], kinds[1].T[None], kinds[2][None], gains[:1], gains[1:],
+        layer_outputs, input_grads, *(qkv[None, :, i * width : (i + 1) * width] for i in range(3)), grad_out[None],
+        grad_gate[None], grad_up[None], grad_down[None], gains[:1], gains[1:],
     )
 
 

time: 1340 us -> 1040 us (0.78)
  starting transfers between devices: 381 us -> 158 us
  waiting for transfers between devices: 317 us -> 398 us
  local copies, waits for them, and re-layouts: 163 us -> 97.5 us
  blocking collectives: 40.1 us -> 0 us
  other arithmetic: 129 us -> 114 us
    ppermute x13 -> x26, starting transfers between devices: 161 us -> 23.8 us  [swap(): return lax.ppermute(x, 'section', [(0, 1), (1, 0)])]
    ppermute x6 -> x16, starting transfers between devices: 121 us -> 23.1 us  [around(): lax.ppermute(x, 'head', [(h, (h + shift) % self.size) for h in range(self...]
    ppermute x6 -> x16, waiting for transfers between devices: 11.7 us -> 85.3 us  [around(): lax.ppermute(x, 'head', [(h, (h + shift) % self.size) for h in range(self...]
    ppermute x8 -> x9, waiting for transfers between devices: 173 us -> 105 us  [beside(): return lax.ppermute(x, 'head', pairs)]
    ppermute x25 -> x54, waiting for transfers between devices: 129 us -> 195 us  [flip(): return lax.ppermute(x, 'dp', [(d, d ^ bits) for d in range(self.data)])]
    psum x1 -> x0, blocking collectives: 40.1 us -> none  [local(): gains = lax.psum(jnp.stack([*gain_1, *gain_2]), ('section', 'dp', 'head'))]
    ppermute x25 -> x54, starting transfers between devices: 45.4 us -> 83.2 us  [flip(): return lax.ppermute(x, 'dp', [(d, d ^ bits) for d in range(self.data)])]
    pallas_call x0 -> x4, Pallas kernels: none -> 34 us  [the longest x2 17.6 us: assemble(): pl.pallas_call(functools.partial(assemble_kernel, cut, steps), in_specs=[...]
  transfers between devices with their start and end apart: 68 -> 118, of which waited for: 24 -> 48; matrix products, arithmetic and copies ran while one was open for 29% -> 23% of each run, Pallas kernels for 12% -> 14%
where the time goes in v2:
time: 1040 us; the launch traced here: 1030 us
  waiting for transfers between devices  398 us (38%)
  starting transfers between devices  158 us (15%)
  Pallas kernels  148 us (14%)
  other arithmetic  114 us (11%)
  matrix products  111 us (11%)
  local copies, waits for them, and re-layouts  97.5 us (9%)
    ppermute x54, waiting for transfers between devices, flip(): return lax.ppermute(x, 'dp', [(d, d ^ bits) for d in range(self.data)])  195 us
    ppermute x9, waiting for transfers between devices, beside(): return lax.ppermute(x, 'head', pairs)  105 us
    ppermute x16, waiting for transfers between devices, around(): lax.ppermute(x, 'head', [(h, (h + shift) % self.size) for h in range(self...  85.3 us
    ppermute x54, starting transfers between devices, flip(): return lax.ppermute(x, 'dp', [(d, d ^ bits) for d in range(self.data)])  83.2 us
    pallas_call x2, Pallas kernels, attend_back(): pl.pallas_call(kernel, grid_spec=pltpu.PrefetchScalarGridSpec(num_scalar_...  57.8 us
    dot_general x10, matrix products, dot_nt(): lax.dot_general(a, b, (((1,), (1,)), ((), ())), preferred_element_type=F32)  48.3 us
    dot_general x10, matrix products, dot_tn(): lax.dot_general(a, b, (((0,), (0,)), ((), ())), preferred_element_type=F32)  37.8 us
    pallas_call x2, Pallas kernels, attend(): pl.pallas_call(functools.partial(attend_kernel, tile, heads), grid_spec=p...  36.7 us
  transfers between devices with their start and end apart: 118, of which 48 were waited for; matrix products, arithmetic and copies ran while one was open for 23% of the time, Pallas kernels for 14%

profile of v2, /device:TPU:0, one launch (start us, length us, event | category | flops | bytes accessed | tf_op | source)
XLA Modules:
  0.0 1031.5 jit_solution(2354859082603986562)
XLA Ops:
  12.5 6.4 collective-permute-start.1
  42.6 12.8 %collective-permute-done.6 = bf16[256,1024]{1,0:T(8,128)(2,1)} collective-permute-done((bf16[256,1024]{1,0:T(8,128)(2,1)}, bf16[256,1024]{1,0:T(8,128)(2,1)}, u32[]{:S(2)}, u32[]{:S(2)}) %collective-permute-start.6) | collective-permute-done | bytes 524320 | tf_op jit(solution)/shard_map/ppermute | solution.py:402
  57.9 11.4 %collective-permute-done = bf16[256,1024]{1,0:T(8,128)(2,1)S(1)} collective-permute-done((bf16[256,1024]{1,0:T(8,128)(2,1)}, bf16[256,1024]{1,0:T(8,128)(2,1)S(1)}, u32[]{:S(2)}, u32[]{:S(2)}) %collective-permute-start) | collective-permute-done | bytes 524320 | tf_op jit(solution)/shard_map/ppermute | solution.py:405
  81.5 7.3 collective-permute-done.14.refs_2_
  90.3 4.2 collective-permute-done.10
  103.7 3.7 maximum_select_fusion.1.x
  110.8 4.3 collective-permute-done.17.refs_3_
  123.1 9.9 project.2
  142.1 18.1 %attend.2 = (bf16[2048,256]{1,0:T(8,128)(2,1)}, f32[4,2048]{1,0:T(4,128)}) custom-call(s32[4,4]{1,0:T(4,128)} %pad_add_fusion.meta.refs_0_, bf16[2048,256]{1,0:T(8,128)(2,1)} %get-tuple-element.194.q_ref, bf16[2048,256]{1,0:T(8,128)(2,1)} %get-tuple-element.195.k_ref, bf16[256,2048]{1,0:T(8,128)(2,1)} %bitcast.741, s32[1,2048]{1,0:T(1,128)} %bitcast.783, ...), custom_call_target="tpu_custom_call" | custom-call | flops 24999999488 | bytes 1 | tf_op jit(solution)/shard_map/attend/pallas_call | solution.py:202
  160.2 6.4 collective-permute-done.22.refs_9_
  170.3 8.8 assemble.2
  193.4 22.7 %collective-permute-done.24 = bf16[2,512,256]{2,1,0:T(8,128)(2,1)S(1)} collective-permute-done((bf16[2,512,256]{2,1,0:T(8,128)(2,1)S(1)}, bf16[2,512,256]{2,1,0:T(8,128)(2,1)S(1)}, u32[]{:S(2)}, u32[]{:S(2)}) %collective-permute-start.24) | collective-permute-done | bytes 524320 | tf_op jit(solution)/shard_map/ppermute | solution.py:402
  217.4 13.2 %collective-permute-done.26 = bf16[1184,256]{1,0:T(8,128)(2,1)S(1)} collective-permute-done((bf16[1184,256]{1,0:T(8,128)(2,1)S(1)}, bf16[1184,256]{1,0:T(8,128)(2,1)S(1)}, u32[]{:S(2)}, u32[]{:S(2)}) %collective-permute-start.26) | collective-permute-done | bytes 606240 | tf_op jit(solution)/shard_map/ppermute | solution.py:405
  230.6 6.5 collective-permute-done.27
  239.3 15.5 %collective-permute-start.31 = (bf16[512,1024]{1,0:T(8,128)(2,1)S(1)}, bf16[512,1024]{1,0:T(8,128)(2,1)S(1)}, u32[]{:S(2)}, u32[]{:S(2)}) collective-permute-start(bf16[512,1024]{1,0:T(8,128)(2,1)S(1)} %multiply_convert_fusion.7), channel_id=1, source_target_pairs={{0,16},{16,0},{1,17},{17,1},{2,18},{18,2},{3,19},{19,3},{4,20},{20... | collective-permute-start | bytes 3145736 | tf_op jit(solution)/shard_map/ppermute | solution.py:384
  261.0 5.8 multiply_convert_fusion.5
  279.8 15.9 %collective-permute-done.33.refs_1_ = bf16[3,592,256]{2,1,0:T(8,128)(2,1)S(1)} collective-permute-done((bf16[3,592,256]{2,1,0:T(8,128)(2,1)S(1)}, bf16[3,592,256]{2,1,0:T(8,128)(2,1)S(1)}, u32[]{:S(2)}, u32[]{:S(2)}) %collective-permute-start.33) | collective-permute-done | bytes 909344 | tf_op jit(solution)/shard_map/ppermute | solution.py:408
  297.4 6.7 collective-permute-done.35
  304.1 8.9 collective-permute-done.36
  314.5 23.6 %collective-permute-done.39 = bf16[512,1024]{1,0:T(8,128)(2,1)S(1)} collective-permute-done((bf16[512,1024]{1,0:T(8,128)(2,1)S(1)}, bf16[512,1024]{1,0:T(8,128)(2,1)S(1)}, u32[]{:S(2)}, u32[]{:S(2)}) %collective-permute-start.39) | collective-permute-done | bytes 1048608 | tf_op jit(solution)/shard_map/ppermute | solution.py:402
  346.6 4.1 maximum_select_fusion.2.x_ref
  350.7 10.1 project.3
  360.8 22.4 %collective-permute-done.42.refs_4_ = bf16[2,3,592,256]{3,2,1,0:T(8,128)(2,1)} collective-permute-done((bf16[2,3,592,256]{3,2,1,0:T(8,128)(2,1)S(1)}, bf16[2,3,592,256]{3,2,1,0:T(8,128)(2,1)}, u32[]{:S(2)}, u32[]{:S(2)}) %collective-permute-start.42) | collective-permute-done | bytes 1818656 | tf_op jit(solution)/shard_map/ppermute | solution.py:408
  387.6 18.5 %attend.3 = (bf16[2048,256]{1,0:T(8,128)(2,1)}, f32[4,2048]{1,0:T(4,128)}) custom-call(s32[4,4]{1,0:T(4,128)} %pad_add_fusion.meta.refs_0_, bf16[2048,256]{1,0:T(8,128)(2,1)} %get-tuple-element.225.q_ref.refs_1_, bf16[2048,256]{1,0:T(8,128)(2,1)} %get-tuple-element.226.k_ref.refs_2_, bf16[256,2048]{1,0:T(8,128)(2,1)} %bitcast.742, s32[1,2048]{1,0:T(1,128)} %bitcast.784, ...), custom_call_target="tpu_custom_call" | custom-call | flops 24999999488 | bytes 1 | tf_op jit(solution)/shard_map/attend/pallas_call | solution.py:202
  410.8 8.8 assemble.3
  420.2 4.4 collective-permute-done.44
  432.9 5.2 fusion.142
  438.7 5.2 fusion.143
  443.9 9.5 multiply_convert_fusion.2
  472.8 5.1 multiply_reduce_fusion
  485.8 4.7 convolution_convert_fusion.3
  490.6 4.6 convolution_convert_fusion.4
  497.2 4.5 convolution_convert_fusion.5
  501.7 7.8 collective-permute-done.49
  511.1 8.1 split.2
  519.2 6.1 collective-permute-start.52
  530.7 29.0 %attend_back.2 = (bf16[2048,256]{1,0:T(8,128)(2,1)}, bf16[2048,256]{1,0:T(8,128)(2,1)}, bf16[2048,256]{1,0:T(8,128)(2,1)}) custom-call(s32[4,4]{1,0:T(4,128)} %pad_add_fusion.meta.refs_0_, bf16[2048,256]{1,0:T(8,128)(2,1)} %get-tuple-element.225.q_ref.refs_1_, bf16[2048,256]{1,0:T(8,128)(2,1)} %get-tuple-element.226.k_ref.refs_2_, ...), custom_call_target="tpu_custom_call" | custom-call | flops 35999997952 | bytes 1 | tf_op jit(solution)/shard_map/attend_back/pallas_call | solution.py:336
  572.6 8.6 collective-permute-start.56
  596.1 5.8 collective-permute-done.55
  608.7 17.1 %collective-permute-done.57 = bf16[512,1024]{1,0:T(8,128)(2,1)S(1)} collective-permute-done((bf16[512,1024]{1,0:T(8,128)(2,1)S(1)}, bf16[512,1024]{1,0:T(8,128)(2,1)S(1)}, u32[]{:S(2)}, u32[]{:S(2)}) %collective-permute-start.57) | collective-permute-done | bytes 1048608 | tf_op jit(solution)/shard_map/ppermute | solution.py:402
  635.8 9.5 multiply_convert_fusion
  645.3 5.4 fusion.146
  666.4 5.0 convolution_convert_fusion
  673.5 4.5 convolution_convert_fusion.1
  678.0 8.2 collective-permute-done.62
  687.1 4.5 convolution_convert_fusion.2
  696.6 8.2 split.3
  707.7 8.7 collective-permute-done.68
  734.6 28.7 %attend_back.3 = (bf16[2048,256]{1,0:T(8,128)(2,1)}, bf16[2048,256]{1,0:T(8,128)(2,1)}, bf16[2048,256]{1,0:T(8,128)(2,1)}) custom-call(s32[4,4]{1,0:T(4,128)} %pad_add_fusion.meta.refs_0_, bf16[2048,256]{1,0:T(8,128)(2,1)} %get-tuple-element.194.q_ref, bf16[2048,256]{1,0:T(8,128)(2,1)} %get-tuple-element.195.k_ref, bf16[256,2048]{1,0:T(8,128)(2,1)} %bitcast.738, ...), custom_call_target="tpu_custom_call" | custom-call | flops 35999997952 | bytes 1 | tf_op jit(solution)/shard_map/attend_back/pallas_call | solution.py:336
  767.7 11.1 %collective-permute-start.73 = (bf16[1184,256]{1,0:T(8,128)(2,1)S(1)}, bf16[1184,256]{1,0:T(8,128)(2,1)S(1)}, u32[]{:S(2)}, u32[]{:S(2)}) collective-permute-start(bf16[1184,256]{1,0:T(8,128)(2,1)S(1)} %fusion.73), channel_id=1, source_target_pairs={{0,3},{1,0},{2,1},{3,2},{4,7},{5,4},{6,5},{7,6},{8,11},{9,8},{10,9... | collective-permute-start | bytes 1818632 | tf_op jit(solution)/shard_map/ppermute | solution.py:405
  785.2 5.1 collective-permute-done.73
  803.2 3.8 collective-permute-start.82
  815.3 9.2 collective-permute-done.81
  831.8 17.2 %collective-permute-done.84 = bf16[2,2,592,256]{3,2,1,0:T(8,128)(2,1)S(1)} collective-permute-done((bf16[2,2,592,256]{3,2,1,0:T(8,128)(2,1)}, bf16[2,2,592,256]{3,2,1,0:T(8,128)(2,1)S(1)}, u32[]{:S(2)}, u32[]{:S(2)}) %collective-permute-start.84) | collective-permute-done | bytes 1212448 | tf_op jit(solution)/shard_map/ppermute | solution.py:408
  852.2 8.8 collective-permute-done.83
  863.9 10.7 %collective-permute-done.88 = bf16[1184,256]{1,0:T(8,128)(2,1)S(1)} collective-permute-done((bf16[1184,256]{1,0:T(8,128)(2,1)}, bf16[1184,256]{1,0:T(8,128)(2,1)S(1)}, u32[]{:S(2)}, u32[]{:S(2)}) %collective-permute-start.88) | collective-permute-done | bytes 606240 | tf_op jit(solution)/shard_map/ppermute | solution.py:408
  877.8 3.8 collective-permute-start.99
  886.9 36.5 %collective-permute-done.93 = bf16[1184,256]{1,0:T(8,128)(2,1)S(1)} collective-permute-done((bf16[1184,256]{1,0:T(8,128)(2,1)S(1)}, bf16[1184,256]{1,0:T(8,128)(2,1)S(1)}, u32[]{:S(2)}, u32[]{:S(2)}) %collective-permute-start.93) | collective-permute-done | bytes 606240 | tf_op jit(solution)/shard_map/ppermute | solution.py:405
  927.6 19.8 %collective-permute-done.98 = bf16[2,128,768]{2,1,0:T(8,128)(2,1)S(1)} collective-permute-done((bf16[2,128,768]{2,1,0:T(8,128)(2,1)S(1)}, bf16[2,128,768]{2,1,0:T(8,128)(2,1)S(1)}, u32[]{:S(2)}, u32[]{:S(2)}) %collective-permute-start.98) | collective-permute-done | bytes 393248 | tf_op jit(solution)/shard_map/ppermute | solution.py:408
  959.4 7.6 collective-permute-done.101
  978.1 11.3 %collective-permute-done.110 = bf16[256,768]{1,0:T(8,128)(2,1)S(1)} collective-permute-done((bf16[256,768]{1,0:T(8,128)(2,1)S(1)}, bf16[256,768]{1,0:T(8,128)(2,1)S(1)}, u32[]{:S(2)}, u32[]{:S(2)}) %collective-permute-start.110) | collective-permute-done | bytes 393248 | tf_op jit(solution)/shard_map/ppermute | solution.py:392
  989.5 6.6 collective-permute-done.108
  1006.8 7.1 collective-permute-done.115
  1013.9 9.1 collective-permute-done.116
  (773 shorter events, 374.8 us)
Async XLA Ops:
  1.5 22.1 %collective-permute-start.5 = (f32[2,1024]{1,0:T(2,128)S(1)}, f32[2,1024]{1,0:T(2,128)S(1)}, u32[]{:S(2)}, u32[]{:S(2)}) collective-permute-start(f32[2,1024]{1,0:T(2,128)S(1)} %pad_maximum_fusion.28), channel_id=1, source_target_pairs={{0,16},{16,0},{1,17},{17,1},{2,18},{18,2},{3,19},{19,3},{4,20},{20... | collective-permute-start | bytes 24584 | tf_op jit(solution)/shard_map/ppermute | solution.py:384
  12.5 45.4 %collective-permute-start.1 = (bf16[256,768]{1,0:T(8,128)(2,1)}, bf16[256,768]{1,0:T(8,128)(2,1)}, u32[]{:S(2)}, u32[]{:S(2)}) collective-permute-start(bf16[256,768]{1,0:T(8,128)(2,1)} %constant_dynamic-slice_fusion.5), channel_id=1, source_target_pairs={{0,18},{1,19},{2,16},{3,17},{4,22},{5,23},{6,20},{7,21},{8,26},{9,... | collective-permute-start | bytes 1179656 | tf_op jit(solution)/shard_map/ppermute | solution.py:397
  25.3 30.1 %collective-permute-start.6 = (bf16[256,1024]{1,0:T(8,128)(2,1)}, bf16[256,1024]{1,0:T(8,128)(2,1)}, u32[]{:S(2)}, u32[]{:S(2)}) collective-permute-start(bf16[256,1024]{1,0:T(8,128)(2,1)} %fusion.50), channel_id=1, source_target_pairs={{0,1},{1,0},{2,3},{3,2},{4,5},{5,4},{6,7},{7,6},{8,9},{9,8},{10,11... | collective-permute-start | bytes 1572872 | tf_op jit(solution)/shard_map/ppermute | solution.py:402
  31.5 37.8 %collective-permute-start.3 = (bf16[1184,256]{1,0:T(8,128)(2,1)}, bf16[1184,256]{1,0:T(8,128)(2,1)}, u32[]{:S(2)}, u32[]{:S(2)}) collective-permute-start(bf16[1184,256]{1,0:T(8,128)(2,1)} %constant_dynamic-slice_fusion.4), channel_id=1, source_target_pairs={{0,1},{1,2},{2,3},{3,0},{4,5},{5,6},{6,7},{7,4},{8,9},{9,10},{10,1... | collective-permute-start | bytes 1818632 | tf_op jit(solution)/shard_map/ppermute | solution.py:405
  34.2 35.0 %collective-permute-start = (bf16[256,1024]{1,0:T(8,128)(2,1)}, bf16[256,1024]{1,0:T(8,128)(2,1)S(1)}, u32[]{:S(2)}, u32[]{:S(2)}) collective-permute-start(bf16[256,1024]{1,0:T(8,128)(2,1)} %get-tuple-element.410), channel_id=1, source_target_pairs={{0,2},{1,3},{2,0},{3,1},{4,6},{5,7},{6,4},{7,5},{8,10},{9,11},{10,... | collective-permute-start | bytes 1572872 | tf_op jit(solution)/shard_map/ppermute | solution.py:405
  69.3 27.6 %collective-permute-start.12 = (bf16[1184,256]{1,0:T(8,128)(2,1)}, bf16[1184,256]{1,0:T(8,128)(2,1)S(1)}, u32[]{:S(2)}, u32[]{:S(2)}) collective-permute-start(bf16[1184,256]{1,0:T(8,128)(2,1)} %collective-permute-done.3), channel_id=1, source_target_pairs={{0,1},{1,2},{2,3},{3,0},{4,5},{5,6},{6,7},{7,4},{8,9},{9,10},{10,1... | collective-permute-start | bytes 1818632 | tf_op jit(solution)/shard_map/ppermute | solution.py:405
  74.2 22.6 %collective-permute-start.8 = (bf16[256,1024]{1,0:T(8,128)(2,1)S(1)}, bf16[256,1024]{1,0:T(8,128)(2,1)S(1)}, u32[]{:S(2)}, u32[]{:S(2)}) collective-permute-start(bf16[256,1024]{1,0:T(8,128)(2,1)S(1)} %get-tuple-element.372), channel_id=1, source_target_pairs={{0,1},{1,0},{2,3},{3,2},{4,5},{5,4},{6,7},{7,6},{8,9},{9,8},{10,11... | collective-permute-start | bytes 1572872 | tf_op jit(solution)/shard_map/ppermute | solution.py:402
  94.5 87.6 %collective-permute-start.4 = (bf16[256,1024]{1,0:T(8,128)(2,1)S(1)}, bf16[256,1024]{1,0:T(8,128)(2,1)}, u32[]{:S(2)}, u32[]{:S(2)}) collective-permute-start(bf16[256,1024]{1,0:T(8,128)(2,1)S(1)} %collective-permute-done), channel_id=1, source_target_pairs={{0,16},{16,0},{1,17},{17,1},{2,18},{18,2},{3,19},{19,3},{4,20},{20... | collective-permute-start | bytes 1572872 | tf_op jit(solution)/shard_map/ppermute | solution.py:384
  139.1 27.5 %collective-permute-start.22 = (bf16[2,2,592,256]{3,2,1,0:T(8,128)(2,1)S(1)}, bf16[2,2,592,256]{3,2,1,0:T(8,128)(2,1)S(1)}, u32[]{:S(2)}, u32[]{:S(2)}) collective-permute-start(bf16[2,2,592,256]{3,2,1,0:T(8,128)(2,1)S(1)} %pad_maximum_fusion.10), channel_id=1, source_target_pairs={{0,4},{4,0},{8,12},{12,8},{1,5},{5,1},{9,13},{13,9},{2,6},{6,2},{1... | collective-permute-start | bytes 3637256 | tf_op jit(solution)/shard_map/ppermute | solution.py:408
  140.9 27.3 %collective-permute-start.21 = (bf16[2,2,592,256]{3,2,1,0:T(8,128)(2,1)S(1)}, bf16[2,2,592,256]{3,2,1,0:T(8,128)(2,1)}, u32[]{:S(2)}, u32[]{:S(2)}) collective-permute-start(bf16[2,2,592,256]{3,2,1,0:T(8,128)(2,1)S(1)} %pad_maximum_fusion.9), channel_id=1, source_target_pairs={{0,8},{4,12},{8,0},{12,4},{1,9},{5,13},{9,1},{13,5},{2,10},{6,14},... | collective-permute-start | bytes 3637256 | tf_op jit(solution)/shard_map/ppermute | solution.py:408
  179.7 57.3 %collective-permute-start.28 = (bf16[1024,768]{1,0:T(8,128)(2,1)}, bf16[1024,768]{1,0:T(8,128)(2,1)}, u32[]{:S(2)}, u32[]{:S(2)}) collective-permute-start(bf16[1024,768]{1,0:T(8,128)(2,1)} %pad_maximum_fusion.5), channel_id=1, source_target_pairs={{16,0},{17,1},{18,2},{19,3},{20,4},{21,5},{22,6},{23,7},{24,8},{25... | collective-permute-start | bytes 4718600 | tf_op jit(solution)/shard_map/ppermute | solution.py:387
  184.5 31.6 %collective-permute-start.24 = (bf16[2,512,256]{2,1,0:T(8,128)(2,1)S(1)}, bf16[2,512,256]{2,1,0:T(8,128)(2,1)S(1)}, u32[]{:S(2)}, u32[]{:S(2)}) collective-permute-start(bf16[2,512,256]{2,1,0:T(8,128)(2,1)S(1)} %fusion.92), channel_id=1, source_target_pairs={{0,1},{1,0},{2,3},{3,2},{4,5},{5,4},{6,7},{7,6},{8,9},{9,8},{10,11... | collective-permute-start | bytes 1572872 | tf_op jit(solution)/shard_map/ppermute | solution.py:402
  185.7 31.7 %collective-permute-start.25 = (bf16[1184,256]{1,0:T(8,128)(2,1)S(1)}, bf16[1184,256]{1,0:T(8,128)(2,1)S(1)}, u32[]{:S(2)}, u32[]{:S(2)}) collective-permute-start(bf16[1184,256]{1,0:T(8,128)(2,1)S(1)} %constant_dynamic-slice_fusion.1), channel_id=1, source_target_pairs={{0,1},{1,2},{2,3},{3,0},{4,5},{5,6},{6,7},{7,4},{8,9},{9,10},{10,1... | collective-permute-start | bytes 1818632 | tf_op jit(solution)/shard_map/ppermute | solution.py:405
  187.7 42.9 %collective-permute-start.26 = (bf16[1184,256]{1,0:T(8,128)(2,1)S(1)}, bf16[1184,256]{1,0:T(8,128)(2,1)S(1)}, u32[]{:S(2)}, u32[]{:S(2)}) collective-permute-start(bf16[1184,256]{1,0:T(8,128)(2,1)S(1)} %constant_dynamic-slice_fusion.1), channel_id=1, source_target_pairs={{0,2},{1,3},{2,0},{3,1},{4,6},{5,7},{6,4},{7,5},{8,10},{9,11},{10,... | collective-permute-start | bytes 1818632 | tf_op jit(solution)/shard_map/ppermute | solution.py:405
  188.8 48.3 %collective-permute-start.27 = (bf16[1184,256]{1,0:T(8,128)(2,1)S(1)}, bf16[1184,256]{1,0:T(8,128)(2,1)S(1)}, u32[]{:S(2)}, u32[]{:S(2)}) collective-permute-start(bf16[1184,256]{1,0:T(8,128)(2,1)S(1)} %constant_dynamic-slice_fusion.1), channel_id=1, source_target_pairs={{0,3},{1,0},{2,1},{3,2},{4,7},{5,4},{6,5},{7,6},{8,11},{9,8},{10,9... | collective-permute-start | bytes 1818632 | tf_op jit(solution)/shard_map/ppermute | solution.py:405
  272.6 23.0 %collective-permute-start.33 = (bf16[3,592,256]{2,1,0:T(8,128)(2,1)S(1)}, bf16[3,592,256]{2,1,0:T(8,128)(2,1)S(1)}, u32[]{:S(2)}, u32[]{:S(2)}) collective-permute-start(bf16[3,592,256]{2,1,0:T(8,128)(2,1)S(1)} %get-tuple-element.414), channel_id=1, source_target_pairs={{0,4},{4,0},{8,12},{12,8},{1,5},{5,1},{9,13},{13,9},{2,6},{6,2},{1... | collective-permute-start | bytes 2727944 | tf_op jit(solution)/shard_map/ppermute | solution.py:408
  274.3 23.1 %collective-permute-start.34 = (bf16[3,592,256]{2,1,0:T(8,128)(2,1)S(1)}, bf16[3,592,256]{2,1,0:T(8,128)(2,1)S(1)}, u32[]{:S(2)}, u32[]{:S(2)}) collective-permute-start(bf16[3,592,256]{2,1,0:T(8,128)(2,1)S(1)} %get-tuple-element.413), channel_id=1, source_target_pairs={{0,8},{4,12},{8,0},{12,4},{1,9},{5,13},{9,1},{13,5},{2,10},{6,14},... | collective-permute-start | bytes 2727944 | tf_op jit(solution)/shard_map/ppermute | solution.py:408
  275.6 28.5 %collective-permute-start.35 = (bf16[256,768]{1,0:T(8,128)(2,1)S(1)}, bf16[256,768]{1,0:T(8,128)(2,1)S(1)}, u32[]{:S(2)}, u32[]{:S(2)}) collective-permute-start(bf16[256,768]{1,0:T(8,128)(2,1)S(1)} %collective-permute-done.29), channel_id=1, source_target_pairs={{0,4},{4,0},{8,12},{12,8},{1,5},{5,1},{9,13},{13,9},{2,6},{6,2},{1... | collective-permute-start | bytes 1179656 | tf_op jit(solution)/shard_map/ppermute | solution.py:408
  275.9 37.0 %collective-permute-start.36 = (bf16[256,768]{1,0:T(8,128)(2,1)S(1)}, bf16[256,768]{1,0:T(8,128)(2,1)S(1)}, u32[]{:S(2)}, u32[]{:S(2)}) collective-permute-start(bf16[256,768]{1,0:T(8,128)(2,1)S(1)} %collective-permute-done.29), channel_id=1, source_target_pairs={{0,8},{4,12},{8,0},{12,4},{1,9},{5,13},{9,1},{13,5},{2,10},{6,14},... | collective-permute-start | bytes 1179656 | tf_op jit(solution)/shard_map/ppermute | solution.py:408
  276.7 36.3 %collective-permute-start.37 = (bf16[256,768]{1,0:T(8,128)(2,1)S(1)}, bf16[256,768]{1,0:T(8,128)(2,1)S(1)}, u32[]{:S(2)}, u32[]{:S(2)}) collective-permute-start(bf16[256,768]{1,0:T(8,128)(2,1)S(1)} %collective-permute-done.29), channel_id=1, source_target_pairs={{0,12},{4,8},{8,4},{12,0},{1,13},{5,9},{9,5},{13,1},{2,14},{6,10},... | collective-permute-start | bytes 1179656 | tf_op jit(solution)/shard_map/ppermute | solution.py:408
  314.4 23.7 %collective-permute-start.39 = (bf16[512,1024]{1,0:T(8,128)(2,1)S(1)}, bf16[512,1024]{1,0:T(8,128)(2,1)S(1)}, u32[]{:S(2)}, u32[]{:S(2)}) collective-permute-start(bf16[512,1024]{1,0:T(8,128)(2,1)S(1)} %get-tuple-element.370), channel_id=1, source_target_pairs={{0,1},{1,0},{2,3},{3,2},{4,5},{5,4},{6,7},{7,6},{8,9},{9,8},{10,11... | collective-permute-start | bytes 3145736 | tf_op jit(solution)/shard_map/ppermute | solution.py:402
  340.1 67.6 %collective-permute-start.38 = (bf16[512,1024]{1,0:T(8,128)(2,1)S(1)}, bf16[512,1024]{1,0:T(8,128)(2,1)S(1)}, u32[]{:S(2)}, u32[]{:S(2)}) collective-permute-start(bf16[512,1024]{1,0:T(8,128)(2,1)S(1)} %fusion.57), channel_id=1, source_target_pairs={{16,18},{17,19},{18,16},{19,17},{20,22},{21,23},{22,20},{23,21},{2... | collective-permute-start | bytes 3145736 | tf_op jit(solution)/shard_map/ppermute | solution.py:392
  341.2 42.0 %collective-permute-start.42 = (bf16[2,3,592,256]{3,2,1,0:T(8,128)(2,1)S(1)}, bf16[2,3,592,256]{3,2,1,0:T(8,128)(2,1)}, u32[]{:S(2)}, u32[]{:S(2)}) collective-permute-start(bf16[2,3,592,256]{3,2,1,0:T(8,128)(2,1)S(1)} %pad_maximum_fusion.4), channel_id=1, source_target_pairs={{0,4},{4,0},{8,12},{12,8},{1,5},{5,1},{9,13},{13,9},{2,6},{6,2},{1... | collective-permute-start | bytes 5455880 | tf_op jit(solution)/shard_map/ppermute | solution.py:408
  343.0 42.4 %collective-permute-start.41 = (bf16[2,3,592,256]{3,2,1,0:T(8,128)(2,1)S(1)}, bf16[2,3,592,256]{3,2,1,0:T(8,128)(2,1)}, u32[]{:S(2)}, u32[]{:S(2)}) collective-permute-start(bf16[2,3,592,256]{3,2,1,0:T(8,128)(2,1)S(1)} %pad_maximum_fusion.3), channel_id=1, source_target_pairs={{0,8},{4,12},{8,0},{12,4},{1,9},{5,13},{9,1},{13,5},{2,10},{6,14},... | collective-permute-start | bytes 5455880 | tf_op jit(solution)/shard_map/ppermute | solution.py:408
  483.8 26.0 %collective-permute-start.51 = (bf16[512,1024]{1,0:T(8,128)(2,1)S(1)}, bf16[512,1024]{1,0:T(8,128)(2,1)S(1)}, u32[]{:S(2)}, u32[]{:S(2)}) collective-permute-start(bf16[512,1024]{1,0:T(8,128)(2,1)S(1)} %fusion.59), channel_id=1, source_target_pairs={{0,16},{16,0},{1,17},{17,1},{2,18},{18,2},{3,19},{19,3},{4,20},{20... | collective-permute-start | bytes 3145736 | tf_op jit(solution)/shard_map/ppermute | solution.py:384
  519.2 47.1 %collective-permute-start.52 = (bf16[2,2,592,256]{3,2,1,0:T(8,128)(2,1)}, bf16[2,2,592,256]{3,2,1,0:T(8,128)(2,1)}, u32[]{:S(2)}, u32[]{:S(2)}) collective-permute-start(bf16[2,2,592,256]{3,2,1,0:T(8,128)(2,1)} %get-tuple-element.238), channel_id=1, source_target_pairs={{0,4},{4,0},{8,12},{12,8},{1,5},{5,1},{9,13},{13,9},{2,6},{6,2},{1... | collective-permute-start | bytes 3637256 | tf_op jit(solution)/shard_map/ppermute | solution.py:408
  525.2 41.0 %collective-permute-start.53 = (bf16[2,2,592,256]{3,2,1,0:T(8,128)(2,1)}, bf16[2,2,592,256]{3,2,1,0:T(8,128)(2,1)}, u32[]{:S(2)}, u32[]{:S(2)}) collective-permute-start(bf16[2,2,592,256]{3,2,1,0:T(8,128)(2,1)} %get-tuple-element.240), channel_id=1, source_target_pairs={{0,8},{4,12},{8,0},{12,4},{1,9},{5,13},{9,1},{13,5},{2,10},{6,14},... | collective-permute-start | bytes 3637256 | tf_op jit(solution)/shard_map/ppermute | solution.py:408
  572.6 23.5 %collective-permute-start.56 = (bf16[2,592,256]{2,1,0:T(8,128)(2,1)}, bf16[2,592,256]{2,1,0:T(8,128)(2,1)}, u32[]{:S(2)}, u32[]{:S(2)}) collective-permute-start(bf16[2,592,256]{2,1,0:T(8,128)(2,1)} %fusion.66), channel_id=1, source_target_pairs={{0,4},{4,0},{8,12},{12,8},{1,5},{5,1},{9,13},{13,9},{2,6},{6,2},{1... | collective-permute-start | bytes 1818632 | tf_op jit(solution)/shard_map/ppermute | solution.py:408
  587.1 39.1 %collective-permute-start.58 = (bf16[2,2,592,256]{3,2,1,0:T(8,128)(2,1)}, bf16[2,2,592,256]{3,2,1,0:T(8,128)(2,1)S(1)}, u32[]{:S(2)}, u32[]{:S(2)}) collective-permute-start(bf16[2,2,592,256]{3,2,1,0:T(8,128)(2,1)} %get-tuple-element.254), channel_id=1, source_target_pairs={{0,4},{4,0},{8,12},{12,8},{1,5},{5,1},{9,13},{13,9},{2,6},{6,2},{1... | collective-permute-start | bytes 3637256 | tf_op jit(solution)/shard_map/ppermute | solution.py:408
  587.2 39.9 %collective-permute-start.59 = (bf16[2,2,592,256]{3,2,1,0:T(8,128)(2,1)}, bf16[2,2,592,256]{3,2,1,0:T(8,128)(2,1)S(1)}, u32[]{:S(2)}, u32[]{:S(2)}) collective-permute-start(bf16[2,2,592,256]{3,2,1,0:T(8,128)(2,1)} %get-tuple-element.255), channel_id=1, source_target_pairs={{0,8},{4,12},{8,0},{12,4},{1,9},{5,13},{9,1},{13,5},{2,10},{6,14},... | collective-permute-start | bytes 3637256 | tf_op jit(solution)/shard_map/ppermute | solution.py:408
  602.1 23.8 %collective-permute-start.57 = (bf16[512,1024]{1,0:T(8,128)(2,1)S(1)}, bf16[512,1024]{1,0:T(8,128)(2,1)S(1)}, u32[]{:S(2)}, u32[]{:S(2)}) collective-permute-start(bf16[512,1024]{1,0:T(8,128)(2,1)S(1)} %fusion.60), channel_id=1, source_target_pairs={{0,1},{1,0},{2,3},{3,2},{4,5},{5,4},{6,7},{7,6},{8,9},{9,8},{10,11... | collective-permute-start | bytes 3145736 | tf_op jit(solution)/shard_map/ppermute | solution.py:402
  630.1 64.2 %collective-permute-start.65 = (bf16[1184,256]{1,0:T(8,128)(2,1)S(1)}, bf16[1184,256]{1,0:T(8,128)(2,1)S(1)}, u32[]{:S(2)}, u32[]{:S(2)}) collective-permute-start(bf16[1184,256]{1,0:T(8,128)(2,1)S(1)} %get-tuple-element.428), channel_id=1, source_target_pairs={{0,2},{1,3},{2,0},{3,1},{4,6},{5,7},{6,4},{7,5},{8,10},{9,11},{10,... | collective-permute-start | bytes 1818632 | tf_op jit(solution)/shard_map/ppermute | solution.py:405
  631.7 74.6 %collective-permute-start.66 = (bf16[1184,256]{1,0:T(8,128)(2,1)}, bf16[1184,256]{1,0:T(8,128)(2,1)}, u32[]{:S(2)}, u32[]{:S(2)}) collective-permute-start(bf16[1184,256]{1,0:T(8,128)(2,1)} %get-tuple-element.427), channel_id=1, source_target_pairs={{0,1},{1,2},{2,3},{3,0},{4,5},{5,6},{6,7},{7,4},{8,9},{9,10},{10,1... | collective-permute-start | bytes 1818632 | tf_op jit(solution)/shard_map/ppermute | solution.py:405
  633.2 87.6 %collective-permute-start.70 = (bf16[2,128,768]{2,1,0:T(8,128)(2,1)}, bf16[2,128,768]{2,1,0:T(8,128)(2,1)}, u32[]{:S(2)}, u32[]{:S(2)}) collective-permute-start(bf16[2,128,768]{2,1,0:T(8,128)(2,1)} %pad_maximum_fusion.20), channel_id=1, source_target_pairs={{0,8},{4,12},{8,0},{12,4},{1,9},{5,13},{9,1},{13,5},{2,10},{6,14},... | collective-permute-start | bytes 1179656 | tf_op jit(solution)/shard_map/ppermute | solution.py:408
  665.4 26.3 %collective-permute-start.64 = (bf16[512,1024]{1,0:T(8,128)(2,1)S(1)}, bf16[512,1024]{1,0:T(8,128)(2,1)S(1)}, u32[]{:S(2)}, u32[]{:S(2)}) collective-permute-start(bf16[512,1024]{1,0:T(8,128)(2,1)S(1)} %fusion.62), channel_id=1, source_target_pairs={{0,16},{16,0},{1,17},{17,1},{2,18},{18,2},{3,19},{19,3},{4,20},{20... | collective-permute-start | bytes 3145736 | tf_op jit(solution)/shard_map/ppermute | solution.py:384
  691.6 30.4 %collective-permute-start.69 = (bf16[2,128,768]{2,1,0:T(8,128)(2,1)}, bf16[2,128,768]{2,1,0:T(8,128)(2,1)}, u32[]{:S(2)}, u32[]{:S(2)}) collective-permute-start(bf16[2,128,768]{2,1,0:T(8,128)(2,1)} %pad_maximum_fusion.19), channel_id=1, source_target_pairs={{0,4},{4,0},{8,12},{12,8},{1,5},{5,1},{9,13},{13,9},{2,6},{6,2},{1... | collective-permute-start | bytes 1179656 | tf_op jit(solution)/shard_map/ppermute | solution.py:408
  695.0 24.1 %collective-permute-start.67 = (bf16[2,592,256]{2,1,0:T(8,128)(2,1)}, bf16[2,592,256]{2,1,0:T(8,128)(2,1)}, u32[]{:S(2)}, u32[]{:S(2)}) collective-permute-start(bf16[2,592,256]{2,1,0:T(8,128)(2,1)} %fusion.67), channel_id=1, source_target_pairs={{0,8},{4,12},{8,0},{12,4},{1,9},{5,13},{9,1},{13,5},{2,10},{6,14},... | collective-permute-start | bytes 1818632 | tf_op jit(solution)/shard_map/ppermute | solution.py:408
  706.4 92.2 %collective-permute-start.78 = (bf16[512,1024]{1,0:T(8,128)(2,1)S(1)}, bf16[512,1024]{1,0:T(8,128)(2,1)}, u32[]{:S(2)}, u32[]{:S(2)}) collective-permute-start(bf16[512,1024]{1,0:T(8,128)(2,1)S(1)} %copy-done.3), channel_id=1, source_target_pairs={{16,2},{17,3},{18,0},{19,1},{20,6},{21,7},{22,4},{23,5},{24,10},{2... | collective-permute-start | bytes 3145736 | tf_op jit(solution)/shard_map/ppermute | solution.py:392
  716.4 82.2 %collective-permute-start.77 = (bf16[512,1024]{1,0:T(8,128)(2,1)}, bf16[512,1024]{1,0:T(8,128)(2,1)}, u32[]{:S(2)}, u32[]{:S(2)}) collective-permute-start(bf16[512,1024]{1,0:T(8,128)(2,1)} %get-tuple-element.408), channel_id=1, source_target_pairs={{0,16},{1,17},{2,18},{3,19},{4,20},{5,21},{6,22},{7,23},{8,24},{9,... | collective-permute-start | bytes 3145736 | tf_op jit(solution)/shard_map/ppermute | solution.py:387
  719.1 79.4 %collective-permute-start.79 = (bf16[512,1024]{1,0:T(8,128)(2,1)}, bf16[512,1024]{1,0:T(8,128)(2,1)}, u32[]{:S(2)}, u32[]{:S(2)}) collective-permute-start(bf16[512,1024]{1,0:T(8,128)(2,1)} %get-tuple-element.408), channel_id=1, source_target_pairs={{16,18},{17,19},{18,16},{19,17},{20,22},{21,23},{22,20},{23,21},{2... | collective-permute-start | bytes 3145736 | tf_op jit(solution)/shard_map/ppermute | solution.py:392
  720.7 47.0 %collective-permute-start.71 = (bf16[2,2,592,256]{3,2,1,0:T(8,128)(2,1)}, bf16[2,2,592,256]{3,2,1,0:T(8,128)(2,1)}, u32[]{:S(2)}, u32[]{:S(2)}) collective-permute-start(bf16[2,2,592,256]{3,2,1,0:T(8,128)(2,1)} %get-tuple-element.261), channel_id=1, source_target_pairs={{0,4},{4,0},{8,12},{12,8},{1,5},{5,1},{9,13},{13,9},{2,6},{6,2},{1... | collective-permute-start | bytes 3637256 | tf_op jit(solution)/shard_map/ppermute | solution.py:408
  722.0 60.3 %collective-permute-start.72 = (bf16[2,2,592,256]{3,2,1,0:T(8,128)(2,1)}, bf16[2,2,592,256]{3,2,1,0:T(8,128)(2,1)}, u32[]{:S(2)}, u32[]{:S(2)}) collective-permute-start(bf16[2,2,592,256]{3,2,1,0:T(8,128)(2,1)} %get-tuple-element.263), channel_id=1, source_target_pairs={{0,8},{4,12},{8,0},{12,4},{1,9},{5,13},{9,1},{13,5},{2,10},{6,14},... | collective-permute-start | bytes 3637256 | tf_op jit(solution)/shard_map/ppermute | solution.py:408
  767.7 22.6 %collective-permute-start.73 = (bf16[1184,256]{1,0:T(8,128)(2,1)S(1)}, bf16[1184,256]{1,0:T(8,128)(2,1)S(1)}, u32[]{:S(2)}, u32[]{:S(2)}) collective-permute-start(bf16[1184,256]{1,0:T(8,128)(2,1)S(1)} %fusion.73), channel_id=1, source_target_pairs={{0,3},{1,0},{2,1},{3,2},{4,7},{5,4},{6,5},{7,6},{8,11},{9,8},{10,9... | collective-permute-start | bytes 1818632 | tf_op jit(solution)/shard_map/ppermute | solution.py:405
  795.1 33.6 %collective-permute-start.86 = (bf16[1184,256]{1,0:T(8,128)(2,1)}, bf16[1184,256]{1,0:T(8,128)(2,1)}, u32[]{:S(2)}, u32[]{:S(2)}) collective-permute-start(bf16[1184,256]{1,0:T(8,128)(2,1)} %get-tuple-element.362), channel_id=1, source_target_pairs={{0,4},{4,0},{8,12},{12,8},{1,5},{5,1},{9,13},{13,9},{2,6},{6,2},{1... | collective-permute-start | bytes 1818632 | tf_op jit(solution)/shard_map/ppermute | solution.py:408
  796.5 33.8 %collective-permute-start.87 = (bf16[1184,256]{1,0:T(8,128)(2,1)}, bf16[1184,256]{1,0:T(8,128)(2,1)S(1)}, u32[]{:S(2)}, u32[]{:S(2)}) collective-permute-start(bf16[1184,256]{1,0:T(8,128)(2,1)} %get-tuple-element.362), channel_id=1, source_target_pairs={{0,8},{4,12},{8,0},{12,4},{1,9},{5,13},{9,1},{13,5},{2,10},{6,14},... | collective-permute-start | bytes 1818632 | tf_op jit(solution)/shard_map/ppermute | solution.py:408
  800.2 24.3 %collective-permute-start.81 = (bf16[2,592,256]{2,1,0:T(8,128)(2,1)S(1)}, bf16[2,592,256]{2,1,0:T(8,128)(2,1)S(1)}, u32[]{:S(2)}, u32[]{:S(2)}) collective-permute-start(bf16[2,592,256]{2,1,0:T(8,128)(2,1)S(1)} %fusion.69), channel_id=1, source_target_pairs={{0,8},{4,12},{8,0},{12,4},{1,9},{5,13},{9,1},{13,5},{2,10},{6,14},... | collective-permute-start | bytes 1818632 | tf_op jit(solution)/shard_map/ppermute | solution.py:408
  803.2 23.0 %collective-permute-start.82 = (bf16[2,592,256]{2,1,0:T(8,128)(2,1)S(1)}, bf16[2,592,256]{2,1,0:T(8,128)(2,1)S(1)}, u32[]{:S(2)}, u32[]{:S(2)}) collective-permute-start(bf16[2,592,256]{2,1,0:T(8,128)(2,1)S(1)} %fusion.70), channel_id=1, source_target_pairs={{0,4},{4,0},{8,12},{12,8},{1,5},{5,1},{9,13},{13,9},{2,6},{6,2},{1... | collective-permute-start | bytes 1818632 | tf_op jit(solution)/shard_map/ppermute | solution.py:408
  813.3 35.6 %collective-permute-start.84 = (bf16[2,2,592,256]{3,2,1,0:T(8,128)(2,1)}, bf16[2,2,592,256]{3,2,1,0:T(8,128)(2,1)S(1)}, u32[]{:S(2)}, u32[]{:S(2)}) collective-permute-start(bf16[2,2,592,256]{3,2,1,0:T(8,128)(2,1)} %get-tuple-element.298), channel_id=1, source_target_pairs={{0,4},{4,0},{8,12},{12,8},{1,5},{5,1},{9,13},{13,9},{2,6},{6,2},{1... | collective-permute-start | bytes 3637256 | tf_op jit(solution)/shard_map/ppermute | solution.py:408
  824.5 27.1 %collective-permute-start.85 = (bf16[2,2,592,256]{3,2,1,0:T(8,128)(2,1)}, bf16[2,2,592,256]{3,2,1,0:T(8,128)(2,1)S(1)}, u32[]{:S(2)}, u32[]{:S(2)}) collective-permute-start(bf16[2,2,592,256]{3,2,1,0:T(8,128)(2,1)} %get-tuple-element.299), channel_id=1, source_target_pairs={{0,8},{4,12},{8,0},{12,4},{1,9},{5,13},{9,1},{13,5},{2,10},{6,14},... | collective-permute-start | bytes 3637256 | tf_op jit(solution)/shard_map/ppermute | solution.py:408
  826.4 34.6 %collective-permute-start.83 = (bf16[512,1024]{1,0:T(8,128)(2,1)S(1)}, bf16[512,1024]{1,0:T(8,128)(2,1)S(1)}, u32[]{:S(2)}, u32[]{:S(2)}) collective-permute-start(bf16[512,1024]{1,0:T(8,128)(2,1)S(1)} %fusion.64), channel_id=1, source_target_pairs={{0,1},{1,0},{2,3},{3,2},{4,5},{5,4},{6,7},{7,6},{8,9},{9,8},{10,11... | collective-permute-start | bytes 3145736 | tf_op jit(solution)/shard_map/ppermute | solution.py:402
  829.6 45.3 %collective-permute-start.91 = (bf16[512,1024]{1,0:T(8,128)(2,1)S(1)}, bf16[512,1024]{1,0:T(8,128)(2,1)S(1)}, u32[]{:S(2)}, u32[]{:S(2)}) collective-permute-start(bf16[512,1024]{1,0:T(8,128)(2,1)S(1)} %copy-done.9), channel_id=1, source_target_pairs={{16,18},{17,19},{18,16},{19,17},{20,22},{21,23},{22,20},{23,21},{2... | collective-permute-start | bytes 3145736 | tf_op jit(solution)/shard_map/ppermute | solution.py:392
  830.3 44.6 %collective-permute-start.92 = (bf16[512,1024]{1,0:T(8,128)(2,1)S(1)}, bf16[512,1024]{1,0:T(8,128)(2,1)S(1)}, u32[]{:S(2)}, u32[]{:S(2)}) collective-permute-start(bf16[512,1024]{1,0:T(8,128)(2,1)S(1)} %copy-done.9), channel_id=1, source_target_pairs={{0,16},{1,17},{2,18},{3,19},{4,20},{5,21},{6,22},{7,23},{8,24},{9,... | collective-permute-start | bytes 3145736 | tf_op jit(solution)/shard_map/ppermute | solution.py:387
  849.0 25.7 %collective-permute-start.89 = (bf16[256,768]{1,0:T(8,128)(2,1)S(1)}, bf16[256,768]{1,0:T(8,128)(2,1)S(1)}, u32[]{:S(2)}, u32[]{:S(2)}) collective-permute-start(bf16[256,768]{1,0:T(8,128)(2,1)S(1)} %pad_maximum_fusion.21), channel_id=1, source_target_pairs={{0,16},{1,17},{2,18},{3,19},{4,20},{5,21},{6,22},{7,23},{8,24},{9,... | collective-permute-start | bytes 1179656 | tf_op jit(solution)/shard_map/ppermute | solution.py:387
  851.5 23.3 %collective-permute-start.90 = (bf16[256,768]{1,0:T(8,128)(2,1)S(1)}, bf16[256,768]{1,0:T(8,128)(2,1)S(1)}, u32[]{:S(2)}, u32[]{:S(2)}) collective-permute-start(bf16[256,768]{1,0:T(8,128)(2,1)S(1)} %pad_maximum_fusion.21), channel_id=1, source_target_pairs={{16,18},{17,19},{18,16},{19,17},{20,22},{21,23},{22,20},{23,21},{2... | collective-permute-start | bytes 1179656 | tf_op jit(solution)/shard_map/ppermute | solution.py:392
  874.6 48.8 %collective-permute-start.93 = (bf16[1184,256]{1,0:T(8,128)(2,1)S(1)}, bf16[1184,256]{1,0:T(8,128)(2,1)S(1)}, u32[]{:S(2)}, u32[]{:S(2)}) collective-permute-start(bf16[1184,256]{1,0:T(8,128)(2,1)S(1)} %get-tuple-element.426), channel_id=1, source_target_pairs={{0,2},{1,3},{2,0},{3,1},{4,6},{5,7},{6,4},{7,5},{8,10},{9,11},{10,... | collective-permute-start | bytes 1818632 | tf_op jit(solution)/shard_map/ppermute | solution.py:405
  874.6 49.9 %collective-permute-start.94 = (bf16[1184,256]{1,0:T(8,128)(2,1)S(1)}, bf16[1184,256]{1,0:T(8,128)(2,1)S(1)}, u32[]{:S(2)}, u32[]{:S(2)}) collective-permute-start(bf16[1184,256]{1,0:T(8,128)(2,1)S(1)} %get-tuple-element.425), channel_id=1, source_target_pairs={{0,1},{1,2},{2,3},{3,0},{4,5},{5,6},{6,7},{7,4},{8,9},{9,10},{10,1... | collective-permute-start | bytes 1818632 | tf_op jit(solution)/shard_map/ppermute | solution.py:405
  876.5 70.9 %collective-permute-start.100 = (bf16[512,1024]{1,0:T(8,128)(2,1)S(1)}, bf16[512,1024]{1,0:T(8,128)(2,1)S(1)}, u32[]{:S(2)}, u32[]{:S(2)}) collective-permute-start(bf16[512,1024]{1,0:T(8,128)(2,1)S(1)} %get-tuple-element.366), channel_id=1, source_target_pairs={{16,2},{17,3},{18,0},{19,1},{20,6},{21,7},{22,4},{23,5},{24,10},{2... | collective-permute-start | bytes 3145736 | tf_op jit(solution)/shard_map/ppermute | solution.py:392
  877.8 47.8 %collective-permute-start.99 = (f32[4,1024]{1,0:T(4,128)S(1)}, f32[4,1024]{1,0:T(4,128)S(1)}, u32[]{:S(2)}, u32[]{:S(2)}) collective-permute-start(f32[4,1024]{1,0:T(4,128)S(1)} %pad_maximum_fusion.27), channel_id=1, source_target_pairs={{0,16},{16,0},{1,17},{17,1},{2,18},{18,2},{3,19},{19,3},{4,20},{20... | collective-permute-start | bytes 49160 | tf_op jit(solution)/shard_map/ppermute | solution.py:384
  883.4 64.0 %collective-permute-start.96 = (bf16[2,592,256]{2,1,0:T(8,128)(2,1)S(1)}, bf16[2,592,256]{2,1,0:T(8,128)(2,1)S(1)}, u32[]{:S(2)}, u32[]{:S(2)}) collective-permute-start(bf16[2,592,256]{2,1,0:T(8,128)(2,1)S(1)} %fusion.72), channel_id=1, source_target_pairs={{0,4},{4,0},{8,12},{12,8},{1,5},{5,1},{9,13},{13,9},{2,6},{6,2},{1... | collective-permute-start | bytes 1818632 | tf_op jit(solution)/shard_map/ppermute | solution.py:408
  923.5 23.9 %collective-permute-start.95 = (bf16[2,592,256]{2,1,0:T(8,128)(2,1)S(1)}, bf16[2,592,256]{2,1,0:T(8,128)(2,1)S(1)}, u32[]{:S(2)}, u32[]{:S(2)}) collective-permute-start(bf16[2,592,256]{2,1,0:T(8,128)(2,1)S(1)} %fusion.71), channel_id=1, source_target_pairs={{0,8},{4,12},{8,0},{12,4},{1,9},{5,13},{9,1},{13,5},{2,10},{6,14},... | collective-permute-start | bytes 1818632 | tf_op jit(solution)/shard_map/ppermute | solution.py:408
  924.6 22.8 %collective-permute-start.98 = (bf16[2,128,768]{2,1,0:T(8,128)(2,1)S(1)}, bf16[2,128,768]{2,1,0:T(8,128)(2,1)S(1)}, u32[]{:S(2)}, u32[]{:S(2)}) collective-permute-start(bf16[2,128,768]{2,1,0:T(8,128)(2,1)S(1)} %pad_maximum_fusion.23), channel_id=1, source_target_pairs={{0,8},{4,12},{8,0},{12,4},{1,9},{5,13},{9,1},{13,5},{2,10},{6,14},... | collective-permute-start | bytes 1179656 | tf_op jit(solution)/shard_map/ppermute | solution.py:408
  970.9 25.2 %collective-permute-start.108 = (bf16[1184,256]{1,0:T(8,128)(2,1)S(1)}, bf16[1184,256]{1,0:T(8,128)(2,1)S(1)}, u32[]{:S(2)}, u32[]{:S(2)}) collective-permute-start(bf16[1184,256]{1,0:T(8,128)(2,1)S(1)} %get-tuple-element.360), channel_id=1, source_target_pairs={{0,8},{4,12},{8,0},{12,4},{1,9},{5,13},{9,1},{13,5},{2,10},{6,14},... | collective-permute-start | bytes 1818632 | tf_op jit(solution)/shard_map/ppermute | solution.py:408
  971.8 24.2 %collective-permute-start.109 = (bf16[1184,256]{1,0:T(8,128)(2,1)S(1)}, bf16[1184,256]{1,0:T(8,128)(2,1)S(1)}, u32[]{:S(2)}, u32[]{:S(2)}) collective-permute-start(bf16[1184,256]{1,0:T(8,128)(2,1)S(1)} %get-tuple-element.360), channel_id=1, source_target_pairs={{0,12},{4,8},{8,4},{12,0},{1,13},{5,9},{9,5},{13,1},{2,14},{6,10},... | collective-permute-start | bytes 1818632 | tf_op jit(solution)/shard_map/ppermute | solution.py:408
  997.3 25.8 %collective-permute-start.114 = (bf16[1184,1024]{1,0:T(8,128)(2,1)S(1)}, bf16[1184,1024]{1,0:T(8,128)(2,1)S(1)}, u32[]{:S(2)}, u32[]{:S(2)}) collective-permute-start(bf16[1184,1024]{1,0:T(8,128)(2,1)S(1)} %maximum_select_fusion.4), channel_id=1, source_target_pairs={{0,16},{16,0},{1,17},{17,1},{2,18},{18,2},{3,19},{19,3},{4,20},{20... | collective-permute-start | bytes 7274504 | tf_op jit(solution)/shard_map/ppermute | solution.py:384
  (198 other events, 2430.6 us)

commit v3 on v2

--- a/solution.py
+++ b/solution.py
@@ -558,6 +558,9 @@
         self.second = self.rows - self.first
         self.columns = D // place.data
 
+    def part(self, share, place):
+        return lax.dynamic_slice_in_dim(share, place.dp * self.columns, self.columns, 1)
+
     def pieces(self):
         units, outs, down = self.units, self.outs, self.down
         return (
@@ -569,7 +572,7 @@
         )
 
 
-def pack_weights(place, cut, w_gate, w_up, w_down, w_out):
+def pack_weights(place, w_gate, w_up, w_down, w_out):
     kinds = (w_gate.T, w_out, w_down, w_up.T)
     halves = [item.reshape(2, -1, D) for item in kinds]
 
@@ -578,9 +581,13 @@
             [lax.dynamic_index_in_dim(item, core, 0, keepdims=False) for item in halves]
         )
 
-    own = half(place.core)
-    other = place.swap(half(1 - place.core))
-    return place.pick(own, other), place.pick(other, own)
+    return half(place.core), half(1 - place.core)
+
+
+def share_weights(place, cut, own, sent):
+    piece = place.pick(cut.part(own, place), place.to_core(cut.part(sent, place), 1))
+    other = place.swap(after(sent, piece))
+    return place.pick(own, other), place.pick(other, own), piece
 
 
 def any_specs(count):
@@ -636,12 +643,25 @@
     return place.flip(first, 2), place.flip(second, 1)
 
 
-def spread_at_once(place, cut, share, piece):
-    size = cut.heads
-    ring = jnp.stack((yield [place.around(piece, step) for step in range(1, size)]))
-    near = yield near_flips(place, cut, ring)
-    far = yield far_flips(place, cut, ring, *near)
-    return assemble(place, cut, share, [(list(range(1, size)), (ring, *near, *far))])
+def fill_kernel(cut, spot, full, gu, down, out, sems):
+    head = spot[1]
+    kinds = {"gate": gu.at[0], "up": gu.at[1], "down": down, "out": out}
+    copies = []
+    for step in range(cut.heads):
+        source = lax.rem(head - step + cut.heads, cut.heads)
+        for part in range(D // cut.columns):
+            columns = pl.ds(part * cut.columns, cut.columns)
+            for kind, row, count, second, at in cut.pieces():
+                index = source if kind == "out" else step
+                block = full.at[part * cut.heads + source, pl.ds(at + second * cut.first, count), :]
+                target = kinds[kind].at[index, pl.ds(row, count), columns]
+                copies.append(pltpu.make_async_copy(block, target, sems.at[len(copies)]))
+    run_copies(copies)
+
+
+def spread_at_once(place, cut, piece):
+    full = yield lax.all_gather(piece, ("dp", "head"), axis=0)
+    return fill(place, cut, fill_kernel, 5 * place.data * cut.heads, (full,))
 
 
 def spread_in_turn(place, cut, share, piece):
@@ -661,34 +681,32 @@
 
 
 def first_qkv(place, w_qkv, part):
-    part = yield place.across_from_zero(part)
     flipped = yield [place.flip(part, bits) for bits in range(1, place.data)]
     return place.pick(w_qkv, place.by_data(part, flipped).reshape(w_qkv.shape))
 
 
-def second_qkv(place, w_qkv, part):
-    own, part = yield place.to_core(w_qkv, 0), place.across(part, 1)
-    flipped = yield [place.flip(part, bits) for bits in range(1, place.data)]
-    return place.pick(own, place.by_data(part, flipped).reshape(w_qkv.shape))
+def second_qkv(place, w_qkv):
+    own, other = yield place.to_core(w_qkv, 0), place.across(w_qkv, 1)
+    return place.pick(own, other)
 
 
 def gather_far(place, far, gain):
-    far = yield far
-    shifted = yield [
-        place.beside(norm(far.astype(F32), gain).astype(BF16), shift)
-        for shift in range(1, place.half)
-    ]
-    return far, shifted
+    normed = norm(far.astype(F32), gain).astype(BF16)
+    return (yield [place.beside(normed, shift) for shift in range(1, place.half)])
 
 
 def assemble(place, cut, share, groups):
     steps = [group[0] for group in groups]
     parts = [part for group in groups for part in group[1]]
-    copies = 5 * (1 + 4 * (cut.heads - 1))
+    kernel = lambda cut, *refs: assemble_kernel(cut, steps, *refs)
+    return fill(place, cut, kernel, 5 * (1 + 4 * (cut.heads - 1)), (share, *parts))
+
+
+def fill(place, cut, kernel, copies, sources):
     shape = lambda *dims: jax.ShapeDtypeStruct(dims, BF16)
     gate_up, down, out = pl.pallas_call(
-        functools.partial(assemble_kernel, cut, steps),
-        in_specs=[pl.BlockSpec(memory_space=pltpu.SMEM)] + any_specs(1 + len(parts)),
+        functools.partial(kernel, cut),
+        in_specs=[pl.BlockSpec(memory_space=pltpu.SMEM)] + any_specs(len(sources)),
         out_specs=[pl.BlockSpec(memory_space=pltpu.VMEM)] * 3,
         out_shape=[
             shape(2, cut.heads, cut.units, D), shape(cut.heads, cut.units, D),
@@ -698,7 +716,7 @@
         compiler_params=pltpu.CompilerParams(vmem_limit_bytes=VMEM_LIMIT),
         cost_estimate=lasting(8),
         name="assemble",
-    )(place.spot(), share, *parts)
+    )(place.spot(), *sources)
     out = place.by_core(out, place.swap(out), 1).reshape(-1, D)
     return gate_up[0].reshape(-1, D), gate_up[1].reshape(-1, D), down.reshape(-1, D), out
 
@@ -778,7 +796,7 @@
     return jnp.concatenate([parts[d] for d in range(place.data)], axis=1)
 
 
-def reduce_qkv(place, grad, core):
+def reduce_qkv(place, grad, core, second_layer):
     grad = grad.reshape(place.data, 2, -1, grad.shape[1])
     first, second = grad[:, 0], grad[:, 1]
     sent = [
@@ -796,9 +814,12 @@
     piece = piece.astype(BF16)
     if core == 0:
         other = yield place.across(piece, 0)
-        return piece.astype(F32) + other.astype(F32)
+        first = (piece.astype(F32) + other.astype(F32)).astype(BF16)
+        summed = place.pick(first, second_layer())
+        flipped = yield [place.flip(summed, bits) for bits in range(1, place.data)]
+        return place.by_data(summed, flipped).astype(F32).reshape(D, -1)
     own, other = yield place.to_core(piece, 1), place.across(piece, 1)
-    return own.astype(F32) + other.astype(F32)
+    return (own.astype(F32) + other.astype(F32)).astype(BF16)
 
 
 def norm(rows, gain):
@@ -819,16 +840,14 @@
 def layer_forward(place, rows, gathered, first_values, w_qkv, chain, gains, tables, later=()):
     cosine, sine, half_tables, low, high, meta, tile = tables
     if later:
-        gathered = chain.step(gathered)
+        gathered = chain.step(chain.step(gathered))
     later = [Chain(begin(gathered)) for begin in later]
     queries, keys, own_values, mixed = project(gathered, w_qkv, cosine, sine, first_values)
     queries = chain.step(queries)
     attended_heads, sums = attend(queries, keys, mixed, low, high, meta, tile)
-    if later:
-        attended_heads = chain.step(attended_heads)
+    for other in (chain, *later[1:]) if later else ():
+        attended_heads = other.step(attended_heads)
     attended = place.heads_to_slots(attended_heads)
-    for other in later:
-        attended = other.step(attended)
     gate_w, up_w, down_w, out_w = spread = chain.result
     middle = rows + dot_nn(attended, out_w)
     ffn_normed = place.gather_cores(norm(middle, gains[1]).astype(BF16))
@@ -836,8 +855,6 @@
     up = dot_nt(ffn_normed, up_w)
     activation = (jax.nn.silu(gate) * up).astype(BF16)
     result = middle + place.scatter_cores(dot_nn(activation, down_w))
-    for other in later:
-        result = other.step(result)
     kept = (
         rows, gathered, queries, keys, mixed, attended_heads, sums, attended, middle, ffn_normed,
         gate, up, activation,
@@ -850,7 +867,7 @@
     return place.by_core(own, place.swap(own), 1).reshape(-1, x.shape[1])
 
 
-def layer_backward(place, cut, grad, share, carry, w_qkv, spread, gains, kept, tables, earlier=((), (), ())):
+def layer_backward(place, cut, grad, share, carry, w_qkv, spread, gains, kept, tables, layer, earlier, second_layer=None):
     cosine, sine, half_tables, low, high, meta, tile = tables
     gate_w, up_w, down_w, out_w = spread
     (
@@ -862,6 +879,8 @@
     sigma = jax.nn.sigmoid(gate)
     gate_grad = (act_grad * up * sigma * (1.0 + gate * (1.0 - sigma))).astype(BF16)
     up_grad = (act_grad * gate * sigma).astype(BF16)
+    for other in earlier[0]:
+        up_grad = other.step(up_grad)
     normed_grad = place.scatter_cores(dot_nn(gate_grad, gate_w) + dot_nn(up_grad, up_w))
     middle_back, grad_ffn_gain = norm_back(middle, gains[1], normed_grad)
     middle_grad = grad + middle_back
@@ -877,27 +896,25 @@
         out_grad.astype(BF16),
     )
     heads_grad = after(heads_grad, *split[0], *split[1])
-    for other in earlier[0]:
+    for other in earlier[1]:
         heads_grad = other.step(heads_grad)
     far = Chain(reduce_far(place, cut, split[0]))
+    near = Chain(reduce_near(place, cut, split[1], far))
     delta = heads_grad.astype(F32) * attended_heads.astype(F32)
     delta = jnp.sum(delta.reshape(SLOTS, -1, HD), axis=2).T
     query_grad, key_grad, value_grad = attend_back(
         queries, keys, mixed, heads_grad, sums, delta, low, high, meta, cosine, sine, half_tables,
         share, carry, tile,
     )
+    for other in (far, near, *earlier[2]):
+        query_grad = other.step(query_grad)
     lin_grad = jnp.concatenate([query_grad, key_grad, value_grad], axis=1)
-    partial = far.step(dot_nt(lin_grad, w_qkv))
-    for other in earlier[1]:
-        partial = other.step(partial)
-    near = Chain(reduce_near(place, cut, after(split[1], partial), far))
-    lin_grad = after(lin_grad, partial)
-    qkv_grad = dot_tn(gathered, lin_grad).astype(BF16)
-    input_back = place.scatter_row(partial, far.step)
-    input_back = near.step(input_back)
-    for other in earlier[2]:
+    partial = dot_nt(lin_grad, w_qkv)
+    qkv_grad = dot_tn(gathered, after(lin_grad, partial)).astype(BF16)
+    qkv_grad = Chain(reduce_qkv(place, qkv_grad, layer, second_layer))
+    input_back = place.scatter_row(partial, lambda x: qkv_grad.step(far.step(x)))
+    for other in (near, qkv_grad, far) if layer == 0 else (near, qkv_grad):
         input_back = other.step(input_back)
-    qkv_grad = after(qkv_grad, input_back)
     rows_back, grad_attn_gain = norm_back(rows, gains[0], input_back)
     return middle_grad + rows_back, value_grad, (far, near), qkv_grad, (grad_attn_gain, grad_ffn_gain)
 
@@ -920,14 +937,10 @@
     mine, sent = mine_and_sent(hidden_in)
     half_block = lambda x: lax.dynamic_slice_in_dim(x, place.core * count, count, 0)
     far = place.around(half_block(sent), place.half)
-
     w_qkv = jnp.concatenate([w_query[0], w_key[0], w_value[0]], axis=1)
     part = lax.dynamic_slice_in_dim(w_qkv, place.dp * cut.columns, cut.columns, 0)
-    share_1, share_2 = pack_weights(place, cut, w_gate[0], w_up[0], w_down[0], w_out[0])
-    piece_1, piece_2 = (
-        lax.dynamic_slice_in_dim(share, place.dp * cut.columns, cut.columns, 1)
-        for share in (share_1, share_2)
-    )
+    part_1 = place.across_from_zero(part)
+    own_packed, sent_packed = pack_weights(place, w_gate[0], w_up[0], w_down[0], w_out[0])
     own_gains = jnp.concatenate([attn_gain, ffn_gain])
     other_gains = place.swap(own_gains)
     gains_1 = place.pick(own_gains, other_gains)
@@ -945,15 +958,19 @@
 
     near = norm(half_block(mine).astype(F32), gains_1[0]).astype(BF16)
     near_shifted = [place.beside(near, shift) for shift in range(1, place.half)]
+    far, part_1, own_packed, sent_packed = lax.optimization_barrier(
+        (far, part_1, own_packed, sent_packed)
+    )
+    share_1, share_2, piece_1 = share_weights(place, cut, own_packed, sent_packed)
+    piece_2 = cut.part(share_2, place)
+    chain_far = Chain(gather_far(place, far, gains_1[0]))
     chain_1 = Chain(spread_in_turn(place, cut, share_1, piece_1))
-    chain_far = Chain(gather_far(place, far, gains_1[0]))
-    chain_qkv = Chain(first_qkv(place, w_qkv, part))
-    for _ in range(2):
-        started = (chain_far, chain_qkv, chain_1)
-        arrived = lax.optimization_barrier([chain.flight for chain in started])
-        for chain, item in zip(started, arrived):
-            chain.advance(item)
-    (far, far_shifted), w_qkv_1 = chain_far.result, chain_qkv.result
+    chain_qkv = Chain(first_qkv(place, w_qkv, part_1))
+    started = (chain_far, chain_qkv, chain_1)
+    arrived = lax.optimization_barrier([chain.flight for chain in started])
+    for chain, item in zip(started, arrived):
+        chain.advance(item)
+    far_shifted, w_qkv_1 = chain_far.result, chain_qkv.result
     blocks = [
         join_halves(place, near, near_shifted),
         join_halves(place, norm(far.astype(F32), gains_1[0]).astype(BF16), far_shifted),
@@ -964,34 +981,37 @@
     result_1, values_1, spread_1, kept_1, (chain_2, chain_qkv) = layer_forward(
         place, rows, gathered, None, w_qkv_1, chain_1, gains_1, tables,
         (
-            lambda x: spread_at_once(place, cut, share_2, after(piece_2, x)),
-            lambda x: second_qkv(place, w_qkv, after(part, x)),
+            lambda x: spread_at_once(place, cut, after(piece_2, x)),
+            lambda x: second_qkv(place, after(w_qkv, x)),
         ),
     )
     hidden_1 = result_1.astype(BF16)
-    w_qkv_2 = chain_qkv.result
     rows = hidden_1.astype(F32)
     gathered = place.gather_row(norm(rows, gains_2[0]).astype(BF16))
+    w_qkv_2 = chain_qkv.result
     result_2, _, spread_2, kept_2, _ = layer_forward(
         place, rows, gathered, values_1, w_qkv_2, chain_2, gains_2, tables
     )
     hidden_2 = result_2.astype(BF16)
-
-    mine, sent = mine_and_sent(cotangent)
-    grad = place.pick(mine, place.across(sent.astype(BF16), 1).astype(F32))
-    grad_2, carry, ffn_2, qkv_2, gain_2 = layer_backward(
-        place, cut, grad, 0.5, None, w_qkv_2, spread_2, gains_2, kept_2, tables
-    )
-    grad_2 = grad_2.astype(BF16)
-    far_2, near_2 = ffn_2
-    qkv_2 = Chain(reduce_qkv(place, qkv_2, 1))
 
     def bring(first, second):
         near = place.to_core(second.astype(BF16), 1)
         near, *far = yield near, place.across(first.astype(BF16), 0), place.across(second.astype(BF16), 1)
         return near, place.pick(*far)
 
-    def bring_one(block, core):
+    outputs = Chain(bring(hidden_1, hidden_2))
+    mine, sent = mine_and_sent(cotangent)
+    grad = place.pick(mine, place.across(sent.astype(BF16), 1).astype(F32))
+    grad_2, carry, ffn_2, qkv_2, gain_2 = layer_backward(
+        place, cut, grad, 0.5, None, w_qkv_2, spread_2, gains_2, kept_2, tables, 1,
+        ((), (), (outputs,)),
+    )
+    grad_2 = grad_2.astype(BF16)
+    far_2, near_2 = ffn_2
+
+    def bring_one(block, core, wait=0):
+        for _ in range(wait):
+            block = yield block
         moved = (place.across(block.astype(BF16), core),)
         moved = yield moved if core == 0 else (*moved, place.to_core(block.astype(BF16), 1))
         return moved
@@ -999,11 +1019,10 @@
     def both_rows(near, far):
         return jnp.where(place.row == 0, jnp.stack([near, far]), jnp.stack([far, near]))[None]
 
-    outputs = Chain(bring(hidden_1, hidden_2))
     grads_2 = Chain(bring_one(grad_2, 1))
     grad_1, _, (far_1, near_1), qkv_1, gain_1 = layer_backward(
-        place, cut, grad_2.astype(F32), 1.0, carry, w_qkv_1, spread_1, gains_1, kept_1, tables,
-        ((far_2, near_2, qkv_2), (near_2, qkv_2, outputs), (near_2, qkv_2, grads_2)),
+        place, cut, grad_2.astype(F32), 1.0, carry, w_qkv_1, spread_1, gains_1, kept_1, tables, 0,
+        ((far_2, near_2, qkv_2), (near_2, grads_2), ()), lambda: qkv_2.result,
     )
 
     def sum_gains(gains):
@@ -1011,12 +1030,11 @@
         gains = gains + sum((yield [place.flip(gains, bits) for bits in range(1, place.data)]))
         return gains + sum((yield [place.around(gains, k) for k in range(1, place.size)]))
 
-    grads_1 = Chain(bring_one(grad_1, 0))
-    qkv_1 = Chain(reduce_qkv(place, qkv_1, 0))
+    grads_1 = Chain(bring_one(grad_1, 0, 1))
     gains = Chain(sum_gains(jnp.stack([*gain_1, *gain_2])))
-    _, ffn_1, qkv_1, gains, grads_1 = lockstep(far_1, near_1, qkv_1, gains, grads_1)
-
-    ffn_2, qkv_2, grads_2 = near_2.result, qkv_2.result, grads_2.result
+    ffn_1, qkv_1, gains, grads_1 = lockstep(near_1, qkv_1, gains, grads_1)
+
+    ffn_2, grads_2 = near_2.result, grads_2.result
     near, far = outputs.result
     layer_outputs = both_rows(place.pick(hidden_1, near), far)
     near = place.pick(grad_1, grads_2[1].astype(F32))
@@ -1024,11 +1042,6 @@
 
     own = place.pick(ffn_1, ffn_2)
     other = place.swap(place.pick(ffn_2, ffn_1))
-    qkv = place.pick(qkv_1, qkv_2).astype(BF16)
-    flipped = [place.flip(qkv, bits) for bits in range(1, place.data)]
-    other, flipped = lax.optimization_barrier((other, flipped))
-    qkv = place.by_data(qkv, flipped).astype(F32).reshape(D, 3 * width)
-
     ffn = place.by_core(own, other, 0).astype(F32)
     units, outs = cut.units, cut.outs
     grad_gate = ffn[:, :units].reshape(-1, D).T
@@ -1037,7 +1050,7 @@
     grad_up = ffn[:, 2 * units + outs :].reshape(-1, D).T
     gains = place.pick(gains[:2], gains[2:])
     return (
-        layer_outputs, input_grads, *(qkv[None, :, i * width : (i + 1) * width] for i in range(3)), grad_out[None],
+        layer_outputs, input_grads, *(qkv_1[None, :, i * width : (i + 1) * width] for i in range(3)), grad_out[None],
         grad_gate[None], grad_up[None], grad_down[None], gains[:1], gains[1:],
     )
 

time: 1040 us -> 962 us (0.925)
  waiting for transfers between devices: 398 us -> 312 us
  between operations: 4.13 us -> 17.5 us
  Pallas kernels: 148 us -> 160 us
    ppermute x54 -> x47, waiting for transfers between devices: 195 us -> 117 us  [flip(): return lax.ppermute(x, 'dp', [(d, d ^ bits) for d in range(self.data)])]
    ppermute x16 -> x13, waiting for transfers between devices: 85.3 us -> 55 us  [around(): lax.ppermute(x, 'head', [(h, (h + shift) % self.size) for h in range(self...]
    ppermute x9, waiting for transfers between devices: 105 us -> 125 us  [beside(): return lax.ppermute(x, 'head', pairs)]
    ppermute x54 -> x47, starting transfers between devices: 83.2 us -> 64 us  [flip(): return lax.ppermute(x, 'dp', [(d, d ^ bits) for d in range(self.data)])]
    ppermute x4 -> x5, starting transfers between devices: 6.68 us -> 20.7 us  [to_core(): return lax.ppermute(x, 'section', [(1 - core, core)])]
    ppermute x26, starting transfers between devices: 23.8 us -> 12.2 us  [swap(): return lax.ppermute(x, 'section', [(0, 1), (1, 0)])]
    unnamed x292 -> x270, local copies, waits for them, and re-layouts: 29.5 us -> 24.9 us
    ppermute x16 -> x13, starting transfers between devices: 23.1 us -> 22.2 us  [around(): lax.ppermute(x, 'head', [(h, (h + shift) % self.size) for h in range(self...]
  transfers between devices with their start and end apart: 118 -> 110, of which waited for: 48 -> 37; matrix products, arithmetic and copies ran while one was open for 23% -> 24% of each run, Pallas kernels for 14% -> 17%
where the time goes in v3:
time: 962 us; the launch traced here: 952 us
  waiting for transfers between devices  312 us (32%)
  Pallas kernels  160 us (17%)
  starting transfers between devices  148 us (15%)
  matrix products  115 us (12%)
  other arithmetic  110 us (11%)
  local copies, waits for them, and re-layouts  88.4 us (9%)
  between operations  17.5 us (2%)
    ppermute x9, waiting for transfers between devices, beside(): return lax.ppermute(x, 'head', pairs)  125 us
    ppermute x47, waiting for transfers between devices, flip(): return lax.ppermute(x, 'dp', [(d, d ^ bits) for d in range(self.data)])  117 us
    pallas_call x2, Pallas kernels, attend_back(): pl.pallas_call(kernel, grid_spec=pltpu.PrefetchScalarGridSpec(num_scalar_...  64.6 us
    ppermute x47, starting transfers between devices, flip(): return lax.ppermute(x, 'dp', [(d, d ^ bits) for d in range(self.data)])  64 us
    ppermute x13, waiting for transfers between devices, around(): lax.ppermute(x, 'head', [(h, (h + shift) % self.size) for h in range(self...  55 us
    dot_general x10, matrix products, dot_nt(): lax.dot_general(a, b, (((1,), (1,)), ((), ())), preferred_element_type=F32)  49.2 us
    pallas_call x2, Pallas kernels, attend(): pl.pallas_call(functools.partial(attend_kernel, tile, heads), grid_spec=p...  41.6 us
    dot_general x10, matrix products, dot_tn(): lax.dot_general(a, b, (((0,), (0,)), ((), ())), preferred_element_type=F32)  37.3 us
  transfers between devices with their start and end apart: 110, of which 37 were waited for; matrix products, arithmetic and copies ran while one was open for 24% of the time, Pallas kernels for 17%

profile of v3, /device:TPU:0, one launch (start us, length us, event | category | flops | bytes accessed | tf_op | source)
XLA Modules:
  0.0 952.3 jit_solution(1462951591232380072)
XLA Ops:
  13.0 6.4 collective-permute-start.1
  34.0 19.4 %collective-permute-done = bf16[256,1024]{1,0:T(8,128)(2,1)S(1)} collective-permute-done((bf16[256,1024]{1,0:T(8,128)(2,1)}, bf16[256,1024]{1,0:T(8,128)(2,1)S(1)}, u32[]{:S(2)}, u32[]{:S(2)}) %collective-permute-start) | collective-permute-done | bytes 524320 | tf_op jit(solution)/shard_map/ppermute | solution.py:405
  67.2 6.1 collective-permute-done.8
  82.2 8.0 collective-permute-done.11
  105.2 3.7 maximum_select_fusion.1.x
  110.4 6.1 collective-permute-done.13
  123.5 8.0 collective-permute-done.18.refs_6_
  144.3 9.9 %project.2 = (bf16[2048,256]{1,0:T(8,128)(2,1)}, bf16[2048,256]{1,0:T(8,128)(2,1)}, bf16[2048,256]{1,0:T(8,128)(2,1)}) custom-call(bf16[2048,1024]{1,0:T(8,128)(2,1)} %maximum_select_fusion.1.x, bf16[1024,768]{1,0:T(8,128)(2,1)} %bitcast_select_fusion.1.w, f32[2048,128]{1,0:T(8,128)} %copy.56.c.cos_ref.refs_10_, f32[2048,128]{1,0:T(8,128)} %copy.57.s.sin_ref.refs_11_), custom_call_target="tpu_custom_call" | custom-call | flops 10000000000 | bytes 1 | tf_op jit(solution)/shard_map/project/pallas_call | solution.py:116
  164.6 20.6 %attend.2 = (bf16[2048,256]{1,0:T(8,128)(2,1)}, f32[4,2048]{1,0:T(4,128)}) custom-call(s32[4,4]{1,0:T(4,128)} %pad_add_fusion.meta.refs_0_, bf16[2048,256]{1,0:T(8,128)(2,1)} %get-tuple-element.183.q_ref, bf16[2048,256]{1,0:T(8,128)(2,1)} %get-tuple-element.184.k_ref, bf16[256,2048]{1,0:T(8,128)(2,1)} %bitcast.724, s32[1,2048]{1,0:T(1,128)} %bitcast.760, ...), custom_call_target="tpu_custom_call" | custom-call | flops 24999999488 | bytes 1 | tf_op jit(solution)/shard_map/attend/pallas_call | solution.py:202
  185.3 8.9 collective-permute-done.22.refs_11_
  194.1 6.4 collective-permute-done.21.refs_10_
  201.9 4.5 collective-permute-start.25
  208.2 9.0 assemble.2
  220.1 7.8 collective-permute-done.26
  240.5 5.8 multiply_convert_fusion.5
  256.3 51.7 %collective-permute-done.31 = bf16[512,1024]{1,0:T(8,128)(2,1)S(1)} collective-permute-done((bf16[512,1024]{1,0:T(8,128)(2,1)S(1)}, bf16[512,1024]{1,0:T(8,128)(2,1)S(1)}, u32[]{:S(2)}, u32[]{:S(2)}) %collective-permute-start.31) | collective-permute-done | bytes 1048608 | tf_op jit(solution)/shard_map/ppermute | solution.py:402
  313.4 3.8 maximum_select_fusion.2.x_ref
  317.2 10.1 %project.3 = (bf16[2048,256]{1,0:T(8,128)(2,1)}, bf16[2048,256]{1,0:T(8,128)(2,1)}, bf16[2048,256]{1,0:T(8,128)(2,1)}, bf16[2048,256]{1,0:T(8,128)(2,1)}) custom-call(bf16[2048,1024]{1,0:T(8,128)(2,1)} %maximum_select_fusion.2.x_ref, bf16[1024,768]{1,0:T(8,128)(2,1)} %broadcast_select_fusion.1.w_ref, f32[2048,128]{1,0:T(8,128)} %copy.56.c.cos_ref.refs_10_, ...), custom_call_target="tpu_custom_call" | custom-call | flops 10000000000 | bytes 1 | tf_op jit(solution)/shard_map/project/pallas_call | solution.py:116
  329.5 20.9 %attend.3 = (bf16[2048,256]{1,0:T(8,128)(2,1)}, f32[4,2048]{1,0:T(4,128)}) custom-call(s32[4,4]{1,0:T(4,128)} %pad_add_fusion.meta.refs_0_, bf16[2048,256]{1,0:T(8,128)(2,1)} %get-tuple-element.204.q_ref.refs_1_, bf16[2048,256]{1,0:T(8,128)(2,1)} %get-tuple-element.205.k_ref.refs_2_, bf16[256,2048]{1,0:T(8,128)(2,1)} %bitcast.725, s32[1,2048]{1,0:T(1,128)} %bitcast.761, ...), custom_call_target="tpu_custom_call" | custom-call | flops 24999999488 | bytes 1 | tf_op jit(solution)/shard_map/attend/pallas_call | solution.py:202
  358.7 9.0 assemble.3
  379.6 5.3 fusion.148
  385.6 5.3 fusion.149
  390.9 10.5 %multiply_convert_fusion.2 = (bf16[1024,1408]{1,0:T(8,128)(2,1)}, bf16[1024,1408]{1,0:T(8,128)(2,1)}, bf16[1024,1408]{1,0:T(8,128)(2,1)}) fusion(f32[1024,1408]{1,0:T(8,128)} %fusion.149, f32[1024,1408]{1,0:T(8,128)} %fusion.148, bf16[1024,1024]{1,0:T(8,128)(2,1)S(1)} %bitcast.686, bf16[1408,1024]{1,0:T(8,128)(2,1)S(1)} %bitcast.665), kind=kOutput, calls=%fused_computation.2 | convolution fusion | flops 2975858688 | bytes 25165824 | tf_op jit(solution)/shard_map/dot_general | solution.py:34
  401.4 6.2 fusion.151
  427.0 4.9 convolution_convert_fusion.3
  431.9 4.5 convolution_convert_fusion.4
  438.7 4.5 convolution_convert_fusion.5
  443.2 7.9 collective-permute-done.40
  453.6 8.2 split.2
  463.0 4.0 collective-permute-start.44
  473.4 7.4 collective-permute-start.48
  496.4 32.1 %attend_back.2 = (bf16[2048,256]{1,0:T(8,128)(2,1)}, bf16[2048,256]{1,0:T(8,128)(2,1)}, bf16[2048,256]{1,0:T(8,128)(2,1)}) custom-call(s32[4,4]{1,0:T(4,128)} %pad_add_fusion.meta.refs_0_, bf16[2048,256]{1,0:T(8,128)(2,1)} %get-tuple-element.204.q_ref.refs_1_, bf16[2048,256]{1,0:T(8,128)(2,1)} %get-tuple-element.205.k_ref.refs_2_, ...), custom_call_target="tpu_custom_call" | custom-call | flops 35999997952 | bytes 1 | tf_op jit(solution)/shard_map/attend_back/pallas_call | solution.py:336
  531.5 3.5 fusion.152
  535.0 3.6 convolution_convert_fusion.7
  540.6 4.2 collective-permute-start.54
  556.3 11.8 %collective-permute-done.53 = bf16[2,592,256]{2,1,0:T(8,128)(2,1)} collective-permute-done((bf16[2,592,256]{2,1,0:T(8,128)(2,1)}, bf16[2,592,256]{2,1,0:T(8,128)(2,1)}, u32[]{:S(2)}, u32[]{:S(2)}) %collective-permute-start.53) | collective-permute-done | bytes 606240 | tf_op jit(solution)/shard_map/ppermute | solution.py:408
  572.8 5.2 collective-permute-start.62
  582.3 21.8 %collective-permute-done.56 = bf16[512,1024]{1,0:T(8,128)(2,1)S(1)} collective-permute-done((bf16[512,1024]{1,0:T(8,128)(2,1)S(1)}, bf16[512,1024]{1,0:T(8,128)(2,1)S(1)}, u32[]{:S(2)}, u32[]{:S(2)}) %collective-permute-start.56) | collective-permute-done | bytes 1048608 | tf_op jit(solution)/shard_map/ppermute | solution.py:402
  606.2 3.6 collective-permute-done.59
  615.3 5.7 collective-permute-start.64
  622.9 9.1 multiply_convert_fusion
  631.9 6.5 collective-permute-done.64
  638.4 5.6 fusion.153
  652.0 8.3 collective-permute-start.75
  670.7 4.5 convolution_convert_fusion
  677.8 4.5 convolution_convert_fusion.1
  682.3 9.5 %collective-permute-done.68 = bf16[2,512,256]{2,1,0:T(8,128)(2,1)S(1)} collective-permute-done((bf16[2,512,256]{2,1,0:T(8,128)(2,1)S(1)}, bf16[2,512,256]{2,1,0:T(8,128)(2,1)S(1)}, u32[]{:S(2)}, u32[]{:S(2)}) %collective-permute-start.68) | collective-permute-done | bytes 524320 | tf_op jit(solution)/shard_map/ppermute | solution.py:402
  692.1 4.6 convolution_convert_fusion.2
  701.3 8.2 split.3
  710.1 15.8 %collective-permute-done.72 = bf16[1184,256]{1,0:T(8,128)(2,1)S(1)} collective-permute-done((bf16[1184,256]{1,0:T(8,128)(2,1)}, bf16[1184,256]{1,0:T(8,128)(2,1)S(1)}, u32[]{:S(2)}, u32[]{:S(2)}) %collective-permute-start.72) | collective-permute-done | bytes 606240 | tf_op jit(solution)/shard_map/ppermute | solution.py:408
  736.3 32.6 %attend_back.3 = (bf16[2048,256]{1,0:T(8,128)(2,1)}, bf16[2048,256]{1,0:T(8,128)(2,1)}, bf16[2048,256]{1,0:T(8,128)(2,1)}) custom-call(s32[4,4]{1,0:T(4,128)} %pad_add_fusion.meta.refs_0_, bf16[2048,256]{1,0:T(8,128)(2,1)} %get-tuple-element.183.q_ref, bf16[2048,256]{1,0:T(8,128)(2,1)} %get-tuple-element.184.k_ref, bf16[256,2048]{1,0:T(8,128)(2,1)} %bitcast.721, ...), custom_call_target="tpu_custom_call" | custom-call | flops 35999997952 | bytes 1 | tf_op jit(solution)/shard_map/attend_back/pallas_call | solution.py:336
  773.9 5.2 collective-permute-start.81
  789.0 3.6 convolution_convert_fusion.6
  806.4 3.7 collective-permute-start.90
  810.6 5.9 collective-permute-done.87
  818.2 23.3 %collective-permute-done.85 = bf16[512,1024]{1,0:T(8,128)(2,1)S(1)} collective-permute-done((bf16[512,1024]{1,0:T(8,128)(2,1)S(1)}, bf16[512,1024]{1,0:T(8,128)(2,1)S(1)}, u32[]{:S(2)}, u32[]{:S(2)}) %collective-permute-start.85) | collective-permute-done | bytes 1048608 | tf_op jit(solution)/shard_map/ppermute | solution.py:402
  847.6 7.4 collective-permute-done.91
  861.5 11.9 %collective-permute-done.93 = bf16[256,768]{1,0:T(8,128)(2,1)S(1)} collective-permute-done((bf16[256,768]{1,0:T(8,128)(2,1)S(1)}, bf16[256,768]{1,0:T(8,128)(2,1)S(1)}, u32[]{:S(2)}, u32[]{:S(2)}) %collective-permute-start.93) | collective-permute-done | bytes 393248 | tf_op jit(solution)/shard_map/ppermute | solution.py:392
  873.5 4.6 collective-permute-done.92
  887.7 7.4 collective-permute-done.100
  896.4 5.7 collective-permute-done.98
  904.4 12.0 %collective-permute-done.99 = bf16[256,768]{1,0:T(8,128)(2,1)S(1)} collective-permute-done((bf16[256,768]{1,0:T(8,128)(2,1)S(1)}, bf16[256,768]{1,0:T(8,128)(2,1)S(1)}, u32[]{:S(2)}, u32[]{:S(2)}) %collective-permute-start.99) | collective-permute-done | bytes 393248 | tf_op jit(solution)/shard_map/ppermute | solution.py:408
  916.4 11.4 %collective-permute-done.97 = bf16[1184,256]{1,0:T(8,128)(2,1)S(1)} collective-permute-done((bf16[1184,256]{1,0:T(8,128)(2,1)S(1)}, bf16[1184,256]{1,0:T(8,128)(2,1)S(1)}, u32[]{:S(2)}, u32[]{:S(2)}) %collective-permute-start.97) | collective-permute-done | bytes 606240 | tf_op jit(solution)/shard_map/ppermute | solution.py:408
  940.2 3.7 fusion.134
  (727 shorter events, 333.3 us)
Async XLA Ops:
  7.2 322.3 %all-gather.3.cloned.1.call-start = ((), (), s32[]{:S(2)}) async-start(), calls=%async_computation | async-start | bytes 10305536 | tf_op jit(solution)/shard_map/all_gather | solution.py:663
  8.0 18.6 %collective-permute-start.3 = (f32[2,1024]{1,0:T(2,128)S(1)}, f32[2,1024]{1,0:T(2,128)S(1)}, u32[]{:S(2)}, u32[]{:S(2)}) collective-permute-start(f32[2,1024]{1,0:T(2,128)S(1)} %pad_maximum_fusion.27), channel_id=1, source_target_pairs={{0,16},{16,0},{1,17},{17,1},{2,18},{18,2},{3,19},{19,3},{4,20},{20... | collective-permute-start | bytes 24584 | tf_op jit(solution)/shard_map/ppermute | solution.py:384
  13.0 21.0 %collective-permute-start.1 = (bf16[256,768]{1,0:T(8,128)(2,1)}, bf16[256,768]{1,0:T(8,128)(2,1)}, u32[]{:S(2)}, u32[]{:S(2)}) collective-permute-start(bf16[256,768]{1,0:T(8,128)(2,1)} %constant_dynamic-slice_fusion.4), channel_id=1, source_target_pairs={{0,18},{1,19},{2,16},{3,17},{4,22},{5,23},{6,20},{7,21},{8,26},{9,... | collective-permute-start | bytes 1179656 | tf_op jit(solution)/shard_map/ppermute | solution.py:397
  30.7 22.7 %collective-permute-start = (bf16[256,1024]{1,0:T(8,128)(2,1)}, bf16[256,1024]{1,0:T(8,128)(2,1)S(1)}, u32[]{:S(2)}, u32[]{:S(2)}) collective-permute-start(bf16[256,1024]{1,0:T(8,128)(2,1)} %get-tuple-element.382), channel_id=1, source_target_pairs={{0,2},{1,3},{2,0},{3,1},{4,6},{5,7},{6,4},{7,5},{8,10},{9,11},{10,... | collective-permute-start | bytes 1572872 | tf_op jit(solution)/shard_map/ppermute | solution.py:405
  32.0 31.6 %collective-permute-start.4 = (bf16[256,1024]{1,0:T(8,128)(2,1)S(1)}, bf16[256,1024]{1,0:T(8,128)(2,1)S(1)}, u32[]{:S(2)}, u32[]{:S(2)}) collective-permute-start(bf16[256,1024]{1,0:T(8,128)(2,1)S(1)} %fusion.51), channel_id=1, source_target_pairs={{0,1},{1,0},{2,3},{3,2},{4,5},{5,4},{6,7},{7,6},{8,9},{9,8},{10,11... | collective-permute-start | bytes 1572872 | tf_op jit(solution)/shard_map/ppermute | solution.py:402
  54.9 18.4 %collective-permute-start.8 = (bf16[256,768]{1,0:T(8,128)(2,1)}, bf16[256,768]{1,0:T(8,128)(2,1)}, u32[]{:S(2)}, u32[]{:S(2)}) collective-permute-start(bf16[256,768]{1,0:T(8,128)(2,1)} %collective-permute-done.1), channel_id=1, source_target_pairs={{0,8},{4,12},{8,0},{12,4},{1,9},{5,13},{9,1},{13,5},{2,10},{6,14},... | collective-permute-start | bytes 1179656 | tf_op jit(solution)/shard_map/ppermute | solution.py:408
  56.4 25.8 %collective-permute-start.9 = (bf16[256,768]{1,0:T(8,128)(2,1)}, bf16[256,768]{1,0:T(8,128)(2,1)}, u32[]{:S(2)}, u32[]{:S(2)}) collective-permute-start(bf16[256,768]{1,0:T(8,128)(2,1)} %collective-permute-done.1), channel_id=1, source_target_pairs={{0,12},{4,8},{8,4},{12,0},{1,13},{5,9},{9,5},{13,1},{2,14},{6,10},... | collective-permute-start | bytes 1179656 | tf_op jit(solution)/shard_map/ppermute | solution.py:408
  61.8 20.4 %collective-permute-start.6 = (bf16[256,1024]{1,0:T(8,128)(2,1)}, bf16[256,1024]{1,0:T(8,128)(2,1)}, u32[]{:S(2)}, u32[]{:S(2)}) collective-permute-start(bf16[256,1024]{1,0:T(8,128)(2,1)} %get-tuple-element.346), channel_id=1, source_target_pairs={{0,1},{1,0},{2,3},{3,2},{4,5},{5,4},{6,7},{7,6},{8,9},{9,8},{10,11... | collective-permute-start | bytes 1572872 | tf_op jit(solution)/shard_map/ppermute | solution.py:402
  63.6 26.6 %collective-permute-start.11 = (bf16[1184,256]{1,0:T(8,128)(2,1)}, bf16[1184,256]{1,0:T(8,128)(2,1)}, u32[]{:S(2)}, u32[]{:S(2)}) collective-permute-start(bf16[1184,256]{1,0:T(8,128)(2,1)} %broadcast_select_fusion.2), channel_id=1, source_target_pairs={{0,1},{1,2},{2,3},{3,0},{4,5},{5,6},{6,7},{7,4},{8,9},{9,10},{10,1... | collective-permute-start | bytes 1818632 | tf_op jit(solution)/shard_map/ppermute | solution.py:405
  65.7 30.4 %collective-permute-start.5 = (bf16[2,256,1024]{2,1,0:T(8,128)(2,1)}, bf16[2,256,1024]{2,1,0:T(8,128)(2,1)}, u32[]{:S(2)}, u32[]{:S(2)}) collective-permute-start(bf16[2,256,1024]{2,1,0:T(8,128)(2,1)} %bitcast_dynamic-update-slice_fusion.16), channel_id=1, source_target_pairs={{0,16},{16,0},{1,17},{17,1},{2,18},{18,2},{3,19},{19,3},{4,20},{20... | collective-permute-start | bytes 3145736 | tf_op jit(solution)/shard_map/ppermute | solution.py:384
  73.3 20.1 %collective-permute-start.2 = (bf16[256,1024]{1,0:T(8,128)(2,1)S(1)}, bf16[256,1024]{1,0:T(8,128)(2,1)}, u32[]{:S(2)}, u32[]{:S(2)}) collective-permute-start(bf16[256,1024]{1,0:T(8,128)(2,1)S(1)} %collective-permute-done), channel_id=1, source_target_pairs={{0,16},{16,0},{1,17},{17,1},{2,18},{18,2},{3,19},{19,3},{4,20},{20... | collective-permute-start | bytes 1572872 | tf_op jit(solution)/shard_map/ppermute | solution.py:384
  95.7 45.9 %collective-permute-start.27 = (bf16[1184,1024]{1,0:T(8,128)(2,1)S(1)}, bf16[1184,1024]{1,0:T(8,128)(2,1)S(1)}, u32[]{:S(2)}, u32[]{:S(2)}) collective-permute-start(bf16[1184,1024]{1,0:T(8,128)(2,1)S(1)} %copy-done.18), channel_id=1, source_target_pairs={{0,16},{16,0},{1,17},{17,1},{2,18},{18,2},{3,19},{19,3},{4,20},{20... | collective-permute-start | bytes 7274504 | tf_op jit(solution)/shard_map/ppermute | solution.py:384
  135.9 64.7 %collective-permute-start.23 = (bf16[1024,768]{1,0:T(8,128)(2,1)}, bf16[1024,768]{1,0:T(8,128)(2,1)}, u32[]{:S(2)}, u32[]{:S(2)}) collective-permute-start(bf16[1024,768]{1,0:T(8,128)(2,1)} %pad_maximum_fusion.2), channel_id=1, source_target_pairs={{16,0},{17,1},{18,2},{19,3},{20,4},{21,5},{22,6},{23,7},{24,8},{25... | collective-permute-start | bytes 4718600 | tf_op jit(solution)/shard_map/ppermute | solution.py:387
  137.2 63.4 %collective-permute-start.24 = (bf16[1024,768]{1,0:T(8,128)(2,1)}, bf16[1024,768]{1,0:T(8,128)(2,1)}, u32[]{:S(2)}, u32[]{:S(2)}) collective-permute-start(bf16[1024,768]{1,0:T(8,128)(2,1)} %pad_maximum_fusion.2), channel_id=1, source_target_pairs={{16,18},{17,19},{18,16},{19,17},{20,22},{21,23},{22,20},{23,21},{2... | collective-permute-start | bytes 4718600 | tf_op jit(solution)/shard_map/ppermute | solution.py:392
  140.6 18.1 %collective-permute-start.19 = (bf16[2,592,256]{2,1,0:T(8,128)(2,1)}, bf16[2,592,256]{2,1,0:T(8,128)(2,1)}, u32[]{:S(2)}, u32[]{:S(2)}) collective-permute-start(bf16[2,592,256]{2,1,0:T(8,128)(2,1)} %get-tuple-element.398), channel_id=1, source_target_pairs={{0,4},{4,0},{8,12},{12,8},{1,5},{5,1},{9,13},{13,9},{2,6},{6,2},{1... | collective-permute-start | bytes 1818632 | tf_op jit(solution)/shard_map/ppermute | solution.py:408
  160.1 34.0 %collective-permute-start.22 = (bf16[2,2,592,256]{3,2,1,0:T(8,128)(2,1)S(1)}, bf16[2,2,592,256]{3,2,1,0:T(8,128)(2,1)S(1)}, u32[]{:S(2)}, u32[]{:S(2)}) collective-permute-start(bf16[2,2,592,256]{3,2,1,0:T(8,128)(2,1)S(1)} %pad_maximum_fusion.7), channel_id=1, source_target_pairs={{0,4},{4,0},{8,12},{12,8},{1,5},{5,1},{9,13},{13,9},{2,6},{6,2},{1... | collective-permute-start | bytes 3637256 | tf_op jit(solution)/shard_map/ppermute | solution.py:408
  163.0 37.6 %collective-permute-start.21 = (bf16[2,2,592,256]{3,2,1,0:T(8,128)(2,1)S(1)}, bf16[2,2,592,256]{3,2,1,0:T(8,128)(2,1)}, u32[]{:S(2)}, u32[]{:S(2)}) collective-permute-start(bf16[2,2,592,256]{3,2,1,0:T(8,128)(2,1)S(1)} %pad_maximum_fusion.6), channel_id=1, source_target_pairs={{0,8},{4,12},{8,0},{12,4},{1,9},{5,13},{9,1},{13,5},{2,10},{6,14},... | collective-permute-start | bytes 3637256 | tf_op jit(solution)/shard_map/ppermute | solution.py:408
  208.1 19.8 %collective-permute-start.26 = (bf16[2,512,256]{2,1,0:T(8,128)(2,1)S(1)}, bf16[2,512,256]{2,1,0:T(8,128)(2,1)S(1)}, u32[]{:S(2)}, u32[]{:S(2)}) collective-permute-start(bf16[2,512,256]{2,1,0:T(8,128)(2,1)S(1)} %fusion.93), channel_id=1, source_target_pairs={{0,1},{1,0},{2,3},{3,2},{4,5},{5,4},{6,7},{7,6},{8,9},{9,8},{10,11... | collective-permute-start | bytes 1572872 | tf_op jit(solution)/shard_map/ppermute | solution.py:402
  254.3 53.7 %collective-permute-start.31 = (bf16[512,1024]{1,0:T(8,128)(2,1)S(1)}, bf16[512,1024]{1,0:T(8,128)(2,1)S(1)}, u32[]{:S(2)}, u32[]{:S(2)}) collective-permute-start(bf16[512,1024]{1,0:T(8,128)(2,1)S(1)} %get-tuple-element.342), channel_id=1, source_target_pairs={{0,1},{1,0},{2,3},{3,2},{4,5},{5,4},{6,7},{7,6},{8,9},{9,8},{10,11... | collective-permute-start | bytes 3145736 | tf_op jit(solution)/shard_map/ppermute | solution.py:402
  309.9 43.7 %collective-permute-start.33 = (bf16[512,1024]{1,0:T(8,128)(2,1)S(1)}, bf16[512,1024]{1,0:T(8,128)(2,1)S(1)}, u32[]{:S(2)}, u32[]{:S(2)}) collective-permute-start(bf16[512,1024]{1,0:T(8,128)(2,1)S(1)} %fusion.58), channel_id=1, source_target_pairs={{16,18},{17,19},{18,16},{19,17},{20,22},{21,23},{22,20},{23,21},{2... | collective-permute-start | bytes 3145736 | tf_op jit(solution)/shard_map/ppermute | solution.py:392
  425.2 27.0 %collective-permute-start.42 = (bf16[512,1024]{1,0:T(8,128)(2,1)S(1)}, bf16[512,1024]{1,0:T(8,128)(2,1)S(1)}, u32[]{:S(2)}, u32[]{:S(2)}) collective-permute-start(bf16[512,1024]{1,0:T(8,128)(2,1)S(1)} %fusion.60), channel_id=1, source_target_pairs={{0,16},{16,0},{1,17},{17,1},{2,18},{18,2},{3,19},{19,3},{4,20},{20... | collective-permute-start | bytes 3145736 | tf_op jit(solution)/shard_map/ppermute | solution.py:384
  452.2 28.6 %collective-permute-start.41 = (bf16[1024,256]{1,0:T(8,128)(2,1)}, bf16[1024,256]{1,0:T(8,128)(2,1)}, u32[]{:S(2)}, u32[]{:S(2)}) collective-permute-start(bf16[1024,256]{1,0:T(8,128)(2,1)} %bitcast.144), channel_id=1, source_target_pairs={{0,16},{16,0},{1,17},{17,1},{2,18},{18,2},{3,19},{19,3},{4,20},{20... | collective-permute-start | bytes 1572872 | tf_op jit(solution)/shard_map/ppermute | solution.py:384
  461.8 30.7 %collective-permute-start.43 = (bf16[2,2,592,256]{3,2,1,0:T(8,128)(2,1)}, bf16[2,2,592,256]{3,2,1,0:T(8,128)(2,1)}, u32[]{:S(2)}, u32[]{:S(2)}) collective-permute-start(bf16[2,2,592,256]{3,2,1,0:T(8,128)(2,1)} %get-tuple-element.216), channel_id=1, source_target_pairs={{0,4},{4,0},{8,12},{12,8},{1,5},{5,1},{9,13},{13,9},{2,6},{6,2},{1... | collective-permute-start | bytes 3637256 | tf_op jit(solution)/shard_map/ppermute | solution.py:408
  463.0 31.4 %collective-permute-start.44 = (bf16[2,2,592,256]{3,2,1,0:T(8,128)(2,1)}, bf16[2,2,592,256]{3,2,1,0:T(8,128)(2,1)}, u32[]{:S(2)}, u32[]{:S(2)}) collective-permute-start(bf16[2,2,592,256]{3,2,1,0:T(8,128)(2,1)} %get-tuple-element.218), channel_id=1, source_target_pairs={{0,8},{4,12},{8,0},{12,4},{1,9},{5,13},{9,1},{13,5},{2,10},{6,14},... | collective-permute-start | bytes 3637256 | tf_op jit(solution)/shard_map/ppermute | solution.py:408
  469.8 58.7 %collective-permute-start.49 = (bf16[512,1024]{1,0:T(8,128)(2,1)S(1)}, bf16[512,1024]{1,0:T(8,128)(2,1)}, u32[]{:S(2)}, u32[]{:S(2)}) collective-permute-start(bf16[512,1024]{1,0:T(8,128)(2,1)S(1)} %get-tuple-element.344), channel_id=1, source_target_pairs={{16,2},{17,3},{18,0},{19,1},{20,6},{21,7},{22,4},{23,5},{24,10},{2... | collective-permute-start | bytes 3145736 | tf_op jit(solution)/shard_map/ppermute | solution.py:392
  473.4 55.1 %collective-permute-start.48 = (bf16[512,1024]{1,0:T(8,128)(2,1)}, bf16[512,1024]{1,0:T(8,128)(2,1)}, u32[]{:S(2)}, u32[]{:S(2)}) collective-permute-start(bf16[512,1024]{1,0:T(8,128)(2,1)} %get-tuple-element.380), channel_id=1, source_target_pairs={{0,16},{1,17},{2,18},{3,19},{4,20},{5,21},{6,22},{7,23},{8,24},{9,... | collective-permute-start | bytes 3145736 | tf_op jit(solution)/shard_map/ppermute | solution.py:387
  480.8 47.7 %collective-permute-start.50 = (bf16[512,1024]{1,0:T(8,128)(2,1)}, bf16[512,1024]{1,0:T(8,128)(2,1)}, u32[]{:S(2)}, u32[]{:S(2)}) collective-permute-start(bf16[512,1024]{1,0:T(8,128)(2,1)} %get-tuple-element.380), channel_id=1, source_target_pairs={{16,18},{17,19},{18,16},{19,17},{20,22},{21,23},{22,20},{23,21},{2... | collective-permute-start | bytes 3145736 | tf_op jit(solution)/shard_map/ppermute | solution.py:392
  492.5 36.0 %collective-permute-start.45 = (bf16[2,2,592,256]{3,2,1,0:T(8,128)(2,1)}, bf16[2,2,592,256]{3,2,1,0:T(8,128)(2,1)S(1)}, u32[]{:S(2)}, u32[]{:S(2)}) collective-permute-start(bf16[2,2,592,256]{3,2,1,0:T(8,128)(2,1)} %get-tuple-element.220), channel_id=1, source_target_pairs={{0,4},{4,0},{8,12},{12,8},{1,5},{5,1},{9,13},{13,9},{2,6},{6,2},{1... | collective-permute-start | bytes 3637256 | tf_op jit(solution)/shard_map/ppermute | solution.py:408
  494.4 34.1 %collective-permute-start.46 = (bf16[2,2,592,256]{3,2,1,0:T(8,128)(2,1)}, bf16[2,2,592,256]{3,2,1,0:T(8,128)(2,1)S(1)}, u32[]{:S(2)}, u32[]{:S(2)}) collective-permute-start(bf16[2,2,592,256]{3,2,1,0:T(8,128)(2,1)} %get-tuple-element.222), channel_id=1, source_target_pairs={{0,8},{4,12},{8,0},{12,4},{1,9},{5,13},{9,1},{13,5},{2,10},{6,14},... | collective-permute-start | bytes 3637256 | tf_op jit(solution)/shard_map/ppermute | solution.py:408
  539.7 28.5 %collective-permute-start.55 = (bf16[2,128,768]{2,1,0:T(8,128)(2,1)}, bf16[2,128,768]{2,1,0:T(8,128)(2,1)}, u32[]{:S(2)}, u32[]{:S(2)}) collective-permute-start(bf16[2,128,768]{2,1,0:T(8,128)(2,1)} %pad_maximum_fusion.17), channel_id=1, source_target_pairs={{0,8},{4,12},{8,0},{12,4},{1,9},{5,13},{9,1},{13,5},{2,10},{6,14},... | collective-permute-start | bytes 1179656 | tf_op jit(solution)/shard_map/ppermute | solution.py:408
  540.6 27.6 %collective-permute-start.54 = (bf16[2,128,768]{2,1,0:T(8,128)(2,1)}, bf16[2,128,768]{2,1,0:T(8,128)(2,1)}, u32[]{:S(2)}, u32[]{:S(2)}) collective-permute-start(bf16[2,128,768]{2,1,0:T(8,128)(2,1)} %pad_maximum_fusion.16), channel_id=1, source_target_pairs={{0,4},{4,0},{8,12},{12,8},{1,5},{5,1},{9,13},{13,9},{2,6},{6,2},{1... | collective-permute-start | bytes 1179656 | tf_op jit(solution)/shard_map/ppermute | solution.py:408
  547.3 20.8 %collective-permute-start.53 = (bf16[2,592,256]{2,1,0:T(8,128)(2,1)}, bf16[2,592,256]{2,1,0:T(8,128)(2,1)}, u32[]{:S(2)}, u32[]{:S(2)}) collective-permute-start(bf16[2,592,256]{2,1,0:T(8,128)(2,1)} %fusion.67), channel_id=1, source_target_pairs={{0,4},{4,0},{8,12},{12,8},{1,5},{5,1},{9,13},{13,9},{2,6},{6,2},{1... | collective-permute-start | bytes 1818632 | tf_op jit(solution)/shard_map/ppermute | solution.py:408
  553.1 52.8 %collective-permute-start.58 = (bf16[2,592,256]{2,1,0:T(8,128)(2,1)}, bf16[2,592,256]{2,1,0:T(8,128)(2,1)S(1)}, u32[]{:S(2)}, u32[]{:S(2)}) collective-permute-start(bf16[2,592,256]{2,1,0:T(8,128)(2,1)} %fusion.69), channel_id=1, source_target_pairs={{0,4},{4,0},{8,12},{12,8},{1,5},{5,1},{9,13},{13,9},{2,6},{6,2},{1... | collective-permute-start | bytes 1818632 | tf_op jit(solution)/shard_map/ppermute | solution.py:408
  568.1 38.1 %collective-permute-start.57 = (bf16[2,592,256]{2,1,0:T(8,128)(2,1)S(1)}, bf16[2,592,256]{2,1,0:T(8,128)(2,1)S(1)}, u32[]{:S(2)}, u32[]{:S(2)}) collective-permute-start(bf16[2,592,256]{2,1,0:T(8,128)(2,1)S(1)} %fusion.68), channel_id=1, source_target_pairs={{0,8},{4,12},{8,0},{12,4},{1,9},{5,13},{9,1},{13,5},{2,10},{6,14},... | collective-permute-start | bytes 1818632 | tf_op jit(solution)/shard_map/ppermute | solution.py:408
  568.3 35.8 %collective-permute-start.56 = (bf16[512,1024]{1,0:T(8,128)(2,1)S(1)}, bf16[512,1024]{1,0:T(8,128)(2,1)S(1)}, u32[]{:S(2)}, u32[]{:S(2)}) collective-permute-start(bf16[512,1024]{1,0:T(8,128)(2,1)S(1)} %fusion.62), channel_id=1, source_target_pairs={{0,1},{1,0},{2,3},{3,2},{4,5},{5,4},{6,7},{7,6},{8,9},{9,8},{10,11... | collective-permute-start | bytes 3145736 | tf_op jit(solution)/shard_map/ppermute | solution.py:402
  572.8 59.1 %collective-permute-start.62 = (bf16[1184,256]{1,0:T(8,128)(2,1)S(1)}, bf16[1184,256]{1,0:T(8,128)(2,1)S(1)}, u32[]{:S(2)}, u32[]{:S(2)}) collective-permute-start(bf16[1184,256]{1,0:T(8,128)(2,1)S(1)} %get-tuple-element.396), channel_id=1, source_target_pairs={{0,2},{1,3},{2,0},{3,1},{4,6},{5,7},{6,4},{7,5},{8,10},{9,11},{10,... | collective-permute-start | bytes 1818632 | tf_op jit(solution)/shard_map/ppermute | solution.py:405
  579.1 27.1 %collective-permute-start.60 = (bf16[128,768]{1,0:T(8,128)(2,1)S(1)}, bf16[128,768]{1,0:T(8,128)(2,1)S(1)}, u32[]{:S(2)}, u32[]{:S(2)}) collective-permute-start(bf16[128,768]{1,0:T(8,128)(2,1)S(1)} %fusion.113), channel_id=1, source_target_pairs={{0,4},{4,0},{8,12},{12,8},{1,5},{5,1},{9,13},{13,9},{2,6},{6,2},{1... | collective-permute-start | bytes 589832 | tf_op jit(solution)/shard_map/ppermute | solution.py:408
  605.9 26.0 %collective-permute-start.63 = (bf16[1184,256]{1,0:T(8,128)(2,1)S(1)}, bf16[1184,256]{1,0:T(8,128)(2,1)S(1)}, u32[]{:S(2)}, u32[]{:S(2)}) collective-permute-start(bf16[1184,256]{1,0:T(8,128)(2,1)S(1)} %get-tuple-element.395), channel_id=1, source_target_pairs={{0,1},{1,2},{2,3},{3,0},{4,5},{5,6},{6,7},{7,4},{8,9},{9,10},{10,1... | collective-permute-start | bytes 1818632 | tf_op jit(solution)/shard_map/ppermute | solution.py:405
  611.8 26.6 %collective-permute-start.65 = (bf16[256,768]{1,0:T(8,128)(2,1)S(1)}, bf16[256,768]{1,0:T(8,128)(2,1)S(1)}, u32[]{:S(2)}, u32[]{:S(2)}) collective-permute-start(bf16[256,768]{1,0:T(8,128)(2,1)S(1)} %pad_maximum_fusion.18), channel_id=1, source_target_pairs={{0,16},{1,17},{2,18},{3,19},{4,20},{5,21},{6,22},{7,23},{8,24},{9,... | collective-permute-start | bytes 1179656 | tf_op jit(solution)/shard_map/ppermute | solution.py:387
  614.3 24.1 %collective-permute-start.66 = (bf16[256,768]{1,0:T(8,128)(2,1)S(1)}, bf16[256,768]{1,0:T(8,128)(2,1)S(1)}, u32[]{:S(2)}, u32[]{:S(2)}) collective-permute-start(bf16[256,768]{1,0:T(8,128)(2,1)S(1)} %pad_maximum_fusion.18), channel_id=1, source_target_pairs={{16,18},{17,19},{18,16},{19,17},{20,22},{21,23},{22,20},{23,21},{2... | collective-permute-start | bytes 1179656 | tf_op jit(solution)/shard_map/ppermute | solution.py:392
  615.3 23.1 %collective-permute-start.64 = (bf16[1184,256]{1,0:T(8,128)(2,1)S(1)}, bf16[1184,256]{1,0:T(8,128)(2,1)S(1)}, u32[]{:S(2)}, u32[]{:S(2)}) collective-permute-start(bf16[1184,256]{1,0:T(8,128)(2,1)S(1)} %fusion.75), channel_id=1, source_target_pairs={{0,3},{1,0},{2,1},{3,2},{4,7},{5,4},{6,5},{7,6},{8,11},{9,8},{10,9... | collective-permute-start | bytes 1818632 | tf_op jit(solution)/shard_map/ppermute | solution.py:405
  651.3 77.2 %collective-permute-start.74 = (bf16[512,1024]{1,0:T(8,128)(2,1)S(1)}, bf16[512,1024]{1,0:T(8,128)(2,1)S(1)}, u32[]{:S(2)}, u32[]{:S(2)}) collective-permute-start(bf16[512,1024]{1,0:T(8,128)(2,1)S(1)} %fusion.16), channel_id=1, source_target_pairs={{16,18},{17,19},{18,16},{19,17},{20,22},{21,23},{22,20},{23,21},{2... | collective-permute-start | bytes 3145736 | tf_op jit(solution)/shard_map/ppermute | solution.py:392
  652.0 77.3 %collective-permute-start.75 = (bf16[512,1024]{1,0:T(8,128)(2,1)S(1)}, bf16[512,1024]{1,0:T(8,128)(2,1)}, u32[]{:S(2)}, u32[]{:S(2)}) collective-permute-start(bf16[512,1024]{1,0:T(8,128)(2,1)S(1)} %fusion.16), channel_id=1, source_target_pairs={{0,16},{1,17},{2,18},{3,19},{4,20},{5,21},{6,22},{7,23},{8,24},{9,... | collective-permute-start | bytes 3145736 | tf_op jit(solution)/shard_map/ppermute | solution.py:387
  661.7 47.7 %collective-permute-start.71 = (bf16[1184,256]{1,0:T(8,128)(2,1)}, bf16[1184,256]{1,0:T(8,128)(2,1)}, u32[]{:S(2)}, u32[]{:S(2)}) collective-permute-start(bf16[1184,256]{1,0:T(8,128)(2,1)} %get-tuple-element.334), channel_id=1, source_target_pairs={{0,4},{4,0},{8,12},{12,8},{1,5},{5,1},{9,13},{13,9},{2,6},{6,2},{1... | collective-permute-start | bytes 1818632 | tf_op jit(solution)/shard_map/ppermute | solution.py:408
  669.6 27.9 %collective-permute-start.70 = (bf16[512,1024]{1,0:T(8,128)(2,1)S(1)}, bf16[512,1024]{1,0:T(8,128)(2,1)S(1)}, u32[]{:S(2)}, u32[]{:S(2)}) collective-permute-start(bf16[512,1024]{1,0:T(8,128)(2,1)S(1)} %fusion.64), channel_id=1, source_target_pairs={{0,16},{16,0},{1,17},{17,1},{2,18},{18,2},{3,19},{19,3},{4,20},{20... | collective-permute-start | bytes 3145736 | tf_op jit(solution)/shard_map/ppermute | solution.py:384
  696.6 29.2 %collective-permute-start.72 = (bf16[1184,256]{1,0:T(8,128)(2,1)}, bf16[1184,256]{1,0:T(8,128)(2,1)S(1)}, u32[]{:S(2)}, u32[]{:S(2)}) collective-permute-start(bf16[1184,256]{1,0:T(8,128)(2,1)} %get-tuple-element.334), channel_id=1, source_target_pairs={{0,8},{4,12},{8,0},{12,4},{1,9},{5,13},{9,1},{13,5},{2,10},{6,14},... | collective-permute-start | bytes 1818632 | tf_op jit(solution)/shard_map/ppermute | solution.py:408
  697.5 29.0 %collective-permute-start.73 = (bf16[1184,256]{1,0:T(8,128)(2,1)}, bf16[1184,256]{1,0:T(8,128)(2,1)S(1)}, u32[]{:S(2)}, u32[]{:S(2)}) collective-permute-start(bf16[1184,256]{1,0:T(8,128)(2,1)} %get-tuple-element.334), channel_id=1, source_target_pairs={{0,12},{4,8},{8,4},{12,0},{1,13},{5,9},{9,5},{13,1},{2,14},{6,10},... | collective-permute-start | bytes 1818632 | tf_op jit(solution)/shard_map/ppermute | solution.py:408
  709.4 60.7 %collective-permute-start.76 = (bf16[2,2,592,256]{3,2,1,0:T(8,128)(2,1)}, bf16[2,2,592,256]{3,2,1,0:T(8,128)(2,1)}, u32[]{:S(2)}, u32[]{:S(2)}) collective-permute-start(bf16[2,2,592,256]{3,2,1,0:T(8,128)(2,1)} %get-tuple-element.258), channel_id=1, source_target_pairs={{0,4},{4,0},{8,12},{12,8},{1,5},{5,1},{9,13},{13,9},{2,6},{6,2},{1... | collective-permute-start | bytes 3637256 | tf_op jit(solution)/shard_map/ppermute | solution.py:408
  725.9 44.3 %collective-permute-start.77 = (bf16[2,2,592,256]{3,2,1,0:T(8,128)(2,1)}, bf16[2,2,592,256]{3,2,1,0:T(8,128)(2,1)}, u32[]{:S(2)}, u32[]{:S(2)}) collective-permute-start(bf16[2,2,592,256]{3,2,1,0:T(8,128)(2,1)} %get-tuple-element.260), channel_id=1, source_target_pairs={{0,8},{4,12},{8,0},{12,4},{1,9},{5,13},{9,1},{13,5},{2,10},{6,14},... | collective-permute-start | bytes 3637256 | tf_op jit(solution)/shard_map/ppermute | solution.py:408
  726.5 52.6 %collective-permute-start.78 = (bf16[2,2,592,256]{3,2,1,0:T(8,128)(2,1)}, bf16[2,2,592,256]{3,2,1,0:T(8,128)(2,1)}, u32[]{:S(2)}, u32[]{:S(2)}) collective-permute-start(bf16[2,2,592,256]{3,2,1,0:T(8,128)(2,1)} %get-tuple-element.262), channel_id=1, source_target_pairs={{0,4},{4,0},{8,12},{12,8},{1,5},{5,1},{9,13},{13,9},{2,6},{6,2},{1... | collective-permute-start | bytes 3637256 | tf_op jit(solution)/shard_map/ppermute | solution.py:408
  728.6 53.2 %collective-permute-start.79 = (bf16[2,2,592,256]{3,2,1,0:T(8,128)(2,1)}, bf16[2,2,592,256]{3,2,1,0:T(8,128)(2,1)}, u32[]{:S(2)}, u32[]{:S(2)}) collective-permute-start(bf16[2,2,592,256]{3,2,1,0:T(8,128)(2,1)} %get-tuple-element.264), channel_id=1, source_target_pairs={{0,8},{4,12},{8,0},{12,4},{1,9},{5,13},{9,1},{13,5},{2,10},{6,14},... | collective-permute-start | bytes 3637256 | tf_op jit(solution)/shard_map/ppermute | solution.py:408
  772.1 28.2 %collective-permute-start.82 = (bf16[2,592,256]{2,1,0:T(8,128)(2,1)S(1)}, bf16[2,592,256]{2,1,0:T(8,128)(2,1)S(1)}, u32[]{:S(2)}, u32[]{:S(2)}) collective-permute-start(bf16[2,592,256]{2,1,0:T(8,128)(2,1)S(1)} %fusion.71), channel_id=1, source_target_pairs={{0,4},{4,0},{8,12},{12,8},{1,5},{5,1},{9,13},{13,9},{2,6},{6,2},{1... | collective-permute-start | bytes 1818632 | tf_op jit(solution)/shard_map/ppermute | solution.py:408
  773.9 27.8 %collective-permute-start.81 = (bf16[2,592,256]{2,1,0:T(8,128)(2,1)S(1)}, bf16[2,592,256]{2,1,0:T(8,128)(2,1)S(1)}, u32[]{:S(2)}, u32[]{:S(2)}) collective-permute-start(bf16[2,592,256]{2,1,0:T(8,128)(2,1)S(1)} %fusion.70), channel_id=1, source_target_pairs={{0,8},{4,12},{8,0},{12,4},{1,9},{5,13},{9,1},{13,5},{2,10},{6,14},... | collective-permute-start | bytes 1818632 | tf_op jit(solution)/shard_map/ppermute | solution.py:408
  800.3 44.2 %collective-permute-start.86 = (bf16[2,592,256]{2,1,0:T(8,128)(2,1)S(1)}, bf16[2,592,256]{2,1,0:T(8,128)(2,1)S(1)}, u32[]{:S(2)}, u32[]{:S(2)}) collective-permute-start(bf16[2,592,256]{2,1,0:T(8,128)(2,1)S(1)} %fusion.72), channel_id=1, source_target_pairs={{0,8},{4,12},{8,0},{12,4},{1,9},{5,13},{9,1},{13,5},{2,10},{6,14},... | collective-permute-start | bytes 1818632 | tf_op jit(solution)/shard_map/ppermute | solution.py:408
  806.0 35.6 %collective-permute-start.85 = (bf16[512,1024]{1,0:T(8,128)(2,1)S(1)}, bf16[512,1024]{1,0:T(8,128)(2,1)S(1)}, u32[]{:S(2)}, u32[]{:S(2)}) collective-permute-start(bf16[512,1024]{1,0:T(8,128)(2,1)S(1)} %fusion.65), channel_id=1, source_target_pairs={{0,1},{1,0},{2,3},{3,2},{4,5},{5,4},{6,7},{7,6},{8,9},{9,8},{10,11... | collective-permute-start | bytes 3145736 | tf_op jit(solution)/shard_map/ppermute | solution.py:402
  806.4 41.2 %collective-permute-start.90 = (bf16[1184,256]{1,0:T(8,128)(2,1)S(1)}, bf16[1184,256]{1,0:T(8,128)(2,1)S(1)}, u32[]{:S(2)}, u32[]{:S(2)}) collective-permute-start(bf16[1184,256]{1,0:T(8,128)(2,1)S(1)} %get-tuple-element.394), channel_id=1, source_target_pairs={{0,2},{1,3},{2,0},{3,1},{4,6},{5,7},{6,4},{7,5},{8,10},{9,11},{10,... | collective-permute-start | bytes 1818632 | tf_op jit(solution)/shard_map/ppermute | solution.py:405
  810.1 44.9 %collective-permute-start.91 = (bf16[1184,256]{1,0:T(8,128)(2,1)S(1)}, bf16[1184,256]{1,0:T(8,128)(2,1)S(1)}, u32[]{:S(2)}, u32[]{:S(2)}) collective-permute-start(bf16[1184,256]{1,0:T(8,128)(2,1)S(1)} %get-tuple-element.393), channel_id=1, source_target_pairs={{0,1},{1,2},{2,3},{3,0},{4,5},{5,6},{6,7},{7,4},{8,9},{9,10},{10,1... | collective-permute-start | bytes 1818632 | tf_op jit(solution)/shard_map/ppermute | solution.py:405
  816.5 28.0 %collective-permute-start.89 = (bf16[128,768]{1,0:T(8,128)(2,1)S(1)}, bf16[128,768]{1,0:T(8,128)(2,1)S(1)}, u32[]{:S(2)}, u32[]{:S(2)}) collective-permute-start(bf16[128,768]{1,0:T(8,128)(2,1)S(1)} %fusion.115), channel_id=1, source_target_pairs={{0,4},{4,0},{8,12},{12,8},{1,5},{5,1},{9,13},{13,9},{2,6},{6,2},{1... | collective-permute-start | bytes 589832 | tf_op jit(solution)/shard_map/ppermute | solution.py:408
  857.6 20.5 %collective-permute-start.92 = (bf16[1184,256]{1,0:T(8,128)(2,1)S(1)}, bf16[1184,256]{1,0:T(8,128)(2,1)S(1)}, u32[]{:S(2)}, u32[]{:S(2)}) collective-permute-start(bf16[1184,256]{1,0:T(8,128)(2,1)S(1)} %fusion.74), channel_id=1, source_target_pairs={{0,3},{1,0},{2,1},{3,2},{4,7},{5,4},{6,5},{7,6},{8,11},{9,8},{10,9... | collective-permute-start | bytes 1818632 | tf_op jit(solution)/shard_map/ppermute | solution.py:405
  882.4 19.8 %collective-permute-start.98 = (bf16[256,768]{1,0:T(8,128)(2,1)S(1)}, bf16[256,768]{1,0:T(8,128)(2,1)S(1)}, u32[]{:S(2)}, u32[]{:S(2)}) collective-permute-start(bf16[256,768]{1,0:T(8,128)(2,1)S(1)} %get-tuple-element.336), channel_id=1, source_target_pairs={{0,4},{4,0},{8,12},{12,8},{1,5},{5,1},{9,13},{13,9},{2,6},{6,2},{1... | collective-permute-start | bytes 1179656 | tf_op jit(solution)/shard_map/ppermute | solution.py:408
  884.2 32.2 %collective-permute-start.95 = (bf16[1184,256]{1,0:T(8,128)(2,1)S(1)}, bf16[1184,256]{1,0:T(8,128)(2,1)S(1)}, u32[]{:S(2)}, u32[]{:S(2)}) collective-permute-start(bf16[1184,256]{1,0:T(8,128)(2,1)S(1)} %get-tuple-element.332), channel_id=1, source_target_pairs={{0,4},{4,0},{8,12},{12,8},{1,5},{5,1},{9,13},{13,9},{2,6},{6,2},{1... | collective-permute-start | bytes 1818632 | tf_op jit(solution)/shard_map/ppermute | solution.py:408
  885.0 31.4 %collective-permute-start.96 = (bf16[1184,256]{1,0:T(8,128)(2,1)S(1)}, bf16[1184,256]{1,0:T(8,128)(2,1)S(1)}, u32[]{:S(2)}, u32[]{:S(2)}) collective-permute-start(bf16[1184,256]{1,0:T(8,128)(2,1)S(1)} %get-tuple-element.332), channel_id=1, source_target_pairs={{0,8},{4,12},{8,0},{12,4},{1,9},{5,13},{9,1},{13,5},{2,10},{6,14},... | collective-permute-start | bytes 1818632 | tf_op jit(solution)/shard_map/ppermute | solution.py:408
  886.5 41.3 %collective-permute-start.97 = (bf16[1184,256]{1,0:T(8,128)(2,1)S(1)}, bf16[1184,256]{1,0:T(8,128)(2,1)S(1)}, u32[]{:S(2)}, u32[]{:S(2)}) collective-permute-start(bf16[1184,256]{1,0:T(8,128)(2,1)S(1)} %get-tuple-element.332), channel_id=1, source_target_pairs={{0,12},{4,8},{8,4},{12,0},{1,13},{5,9},{9,5},{13,1},{2,14},{6,10},... | collective-permute-start | bytes 1818632 | tf_op jit(solution)/shard_map/ppermute | solution.py:408
  895.1 32.7 %collective-permute-start.104 = (bf16[512,1024]{1,0:T(8,128)(2,1)S(1)}, bf16[512,1024]{1,0:T(8,128)(2,1)S(1)}, u32[]{:S(2)}, u32[]{:S(2)}) collective-permute-start(bf16[512,1024]{1,0:T(8,128)(2,1)S(1)} %get-tuple-element.303), channel_id=1, source_target_pairs={{16,2},{17,3},{18,0},{19,1},{20,6},{21,7},{22,4},{23,5},{24,10},{2... | collective-permute-start | bytes 3145736 | tf_op jit(solution)/shard_map/ppermute | solution.py:392
  (179 other events, 1816.9 us)
Sparse Core Ops, SparseCore 0:
  144.4 161.7 all-gather.2

commit v4 on v3

--- a/solution.py
+++ b/solution.py
@@ -232,8 +232,8 @@
 
 
 def attend_back_kernel(
-    tile, heads, share, meta, q_ref, k_ref, kt_ref, v_ref, do_ref, lse_ref, delta_ref, low_ref, high_ref,
-    cos_ref, sin_ref, cost_ref, sint_ref, carry_ref, dq_ref, dk_ref, dv_ref, dqt, dk, dv
+    tile, heads, share, meta, q_ref, k_ref, kt_ref, v_ref, do_ref, o_ref, lse_ref, low_ref, high_ref,
+    cos_ref, sin_ref, cost_ref, sint_ref, carry_ref, dq_ref, dk_ref, dv_ref, dqt, dk, dv, delta_ref
 ):
     width = heads * HD
     index = pl.program_id(0)
@@ -242,6 +242,22 @@
     @pl.when(index == 0)
     def _():
         dqt[...] = jnp.zeros_like(dqt)
+        lanes = lax.broadcasted_iota(jnp.int32, (delta_ref.shape[0], width), 1)
+        owner = lax.broadcasted_iota(jnp.int32, (delta_ref.shape[0], width), 0)
+        select = jnp.where(
+            (lanes >= owner * HD) & (lanes < (owner + 1) * HD), 1.0, 0.0
+        ).astype(F32)
+
+        def row_sums(qt, carry):
+            here = pl.ds(pl.multiple_of(qt * tile, tile), tile)
+            product = do_ref[here, :].astype(F32) * o_ref[here, :].astype(F32)
+            delta_ref[:, here] = lax.dot_general(
+                select, product, (((1,), (1,)), ((), ())), precision=lax.Precision.HIGHEST,
+                preferred_element_type=F32,
+            )
+            return carry
+
+        lax.fori_loop(0, count, row_sums, 0)
 
     dk[...] = jnp.zeros_like(dk)
     dv[...] = jnp.zeros_like(dv)
@@ -320,7 +336,7 @@
         lax.fori_loop(0, count, finish, 0)
 
 
-def attend_back(queries, keys, mixed, out_grad, sums, delta, low, high, meta, cosine, sine, half_tables, share, carry, tile):
+def attend_back(queries, keys, keys_t, mixed, out_grad, attended, sums, low, high, meta, cosine, sine, half_tables, share, carry, tile):
     width = queries.shape[1]
     heads = width // HD
     whole = lambda shape: pl.BlockSpec(shape, lambda i, meta: (0, 0))
@@ -344,7 +360,7 @@
                 pl.BlockSpec((width, tile), lambda i, meta: (0, i)),
                 rows(width),
                 whole((SLOTS, width)),
-                whole((heads, SLOTS)),
+                whole((SLOTS, width)),
                 whole((heads, SLOTS)),
                 whole((1, SLOTS)),
                 whole((1, SLOTS)),
@@ -359,13 +375,14 @@
                 pltpu.VMEM((width, SLOTS), F32),
                 pltpu.VMEM((tile, width), F32),
                 pltpu.VMEM((tile, width), F32),
+                pltpu.VMEM((8, SLOTS), F32),
             ],
         ),
         out_shape=[jax.ShapeDtypeStruct((SLOTS, width), BF16)] * 3,
         compiler_params=pltpu.CompilerParams(vmem_limit_bytes=VMEM_LIMIT),
         cost_estimate=lasting(36),
         name="attend_back",
-    )(meta, queries, keys, keys.T, mixed, out_grad, sums, delta, low, high, cosine, sine, *half_tables, *extra)
+    )(meta, queries, keys, keys_t, mixed, out_grad, attended, sums, low, high, cosine, sine, *half_tables, *extra)
 
 
 class Place:
@@ -651,9 +668,9 @@
         source = lax.rem(head - step + cut.heads, cut.heads)
         for part in range(D // cut.columns):
             columns = pl.ds(part * cut.columns, cut.columns)
-            for kind, row, count, second, at in cut.pieces():
+            for kind, row, count, late, at in cut.pieces():
                 index = source if kind == "out" else step
-                block = full.at[part * cut.heads + source, pl.ds(at + second * cut.first, count), :]
+                block = full.at[part * cut.heads + source, pl.ds(at + late * cut.first, count), :]
                 target = kinds[kind].at[index, pl.ds(row, count), columns]
                 copies.append(pltpu.make_async_copy(block, target, sems.at[len(copies)]))
     run_copies(copies)
@@ -776,9 +793,11 @@
 def reduce_far(place, cut, part):
     half = cut.heads // 2
     blocks = yield from exchange(place, part)
-    arrived = yield [
+    moved = [
         place.around(blocks[step - half].astype(BF16), -step) for step in range(half, cut.heads)
     ]
+    arrived = [(yield moved[0])]
+    arrived += yield moved[1:]
     return sum(item.astype(F32) for item in arrived)
 
 
@@ -791,8 +810,9 @@
         ]
         total = total + sum(item.astype(F32) for item in arrived)
     total = (total + far.result).astype(BF16)
-    flipped = yield [place.flip(total, bits) for bits in range(1, place.data)]
-    parts = place.by_data(total, flipped)
+    flipped = yield [place.flip(total, bits) for bits in range(1, place.data - 1)]
+    total, across = yield total, place.flip(total, place.data - 1)
+    parts = place.by_data(total, [*flipped, across])
     return jnp.concatenate([parts[d] for d in range(place.data)], axis=1)
 
 
@@ -848,6 +868,7 @@
     for other in (chain, *later[1:]) if later else ():
         attended_heads = other.step(attended_heads)
     attended = place.heads_to_slots(attended_heads)
+    keys_t = keys.T
     gate_w, up_w, down_w, out_w = spread = chain.result
     middle = rows + dot_nn(attended, out_w)
     ffn_normed = place.gather_cores(norm(middle, gains[1]).astype(BF16))
@@ -856,8 +877,8 @@
     activation = (jax.nn.silu(gate) * up).astype(BF16)
     result = middle + place.scatter_cores(dot_nn(activation, down_w))
     kept = (
-        rows, gathered, queries, keys, mixed, attended_heads, sums, attended, middle, ffn_normed,
-        gate, up, activation,
+        rows, gathered, queries, keys, keys_t, mixed, attended_heads, sums, attended, middle,
+        ffn_normed, gate, up, activation,
     )
     return result, own_values, spread, kept, later
 
@@ -871,8 +892,8 @@
     cosine, sine, half_tables, low, high, meta, tile = tables
     gate_w, up_w, down_w, out_w = spread
     (
-        rows, gathered, queries, keys, mixed, attended_heads, sums, attended, middle, ffn_normed,
-        gate, up, activation,
+        rows, gathered, queries, keys, keys_t, mixed, attended_heads, sums, attended, middle,
+        ffn_normed, gate, up, activation,
     ) = kept
     down_grad = place.gather_cores(grad.astype(BF16))
     act_grad = dot_nt(down_grad, down_w)
@@ -900,10 +921,8 @@
         heads_grad = other.step(heads_grad)
     far = Chain(reduce_far(place, cut, split[0]))
     near = Chain(reduce_near(place, cut, split[1], far))
-    delta = heads_grad.astype(F32) * attended_heads.astype(F32)
-    delta = jnp.sum(delta.reshape(SLOTS, -1, HD), axis=2).T
     query_grad, key_grad, value_grad = attend_back(
-        queries, keys, mixed, heads_grad, sums, delta, low, high, meta, cosine, sine, half_tables,
+        queries, keys, keys_t, mixed, heads_grad, attended_heads, sums, low, high, meta, cosine, sine, half_tables,
         share, carry, tile,
     )
     for other in (far, near, *earlier[2]):
@@ -913,7 +932,7 @@
     qkv_grad = dot_tn(gathered, after(lin_grad, partial)).astype(BF16)
     qkv_grad = Chain(reduce_qkv(place, qkv_grad, layer, second_layer))
     input_back = place.scatter_row(partial, lambda x: qkv_grad.step(far.step(x)))
-    for other in (near, qkv_grad, far) if layer == 0 else (near, qkv_grad):
+    for other in (near, qkv_grad, far):
         input_back = other.step(input_back)
     rows_back, grad_attn_gain = norm_back(rows, gains[0], input_back)
     return middle_grad + rows_back, value_grad, (far, near), qkv_grad, (grad_attn_gain, grad_ffn_gain)
@@ -1032,9 +1051,11 @@
 
     grads_1 = Chain(bring_one(grad_1, 0, 1))
     gains = Chain(sum_gains(jnp.stack([*gain_1, *gain_2])))
-    ffn_1, qkv_1, gains, grads_1 = lockstep(near_1, qkv_1, gains, grads_1)
-
-    ffn_2, grads_2 = near_2.result, grads_2.result
+    _, ffn_1, ffn_2, qkv_1, gains, grads_1 = lockstep(
+        far_1, near_1, near_2, qkv_1, gains, grads_1
+    )
+
+    grads_2 = grads_2.result
     near, far = outputs.result
     layer_outputs = both_rows(place.pick(hidden_1, near), far)
     near = place.pick(grad_1, grads_2[1].astype(F32))

time: 962 us -> 941 us (0.978)
    unnamed x270 -> x250, local copies, waits for them, and re-layouts: 24.9 us -> 25 us
  transfers between devices with their start and end apart: 110 -> 110, of which waited for: 37 -> 37; matrix products, arithmetic and copies ran while one was open for 24% -> 22% of each run, Pallas kernels for 17% -> 18%
where the time goes in v4:
time: 941 us; the launch traced here: 931 us
  waiting for transfers between devices  310 us (33%)
  Pallas kernels  166 us (18%)
  starting transfers between devices  141 us (15%)
  matrix products  114 us (12%)
  other arithmetic  103 us (11%)
  local copies, waits for them, and re-layouts  79.8 us (8%)
  between operations  17.5 us (2%)
    ppermute x47, waiting for transfers between devices, flip(): return lax.ppermute(x, 'dp', [(d, d ^ bits) for d in range(self.data)])  126 us
    ppermute x9, waiting for transfers between devices, beside(): return lax.ppermute(x, 'head', pairs)  119 us
    pallas_call x2, Pallas kernels, attend_back(): pl.pallas_call(kernel, grid_spec=pltpu.PrefetchScalarGridSpec(num_scalar_...  69.8 us
    ppermute x47, starting transfers between devices, flip(): return lax.ppermute(x, 'dp', [(d, d ^ bits) for d in range(self.data)])  55.8 us
    dot_general x10, matrix products, dot_nt(): lax.dot_general(a, b, (((1,), (1,)), ((), ())), preferred_element_type=F32)  49.2 us
    ppermute x13, waiting for transfers between devices, around(): lax.ppermute(x, 'head', [(h, (h + shift) % self.size) for h in range(self...  47.4 us
    pallas_call x2, Pallas kernels, attend(): pl.pallas_call(functools.partial(attend_kernel, tile, heads), grid_spec=p...  41.6 us
    dot_general x10, matrix products, dot_tn(): lax.dot_general(a, b, (((0,), (0,)), ((), ())), preferred_element_type=F32)  36.9 us
  transfers between devices with their start and end apart: 110, of which 37 were waited for; matrix products, arithmetic and copies ran while one was open for 22% of the time, Pallas kernels for 18%

profile of v4, /device:TPU:0, one launch (start us, length us, event | category | flops | bytes accessed | tf_op | source)
XLA Modules:
  0.0 930.9 jit_solution(9240382610181626391)
XLA Ops:
  13.0 6.3 collective-permute-start.1
  34.0 19.4 %collective-permute-done = bf16[256,1024]{1,0:T(8,128)(2,1)S(1)} collective-permute-done((bf16[256,1024]{1,0:T(8,128)(2,1)}, bf16[256,1024]{1,0:T(8,128)(2,1)S(1)}, u32[]{:S(2)}, u32[]{:S(2)}) %collective-permute-start) | collective-permute-done | bytes 524320 | tf_op jit(solution)/shard_map/ppermute | solution.py:422
  67.2 6.1 collective-permute-done.8
  82.2 8.1 collective-permute-done.11
  105.3 3.7 maximum_select_fusion.1.x
  110.5 6.1 collective-permute-done.13
  123.6 8.0 collective-permute-done.18.refs_6_
  144.4 9.9 %project.2 = (bf16[2048,256]{1,0:T(8,128)(2,1)}, bf16[2048,256]{1,0:T(8,128)(2,1)}, bf16[2048,256]{1,0:T(8,128)(2,1)}) custom-call(bf16[2048,1024]{1,0:T(8,128)(2,1)} %maximum_select_fusion.1.x, bf16[1024,768]{1,0:T(8,128)(2,1)} %bitcast_select_fusion.1.w, f32[2048,128]{1,0:T(8,128)} %copy.54.c.cos_ref.refs_10_, f32[2048,128]{1,0:T(8,128)} %copy.55.s.sin_ref.refs_11_), custom_call_target="tpu_custom_call" | custom-call | flops 10000000000 | bytes 1 | tf_op jit(solution)/shard_map/project/pallas_call | solution.py:116
  165.7 20.8 %attend.2 = (bf16[2048,256]{1,0:T(8,128)(2,1)}, f32[4,2048]{1,0:T(4,128)}) custom-call(s32[4,4]{1,0:T(4,128)} %pad_add_fusion.meta.refs_0_, bf16[2048,256]{1,0:T(8,128)(2,1)} %get-tuple-element.186.q_ref, bf16[2048,256]{1,0:T(8,128)(2,1)} %get-tuple-element.187.k_ref, bf16[256,2048]{1,0:T(8,128)(2,1)} %bitcast.714, s32[1,2048]{1,0:T(1,128)} %bitcast.750, ...), custom_call_target="tpu_custom_call" | custom-call | flops 24999999488 | bytes 1 | tf_op jit(solution)/shard_map/attend/pallas_call | solution.py:202
  186.5 7.9 collective-permute-done.22.refs_11_
  194.4 7.7 collective-permute-done.21.refs_10_
  208.4 9.0 assemble.2
  218.8 9.3 collective-permute-done.26
  237.1 3.5 fusion.144
  240.7 5.8 multiply_convert_fusion.5
  256.7 51.4 %collective-permute-done.31 = bf16[512,1024]{1,0:T(8,128)(2,1)S(1)} collective-permute-done((bf16[512,1024]{1,0:T(8,128)(2,1)S(1)}, bf16[512,1024]{1,0:T(8,128)(2,1)S(1)}, u32[]{:S(2)}, u32[]{:S(2)}) %collective-permute-start.31) | collective-permute-done | bytes 1048608 | tf_op jit(solution)/shard_map/ppermute | solution.py:419
  313.5 3.8 maximum_select_fusion.2.x_ref
  317.3 10.1 %project.3 = (bf16[2048,256]{1,0:T(8,128)(2,1)}, bf16[2048,256]{1,0:T(8,128)(2,1)}, bf16[2048,256]{1,0:T(8,128)(2,1)}, bf16[2048,256]{1,0:T(8,128)(2,1)}) custom-call(bf16[2048,1024]{1,0:T(8,128)(2,1)} %maximum_select_fusion.2.x_ref, bf16[1024,768]{1,0:T(8,128)(2,1)} %broadcast_select_fusion.1.w_ref, f32[2048,128]{1,0:T(8,128)} %copy.54.c.cos_ref.refs_10_, ...), custom_call_target="tpu_custom_call" | custom-call | flops 10000000000 | bytes 1 | tf_op jit(solution)/shard_map/project/pallas_call | solution.py:116
  329.7 20.9 %attend.3 = (bf16[2048,256]{1,0:T(8,128)(2,1)}, f32[4,2048]{1,0:T(4,128)}) custom-call(s32[4,4]{1,0:T(4,128)} %pad_add_fusion.meta.refs_0_, bf16[2048,256]{1,0:T(8,128)(2,1)} %get-tuple-element.207.q_ref.refs_1_, bf16[2048,256]{1,0:T(8,128)(2,1)} %get-tuple-element.208.k_ref.refs_2_, bf16[256,2048]{1,0:T(8,128)(2,1)} %bitcast.715, s32[1,2048]{1,0:T(1,128)} %bitcast.751, ...), custom_call_target="tpu_custom_call" | custom-call | flops 24999999488 | bytes 1 | tf_op jit(solution)/shard_map/attend/pallas_call | solution.py:202
  358.8 9.0 assemble.3
  379.7 5.2 fusion.146
  385.6 5.3 fusion.147
  390.9 10.5 %multiply_convert_fusion.2 = (bf16[1024,1408]{1,0:T(8,128)(2,1)}, bf16[1024,1408]{1,0:T(8,128)(2,1)}, bf16[1024,1408]{1,0:T(8,128)(2,1)}) fusion(f32[1024,1408]{1,0:T(8,128)} %fusion.147, f32[1024,1408]{1,0:T(8,128)} %fusion.146, bf16[1024,1024]{1,0:T(8,128)(2,1)S(1)} %bitcast.676, bf16[1408,1024]{1,0:T(8,128)(2,1)S(1)} %bitcast.655), kind=kOutput, calls=%fused_computation.2 | convolution fusion | flops 2975858688 | bytes 25165824 | tf_op jit(solution)/shard_map/dot_general | solution.py:34
  401.4 6.2 fusion.149
  411.4 3.4 convolution_add_fusion.1
  427.0 4.8 convolution_convert_fusion.3
  431.9 4.5 convolution_convert_fusion.4
  438.6 4.5 convolution_convert_fusion.5
  444.5 8.1 split.2
  465.8 8.5 collective-permute-start.48
  477.8 4.0 collective-permute-done.43
  485.8 34.9 %attend_back.2 = (bf16[2048,256]{1,0:T(8,128)(2,1)}, bf16[2048,256]{1,0:T(8,128)(2,1)}, bf16[2048,256]{1,0:T(8,128)(2,1)}) custom-call(s32[4,4]{1,0:T(4,128)} %pad_add_fusion.meta.refs_0_, bf16[2048,256]{1,0:T(8,128)(2,1)} %get-tuple-element.207.q_ref.refs_1_, bf16[2048,256]{1,0:T(8,128)(2,1)} %get-tuple-element.208.k_ref.refs_2_, ...), custom_call_target="tpu_custom_call" | custom-call | flops 35999997952 | bytes 1 | tf_op jit(solution)/shard_map/attend_back/pallas_call | solution.py:352
  524.1 3.5 fusion.150
  527.7 3.5 convolution_convert_fusion.7
  531.5 4.0 collective-permute-start.55
  546.5 15.2 %collective-permute-done.53 = bf16[2,592,256]{2,1,0:T(8,128)(2,1)} collective-permute-done((bf16[2,592,256]{2,1,0:T(8,128)(2,1)S(1)}, bf16[2,592,256]{2,1,0:T(8,128)(2,1)}, u32[]{:S(2)}, u32[]{:S(2)}) %collective-permute-start.53) | collective-permute-done | bytes 606240 | tf_op jit(solution)/shard_map/ppermute | solution.py:425
  566.3 4.6 collective-permute-start.61
  575.3 21.4 %collective-permute-done.56 = bf16[512,1024]{1,0:T(8,128)(2,1)S(1)} collective-permute-done((bf16[512,1024]{1,0:T(8,128)(2,1)S(1)}, bf16[512,1024]{1,0:T(8,128)(2,1)S(1)}, u32[]{:S(2)}, u32[]{:S(2)}) %collective-permute-start.56) | collective-permute-done | bytes 1048608 | tf_op jit(solution)/shard_map/ppermute | solution.py:419
  598.8 3.6 collective-permute-done.59
  607.4 6.6 collective-permute-start.64
  615.8 9.1 multiply_convert_fusion
  624.9 6.1 collective-permute-done.64
  631.7 5.4 fusion.151
  637.2 3.5 convolution_add_fusion
  646.6 6.8 collective-permute-start.74
  662.1 4.5 convolution_convert_fusion
  666.6 4.5 convolution_convert_fusion.1
  674.8 4.5 convolution_convert_fusion.2
  679.3 7.2 collective-permute-done.68
  688.0 8.1 split.3
  702.3 34.9 %attend_back.3 = (bf16[2048,256]{1,0:T(8,128)(2,1)}, bf16[2048,256]{1,0:T(8,128)(2,1)}, bf16[2048,256]{1,0:T(8,128)(2,1)}) custom-call(s32[4,4]{1,0:T(4,128)} %pad_add_fusion.meta.refs_0_, bf16[2048,256]{1,0:T(8,128)(2,1)} %get-tuple-element.186.q_ref, bf16[2048,256]{1,0:T(8,128)(2,1)} %get-tuple-element.187.k_ref, bf16[256,2048]{1,0:T(8,128)(2,1)} %bitcast.711, ...), custom_call_target="tpu_custom_call" | custom-call | flops 35999997952 | bytes 1 | tf_op jit(solution)/shard_map/attend_back/pallas_call | solution.py:352
  737.2 14.2 %collective-permute-done.77 = bf16[2,2,592,256]{3,2,1,0:T(8,128)(2,1)S(1)} collective-permute-done((bf16[2,2,592,256]{3,2,1,0:T(8,128)(2,1)}, bf16[2,2,592,256]{3,2,1,0:T(8,128)(2,1)S(1)}, u32[]{:S(2)}, u32[]{:S(2)}) %collective-permute-start.77) | collective-permute-done | bytes 1212448 | tf_op jit(solution)/shard_map/ppermute | solution.py:425
  755.7 3.5 fusion.152
  759.2 3.5 convolution_convert_fusion.6
  774.2 15.9 %collective-permute-done.81 = bf16[2,592,256]{2,1,0:T(8,128)(2,1)} collective-permute-done((bf16[2,592,256]{2,1,0:T(8,128)(2,1)S(1)}, bf16[2,592,256]{2,1,0:T(8,128)(2,1)}, u32[]{:S(2)}, u32[]{:S(2)}) %collective-permute-start.81) | collective-permute-done | bytes 606240 | tf_op jit(solution)/shard_map/ppermute | solution.py:425
  800.3 26.5 %collective-permute-done.84 = bf16[512,1024]{1,0:T(8,128)(2,1)S(1)} collective-permute-done((bf16[512,1024]{1,0:T(8,128)(2,1)S(1)}, bf16[512,1024]{1,0:T(8,128)(2,1)S(1)}, u32[]{:S(2)}, u32[]{:S(2)}) %collective-permute-start.84) | collective-permute-done | bytes 1048608 | tf_op jit(solution)/shard_map/ppermute | solution.py:419
  829.7 5.0 collective-permute-done.88
  843.3 11.6 %collective-permute-done.93 = bf16[256,768]{1,0:T(8,128)(2,1)S(1)} collective-permute-done((bf16[256,768]{1,0:T(8,128)(2,1)S(1)}, bf16[256,768]{1,0:T(8,128)(2,1)S(1)}, u32[]{:S(2)}, u32[]{:S(2)}) %collective-permute-start.93) | collective-permute-done | bytes 393248 | tf_op jit(solution)/shard_map/ppermute | solution.py:409
  854.9 4.0 collective-permute-done.91
  870.3 16.4 %collective-permute-done.97 = bf16[256,768]{1,0:T(8,128)(2,1)S(1)} collective-permute-done((bf16[256,768]{1,0:T(8,128)(2,1)S(1)}, bf16[256,768]{1,0:T(8,128)(2,1)S(1)}, u32[]{:S(2)}, u32[]{:S(2)}) %collective-permute-start.97) | collective-permute-done | bytes 393248 | tf_op jit(solution)/shard_map/ppermute | solution.py:425
  890.0 9.6 %collective-permute-done.99 = bf16[256,768]{1,0:T(8,128)(2,1)S(1)} collective-permute-done((bf16[256,768]{1,0:T(8,128)(2,1)S(1)}, bf16[256,768]{1,0:T(8,128)(2,1)S(1)}, u32[]{:S(2)}, u32[]{:S(2)}) %collective-permute-start.99) | collective-permute-done | bytes 393248 | tf_op jit(solution)/shard_map/ppermute | solution.py:425
  899.7 4.8 collective-permute-start.106
  904.9 5.5 collective-permute-done.104
  918.9 3.7 fusion.132
  (703 shorter events, 305.4 us)
Async XLA Ops:
  7.2 322.5 %all-gather.3.cloned.1.call-start = ((), (), s32[]{:S(2)}) async-start(), calls=%async_computation | async-start | bytes 10305536 | tf_op jit(solution)/shard_map/all_gather | solution.py:680
  8.0 18.6 %collective-permute-start.3 = (f32[2,1024]{1,0:T(2,128)S(1)}, f32[2,1024]{1,0:T(2,128)S(1)}, u32[]{:S(2)}, u32[]{:S(2)}) collective-permute-start(f32[2,1024]{1,0:T(2,128)S(1)} %pad_maximum_fusion.27), channel_id=1, source_target_pairs={{0,16},{16,0},{1,17},{17,1},{2,18},{18,2},{3,19},{19,3},{4,20},{20... | collective-permute-start | bytes 24584 | tf_op jit(solution)/shard_map/ppermute | solution.py:401
  13.0 21.0 %collective-permute-start.1 = (bf16[256,768]{1,0:T(8,128)(2,1)}, bf16[256,768]{1,0:T(8,128)(2,1)}, u32[]{:S(2)}, u32[]{:S(2)}) collective-permute-start(bf16[256,768]{1,0:T(8,128)(2,1)} %constant_dynamic-slice_fusion.4), channel_id=1, source_target_pairs={{0,18},{1,19},{2,16},{3,17},{4,22},{5,23},{6,20},{7,21},{8,26},{9,... | collective-permute-start | bytes 1179656 | tf_op jit(solution)/shard_map/ppermute | solution.py:414
  30.7 22.7 %collective-permute-start = (bf16[256,1024]{1,0:T(8,128)(2,1)}, bf16[256,1024]{1,0:T(8,128)(2,1)S(1)}, u32[]{:S(2)}, u32[]{:S(2)}) collective-permute-start(bf16[256,1024]{1,0:T(8,128)(2,1)} %get-tuple-element.384), channel_id=1, source_target_pairs={{0,2},{1,3},{2,0},{3,1},{4,6},{5,7},{6,4},{7,5},{8,10},{9,11},{10,... | collective-permute-start | bytes 1572872 | tf_op jit(solution)/shard_map/ppermute | solution.py:422
  32.0 31.6 %collective-permute-start.4 = (bf16[256,1024]{1,0:T(8,128)(2,1)S(1)}, bf16[256,1024]{1,0:T(8,128)(2,1)S(1)}, u32[]{:S(2)}, u32[]{:S(2)}) collective-permute-start(bf16[256,1024]{1,0:T(8,128)(2,1)S(1)} %fusion.51), channel_id=1, source_target_pairs={{0,1},{1,0},{2,3},{3,2},{4,5},{5,4},{6,7},{7,6},{8,9},{9,8},{10,11... | collective-permute-start | bytes 1572872 | tf_op jit(solution)/shard_map/ppermute | solution.py:419
  56.4 25.7 %collective-permute-start.9 = (bf16[256,768]{1,0:T(8,128)(2,1)}, bf16[256,768]{1,0:T(8,128)(2,1)}, u32[]{:S(2)}, u32[]{:S(2)}) collective-permute-start(bf16[256,768]{1,0:T(8,128)(2,1)} %collective-permute-done.1), channel_id=1, source_target_pairs={{0,12},{4,8},{8,4},{12,0},{1,13},{5,9},{9,5},{13,1},{2,14},{6,10},... | collective-permute-start | bytes 1179656 | tf_op jit(solution)/shard_map/ppermute | solution.py:425
  61.8 20.4 %collective-permute-start.6 = (bf16[256,1024]{1,0:T(8,128)(2,1)}, bf16[256,1024]{1,0:T(8,128)(2,1)}, u32[]{:S(2)}, u32[]{:S(2)}) collective-permute-start(bf16[256,1024]{1,0:T(8,128)(2,1)} %get-tuple-element.348), channel_id=1, source_target_pairs={{0,1},{1,0},{2,3},{3,2},{4,5},{5,4},{6,7},{7,6},{8,9},{9,8},{10,11... | collective-permute-start | bytes 1572872 | tf_op jit(solution)/shard_map/ppermute | solution.py:419
  63.6 26.6 %collective-permute-start.11 = (bf16[1184,256]{1,0:T(8,128)(2,1)}, bf16[1184,256]{1,0:T(8,128)(2,1)}, u32[]{:S(2)}, u32[]{:S(2)}) collective-permute-start(bf16[1184,256]{1,0:T(8,128)(2,1)} %broadcast_select_fusion.2), channel_id=1, source_target_pairs={{0,1},{1,2},{2,3},{3,0},{4,5},{5,6},{6,7},{7,4},{8,9},{9,10},{10,1... | collective-permute-start | bytes 1818632 | tf_op jit(solution)/shard_map/ppermute | solution.py:422
  65.7 30.4 %collective-permute-start.5 = (bf16[2,256,1024]{2,1,0:T(8,128)(2,1)}, bf16[2,256,1024]{2,1,0:T(8,128)(2,1)}, u32[]{:S(2)}, u32[]{:S(2)}) collective-permute-start(bf16[2,256,1024]{2,1,0:T(8,128)(2,1)} %bitcast_dynamic-update-slice_fusion.16), channel_id=1, source_target_pairs={{0,16},{16,0},{1,17},{17,1},{2,18},{18,2},{3,19},{19,3},{4,20},{20... | collective-permute-start | bytes 3145736 | tf_op jit(solution)/shard_map/ppermute | solution.py:401
  73.3 20.1 %collective-permute-start.2 = (bf16[256,1024]{1,0:T(8,128)(2,1)S(1)}, bf16[256,1024]{1,0:T(8,128)(2,1)}, u32[]{:S(2)}, u32[]{:S(2)}) collective-permute-start(bf16[256,1024]{1,0:T(8,128)(2,1)S(1)} %collective-permute-done), channel_id=1, source_target_pairs={{0,16},{16,0},{1,17},{17,1},{2,18},{18,2},{3,19},{19,3},{4,20},{20... | collective-permute-start | bytes 1572872 | tf_op jit(solution)/shard_map/ppermute | solution.py:401
  95.7 46.1 %collective-permute-start.27 = (bf16[1184,1024]{1,0:T(8,128)(2,1)S(1)}, bf16[1184,1024]{1,0:T(8,128)(2,1)S(1)}, u32[]{:S(2)}, u32[]{:S(2)}) collective-permute-start(bf16[1184,1024]{1,0:T(8,128)(2,1)S(1)} %copy-done.13), channel_id=1, source_target_pairs={{0,16},{16,0},{1,17},{17,1},{2,18},{18,2},{3,19},{19,3},{4,20},{20... | collective-permute-start | bytes 7274504 | tf_op jit(solution)/shard_map/ppermute | solution.py:401
  136.0 66.0 %collective-permute-start.23 = (bf16[1024,768]{1,0:T(8,128)(2,1)}, bf16[1024,768]{1,0:T(8,128)(2,1)}, u32[]{:S(2)}, u32[]{:S(2)}) collective-permute-start(bf16[1024,768]{1,0:T(8,128)(2,1)} %pad_maximum_fusion.2), channel_id=1, source_target_pairs={{16,0},{17,1},{18,2},{19,3},{20,4},{21,5},{22,6},{23,7},{24,8},{25... | collective-permute-start | bytes 4718600 | tf_op jit(solution)/shard_map/ppermute | solution.py:404
  137.3 64.8 %collective-permute-start.24 = (bf16[1024,768]{1,0:T(8,128)(2,1)}, bf16[1024,768]{1,0:T(8,128)(2,1)}, u32[]{:S(2)}, u32[]{:S(2)}) collective-permute-start(bf16[1024,768]{1,0:T(8,128)(2,1)} %pad_maximum_fusion.2), channel_id=1, source_target_pairs={{16,18},{17,19},{18,16},{19,17},{20,22},{21,23},{22,20},{23,21},{2... | collective-permute-start | bytes 4718600 | tf_op jit(solution)/shard_map/ppermute | solution.py:409
  160.2 34.2 %collective-permute-start.22 = (bf16[2,2,592,256]{3,2,1,0:T(8,128)(2,1)S(1)}, bf16[2,2,592,256]{3,2,1,0:T(8,128)(2,1)}, u32[]{:S(2)}, u32[]{:S(2)}) collective-permute-start(bf16[2,2,592,256]{3,2,1,0:T(8,128)(2,1)S(1)} %pad_maximum_fusion.7), channel_id=1, source_target_pairs={{0,4},{4,0},{8,12},{12,8},{1,5},{5,1},{9,13},{13,9},{2,6},{6,2},{1... | collective-permute-start | bytes 3637256 | tf_op jit(solution)/shard_map/ppermute | solution.py:425
  164.1 37.9 %collective-permute-start.21 = (bf16[2,2,592,256]{3,2,1,0:T(8,128)(2,1)}, bf16[2,2,592,256]{3,2,1,0:T(8,128)(2,1)}, u32[]{:S(2)}, u32[]{:S(2)}) collective-permute-start(bf16[2,2,592,256]{3,2,1,0:T(8,128)(2,1)} %pad_maximum_fusion.6), channel_id=1, source_target_pairs={{0,8},{4,12},{8,0},{12,4},{1,9},{5,13},{9,1},{13,5},{2,10},{6,14},... | collective-permute-start | bytes 3637256 | tf_op jit(solution)/shard_map/ppermute | solution.py:425
  208.3 19.8 %collective-permute-start.26 = (bf16[2,512,256]{2,1,0:T(8,128)(2,1)S(1)}, bf16[2,512,256]{2,1,0:T(8,128)(2,1)S(1)}, u32[]{:S(2)}, u32[]{:S(2)}) collective-permute-start(bf16[2,512,256]{2,1,0:T(8,128)(2,1)S(1)} %fusion.93), channel_id=1, source_target_pairs={{0,1},{1,0},{2,3},{3,2},{4,5},{5,4},{6,7},{7,6},{8,9},{9,8},{10,11... | collective-permute-start | bytes 1572872 | tf_op jit(solution)/shard_map/ppermute | solution.py:419
  254.5 53.6 %collective-permute-start.31 = (bf16[512,1024]{1,0:T(8,128)(2,1)S(1)}, bf16[512,1024]{1,0:T(8,128)(2,1)S(1)}, u32[]{:S(2)}, u32[]{:S(2)}) collective-permute-start(bf16[512,1024]{1,0:T(8,128)(2,1)S(1)} %get-tuple-element.344), channel_id=1, source_target_pairs={{0,1},{1,0},{2,3},{3,2},{4,5},{5,4},{6,7},{7,6},{8,9},{9,8},{10,11... | collective-permute-start | bytes 3145736 | tf_op jit(solution)/shard_map/ppermute | solution.py:419
  310.0 43.7 %collective-permute-start.33 = (bf16[512,1024]{1,0:T(8,128)(2,1)S(1)}, bf16[512,1024]{1,0:T(8,128)(2,1)S(1)}, u32[]{:S(2)}, u32[]{:S(2)}) collective-permute-start(bf16[512,1024]{1,0:T(8,128)(2,1)S(1)} %fusion.58), channel_id=1, source_target_pairs={{16,18},{17,19},{18,16},{19,17},{20,22},{21,23},{22,20},{23,21},{2... | collective-permute-start | bytes 3145736 | tf_op jit(solution)/shard_map/ppermute | solution.py:409
  436.8 19.7 %collective-permute-start.40 = (bf16[2,512,256]{2,1,0:T(8,128)(2,1)S(1)}, bf16[2,512,256]{2,1,0:T(8,128)(2,1)S(1)}, u32[]{:S(2)}, u32[]{:S(2)}) collective-permute-start(bf16[2,512,256]{2,1,0:T(8,128)(2,1)S(1)} %get-tuple-element.413), channel_id=1, source_target_pairs={{0,1},{1,0},{2,3},{3,2},{4,5},{5,4},{6,7},{7,6},{8,9},{9,8},{10,11... | collective-permute-start | bytes 1572872 | tf_op jit(solution)/shard_map/ppermute | solution.py:419
  452.6 29.2 %collective-permute-start.43 = (bf16[2,2,592,256]{3,2,1,0:T(8,128)(2,1)}, bf16[2,2,592,256]{3,2,1,0:T(8,128)(2,1)}, u32[]{:S(2)}, u32[]{:S(2)}) collective-permute-start(bf16[2,2,592,256]{3,2,1,0:T(8,128)(2,1)} %get-tuple-element.219), channel_id=1, source_target_pairs={{0,4},{4,0},{8,12},{12,8},{1,5},{5,1},{9,13},{13,9},{2,6},{6,2},{1... | collective-permute-start | bytes 3637256 | tf_op jit(solution)/shard_map/ppermute | solution.py:425
  454.1 29.7 %collective-permute-start.44 = (bf16[2,2,592,256]{3,2,1,0:T(8,128)(2,1)}, bf16[2,2,592,256]{3,2,1,0:T(8,128)(2,1)}, u32[]{:S(2)}, u32[]{:S(2)}) collective-permute-start(bf16[2,2,592,256]{3,2,1,0:T(8,128)(2,1)} %get-tuple-element.221), channel_id=1, source_target_pairs={{0,8},{4,12},{8,0},{12,4},{1,9},{5,13},{9,1},{13,5},{2,10},{6,14},... | collective-permute-start | bytes 3637256 | tf_op jit(solution)/shard_map/ppermute | solution.py:425
  462.3 58.5 %collective-permute-start.49 = (bf16[512,1024]{1,0:T(8,128)(2,1)S(1)}, bf16[512,1024]{1,0:T(8,128)(2,1)}, u32[]{:S(2)}, u32[]{:S(2)}) collective-permute-start(bf16[512,1024]{1,0:T(8,128)(2,1)S(1)} %get-tuple-element.346), channel_id=1, source_target_pairs={{16,2},{17,3},{18,0},{19,1},{20,6},{21,7},{22,4},{23,5},{24,10},{2... | collective-permute-start | bytes 3145736 | tf_op jit(solution)/shard_map/ppermute | solution.py:409
  465.8 55.0 %collective-permute-start.48 = (bf16[512,1024]{1,0:T(8,128)(2,1)}, bf16[512,1024]{1,0:T(8,128)(2,1)}, u32[]{:S(2)}, u32[]{:S(2)}) collective-permute-start(bf16[512,1024]{1,0:T(8,128)(2,1)} %get-tuple-element.382), channel_id=1, source_target_pairs={{0,16},{1,17},{2,18},{3,19},{4,20},{5,21},{6,22},{7,23},{8,24},{9,... | collective-permute-start | bytes 3145736 | tf_op jit(solution)/shard_map/ppermute | solution.py:404
  474.3 46.5 %collective-permute-start.50 = (bf16[512,1024]{1,0:T(8,128)(2,1)}, bf16[512,1024]{1,0:T(8,128)(2,1)S(1)}, u32[]{:S(2)}, u32[]{:S(2)}) collective-permute-start(bf16[512,1024]{1,0:T(8,128)(2,1)} %get-tuple-element.382), channel_id=1, source_target_pairs={{16,18},{17,19},{18,16},{19,17},{20,22},{21,23},{22,20},{23,21},{2... | collective-permute-start | bytes 3145736 | tf_op jit(solution)/shard_map/ppermute | solution.py:409
  481.8 39.0 %collective-permute-start.45 = (bf16[2,2,592,256]{3,2,1,0:T(8,128)(2,1)}, bf16[2,2,592,256]{3,2,1,0:T(8,128)(2,1)S(1)}, u32[]{:S(2)}, u32[]{:S(2)}) collective-permute-start(bf16[2,2,592,256]{3,2,1,0:T(8,128)(2,1)} %get-tuple-element.223), channel_id=1, source_target_pairs={{0,4},{4,0},{8,12},{12,8},{1,5},{5,1},{9,13},{13,9},{2,6},{6,2},{1... | collective-permute-start | bytes 3637256 | tf_op jit(solution)/shard_map/ppermute | solution.py:425
  483.8 36.9 %collective-permute-start.46 = (bf16[2,2,592,256]{3,2,1,0:T(8,128)(2,1)}, bf16[2,2,592,256]{3,2,1,0:T(8,128)(2,1)S(1)}, u32[]{:S(2)}, u32[]{:S(2)}) collective-permute-start(bf16[2,2,592,256]{3,2,1,0:T(8,128)(2,1)} %get-tuple-element.225), channel_id=1, source_target_pairs={{0,8},{4,12},{8,0},{12,4},{1,9},{5,13},{9,1},{13,5},{2,10},{6,14},... | collective-permute-start | bytes 3637256 | tf_op jit(solution)/shard_map/ppermute | solution.py:425
  531.5 30.2 %collective-permute-start.55 = (bf16[2,128,768]{2,1,0:T(8,128)(2,1)S(1)}, bf16[2,128,768]{2,1,0:T(8,128)(2,1)}, u32[]{:S(2)}, u32[]{:S(2)}) collective-permute-start(bf16[2,128,768]{2,1,0:T(8,128)(2,1)S(1)} %pad_maximum_fusion.17), channel_id=1, source_target_pairs={{0,8},{4,12},{8,0},{12,4},{1,9},{5,13},{9,1},{13,5},{2,10},{6,14},... | collective-permute-start | bytes 1179656 | tf_op jit(solution)/shard_map/ppermute | solution.py:425
  536.3 25.4 %collective-permute-start.54 = (bf16[2,128,768]{2,1,0:T(8,128)(2,1)}, bf16[2,128,768]{2,1,0:T(8,128)(2,1)}, u32[]{:S(2)}, u32[]{:S(2)}) collective-permute-start(bf16[2,128,768]{2,1,0:T(8,128)(2,1)} %pad_maximum_fusion.16), channel_id=1, source_target_pairs={{0,4},{4,0},{8,12},{12,8},{1,5},{5,1},{9,13},{13,9},{2,6},{6,2},{1... | collective-permute-start | bytes 1179656 | tf_op jit(solution)/shard_map/ppermute | solution.py:425
  537.9 23.7 %collective-permute-start.53 = (bf16[2,592,256]{2,1,0:T(8,128)(2,1)S(1)}, bf16[2,592,256]{2,1,0:T(8,128)(2,1)}, u32[]{:S(2)}, u32[]{:S(2)}) collective-permute-start(bf16[2,592,256]{2,1,0:T(8,128)(2,1)S(1)} %fusion.67), channel_id=1, source_target_pairs={{0,4},{4,0},{8,12},{12,8},{1,5},{5,1},{9,13},{13,9},{2,6},{6,2},{1... | collective-permute-start | bytes 1818632 | tf_op jit(solution)/shard_map/ppermute | solution.py:425
  543.0 18.7 %collective-permute-start.52 = (bf16[2,592,256]{2,1,0:T(8,128)(2,1)S(1)}, bf16[2,592,256]{2,1,0:T(8,128)(2,1)}, u32[]{:S(2)}, u32[]{:S(2)}) collective-permute-start(bf16[2,592,256]{2,1,0:T(8,128)(2,1)S(1)} %fusion.66), channel_id=1, source_target_pairs={{0,8},{4,12},{8,0},{12,4},{1,9},{5,13},{9,1},{13,5},{2,10},{6,14},... | collective-permute-start | bytes 1818632 | tf_op jit(solution)/shard_map/ppermute | solution.py:425
  545.0 53.4 %collective-permute-start.58 = (bf16[2,592,256]{2,1,0:T(8,128)(2,1)S(1)}, bf16[2,592,256]{2,1,0:T(8,128)(2,1)S(1)}, u32[]{:S(2)}, u32[]{:S(2)}) collective-permute-start(bf16[2,592,256]{2,1,0:T(8,128)(2,1)S(1)} %fusion.69), channel_id=1, source_target_pairs={{0,4},{4,0},{8,12},{12,8},{1,5},{5,1},{9,13},{13,9},{2,6},{6,2},{1... | collective-permute-start | bytes 1818632 | tf_op jit(solution)/shard_map/ppermute | solution.py:425
  561.6 37.2 %collective-permute-start.57 = (bf16[2,592,256]{2,1,0:T(8,128)(2,1)S(1)}, bf16[2,592,256]{2,1,0:T(8,128)(2,1)S(1)}, u32[]{:S(2)}, u32[]{:S(2)}) collective-permute-start(bf16[2,592,256]{2,1,0:T(8,128)(2,1)S(1)} %fusion.68), channel_id=1, source_target_pairs={{0,8},{4,12},{8,0},{12,4},{1,9},{5,13},{9,1},{13,5},{2,10},{6,14},... | collective-permute-start | bytes 1818632 | tf_op jit(solution)/shard_map/ppermute | solution.py:425
  561.8 34.9 %collective-permute-start.56 = (bf16[512,1024]{1,0:T(8,128)(2,1)S(1)}, bf16[512,1024]{1,0:T(8,128)(2,1)S(1)}, u32[]{:S(2)}, u32[]{:S(2)}) collective-permute-start(bf16[512,1024]{1,0:T(8,128)(2,1)S(1)} %fusion.62), channel_id=1, source_target_pairs={{0,1},{1,0},{2,3},{3,2},{4,5},{5,4},{6,7},{7,6},{8,9},{9,8},{10,11... | collective-permute-start | bytes 3145736 | tf_op jit(solution)/shard_map/ppermute | solution.py:419
  566.3 36.0 %collective-permute-start.61 = (bf16[1184,256]{1,0:T(8,128)(2,1)S(1)}, bf16[1184,256]{1,0:T(8,128)(2,1)S(1)}, u32[]{:S(2)}, u32[]{:S(2)}) collective-permute-start(bf16[1184,256]{1,0:T(8,128)(2,1)S(1)} %get-tuple-element.398), channel_id=1, source_target_pairs={{0,2},{1,3},{2,0},{3,1},{4,6},{5,7},{6,4},{7,5},{8,10},{9,11},{10,... | collective-permute-start | bytes 1818632 | tf_op jit(solution)/shard_map/ppermute | solution.py:422
  572.1 26.7 %collective-permute-start.60 = (bf16[128,768]{1,0:T(8,128)(2,1)S(1)}, bf16[128,768]{1,0:T(8,128)(2,1)S(1)}, u32[]{:S(2)}, u32[]{:S(2)}) collective-permute-start(bf16[128,768]{1,0:T(8,128)(2,1)S(1)} %fusion.113), channel_id=1, source_target_pairs={{0,4},{4,0},{8,12},{12,8},{1,5},{5,1},{9,13},{13,9},{2,6},{6,2},{1... | collective-permute-start | bytes 589832 | tf_op jit(solution)/shard_map/ppermute | solution.py:425
  598.5 26.4 %collective-permute-start.63 = (bf16[1184,256]{1,0:T(8,128)(2,1)S(1)}, bf16[1184,256]{1,0:T(8,128)(2,1)S(1)}, u32[]{:S(2)}, u32[]{:S(2)}) collective-permute-start(bf16[1184,256]{1,0:T(8,128)(2,1)S(1)} %get-tuple-element.397), channel_id=1, source_target_pairs={{0,1},{1,2},{2,3},{3,0},{4,5},{5,6},{6,7},{7,4},{8,9},{9,10},{10,1... | collective-permute-start | bytes 1818632 | tf_op jit(solution)/shard_map/ppermute | solution.py:422
  604.0 27.0 %collective-permute-start.65 = (bf16[256,768]{1,0:T(8,128)(2,1)S(1)}, bf16[256,768]{1,0:T(8,128)(2,1)S(1)}, u32[]{:S(2)}, u32[]{:S(2)}) collective-permute-start(bf16[256,768]{1,0:T(8,128)(2,1)S(1)} %pad_maximum_fusion.18), channel_id=1, source_target_pairs={{0,16},{1,17},{2,18},{3,19},{4,20},{5,21},{6,22},{7,23},{8,24},{9,... | collective-permute-start | bytes 1179656 | tf_op jit(solution)/shard_map/ppermute | solution.py:404
  606.4 24.5 %collective-permute-start.66 = (bf16[256,768]{1,0:T(8,128)(2,1)S(1)}, bf16[256,768]{1,0:T(8,128)(2,1)S(1)}, u32[]{:S(2)}, u32[]{:S(2)}) collective-permute-start(bf16[256,768]{1,0:T(8,128)(2,1)S(1)} %pad_maximum_fusion.18), channel_id=1, source_target_pairs={{16,18},{17,19},{18,16},{19,17},{20,22},{21,23},{22,20},{23,21},{2... | collective-permute-start | bytes 1179656 | tf_op jit(solution)/shard_map/ppermute | solution.py:409
  607.4 23.5 %collective-permute-start.64 = (bf16[1184,256]{1,0:T(8,128)(2,1)S(1)}, bf16[1184,256]{1,0:T(8,128)(2,1)S(1)}, u32[]{:S(2)}, u32[]{:S(2)}) collective-permute-start(bf16[1184,256]{1,0:T(8,128)(2,1)S(1)} %fusion.75), channel_id=1, source_target_pairs={{0,3},{1,0},{2,1},{3,2},{4,7},{5,4},{6,5},{7,6},{8,11},{9,8},{10,9... | collective-permute-start | bytes 1818632 | tf_op jit(solution)/shard_map/ppermute | solution.py:422
  644.9 56.6 %collective-permute-start.73 = (bf16[512,1024]{1,0:T(8,128)(2,1)S(1)}, bf16[512,1024]{1,0:T(8,128)(2,1)}, u32[]{:S(2)}, u32[]{:S(2)}) collective-permute-start(bf16[512,1024]{1,0:T(8,128)(2,1)S(1)} %fusion.16), channel_id=1, source_target_pairs={{16,18},{17,19},{18,16},{19,17},{20,22},{21,23},{22,20},{23,21},{2... | collective-permute-start | bytes 3145736 | tf_op jit(solution)/shard_map/ppermute | solution.py:409
  646.6 55.6 %collective-permute-start.74 = (bf16[512,1024]{1,0:T(8,128)(2,1)S(1)}, bf16[512,1024]{1,0:T(8,128)(2,1)}, u32[]{:S(2)}, u32[]{:S(2)}) collective-permute-start(bf16[512,1024]{1,0:T(8,128)(2,1)S(1)} %fusion.16), channel_id=1, source_target_pairs={{0,16},{1,17},{2,18},{3,19},{4,20},{5,21},{6,22},{7,23},{8,24},{9,... | collective-permute-start | bytes 3145736 | tf_op jit(solution)/shard_map/ppermute | solution.py:404
  653.8 44.1 %collective-permute-start.71 = (bf16[1184,256]{1,0:T(8,128)(2,1)S(1)}, bf16[1184,256]{1,0:T(8,128)(2,1)S(1)}, u32[]{:S(2)}, u32[]{:S(2)}) collective-permute-start(bf16[1184,256]{1,0:T(8,128)(2,1)S(1)} %fusion.44), channel_id=1, source_target_pairs={{0,4},{4,0},{8,12},{12,8},{1,5},{5,1},{9,13},{13,9},{2,6},{6,2},{1... | collective-permute-start | bytes 1818632 | tf_op jit(solution)/shard_map/ppermute | solution.py:425
  661.1 25.4 %collective-permute-start.70 = (bf16[512,1024]{1,0:T(8,128)(2,1)S(1)}, bf16[512,1024]{1,0:T(8,128)(2,1)S(1)}, u32[]{:S(2)}, u32[]{:S(2)}) collective-permute-start(bf16[512,1024]{1,0:T(8,128)(2,1)S(1)} %fusion.64), channel_id=1, source_target_pairs={{0,16},{16,0},{1,17},{17,1},{2,18},{18,2},{3,19},{19,3},{4,20},{20... | collective-permute-start | bytes 3145736 | tf_op jit(solution)/shard_map/ppermute | solution.py:401
  696.1 41.1 %collective-permute-start.75 = (bf16[2,2,592,256]{3,2,1,0:T(8,128)(2,1)}, bf16[2,2,592,256]{3,2,1,0:T(8,128)(2,1)S(1)}, u32[]{:S(2)}, u32[]{:S(2)}) collective-permute-start(bf16[2,2,592,256]{3,2,1,0:T(8,128)(2,1)} %get-tuple-element.262), channel_id=1, source_target_pairs={{0,4},{4,0},{8,12},{12,8},{1,5},{5,1},{9,13},{13,9},{2,6},{6,2},{1... | collective-permute-start | bytes 3637256 | tf_op jit(solution)/shard_map/ppermute | solution.py:425
  697.9 39.3 %collective-permute-start.76 = (bf16[2,2,592,256]{3,2,1,0:T(8,128)(2,1)}, bf16[2,2,592,256]{3,2,1,0:T(8,128)(2,1)}, u32[]{:S(2)}, u32[]{:S(2)}) collective-permute-start(bf16[2,2,592,256]{3,2,1,0:T(8,128)(2,1)} %get-tuple-element.264), channel_id=1, source_target_pairs={{0,8},{4,12},{8,0},{12,4},{1,9},{5,13},{9,1},{13,5},{2,10},{6,14},... | collective-permute-start | bytes 3637256 | tf_op jit(solution)/shard_map/ppermute | solution.py:425
  701.1 50.4 %collective-permute-start.77 = (bf16[2,2,592,256]{3,2,1,0:T(8,128)(2,1)}, bf16[2,2,592,256]{3,2,1,0:T(8,128)(2,1)S(1)}, u32[]{:S(2)}, u32[]{:S(2)}) collective-permute-start(bf16[2,2,592,256]{3,2,1,0:T(8,128)(2,1)} %get-tuple-element.266), channel_id=1, source_target_pairs={{0,4},{4,0},{8,12},{12,8},{1,5},{5,1},{9,13},{13,9},{2,6},{6,2},{1... | collective-permute-start | bytes 3637256 | tf_op jit(solution)/shard_map/ppermute | solution.py:425
  701.4 51.5 %collective-permute-start.78 = (bf16[2,2,592,256]{3,2,1,0:T(8,128)(2,1)}, bf16[2,2,592,256]{3,2,1,0:T(8,128)(2,1)S(1)}, u32[]{:S(2)}, u32[]{:S(2)}) collective-permute-start(bf16[2,2,592,256]{3,2,1,0:T(8,128)(2,1)} %get-tuple-element.268), channel_id=1, source_target_pairs={{0,8},{4,12},{8,0},{12,4},{1,9},{5,13},{9,1},{13,5},{2,10},{6,14},... | collective-permute-start | bytes 3637256 | tf_op jit(solution)/shard_map/ppermute | solution.py:425
  763.0 27.4 %collective-permute-start.83 = (bf16[2,128,768]{2,1,0:T(8,128)(2,1)S(1)}, bf16[2,128,768]{2,1,0:T(8,128)(2,1)}, u32[]{:S(2)}, u32[]{:S(2)}) collective-permute-start(bf16[2,128,768]{2,1,0:T(8,128)(2,1)S(1)} %pad_maximum_fusion.20), channel_id=1, source_target_pairs={{0,8},{4,12},{8,0},{12,4},{1,9},{5,13},{9,1},{13,5},{2,10},{6,14},... | collective-permute-start | bytes 1179656 | tf_op jit(solution)/shard_map/ppermute | solution.py:425
  764.9 25.5 %collective-permute-start.82 = (bf16[2,128,768]{2,1,0:T(8,128)(2,1)S(1)}, bf16[2,128,768]{2,1,0:T(8,128)(2,1)S(1)}, u32[]{:S(2)}, u32[]{:S(2)}) collective-permute-start(bf16[2,128,768]{2,1,0:T(8,128)(2,1)S(1)} %pad_maximum_fusion.19), channel_id=1, source_target_pairs={{0,4},{4,0},{8,12},{12,8},{1,5},{5,1},{9,13},{13,9},{2,6},{6,2},{1... | collective-permute-start | bytes 1179656 | tf_op jit(solution)/shard_map/ppermute | solution.py:425
  768.8 21.3 %collective-permute-start.81 = (bf16[2,592,256]{2,1,0:T(8,128)(2,1)S(1)}, bf16[2,592,256]{2,1,0:T(8,128)(2,1)}, u32[]{:S(2)}, u32[]{:S(2)}) collective-permute-start(bf16[2,592,256]{2,1,0:T(8,128)(2,1)S(1)} %fusion.71), channel_id=1, source_target_pairs={{0,4},{4,0},{8,12},{12,8},{1,5},{5,1},{9,13},{13,9},{2,6},{6,2},{1... | collective-permute-start | bytes 1818632 | tf_op jit(solution)/shard_map/ppermute | solution.py:425
  770.0 20.4 %collective-permute-start.80 = (bf16[2,592,256]{2,1,0:T(8,128)(2,1)S(1)}, bf16[2,592,256]{2,1,0:T(8,128)(2,1)}, u32[]{:S(2)}, u32[]{:S(2)}) collective-permute-start(bf16[2,592,256]{2,1,0:T(8,128)(2,1)S(1)} %fusion.70), channel_id=1, source_target_pairs={{0,8},{4,12},{8,0},{12,4},{1,9},{5,13},{9,1},{13,5},{2,10},{6,14},... | collective-permute-start | bytes 1818632 | tf_op jit(solution)/shard_map/ppermute | solution.py:425
  772.9 55.5 %collective-permute-start.86 = (bf16[2,592,256]{2,1,0:T(8,128)(2,1)S(1)}, bf16[2,592,256]{2,1,0:T(8,128)(2,1)S(1)}, u32[]{:S(2)}, u32[]{:S(2)}) collective-permute-start(bf16[2,592,256]{2,1,0:T(8,128)(2,1)S(1)} %fusion.73), channel_id=1, source_target_pairs={{0,4},{4,0},{8,12},{12,8},{1,5},{5,1},{9,13},{13,9},{2,6},{6,2},{1... | collective-permute-start | bytes 1818632 | tf_op jit(solution)/shard_map/ppermute | solution.py:425
  790.1 39.3 %collective-permute-start.85 = (bf16[2,592,256]{2,1,0:T(8,128)(2,1)S(1)}, bf16[2,592,256]{2,1,0:T(8,128)(2,1)S(1)}, u32[]{:S(2)}, u32[]{:S(2)}) collective-permute-start(bf16[2,592,256]{2,1,0:T(8,128)(2,1)S(1)} %fusion.72), channel_id=1, source_target_pairs={{0,8},{4,12},{8,0},{12,4},{1,9},{5,13},{9,1},{13,5},{2,10},{6,14},... | collective-permute-start | bytes 1818632 | tf_op jit(solution)/shard_map/ppermute | solution.py:425
  790.5 39.1 %collective-permute-start.87 = (bf16[128,768]{1,0:T(8,128)(2,1)S(1)}, bf16[128,768]{1,0:T(8,128)(2,1)S(1)}, u32[]{:S(2)}, u32[]{:S(2)}) collective-permute-start(bf16[128,768]{1,0:T(8,128)(2,1)S(1)} %fusion.114), channel_id=1, source_target_pairs={{0,8},{4,12},{8,0},{12,4},{1,9},{5,13},{9,1},{13,5},{2,10},{6,14},... | collective-permute-start | bytes 589832 | tf_op jit(solution)/shard_map/ppermute | solution.py:425
  792.5 34.4 %collective-permute-start.84 = (bf16[512,1024]{1,0:T(8,128)(2,1)S(1)}, bf16[512,1024]{1,0:T(8,128)(2,1)S(1)}, u32[]{:S(2)}, u32[]{:S(2)}) collective-permute-start(bf16[512,1024]{1,0:T(8,128)(2,1)S(1)} %fusion.65), channel_id=1, source_target_pairs={{0,1},{1,0},{2,3},{3,2},{4,5},{5,4},{6,7},{7,6},{8,9},{9,8},{10,11... | collective-permute-start | bytes 3145736 | tf_op jit(solution)/shard_map/ppermute | solution.py:419
  797.0 37.7 %collective-permute-start.89 = (bf16[1184,256]{1,0:T(8,128)(2,1)S(1)}, bf16[1184,256]{1,0:T(8,128)(2,1)S(1)}, u32[]{:S(2)}, u32[]{:S(2)}) collective-permute-start(bf16[1184,256]{1,0:T(8,128)(2,1)S(1)} %get-tuple-element.395), channel_id=1, source_target_pairs={{0,2},{1,3},{2,0},{3,1},{4,6},{5,7},{6,4},{7,5},{8,10},{9,11},{10,... | collective-permute-start | bytes 1818632 | tf_op jit(solution)/shard_map/ppermute | solution.py:422
  835.7 19.2 %collective-permute-start.93 = (bf16[256,768]{1,0:T(8,128)(2,1)S(1)}, bf16[256,768]{1,0:T(8,128)(2,1)S(1)}, u32[]{:S(2)}, u32[]{:S(2)}) collective-permute-start(bf16[256,768]{1,0:T(8,128)(2,1)S(1)} %pad_maximum_fusion.21), channel_id=1, source_target_pairs={{16,2},{17,3},{18,0},{19,1},{20,6},{21,7},{22,4},{23,5},{24,10},{2... | collective-permute-start | bytes 1179656 | tf_op jit(solution)/shard_map/ppermute | solution.py:409
  837.4 21.5 %collective-permute-start.91 = (bf16[1184,256]{1,0:T(8,128)(2,1)S(1)}, bf16[1184,256]{1,0:T(8,128)(2,1)S(1)}, u32[]{:S(2)}, u32[]{:S(2)}) collective-permute-start(bf16[1184,256]{1,0:T(8,128)(2,1)S(1)} %fusion.74), channel_id=1, source_target_pairs={{0,3},{1,0},{2,1},{3,2},{4,7},{5,4},{6,5},{7,6},{8,11},{9,8},{10,9... | collective-permute-start | bytes 1818632 | tf_op jit(solution)/shard_map/ppermute | solution.py:422
  862.8 36.8 %collective-permute-start.95 = (bf16[1184,256]{1,0:T(8,128)(2,1)S(1)}, bf16[1184,256]{1,0:T(8,128)(2,1)S(1)}, u32[]{:S(2)}, u32[]{:S(2)}) collective-permute-start(bf16[1184,256]{1,0:T(8,128)(2,1)S(1)} %fusion.33), channel_id=1, source_target_pairs={{0,4},{4,0},{8,12},{12,8},{1,5},{5,1},{9,13},{13,9},{2,6},{6,2},{1... | collective-permute-start | bytes 1818632 | tf_op jit(solution)/shard_map/ppermute | solution.py:425
  864.4 35.2 %collective-permute-start.96 = (bf16[1184,256]{1,0:T(8,128)(2,1)S(1)}, bf16[1184,256]{1,0:T(8,128)(2,1)S(1)}, u32[]{:S(2)}, u32[]{:S(2)}) collective-permute-start(bf16[1184,256]{1,0:T(8,128)(2,1)S(1)} %fusion.33), channel_id=1, source_target_pairs={{0,8},{4,12},{8,0},{12,4},{1,9},{5,13},{9,1},{13,5},{2,10},{6,14},... | collective-permute-start | bytes 1818632 | tf_op jit(solution)/shard_map/ppermute | solution.py:425
  866.6 20.0 %collective-permute-start.97 = (bf16[256,768]{1,0:T(8,128)(2,1)S(1)}, bf16[256,768]{1,0:T(8,128)(2,1)S(1)}, u32[]{:S(2)}, u32[]{:S(2)}) collective-permute-start(bf16[256,768]{1,0:T(8,128)(2,1)S(1)} %get-tuple-element.338), channel_id=1, source_target_pairs={{0,4},{4,0},{8,12},{12,8},{1,5},{5,1},{9,13},{13,9},{2,6},{6,2},{1... | collective-permute-start | bytes 1179656 | tf_op jit(solution)/shard_map/ppermute | solution.py:425
  868.0 31.6 %collective-permute-start.103 = (bf16[512,1024]{1,0:T(8,128)(2,1)S(1)}, bf16[512,1024]{1,0:T(8,128)(2,1)S(1)}, u32[]{:S(2)}, u32[]{:S(2)}) collective-permute-start(bf16[512,1024]{1,0:T(8,128)(2,1)S(1)} %get-tuple-element.307), channel_id=1, source_target_pairs={{16,2},{17,3},{18,0},{19,1},{20,6},{21,7},{22,4},{23,5},{24,10},{2... | collective-permute-start | bytes 3145736 | tf_op jit(solution)/shard_map/ppermute | solution.py:409
  869.4 18.9 %collective-permute-start.98 = (bf16[256,768]{1,0:T(8,128)(2,1)S(1)}, bf16[256,768]{1,0:T(8,128)(2,1)S(1)}, u32[]{:S(2)}, u32[]{:S(2)}) collective-permute-start(bf16[256,768]{1,0:T(8,128)(2,1)S(1)} %get-tuple-element.338), channel_id=1, source_target_pairs={{0,8},{4,12},{8,0},{12,4},{1,9},{5,13},{9,1},{13,5},{2,10},{6,14},... | collective-permute-start | bytes 1179656 | tf_op jit(solution)/shard_map/ppermute | solution.py:425
  888.2 22.2 %collective-permute-start.104 = (bf16[1184,256]{1,0:T(8,128)(2,1)S(1)}, bf16[1184,256]{1,0:T(8,128)(2,1)S(1)}, u32[]{:S(2)}, u32[]{:S(2)}) collective-permute-start(bf16[1184,256]{1,0:T(8,128)(2,1)S(1)} %fusion.33), channel_id=1, source_target_pairs={{0,12},{4,8},{8,4},{12,0},{1,13},{5,9},{9,5},{13,1},{2,14},{6,10},... | collective-permute-start | bytes 1818632 | tf_op jit(solution)/shard_map/ppermute | solution.py:425
  (169 other events, 1681.2 us)
Sparse Core Ops, SparseCore 0:
  144.5 161.7 all-gather.2

commit v5 on v4

--- a/solution.py
+++ b/solution.py
@@ -103,7 +103,7 @@
 
 def project(gathered, w_qkv, cosine, sine, first_values):
     width = w_qkv.shape[1] // 3
-    tile = min(256, SLOTS)
+    tile = min(1024, SLOTS)
     table = cosine.shape[1]
     row = lambda cols: pl.BlockSpec((tile, cols), lambda i: (i, 0))
     shape = jax.ShapeDtypeStruct((SLOTS, width), BF16)

time: 941 us -> 938 us (level)
  Pallas kernels: 166 us -> 150 us
  waiting for transfers between devices: 310 us -> 321 us
    ppermute x47, starting transfers between devices: 55.8 us -> 67.5 us  [flip(): return lax.ppermute(x, 'dp', [(d, d ^ bits) for d in range(self.data)])]
  transfers between devices with their start and end apart: 110 -> 110, of which waited for: 37 -> 35; matrix products, arithmetic and copies ran while one was open for 22% -> 23% of each run, Pallas kernels for 18% -> 16%
where the time goes in v5:
time: 938 us; the launch traced here: 928 us
  waiting for transfers between devices  321 us (34%)
  Pallas kernels  150 us (16%)
  starting transfers between devices  143 us (15%)
  matrix products  114 us (12%)
  other arithmetic  103 us (11%)
  local copies, waits for them, and re-layouts  79.6 us (8%)
  between operations  17.5 us (2%)
    ppermute x47, waiting for transfers between devices, flip(): return lax.ppermute(x, 'dp', [(d, d ^ bits) for d in range(self.data)])  132 us
    ppermute x9, waiting for transfers between devices, beside(): return lax.ppermute(x, 'head', pairs)  122 us
    ppermute x47, starting transfers between devices, flip(): return lax.ppermute(x, 'dp', [(d, d ^ bits) for d in range(self.data)])  67.5 us
    pallas_call x2, Pallas kernels, attend_back(): pl.pallas_call(kernel, grid_spec=pltpu.PrefetchScalarGridSpec(num_scalar_...  62.8 us
    ppermute x13, waiting for transfers between devices, around(): lax.ppermute(x, 'head', [(h, (h + shift) % self.size) for h in range(self...  51 us
    dot_general x10, matrix products, dot_nt(): lax.dot_general(a, b, (((1,), (1,)), ((), ())), preferred_element_type=F32)  49.1 us
    dot_general x10, matrix products, dot_tn(): lax.dot_general(a, b, (((0,), (0,)), ((), ())), preferred_element_type=F32)  36.9 us
    pallas_call x2, Pallas kernels, attend(): pl.pallas_call(functools.partial(attend_kernel, tile, heads), grid_spec=p...  36.8 us
  transfers between devices with their start and end apart: 110, of which 35 were waited for; matrix products, arithmetic and copies ran while one was open for 23% of the time, Pallas kernels for 16%

profile of v5, /device:TPU:0, one launch (start us, length us, event | category | flops | bytes accessed | tf_op | source)
XLA Modules:
  0.0 927.7 jit_solution(4190002145159902010)
XLA Ops:
  13.0 6.3 collective-permute-start.1
  34.0 19.4 %collective-permute-done = bf16[256,1024]{1,0:T(8,128)(2,1)S(1)} collective-permute-done((bf16[256,1024]{1,0:T(8,128)(2,1)}, bf16[256,1024]{1,0:T(8,128)(2,1)S(1)}, u32[]{:S(2)}, u32[]{:S(2)}) %collective-permute-start) | collective-permute-done | bytes 524320 | tf_op jit(solution)/shard_map/ppermute | solution.py:422
  67.2 6.1 collective-permute-done.8
  82.2 8.1 collective-permute-done.11
  105.3 3.7 maximum_select_fusion.1.x
  110.5 6.1 collective-permute-done.13
  123.6 8.0 collective-permute-done.18.refs_6_
  144.4 7.9 project.2
  163.7 18.3 %attend.2 = (bf16[2048,256]{1,0:T(8,128)(2,1)}, f32[4,2048]{1,0:T(4,128)}) custom-call(s32[4,4]{1,0:T(4,128)} %pad_add_fusion.meta.refs_0_, bf16[2048,256]{1,0:T(8,128)(2,1)} %get-tuple-element.186.q_ref, bf16[2048,256]{1,0:T(8,128)(2,1)} %get-tuple-element.187.k_ref, bf16[256,2048]{1,0:T(8,128)(2,1)} %bitcast.714, s32[1,2048]{1,0:T(1,128)} %bitcast.750, ...), custom_call_target="tpu_custom_call" | custom-call | flops 24999999488 | bytes 1 | tf_op jit(solution)/shard_map/attend/pallas_call | solution.py:202
  182.0 9.3 %collective-permute-done.22.refs_11_ = bf16[2,2,592,256]{3,2,1,0:T(8,128)(2,1)} collective-permute-done((bf16[2,2,592,256]{3,2,1,0:T(8,128)(2,1)S(1)}, bf16[2,2,592,256]{3,2,1,0:T(8,128)(2,1)}, u32[]{:S(2)}, u32[]{:S(2)}) %collective-permute-start.22) | collective-permute-done | bytes 1212448 | tf_op jit(solution)/shard_map/ppermute | solution.py:425
  191.3 8.5 collective-permute-done.21.refs_10_
  201.1 7.4 collective-permute-start.25
  210.3 9.0 assemble.2
  220.8 6.6 collective-permute-done.26
  236.3 3.5 fusion.144
  239.9 5.8 multiply_convert_fusion.5
  255.3 51.9 %collective-permute-done.31 = bf16[512,1024]{1,0:T(8,128)(2,1)S(1)} collective-permute-done((bf16[512,1024]{1,0:T(8,128)(2,1)S(1)}, bf16[512,1024]{1,0:T(8,128)(2,1)S(1)}, u32[]{:S(2)}, u32[]{:S(2)}) %collective-permute-start.31) | collective-permute-done | bytes 1048608 | tf_op jit(solution)/shard_map/ppermute | solution.py:419
  312.7 3.8 maximum_select_fusion.2.x_ref
  316.4 8.0 project.3
  326.7 18.4 %attend.3 = (bf16[2048,256]{1,0:T(8,128)(2,1)}, f32[4,2048]{1,0:T(4,128)}) custom-call(s32[4,4]{1,0:T(4,128)} %pad_add_fusion.meta.refs_0_, bf16[2048,256]{1,0:T(8,128)(2,1)} %get-tuple-element.207.q_ref.refs_1_, bf16[2048,256]{1,0:T(8,128)(2,1)} %get-tuple-element.208.k_ref.refs_2_, bf16[256,2048]{1,0:T(8,128)(2,1)} %bitcast.715, s32[1,2048]{1,0:T(1,128)} %bitcast.751, ...), custom_call_target="tpu_custom_call" | custom-call | flops 24999999488 | bytes 1 | tf_op jit(solution)/shard_map/attend/pallas_call | solution.py:202
  353.4 9.0 assemble.3
  374.3 5.2 fusion.146
  380.2 5.3 fusion.147
  385.5 10.5 %multiply_convert_fusion.2 = (bf16[1024,1408]{1,0:T(8,128)(2,1)}, bf16[1024,1408]{1,0:T(8,128)(2,1)}, bf16[1024,1408]{1,0:T(8,128)(2,1)}) fusion(f32[1024,1408]{1,0:T(8,128)} %fusion.147, f32[1024,1408]{1,0:T(8,128)} %fusion.146, bf16[1024,1024]{1,0:T(8,128)(2,1)S(1)} %bitcast.676, bf16[1408,1024]{1,0:T(8,128)(2,1)S(1)} %bitcast.655), kind=kOutput, calls=%fused_computation.2 | convolution fusion | flops 2975858688 | bytes 25165824 | tf_op jit(solution)/shard_map/dot_general | solution.py:34
  396.0 6.2 fusion.149
  406.0 3.4 convolution_add_fusion.1
  421.7 4.8 convolution_convert_fusion.3
  426.5 4.5 convolution_convert_fusion.4
  433.2 4.5 convolution_convert_fusion.5
  439.1 8.1 split.2
  448.1 7.0 collective-permute-start.44
  464.5 5.5 collective-permute-start.48
  477.2 5.2 collective-permute-done.44
  484.4 31.4 %attend_back.2 = (bf16[2048,256]{1,0:T(8,128)(2,1)}, bf16[2048,256]{1,0:T(8,128)(2,1)}, bf16[2048,256]{1,0:T(8,128)(2,1)}) custom-call(s32[4,4]{1,0:T(4,128)} %pad_add_fusion.meta.refs_0_, bf16[2048,256]{1,0:T(8,128)(2,1)} %get-tuple-element.207.q_ref.refs_1_, bf16[2048,256]{1,0:T(8,128)(2,1)} %get-tuple-element.208.k_ref.refs_2_, ...), custom_call_target="tpu_custom_call" | custom-call | flops 35999997952 | bytes 1 | tf_op jit(solution)/shard_map/attend_back/pallas_call | solution.py:352
  519.3 3.5 fusion.150
  522.8 3.5 convolution_convert_fusion.7
  526.6 9.5 %collective-permute-start.55 = (bf16[2,128,768]{2,1,0:T(8,128)(2,1)S(1)}, bf16[2,128,768]{2,1,0:T(8,128)(2,1)}, u32[]{:S(2)}, u32[]{:S(2)}) collective-permute-start(bf16[2,128,768]{2,1,0:T(8,128)(2,1)S(1)} %pad_maximum_fusion.17), channel_id=1, source_target_pairs={{0,8},{4,12},{8,0},{12,4},{1,9},{5,13},{9,1},{13,5},{2,10},{6,14},... | collective-permute-start | bytes 1179656 | tf_op jit(solution)/shard_map/ppermute | solution.py:425
  547.1 15.2 %collective-permute-done.53 = bf16[2,592,256]{2,1,0:T(8,128)(2,1)} collective-permute-done((bf16[2,592,256]{2,1,0:T(8,128)(2,1)S(1)}, bf16[2,592,256]{2,1,0:T(8,128)(2,1)}, u32[]{:S(2)}, u32[]{:S(2)}) %collective-permute-start.53) | collective-permute-done | bytes 606240 | tf_op jit(solution)/shard_map/ppermute | solution.py:425
  570.4 27.1 %collective-permute-done.56 = bf16[512,1024]{1,0:T(8,128)(2,1)S(1)} collective-permute-done((bf16[512,1024]{1,0:T(8,128)(2,1)S(1)}, bf16[512,1024]{1,0:T(8,128)(2,1)S(1)}, u32[]{:S(2)}, u32[]{:S(2)}) %collective-permute-start.56) | collective-permute-done | bytes 1048608 | tf_op jit(solution)/shard_map/ppermute | solution.py:419
  599.5 3.6 collective-permute-done.59
  611.6 9.0 multiply_convert_fusion
  620.7 8.8 collective-permute-done.64
  630.2 5.4 fusion.151
  635.7 3.5 convolution_add_fusion
  645.1 5.6 collective-permute-start.74
  659.0 4.5 convolution_convert_fusion
  663.5 4.5 convolution_convert_fusion.1
  670.7 4.5 convolution_convert_fusion.2
  675.2 7.2 collective-permute-done.68
  685.3 8.1 split.3
  699.9 31.4 %attend_back.3 = (bf16[2048,256]{1,0:T(8,128)(2,1)}, bf16[2048,256]{1,0:T(8,128)(2,1)}, bf16[2048,256]{1,0:T(8,128)(2,1)}) custom-call(s32[4,4]{1,0:T(4,128)} %pad_add_fusion.meta.refs_0_, bf16[2048,256]{1,0:T(8,128)(2,1)} %get-tuple-element.186.q_ref, bf16[2048,256]{1,0:T(8,128)(2,1)} %get-tuple-element.187.k_ref, bf16[256,2048]{1,0:T(8,128)(2,1)} %bitcast.711, ...), custom_call_target="tpu_custom_call" | custom-call | flops 35999997952 | bytes 1 | tf_op jit(solution)/shard_map/attend_back/pallas_call | solution.py:352
  731.3 17.5 %collective-permute-done.77 = bf16[2,2,592,256]{3,2,1,0:T(8,128)(2,1)S(1)} collective-permute-done((bf16[2,2,592,256]{3,2,1,0:T(8,128)(2,1)}, bf16[2,2,592,256]{3,2,1,0:T(8,128)(2,1)S(1)}, u32[]{:S(2)}, u32[]{:S(2)}) %collective-permute-start.77) | collective-permute-done | bytes 1212448 | tf_op jit(solution)/shard_map/ppermute | solution.py:425
  753.9 3.5 fusion.152
  757.4 3.5 convolution_convert_fusion.6
  771.3 15.9 %collective-permute-done.81 = bf16[2,592,256]{2,1,0:T(8,128)(2,1)} collective-permute-done((bf16[2,592,256]{2,1,0:T(8,128)(2,1)S(1)}, bf16[2,592,256]{2,1,0:T(8,128)(2,1)}, u32[]{:S(2)}, u32[]{:S(2)}) %collective-permute-start.81) | collective-permute-done | bytes 606240 | tf_op jit(solution)/shard_map/ppermute | solution.py:425
  797.2 26.1 %collective-permute-done.84 = bf16[512,1024]{1,0:T(8,128)(2,1)S(1)} collective-permute-done((bf16[512,1024]{1,0:T(8,128)(2,1)S(1)}, bf16[512,1024]{1,0:T(8,128)(2,1)S(1)}, u32[]{:S(2)}, u32[]{:S(2)}) %collective-permute-start.84) | collective-permute-done | bytes 1048608 | tf_op jit(solution)/shard_map/ppermute | solution.py:419
  827.0 4.3 collective-permute-done.88
  840.9 11.3 %collective-permute-done.93 = bf16[256,768]{1,0:T(8,128)(2,1)S(1)} collective-permute-done((bf16[256,768]{1,0:T(8,128)(2,1)S(1)}, bf16[256,768]{1,0:T(8,128)(2,1)S(1)}, u32[]{:S(2)}, u32[]{:S(2)}) %collective-permute-start.93) | collective-permute-done | bytes 393248 | tf_op jit(solution)/shard_map/ppermute | solution.py:409
  852.2 3.9 collective-permute-done.91
  867.5 16.2 %collective-permute-done.97 = bf16[256,768]{1,0:T(8,128)(2,1)S(1)} collective-permute-done((bf16[256,768]{1,0:T(8,128)(2,1)S(1)}, bf16[256,768]{1,0:T(8,128)(2,1)S(1)}, u32[]{:S(2)}, u32[]{:S(2)}) %collective-permute-start.97) | collective-permute-done | bytes 393248 | tf_op jit(solution)/shard_map/ppermute | solution.py:425
  887.0 9.6 %collective-permute-done.99 = bf16[256,768]{1,0:T(8,128)(2,1)S(1)} collective-permute-done((bf16[256,768]{1,0:T(8,128)(2,1)S(1)}, bf16[256,768]{1,0:T(8,128)(2,1)S(1)}, u32[]{:S(2)}, u32[]{:S(2)}) %collective-permute-start.99) | collective-permute-done | bytes 393248 | tf_op jit(solution)/shard_map/ppermute | solution.py:425
  896.8 6.3 collective-permute-start.106
  903.4 3.9 collective-permute-done.104
  915.7 3.7 fusion.132
  (703 shorter events, 302.7 us)
Async XLA Ops:
  7.2 319.5 %all-gather.3.cloned.1.call-start = ((), (), s32[]{:S(2)}) async-start(), calls=%async_computation | async-start | bytes 10305536 | tf_op jit(solution)/shard_map/all_gather | solution.py:680
  8.0 18.6 %collective-permute-start.3 = (f32[2,1024]{1,0:T(2,128)S(1)}, f32[2,1024]{1,0:T(2,128)S(1)}, u32[]{:S(2)}, u32[]{:S(2)}) collective-permute-start(f32[2,1024]{1,0:T(2,128)S(1)} %pad_maximum_fusion.27), channel_id=1, source_target_pairs={{0,16},{16,0},{1,17},{17,1},{2,18},{18,2},{3,19},{19,3},{4,20},{20... | collective-permute-start | bytes 24584 | tf_op jit(solution)/shard_map/ppermute | solution.py:401
  13.0 21.0 %collective-permute-start.1 = (bf16[256,768]{1,0:T(8,128)(2,1)}, bf16[256,768]{1,0:T(8,128)(2,1)}, u32[]{:S(2)}, u32[]{:S(2)}) collective-permute-start(bf16[256,768]{1,0:T(8,128)(2,1)} %constant_dynamic-slice_fusion.4), channel_id=1, source_target_pairs={{0,18},{1,19},{2,16},{3,17},{4,22},{5,23},{6,20},{7,21},{8,26},{9,... | collective-permute-start | bytes 1179656 | tf_op jit(solution)/shard_map/ppermute | solution.py:414
  30.7 22.7 %collective-permute-start = (bf16[256,1024]{1,0:T(8,128)(2,1)}, bf16[256,1024]{1,0:T(8,128)(2,1)S(1)}, u32[]{:S(2)}, u32[]{:S(2)}) collective-permute-start(bf16[256,1024]{1,0:T(8,128)(2,1)} %get-tuple-element.384), channel_id=1, source_target_pairs={{0,2},{1,3},{2,0},{3,1},{4,6},{5,7},{6,4},{7,5},{8,10},{9,11},{10,... | collective-permute-start | bytes 1572872 | tf_op jit(solution)/shard_map/ppermute | solution.py:422
  32.0 31.6 %collective-permute-start.4 = (bf16[256,1024]{1,0:T(8,128)(2,1)S(1)}, bf16[256,1024]{1,0:T(8,128)(2,1)S(1)}, u32[]{:S(2)}, u32[]{:S(2)}) collective-permute-start(bf16[256,1024]{1,0:T(8,128)(2,1)S(1)} %fusion.51), channel_id=1, source_target_pairs={{0,1},{1,0},{2,3},{3,2},{4,5},{5,4},{6,7},{7,6},{8,9},{9,8},{10,11... | collective-permute-start | bytes 1572872 | tf_op jit(solution)/shard_map/ppermute | solution.py:419
  54.9 18.4 %collective-permute-start.8 = (bf16[256,768]{1,0:T(8,128)(2,1)}, bf16[256,768]{1,0:T(8,128)(2,1)}, u32[]{:S(2)}, u32[]{:S(2)}) collective-permute-start(bf16[256,768]{1,0:T(8,128)(2,1)} %collective-permute-done.1), channel_id=1, source_target_pairs={{0,8},{4,12},{8,0},{12,4},{1,9},{5,13},{9,1},{13,5},{2,10},{6,14},... | collective-permute-start | bytes 1179656 | tf_op jit(solution)/shard_map/ppermute | solution.py:425
  56.4 25.7 %collective-permute-start.9 = (bf16[256,768]{1,0:T(8,128)(2,1)}, bf16[256,768]{1,0:T(8,128)(2,1)}, u32[]{:S(2)}, u32[]{:S(2)}) collective-permute-start(bf16[256,768]{1,0:T(8,128)(2,1)} %collective-permute-done.1), channel_id=1, source_target_pairs={{0,12},{4,8},{8,4},{12,0},{1,13},{5,9},{9,5},{13,1},{2,14},{6,10},... | collective-permute-start | bytes 1179656 | tf_op jit(solution)/shard_map/ppermute | solution.py:425
  61.8 20.4 %collective-permute-start.6 = (bf16[256,1024]{1,0:T(8,128)(2,1)}, bf16[256,1024]{1,0:T(8,128)(2,1)}, u32[]{:S(2)}, u32[]{:S(2)}) collective-permute-start(bf16[256,1024]{1,0:T(8,128)(2,1)} %get-tuple-element.348), channel_id=1, source_target_pairs={{0,1},{1,0},{2,3},{3,2},{4,5},{5,4},{6,7},{7,6},{8,9},{9,8},{10,11... | collective-permute-start | bytes 1572872 | tf_op jit(solution)/shard_map/ppermute | solution.py:419
  63.6 26.6 %collective-permute-start.11 = (bf16[1184,256]{1,0:T(8,128)(2,1)}, bf16[1184,256]{1,0:T(8,128)(2,1)}, u32[]{:S(2)}, u32[]{:S(2)}) collective-permute-start(bf16[1184,256]{1,0:T(8,128)(2,1)} %broadcast_select_fusion.2), channel_id=1, source_target_pairs={{0,1},{1,2},{2,3},{3,0},{4,5},{5,6},{6,7},{7,4},{8,9},{9,10},{10,1... | collective-permute-start | bytes 1818632 | tf_op jit(solution)/shard_map/ppermute | solution.py:422
  65.7 30.4 %collective-permute-start.5 = (bf16[2,256,1024]{2,1,0:T(8,128)(2,1)}, bf16[2,256,1024]{2,1,0:T(8,128)(2,1)}, u32[]{:S(2)}, u32[]{:S(2)}) collective-permute-start(bf16[2,256,1024]{2,1,0:T(8,128)(2,1)} %bitcast_dynamic-update-slice_fusion.16), channel_id=1, source_target_pairs={{0,16},{16,0},{1,17},{17,1},{2,18},{18,2},{3,19},{19,3},{4,20},{20... | collective-permute-start | bytes 3145736 | tf_op jit(solution)/shard_map/ppermute | solution.py:401
  73.3 20.1 %collective-permute-start.2 = (bf16[256,1024]{1,0:T(8,128)(2,1)S(1)}, bf16[256,1024]{1,0:T(8,128)(2,1)}, u32[]{:S(2)}, u32[]{:S(2)}) collective-permute-start(bf16[256,1024]{1,0:T(8,128)(2,1)S(1)} %collective-permute-done), channel_id=1, source_target_pairs={{0,16},{16,0},{1,17},{17,1},{2,18},{18,2},{3,19},{19,3},{4,20},{20... | collective-permute-start | bytes 1572872 | tf_op jit(solution)/shard_map/ppermute | solution.py:401
  95.7 46.1 %collective-permute-start.27 = (bf16[1184,1024]{1,0:T(8,128)(2,1)S(1)}, bf16[1184,1024]{1,0:T(8,128)(2,1)S(1)}, u32[]{:S(2)}, u32[]{:S(2)}) collective-permute-start(bf16[1184,1024]{1,0:T(8,128)(2,1)S(1)} %copy-done.13), channel_id=1, source_target_pairs={{0,16},{16,0},{1,17},{17,1},{2,18},{18,2},{3,19},{19,3},{4,20},{20... | collective-permute-start | bytes 7274504 | tf_op jit(solution)/shard_map/ppermute | solution.py:401
  136.0 63.8 %collective-permute-start.23 = (bf16[1024,768]{1,0:T(8,128)(2,1)}, bf16[1024,768]{1,0:T(8,128)(2,1)}, u32[]{:S(2)}, u32[]{:S(2)}) collective-permute-start(bf16[1024,768]{1,0:T(8,128)(2,1)} %pad_maximum_fusion.2), channel_id=1, source_target_pairs={{16,0},{17,1},{18,2},{19,3},{20,4},{21,5},{22,6},{23,7},{24,8},{25... | collective-permute-start | bytes 4718600 | tf_op jit(solution)/shard_map/ppermute | solution.py:404
  137.3 62.5 %collective-permute-start.24 = (bf16[1024,768]{1,0:T(8,128)(2,1)}, bf16[1024,768]{1,0:T(8,128)(2,1)}, u32[]{:S(2)}, u32[]{:S(2)}) collective-permute-start(bf16[1024,768]{1,0:T(8,128)(2,1)} %pad_maximum_fusion.2), channel_id=1, source_target_pairs={{16,18},{17,19},{18,16},{19,17},{20,22},{21,23},{22,20},{23,21},{2... | collective-permute-start | bytes 4718600 | tf_op jit(solution)/shard_map/ppermute | solution.py:409
  158.3 33.0 %collective-permute-start.22 = (bf16[2,2,592,256]{3,2,1,0:T(8,128)(2,1)S(1)}, bf16[2,2,592,256]{3,2,1,0:T(8,128)(2,1)}, u32[]{:S(2)}, u32[]{:S(2)}) collective-permute-start(bf16[2,2,592,256]{3,2,1,0:T(8,128)(2,1)S(1)} %pad_maximum_fusion.7), channel_id=1, source_target_pairs={{0,4},{4,0},{8,12},{12,8},{1,5},{5,1},{9,13},{13,9},{2,6},{6,2},{1... | collective-permute-start | bytes 3637256 | tf_op jit(solution)/shard_map/ppermute | solution.py:425
  162.3 37.5 %collective-permute-start.21 = (bf16[2,2,592,256]{3,2,1,0:T(8,128)(2,1)}, bf16[2,2,592,256]{3,2,1,0:T(8,128)(2,1)}, u32[]{:S(2)}, u32[]{:S(2)}) collective-permute-start(bf16[2,2,592,256]{3,2,1,0:T(8,128)(2,1)} %pad_maximum_fusion.6), channel_id=1, source_target_pairs={{0,8},{4,12},{8,0},{12,4},{1,9},{5,13},{9,1},{13,5},{2,10},{6,14},... | collective-permute-start | bytes 3637256 | tf_op jit(solution)/shard_map/ppermute | solution.py:425
  253.8 53.5 %collective-permute-start.31 = (bf16[512,1024]{1,0:T(8,128)(2,1)S(1)}, bf16[512,1024]{1,0:T(8,128)(2,1)S(1)}, u32[]{:S(2)}, u32[]{:S(2)}) collective-permute-start(bf16[512,1024]{1,0:T(8,128)(2,1)S(1)} %get-tuple-element.344), channel_id=1, source_target_pairs={{0,1},{1,0},{2,3},{3,2},{4,5},{5,4},{6,7},{7,6},{8,9},{9,8},{10,11... | collective-permute-start | bytes 3145736 | tf_op jit(solution)/shard_map/ppermute | solution.py:419
  309.2 39.2 %collective-permute-start.33 = (bf16[512,1024]{1,0:T(8,128)(2,1)S(1)}, bf16[512,1024]{1,0:T(8,128)(2,1)S(1)}, u32[]{:S(2)}, u32[]{:S(2)}) collective-permute-start(bf16[512,1024]{1,0:T(8,128)(2,1)S(1)} %fusion.58), channel_id=1, source_target_pairs={{16,18},{17,19},{18,16},{19,17},{20,22},{21,23},{22,20},{23,21},{2... | collective-permute-start | bytes 3145736 | tf_op jit(solution)/shard_map/ppermute | solution.py:409
  431.4 23.7 %collective-permute-start.40 = (bf16[2,512,256]{2,1,0:T(8,128)(2,1)S(1)}, bf16[2,512,256]{2,1,0:T(8,128)(2,1)S(1)}, u32[]{:S(2)}, u32[]{:S(2)}) collective-permute-start(bf16[2,512,256]{2,1,0:T(8,128)(2,1)S(1)} %get-tuple-element.413), channel_id=1, source_target_pairs={{0,1},{1,0},{2,3},{3,2},{4,5},{5,4},{6,7},{7,6},{8,9},{9,8},{10,11... | collective-permute-start | bytes 1572872 | tf_op jit(solution)/shard_map/ppermute | solution.py:419
  447.2 29.2 %collective-permute-start.43 = (bf16[2,2,592,256]{3,2,1,0:T(8,128)(2,1)}, bf16[2,2,592,256]{3,2,1,0:T(8,128)(2,1)}, u32[]{:S(2)}, u32[]{:S(2)}) collective-permute-start(bf16[2,2,592,256]{3,2,1,0:T(8,128)(2,1)} %get-tuple-element.219), channel_id=1, source_target_pairs={{0,4},{4,0},{8,12},{12,8},{1,5},{5,1},{9,13},{13,9},{2,6},{6,2},{1... | collective-permute-start | bytes 3637256 | tf_op jit(solution)/shard_map/ppermute | solution.py:425
  448.1 34.3 %collective-permute-start.44 = (bf16[2,2,592,256]{3,2,1,0:T(8,128)(2,1)}, bf16[2,2,592,256]{3,2,1,0:T(8,128)(2,1)}, u32[]{:S(2)}, u32[]{:S(2)}) collective-permute-start(bf16[2,2,592,256]{3,2,1,0:T(8,128)(2,1)} %get-tuple-element.221), channel_id=1, source_target_pairs={{0,8},{4,12},{8,0},{12,4},{1,9},{5,13},{9,1},{13,5},{2,10},{6,14},... | collective-permute-start | bytes 3637256 | tf_op jit(solution)/shard_map/ppermute | solution.py:425
  460.9 55.0 %collective-permute-start.49 = (bf16[512,1024]{1,0:T(8,128)(2,1)S(1)}, bf16[512,1024]{1,0:T(8,128)(2,1)}, u32[]{:S(2)}, u32[]{:S(2)}) collective-permute-start(bf16[512,1024]{1,0:T(8,128)(2,1)S(1)} %get-tuple-element.346), channel_id=1, source_target_pairs={{16,2},{17,3},{18,0},{19,1},{20,6},{21,7},{22,4},{23,5},{24,10},{2... | collective-permute-start | bytes 3145736 | tf_op jit(solution)/shard_map/ppermute | solution.py:409
  464.5 51.4 %collective-permute-start.48 = (bf16[512,1024]{1,0:T(8,128)(2,1)}, bf16[512,1024]{1,0:T(8,128)(2,1)}, u32[]{:S(2)}, u32[]{:S(2)}) collective-permute-start(bf16[512,1024]{1,0:T(8,128)(2,1)} %get-tuple-element.382), channel_id=1, source_target_pairs={{0,16},{1,17},{2,18},{3,19},{4,20},{5,21},{6,22},{7,23},{8,24},{9,... | collective-permute-start | bytes 3145736 | tf_op jit(solution)/shard_map/ppermute | solution.py:404
  469.9 46.0 %collective-permute-start.50 = (bf16[512,1024]{1,0:T(8,128)(2,1)}, bf16[512,1024]{1,0:T(8,128)(2,1)S(1)}, u32[]{:S(2)}, u32[]{:S(2)}) collective-permute-start(bf16[512,1024]{1,0:T(8,128)(2,1)} %get-tuple-element.382), channel_id=1, source_target_pairs={{16,18},{17,19},{18,16},{19,17},{20,22},{21,23},{22,20},{23,21},{2... | collective-permute-start | bytes 3145736 | tf_op jit(solution)/shard_map/ppermute | solution.py:409
  476.4 39.5 %collective-permute-start.45 = (bf16[2,2,592,256]{3,2,1,0:T(8,128)(2,1)}, bf16[2,2,592,256]{3,2,1,0:T(8,128)(2,1)S(1)}, u32[]{:S(2)}, u32[]{:S(2)}) collective-permute-start(bf16[2,2,592,256]{3,2,1,0:T(8,128)(2,1)} %get-tuple-element.223), channel_id=1, source_target_pairs={{0,4},{4,0},{8,12},{12,8},{1,5},{5,1},{9,13},{13,9},{2,6},{6,2},{1... | collective-permute-start | bytes 3637256 | tf_op jit(solution)/shard_map/ppermute | solution.py:425
  482.4 33.4 %collective-permute-start.46 = (bf16[2,2,592,256]{3,2,1,0:T(8,128)(2,1)}, bf16[2,2,592,256]{3,2,1,0:T(8,128)(2,1)S(1)}, u32[]{:S(2)}, u32[]{:S(2)}) collective-permute-start(bf16[2,2,592,256]{3,2,1,0:T(8,128)(2,1)} %get-tuple-element.225), channel_id=1, source_target_pairs={{0,8},{4,12},{8,0},{12,4},{1,9},{5,13},{9,1},{13,5},{2,10},{6,14},... | collective-permute-start | bytes 3637256 | tf_op jit(solution)/shard_map/ppermute | solution.py:425
  526.6 35.7 %collective-permute-start.55 = (bf16[2,128,768]{2,1,0:T(8,128)(2,1)S(1)}, bf16[2,128,768]{2,1,0:T(8,128)(2,1)}, u32[]{:S(2)}, u32[]{:S(2)}) collective-permute-start(bf16[2,128,768]{2,1,0:T(8,128)(2,1)S(1)} %pad_maximum_fusion.17), channel_id=1, source_target_pairs={{0,8},{4,12},{8,0},{12,4},{1,9},{5,13},{9,1},{13,5},{2,10},{6,14},... | collective-permute-start | bytes 1179656 | tf_op jit(solution)/shard_map/ppermute | solution.py:425
  536.9 25.4 %collective-permute-start.54 = (bf16[2,128,768]{2,1,0:T(8,128)(2,1)}, bf16[2,128,768]{2,1,0:T(8,128)(2,1)}, u32[]{:S(2)}, u32[]{:S(2)}) collective-permute-start(bf16[2,128,768]{2,1,0:T(8,128)(2,1)} %pad_maximum_fusion.16), channel_id=1, source_target_pairs={{0,4},{4,0},{8,12},{12,8},{1,5},{5,1},{9,13},{13,9},{2,6},{6,2},{1... | collective-permute-start | bytes 1179656 | tf_op jit(solution)/shard_map/ppermute | solution.py:425
  538.6 23.7 %collective-permute-start.53 = (bf16[2,592,256]{2,1,0:T(8,128)(2,1)S(1)}, bf16[2,592,256]{2,1,0:T(8,128)(2,1)}, u32[]{:S(2)}, u32[]{:S(2)}) collective-permute-start(bf16[2,592,256]{2,1,0:T(8,128)(2,1)S(1)} %fusion.67), channel_id=1, source_target_pairs={{0,4},{4,0},{8,12},{12,8},{1,5},{5,1},{9,13},{13,9},{2,6},{6,2},{1... | collective-permute-start | bytes 1818632 | tf_op jit(solution)/shard_map/ppermute | solution.py:425
  543.6 18.7 %collective-permute-start.52 = (bf16[2,592,256]{2,1,0:T(8,128)(2,1)S(1)}, bf16[2,592,256]{2,1,0:T(8,128)(2,1)}, u32[]{:S(2)}, u32[]{:S(2)}) collective-permute-start(bf16[2,592,256]{2,1,0:T(8,128)(2,1)S(1)} %fusion.66), channel_id=1, source_target_pairs={{0,8},{4,12},{8,0},{12,4},{1,9},{5,13},{9,1},{13,5},{2,10},{6,14},... | collective-permute-start | bytes 1818632 | tf_op jit(solution)/shard_map/ppermute | solution.py:425
  545.7 53.5 %collective-permute-start.58 = (bf16[2,592,256]{2,1,0:T(8,128)(2,1)S(1)}, bf16[2,592,256]{2,1,0:T(8,128)(2,1)S(1)}, u32[]{:S(2)}, u32[]{:S(2)}) collective-permute-start(bf16[2,592,256]{2,1,0:T(8,128)(2,1)S(1)} %fusion.69), channel_id=1, source_target_pairs={{0,4},{4,0},{8,12},{12,8},{1,5},{5,1},{9,13},{13,9},{2,6},{6,2},{1... | collective-permute-start | bytes 1818632 | tf_op jit(solution)/shard_map/ppermute | solution.py:425
  562.3 37.2 %collective-permute-start.57 = (bf16[2,592,256]{2,1,0:T(8,128)(2,1)S(1)}, bf16[2,592,256]{2,1,0:T(8,128)(2,1)S(1)}, u32[]{:S(2)}, u32[]{:S(2)}) collective-permute-start(bf16[2,592,256]{2,1,0:T(8,128)(2,1)S(1)} %fusion.68), channel_id=1, source_target_pairs={{0,8},{4,12},{8,0},{12,4},{1,9},{5,13},{9,1},{13,5},{2,10},{6,14},... | collective-permute-start | bytes 1818632 | tf_op jit(solution)/shard_map/ppermute | solution.py:425
  562.5 34.9 %collective-permute-start.56 = (bf16[512,1024]{1,0:T(8,128)(2,1)S(1)}, bf16[512,1024]{1,0:T(8,128)(2,1)S(1)}, u32[]{:S(2)}, u32[]{:S(2)}) collective-permute-start(bf16[512,1024]{1,0:T(8,128)(2,1)S(1)} %fusion.62), channel_id=1, source_target_pairs={{0,1},{1,0},{2,3},{3,2},{4,5},{5,4},{6,7},{7,6},{8,9},{9,8},{10,11... | collective-permute-start | bytes 3145736 | tf_op jit(solution)/shard_map/ppermute | solution.py:419
  566.9 36.1 %collective-permute-start.61 = (bf16[1184,256]{1,0:T(8,128)(2,1)S(1)}, bf16[1184,256]{1,0:T(8,128)(2,1)S(1)}, u32[]{:S(2)}, u32[]{:S(2)}) collective-permute-start(bf16[1184,256]{1,0:T(8,128)(2,1)S(1)} %get-tuple-element.398), channel_id=1, source_target_pairs={{0,2},{1,3},{2,0},{3,1},{4,6},{5,7},{6,4},{7,5},{8,10},{9,11},{10,... | collective-permute-start | bytes 1818632 | tf_op jit(solution)/shard_map/ppermute | solution.py:422
  568.6 30.9 %collective-permute-start.60 = (bf16[128,768]{1,0:T(8,128)(2,1)S(1)}, bf16[128,768]{1,0:T(8,128)(2,1)S(1)}, u32[]{:S(2)}, u32[]{:S(2)}) collective-permute-start(bf16[128,768]{1,0:T(8,128)(2,1)S(1)} %fusion.113), channel_id=1, source_target_pairs={{0,4},{4,0},{8,12},{12,8},{1,5},{5,1},{9,13},{13,9},{2,6},{6,2},{1... | collective-permute-start | bytes 589832 | tf_op jit(solution)/shard_map/ppermute | solution.py:425
  599.2 21.5 %collective-permute-start.63 = (bf16[1184,256]{1,0:T(8,128)(2,1)S(1)}, bf16[1184,256]{1,0:T(8,128)(2,1)S(1)}, u32[]{:S(2)}, u32[]{:S(2)}) collective-permute-start(bf16[1184,256]{1,0:T(8,128)(2,1)S(1)} %get-tuple-element.397), channel_id=1, source_target_pairs={{0,1},{1,2},{2,3},{3,0},{4,5},{5,6},{6,7},{7,4},{8,9},{9,10},{10,1... | collective-permute-start | bytes 1818632 | tf_op jit(solution)/shard_map/ppermute | solution.py:422
  604.7 24.7 %collective-permute-start.65 = (bf16[256,768]{1,0:T(8,128)(2,1)S(1)}, bf16[256,768]{1,0:T(8,128)(2,1)S(1)}, u32[]{:S(2)}, u32[]{:S(2)}) collective-permute-start(bf16[256,768]{1,0:T(8,128)(2,1)S(1)} %pad_maximum_fusion.18), channel_id=1, source_target_pairs={{0,16},{1,17},{2,18},{3,19},{4,20},{5,21},{6,22},{7,23},{8,24},{9,... | collective-permute-start | bytes 1179656 | tf_op jit(solution)/shard_map/ppermute | solution.py:404
  607.1 22.3 %collective-permute-start.66 = (bf16[256,768]{1,0:T(8,128)(2,1)S(1)}, bf16[256,768]{1,0:T(8,128)(2,1)S(1)}, u32[]{:S(2)}, u32[]{:S(2)}) collective-permute-start(bf16[256,768]{1,0:T(8,128)(2,1)S(1)} %pad_maximum_fusion.18), channel_id=1, source_target_pairs={{16,18},{17,19},{18,16},{19,17},{20,22},{21,23},{22,20},{23,21},{2... | collective-permute-start | bytes 1179656 | tf_op jit(solution)/shard_map/ppermute | solution.py:409
  608.2 21.3 %collective-permute-start.64 = (bf16[1184,256]{1,0:T(8,128)(2,1)S(1)}, bf16[1184,256]{1,0:T(8,128)(2,1)S(1)}, u32[]{:S(2)}, u32[]{:S(2)}) collective-permute-start(bf16[1184,256]{1,0:T(8,128)(2,1)S(1)} %fusion.75), channel_id=1, source_target_pairs={{0,3},{1,0},{2,1},{3,2},{4,7},{5,4},{6,5},{7,6},{8,11},{9,8},{10,9... | collective-permute-start | bytes 1818632 | tf_op jit(solution)/shard_map/ppermute | solution.py:422
  643.4 55.0 %collective-permute-start.73 = (bf16[512,1024]{1,0:T(8,128)(2,1)S(1)}, bf16[512,1024]{1,0:T(8,128)(2,1)}, u32[]{:S(2)}, u32[]{:S(2)}) collective-permute-start(bf16[512,1024]{1,0:T(8,128)(2,1)S(1)} %fusion.16), channel_id=1, source_target_pairs={{16,18},{17,19},{18,16},{19,17},{20,22},{21,23},{22,20},{23,21},{2... | collective-permute-start | bytes 3145736 | tf_op jit(solution)/shard_map/ppermute | solution.py:409
  645.1 54.7 %collective-permute-start.74 = (bf16[512,1024]{1,0:T(8,128)(2,1)S(1)}, bf16[512,1024]{1,0:T(8,128)(2,1)}, u32[]{:S(2)}, u32[]{:S(2)}) collective-permute-start(bf16[512,1024]{1,0:T(8,128)(2,1)S(1)} %fusion.16), channel_id=1, source_target_pairs={{0,16},{1,17},{2,18},{3,19},{4,20},{5,21},{6,22},{7,23},{8,24},{9,... | collective-permute-start | bytes 3145736 | tf_op jit(solution)/shard_map/ppermute | solution.py:404
  651.0 45.1 %collective-permute-start.71 = (bf16[1184,256]{1,0:T(8,128)(2,1)S(1)}, bf16[1184,256]{1,0:T(8,128)(2,1)S(1)}, u32[]{:S(2)}, u32[]{:S(2)}) collective-permute-start(bf16[1184,256]{1,0:T(8,128)(2,1)S(1)} %fusion.44), channel_id=1, source_target_pairs={{0,4},{4,0},{8,12},{12,8},{1,5},{5,1},{9,13},{13,9},{2,6},{6,2},{1... | collective-permute-start | bytes 1818632 | tf_op jit(solution)/shard_map/ppermute | solution.py:425
  658.0 25.9 %collective-permute-start.70 = (bf16[512,1024]{1,0:T(8,128)(2,1)S(1)}, bf16[512,1024]{1,0:T(8,128)(2,1)S(1)}, u32[]{:S(2)}, u32[]{:S(2)}) collective-permute-start(bf16[512,1024]{1,0:T(8,128)(2,1)S(1)} %fusion.64), channel_id=1, source_target_pairs={{0,16},{16,0},{1,17},{17,1},{2,18},{18,2},{3,19},{19,3},{4,20},{20... | collective-permute-start | bytes 3145736 | tf_op jit(solution)/shard_map/ppermute | solution.py:401
  693.5 37.8 %collective-permute-start.75 = (bf16[2,2,592,256]{3,2,1,0:T(8,128)(2,1)}, bf16[2,2,592,256]{3,2,1,0:T(8,128)(2,1)S(1)}, u32[]{:S(2)}, u32[]{:S(2)}) collective-permute-start(bf16[2,2,592,256]{3,2,1,0:T(8,128)(2,1)} %get-tuple-element.262), channel_id=1, source_target_pairs={{0,4},{4,0},{8,12},{12,8},{1,5},{5,1},{9,13},{13,9},{2,6},{6,2},{1... | collective-permute-start | bytes 3637256 | tf_op jit(solution)/shard_map/ppermute | solution.py:425
  696.2 35.1 %collective-permute-start.76 = (bf16[2,2,592,256]{3,2,1,0:T(8,128)(2,1)}, bf16[2,2,592,256]{3,2,1,0:T(8,128)(2,1)}, u32[]{:S(2)}, u32[]{:S(2)}) collective-permute-start(bf16[2,2,592,256]{3,2,1,0:T(8,128)(2,1)} %get-tuple-element.264), channel_id=1, source_target_pairs={{0,8},{4,12},{8,0},{12,4},{1,9},{5,13},{9,1},{13,5},{2,10},{6,14},... | collective-permute-start | bytes 3637256 | tf_op jit(solution)/shard_map/ppermute | solution.py:425
  697.0 51.7 %collective-permute-start.77 = (bf16[2,2,592,256]{3,2,1,0:T(8,128)(2,1)}, bf16[2,2,592,256]{3,2,1,0:T(8,128)(2,1)S(1)}, u32[]{:S(2)}, u32[]{:S(2)}) collective-permute-start(bf16[2,2,592,256]{3,2,1,0:T(8,128)(2,1)} %get-tuple-element.266), channel_id=1, source_target_pairs={{0,4},{4,0},{8,12},{12,8},{1,5},{5,1},{9,13},{13,9},{2,6},{6,2},{1... | collective-permute-start | bytes 3637256 | tf_op jit(solution)/shard_map/ppermute | solution.py:425
  698.4 52.8 %collective-permute-start.78 = (bf16[2,2,592,256]{3,2,1,0:T(8,128)(2,1)}, bf16[2,2,592,256]{3,2,1,0:T(8,128)(2,1)S(1)}, u32[]{:S(2)}, u32[]{:S(2)}) collective-permute-start(bf16[2,2,592,256]{3,2,1,0:T(8,128)(2,1)} %get-tuple-element.268), channel_id=1, source_target_pairs={{0,8},{4,12},{8,0},{12,4},{1,9},{5,13},{9,1},{13,5},{2,10},{6,14},... | collective-permute-start | bytes 3637256 | tf_op jit(solution)/shard_map/ppermute | solution.py:425
  761.2 27.4 %collective-permute-start.83 = (bf16[2,128,768]{2,1,0:T(8,128)(2,1)S(1)}, bf16[2,128,768]{2,1,0:T(8,128)(2,1)}, u32[]{:S(2)}, u32[]{:S(2)}) collective-permute-start(bf16[2,128,768]{2,1,0:T(8,128)(2,1)S(1)} %pad_maximum_fusion.20), channel_id=1, source_target_pairs={{0,8},{4,12},{8,0},{12,4},{1,9},{5,13},{9,1},{13,5},{2,10},{6,14},... | collective-permute-start | bytes 1179656 | tf_op jit(solution)/shard_map/ppermute | solution.py:425
  762.0 26.7 %collective-permute-start.82 = (bf16[2,128,768]{2,1,0:T(8,128)(2,1)S(1)}, bf16[2,128,768]{2,1,0:T(8,128)(2,1)S(1)}, u32[]{:S(2)}, u32[]{:S(2)}) collective-permute-start(bf16[2,128,768]{2,1,0:T(8,128)(2,1)S(1)} %pad_maximum_fusion.19), channel_id=1, source_target_pairs={{0,4},{4,0},{8,12},{12,8},{1,5},{5,1},{9,13},{13,9},{2,6},{6,2},{1... | collective-permute-start | bytes 1179656 | tf_op jit(solution)/shard_map/ppermute | solution.py:425
  764.7 22.4 %collective-permute-start.81 = (bf16[2,592,256]{2,1,0:T(8,128)(2,1)S(1)}, bf16[2,592,256]{2,1,0:T(8,128)(2,1)}, u32[]{:S(2)}, u32[]{:S(2)}) collective-permute-start(bf16[2,592,256]{2,1,0:T(8,128)(2,1)S(1)} %fusion.71), channel_id=1, source_target_pairs={{0,4},{4,0},{8,12},{12,8},{1,5},{5,1},{9,13},{13,9},{2,6},{6,2},{1... | collective-permute-start | bytes 1818632 | tf_op jit(solution)/shard_map/ppermute | solution.py:425
  766.6 22.0 %collective-permute-start.80 = (bf16[2,592,256]{2,1,0:T(8,128)(2,1)S(1)}, bf16[2,592,256]{2,1,0:T(8,128)(2,1)}, u32[]{:S(2)}, u32[]{:S(2)}) collective-permute-start(bf16[2,592,256]{2,1,0:T(8,128)(2,1)S(1)} %fusion.70), channel_id=1, source_target_pairs={{0,8},{4,12},{8,0},{12,4},{1,9},{5,13},{9,1},{13,5},{2,10},{6,14},... | collective-permute-start | bytes 1818632 | tf_op jit(solution)/shard_map/ppermute | solution.py:425
  768.9 55.4 %collective-permute-start.86 = (bf16[2,592,256]{2,1,0:T(8,128)(2,1)S(1)}, bf16[2,592,256]{2,1,0:T(8,128)(2,1)S(1)}, u32[]{:S(2)}, u32[]{:S(2)}) collective-permute-start(bf16[2,592,256]{2,1,0:T(8,128)(2,1)S(1)} %fusion.73), channel_id=1, source_target_pairs={{0,4},{4,0},{8,12},{12,8},{1,5},{5,1},{9,13},{13,9},{2,6},{6,2},{1... | collective-permute-start | bytes 1818632 | tf_op jit(solution)/shard_map/ppermute | solution.py:425
  787.2 39.5 %collective-permute-start.85 = (bf16[2,592,256]{2,1,0:T(8,128)(2,1)S(1)}, bf16[2,592,256]{2,1,0:T(8,128)(2,1)S(1)}, u32[]{:S(2)}, u32[]{:S(2)}) collective-permute-start(bf16[2,592,256]{2,1,0:T(8,128)(2,1)S(1)} %fusion.72), channel_id=1, source_target_pairs={{0,8},{4,12},{8,0},{12,4},{1,9},{5,13},{9,1},{13,5},{2,10},{6,14},... | collective-permute-start | bytes 1818632 | tf_op jit(solution)/shard_map/ppermute | solution.py:425
  788.8 38.2 %collective-permute-start.87 = (bf16[128,768]{1,0:T(8,128)(2,1)S(1)}, bf16[128,768]{1,0:T(8,128)(2,1)S(1)}, u32[]{:S(2)}, u32[]{:S(2)}) collective-permute-start(bf16[128,768]{1,0:T(8,128)(2,1)S(1)} %fusion.114), channel_id=1, source_target_pairs={{0,8},{4,12},{8,0},{12,4},{1,9},{5,13},{9,1},{13,5},{2,10},{6,14},... | collective-permute-start | bytes 589832 | tf_op jit(solution)/shard_map/ppermute | solution.py:425
  789.6 33.8 %collective-permute-start.84 = (bf16[512,1024]{1,0:T(8,128)(2,1)S(1)}, bf16[512,1024]{1,0:T(8,128)(2,1)S(1)}, u32[]{:S(2)}, u32[]{:S(2)}) collective-permute-start(bf16[512,1024]{1,0:T(8,128)(2,1)S(1)} %fusion.65), channel_id=1, source_target_pairs={{0,1},{1,0},{2,3},{3,2},{4,5},{5,4},{6,7},{7,6},{8,9},{9,8},{10,11... | collective-permute-start | bytes 3145736 | tf_op jit(solution)/shard_map/ppermute | solution.py:419
  794.1 37.2 %collective-permute-start.89 = (bf16[1184,256]{1,0:T(8,128)(2,1)S(1)}, bf16[1184,256]{1,0:T(8,128)(2,1)S(1)}, u32[]{:S(2)}, u32[]{:S(2)}) collective-permute-start(bf16[1184,256]{1,0:T(8,128)(2,1)S(1)} %get-tuple-element.395), channel_id=1, source_target_pairs={{0,2},{1,3},{2,0},{3,1},{4,6},{5,7},{6,4},{7,5},{8,10},{9,11},{10,... | collective-permute-start | bytes 1818632 | tf_op jit(solution)/shard_map/ppermute | solution.py:422
  832.3 19.9 %collective-permute-start.93 = (bf16[256,768]{1,0:T(8,128)(2,1)S(1)}, bf16[256,768]{1,0:T(8,128)(2,1)S(1)}, u32[]{:S(2)}, u32[]{:S(2)}) collective-permute-start(bf16[256,768]{1,0:T(8,128)(2,1)S(1)} %pad_maximum_fusion.21), channel_id=1, source_target_pairs={{16,2},{17,3},{18,0},{19,1},{20,6},{21,7},{22,4},{23,5},{24,10},{2... | collective-permute-start | bytes 1179656 | tf_op jit(solution)/shard_map/ppermute | solution.py:409
  833.9 22.2 %collective-permute-start.91 = (bf16[1184,256]{1,0:T(8,128)(2,1)S(1)}, bf16[1184,256]{1,0:T(8,128)(2,1)S(1)}, u32[]{:S(2)}, u32[]{:S(2)}) collective-permute-start(bf16[1184,256]{1,0:T(8,128)(2,1)S(1)} %fusion.74), channel_id=1, source_target_pairs={{0,3},{1,0},{2,1},{3,2},{4,7},{5,4},{6,5},{7,6},{8,11},{9,8},{10,9... | collective-permute-start | bytes 1818632 | tf_op jit(solution)/shard_map/ppermute | solution.py:422
  860.0 36.6 %collective-permute-start.95 = (bf16[1184,256]{1,0:T(8,128)(2,1)S(1)}, bf16[1184,256]{1,0:T(8,128)(2,1)S(1)}, u32[]{:S(2)}, u32[]{:S(2)}) collective-permute-start(bf16[1184,256]{1,0:T(8,128)(2,1)S(1)} %fusion.33), channel_id=1, source_target_pairs={{0,4},{4,0},{8,12},{12,8},{1,5},{5,1},{9,13},{13,9},{2,6},{6,2},{1... | collective-permute-start | bytes 1818632 | tf_op jit(solution)/shard_map/ppermute | solution.py:425
  860.8 35.8 %collective-permute-start.96 = (bf16[1184,256]{1,0:T(8,128)(2,1)S(1)}, bf16[1184,256]{1,0:T(8,128)(2,1)S(1)}, u32[]{:S(2)}, u32[]{:S(2)}) collective-permute-start(bf16[1184,256]{1,0:T(8,128)(2,1)S(1)} %fusion.33), channel_id=1, source_target_pairs={{0,8},{4,12},{8,0},{12,4},{1,9},{5,13},{9,1},{13,5},{2,10},{6,14},... | collective-permute-start | bytes 1818632 | tf_op jit(solution)/shard_map/ppermute | solution.py:425
  863.6 20.1 %collective-permute-start.97 = (bf16[256,768]{1,0:T(8,128)(2,1)S(1)}, bf16[256,768]{1,0:T(8,128)(2,1)S(1)}, u32[]{:S(2)}, u32[]{:S(2)}) collective-permute-start(bf16[256,768]{1,0:T(8,128)(2,1)S(1)} %get-tuple-element.338), channel_id=1, source_target_pairs={{0,4},{4,0},{8,12},{12,8},{1,5},{5,1},{9,13},{13,9},{2,6},{6,2},{1... | collective-permute-start | bytes 1179656 | tf_op jit(solution)/shard_map/ppermute | solution.py:425
  864.8 31.8 %collective-permute-start.103 = (bf16[512,1024]{1,0:T(8,128)(2,1)S(1)}, bf16[512,1024]{1,0:T(8,128)(2,1)S(1)}, u32[]{:S(2)}, u32[]{:S(2)}) collective-permute-start(bf16[512,1024]{1,0:T(8,128)(2,1)S(1)} %get-tuple-element.307), channel_id=1, source_target_pairs={{16,2},{17,3},{18,0},{19,1},{20,6},{21,7},{22,4},{23,5},{24,10},{2... | collective-permute-start | bytes 3145736 | tf_op jit(solution)/shard_map/ppermute | solution.py:409
  866.2 19.1 %collective-permute-start.98 = (bf16[256,768]{1,0:T(8,128)(2,1)S(1)}, bf16[256,768]{1,0:T(8,128)(2,1)S(1)}, u32[]{:S(2)}, u32[]{:S(2)}) collective-permute-start(bf16[256,768]{1,0:T(8,128)(2,1)S(1)} %get-tuple-element.338), channel_id=1, source_target_pairs={{0,8},{4,12},{8,0},{12,4},{1,9},{5,13},{9,1},{13,5},{2,10},{6,14},... | collective-permute-start | bytes 1179656 | tf_op jit(solution)/shard_map/ppermute | solution.py:425
  885.3 22.0 %collective-permute-start.104 = (bf16[1184,256]{1,0:T(8,128)(2,1)S(1)}, bf16[1184,256]{1,0:T(8,128)(2,1)S(1)}, u32[]{:S(2)}, u32[]{:S(2)}) collective-permute-start(bf16[1184,256]{1,0:T(8,128)(2,1)S(1)} %fusion.33), channel_id=1, source_target_pairs={{0,12},{4,8},{8,4},{12,0},{1,13},{5,9},{9,5},{13,1},{2,14},{6,10},... | collective-permute-start | bytes 1818632 | tf_op jit(solution)/shard_map/ppermute | solution.py:425
  (169 other events, 1703.1 us)
Sparse Core Ops, SparseCore 0:
  144.5 160.8 all-gather.2
